TPU v7x, 32 devices: a whole 2x2x4 slice. The times are simulated.
32 devices in a mesh: rows: 8 (over z, y), cols: 4 (over x, core).
Axes of the slice: x: 2, y: 2, z: 4, core: 2. Of those that a mesh axis runs over, the one named last changes fastest.
Arguments:
- features: bfloat16 [96, 640, 256], P('rows', 'cols'), may hold values from -6 to 6
- weight: bfloat16 [3, 3, 256, 128], replicated, may hold values from -0.125 to 0.125
- cotangent: bfloat16 [96, 640, 128], P('rows', 'cols'), may hold values from -6 to 6
Outputs:
- conv_out: bfloat16 [96, 640, 128], P('rows', 'cols')
- input_grad: bfloat16 [96, 640, 256], P('rows', 'cols')
- weight_grad: float32 [3, 3, 256, 128], replicated
All inputs are finite; a program needn't handle non-finite values.
Results may differ from a plain program's by a relative error of at most 0.001.
Values may be sent and summed in bfloat16 or wider, within the bound.
No kernel may reach another device: no remote copies, remote signals or barrier semaphores. Data moves between devices by JAX's collectives and lax.ppermute only.
A program may use at most 64 MiB of HBM per device.

v0:
```python
import jax
import jax.numpy as jnp
from jax import lax
from jax.sharding import PartitionSpec as P

DILATION_STEP = 12


def extended(cells, sides, width):
    for axis, dim in sides:
        count = lax.axis_size(axis)
        ends = count - 1
        head = lax.slice_in_dim(cells, 0, width, axis=dim)
        tail = lax.slice_in_dim(cells, cells.shape[dim] - width, cells.shape[dim], axis=dim)
        cells = jnp.concatenate(
            [
                lax.ppermute(tail, axis, [(i, (i + 1) % count) for i in range(ends)]),
                cells,
                lax.ppermute(head, axis, [((i + 1) % count, i) for i in range(ends)]),
            ],
            axis=dim,
        )
    return cells


def window(border_padded, row_offset_tap, column_offset_tap, map_height, map_width):
    return border_padded[
        DILATION_STEP * row_offset_tap : DILATION_STEP * row_offset_tap + map_height,
        DILATION_STEP * column_offset_tap : DILATION_STEP * column_offset_tap + map_width,
    ]


def body(features, weight, cotangent):
    map_height, map_width = (features.shape[0], features.shape[1])
    cin, cout = (weight.shape[2], weight.shape[3])
    stacked = jnp.concatenate([features, cotangent], axis=2)
    border_padded = extended(stacked, (("rows", 0), ("cols", 1)), DILATION_STEP)
    padded_feature_map = border_padded[:, :, :cin]
    padded_gradient_map = border_padded[:, :, cin:]
    flat_grad = cotangent.reshape(map_height * map_width, cout)
    output = jnp.zeros((map_height * map_width, cout), jnp.float32)
    back = jnp.zeros((map_height * map_width, cin), jnp.float32)
    kernels = []
    for row_offset_tap in range(3):
        for column_offset_tap in range(3):
            tap_weight = weight[row_offset_tap, column_offset_tap]
            piece = window(
                padded_feature_map, row_offset_tap, column_offset_tap, map_height, map_width
            ).reshape(map_height * map_width, cin)
            output = output + jnp.dot(piece, tap_weight, preferred_element_type=jnp.float32)
            gpiece = window(
                padded_gradient_map,
                2 - row_offset_tap,
                2 - column_offset_tap,
                map_height,
                map_width,
            ).reshape(map_height * map_width, cout)
            back = back + jnp.dot(gpiece, tap_weight.T, preferred_element_type=jnp.float32)
            kernels.append(jnp.dot(piece.T, flat_grad, preferred_element_type=jnp.float32))
    partial_kernel = jnp.stack(kernels).reshape(3, 3, cin, cout)
    total_kernel = lax.psum(partial_kernel, ("rows", "cols"))
    pixels = map_height * lax.axis_size("rows") * map_width * lax.axis_size("cols")
    weight_grad = total_kernel * (1.0 / jnp.sqrt(jnp.float32(pixels)))
    conv_out = output.reshape(map_height, map_width, cout).astype(jnp.bfloat16)
    input_grad = back.reshape(map_height, map_width, cin).astype(jnp.bfloat16)
    return (conv_out, input_grad, weight_grad)


def solution(mesh):
    placed = (P("rows", "cols", None), P(), P("rows", "cols", None))
    return jax.shard_map(
        body,
        mesh=mesh,
        in_specs=placed,
        out_specs=(P("rows", "cols", None), P("rows", "cols", None), P()),
        check_vma=False,
    )
```

profile of v0, /device:TPU:0, one launch (start us, length us, event | category | flops | bytes accessed | tf_op | source)
XLA Modules:
  0.0 250.1 jit_solution(2010681842136582406)
XLA Ops:
  7.2 1.4 constant_dynamic-update-slice_fusion.1
  8.7 0.1 constant_dynamic-update-slice_fusion
  8.8 1.3 collective-permute-start.1
  10.1 5.6 %collective-permute-start = (bf16[12,160,384]{2,1,0:T(8,128)(2,1)S(1)}, bf16[12,160,384]{2,1,0:T(8,128)(2,1)S(1)}, u32[]{:S(2)}, u32[]{:S(2)}) collective-permute-start(bf16[12,160,384]{2,1,0:T(8,128)(2,1)S(1)} %constant_dynamic-update-slice_fusion), channel_id=1, source_target_pairs={{0,4},{4,8},{8,12},{12,16},{16,20},{20,24},{24,28},{1,5},{5,9},{9,... | collective-permute-start | bytes 4423688 | tf_op jit(solution)/shard_map/ppermute | solution.py:17
  15.7 1.4 fusion.39
  17.1 0.4 fusion.37
  17.5 28.4 %collective-permute-done.1 = bf16[12,160,384]{2,1,0:T(8,128)(2,1)S(1)} collective-permute-done((bf16[12,160,384]{2,1,0:T(8,128)(2,1)S(1)}, bf16[12,160,384]{2,1,0:T(8,128)(2,1)S(1)}, u32[]{:S(2)}, u32[]{:S(2)}) %collective-permute-start.1) | collective-permute-done | bytes 1474592 | tf_op jit(solution)/shard_map/ppermute | solution.py:19
  45.9 31.8 %collective-permute-done = bf16[12,160,384]{2,1,0:T(8,128)(2,1)S(1)} collective-permute-done((bf16[12,160,384]{2,1,0:T(8,128)(2,1)S(1)}, bf16[12,160,384]{2,1,0:T(8,128)(2,1)S(1)}, u32[]{:S(2)}, u32[]{:S(2)}) %collective-permute-start) | collective-permute-done | bytes 1474592 | tf_op jit(solution)/shard_map/ppermute | solution.py:17
  77.7 0.1 pad_maximum_fusion.9
  77.8 1.3 collective-permute-start.3
  79.2 1.4 fusion.29
  80.6 3.0 %collective-permute-start.2 = (bf16[36,12,384]{2,1,0:T(8,128)(2,1)S(1)}, bf16[36,12,384]{2,1,0:T(8,128)(2,1)S(1)}, u32[]{:S(2)}, u32[]{:S(2)}) collective-permute-start(bf16[36,12,384]{2,1,0:T(8,128)(2,1)S(1)} %get-tuple-element.17), channel_id=1, source_target_pairs={{0,1},{1,2},{2,3},{4,5},{5,6},{6,7},{8,9},{9,10},{10,11},{12,13},{... | collective-permute-start | bytes 995336 | tf_op jit(solution)/shard_map/ppermute | solution.py:17
  83.7 1.4 fusion.51
  85.1 1.2 pad_maximum_fusion.6
  86.3 1.7 fusion.31
  88.0 1.7 fusion.41
  89.7 1.6 pad_maximum_fusion.3
  91.3 1.7 fusion.23
  93.0 1.7 fusion.45
  94.8 1.8 fusion.49
  96.5 2.1 maximum_maximum_fusion
  98.6 0.5 fusion.22
  99.1 2.8 %fusion.81 = (bf16[12,160,256]{2,1,0:T(8,128)(2,1)}, bf16[12,160,256]{2,1,0:T(8,128)(2,1)S(1)}, bf16[12,160,256]{2,1,0:T(8,128)(2,1)}, bf16[12,160,256]{2,1,0:T(...) fusion(bf16[36,172,384]{2,1,0:T(8,128)(2,1)S(1)} %get-tuple-element.16, ...), kind=kLoop, calls=%fused_computation.108 | loop fusion | bytes 11796480 | tf_op jit(solution)/shard_map/slice | solution.py:27
  101.9 0.5 fusion.21
  102.4 0.5 fusion.20
  102.9 0.5 fusion.19
  103.4 0.5 fusion.18
  103.8 0.5 fusion.17
  104.3 0.5 fusion.16
  104.8 0.5 fusion.15
  105.3 0.5 fusion.14
  105.8 1.4 fusion.25
  107.2 1.8 fusion.47
  109.0 1.8 fusion.43
  110.8 0.4 fusion.33
  111.2 0.3 copy-done.1
  111.5 1.9 fusion.5
  113.5 0.4 fusion.12
  113.9 0.8 copy-done.7
  114.7 0.3 copy-done.9
  115.0 0.3 copy-done.12
  115.3 1.3 fusion.13
  116.6 0.4 fusion.27
  117.0 0.2 copy-done.4
  117.2 1.1 copy-done.3
  118.3 1.5 fusion.6
  119.8 121.1 %all-reduce.2.cloned.1.call-done = f32[3,3,256,128]{3,2,1,0:T(8,128)} async-done(((f32[3,3,256,128]{3,2,1,0:T(8,128)}), f32[3,3,256,128]{3,2,1,0:T(8,128)}) %all-reduce.2.cloned.1.call-update) | async-done | bytes 1179664 | tf_op jit(solution)/shard_map/psum | solution.py:61
  240.9 2.4 broadcast_multiply_fusion
  (38 shorter events, 0.4 us)
Async XLA Ops:
  7.2 8.5 %copy-start.5 = (bf16[12,160,256]{2,1,0:T(8,128)(2,1)S(1)}, bf16[12,160,256]{2,1,0:T(8,128)(2,1)}, u32[]{:S(2)}) copy-start(bf16[12,160,256]{2,1,0:T(8,128)(2,1)} %param.3) | copy-start | bytes 2949124
  7.2 1.5 copy-start.14
  7.2 8.5 %copy-start.13 = (bf16[3,3,256,128]{3,2,1,0:T(8,128)(2,1)S(1)}, bf16[3,3,256,128]{3,2,1,0:T(8,128)(2,1)}, u32[]{:S(2)}) copy-start(bf16[3,3,256,128]{3,2,1,0:T(8,128)(2,1)} %param.4) | copy-start | bytes 1769476
  7.2 233.7 %all-reduce.2.cloned.1.call-start = ((), (), s32[]{:S(2)}) async-start(), calls=%async_computation | async-start | bytes 2359296 | tf_op jit(solution)/shard_map/psum | solution.py:61
  8.7 8.5 %copy-start.15 = (bf16[12,160,128]{2,1,0:T(8,128)(2,1)S(1)}, bf16[12,160,128]{2,1,0:T(8,128)(2,1)}, u32[]{:S(2)}) copy-start(bf16[12,160,128]{2,1,0:T(8,128)(2,1)} %param.5) | copy-start | bytes 1474564
  8.8 37.2 %collective-permute-start.1 = (bf16[12,160,384]{2,1,0:T(8,128)(2,1)S(1)}, bf16[12,160,384]{2,1,0:T(8,128)(2,1)S(1)}, u32[]{:S(2)}, u32[]{:S(2)}) collective-permute-start(bf16[12,160,384]{2,1,0:T(8,128)(2,1)S(1)} %constant_dynamic-update-slice_fusion), channel_id=1, source_target_pairs={{4,0},{8,4},{12,8},{16,12},{20,16},{24,20},{28,24},{5,1},{9,5},{13... | collective-permute-start | bytes 4423688 | tf_op jit(solution)/shard_map/ppermute | solution.py:19
  10.1 67.6 %collective-permute-start = (bf16[12,160,384]{2,1,0:T(8,128)(2,1)S(1)}, bf16[12,160,384]{2,1,0:T(8,128)(2,1)S(1)}, u32[]{:S(2)}, u32[]{:S(2)}) collective-permute-start(bf16[12,160,384]{2,1,0:T(8,128)(2,1)S(1)} %constant_dynamic-update-slice_fusion), channel_id=1, source_target_pairs={{0,4},{4,8},{8,12},{12,16},{16,20},{20,24},{24,28},{1,5},{5,9},{9,... | collective-permute-start | bytes 4423688 | tf_op jit(solution)/shard_map/ppermute | solution.py:17
  77.8 7.2 %collective-permute-start.3 = (bf16[36,12,384]{2,1,0:T(8,128)(2,1)S(1)}, bf16[36,12,384]{2,1,0:T(8,128)(2,1)S(1)}, u32[]{:S(2)}, u32[]{:S(2)}) collective-permute-start(bf16[36,12,384]{2,1,0:T(8,128)(2,1)S(1)} %get-tuple-element.18), channel_id=1, source_target_pairs={{1,0},{2,1},{3,2},{5,4},{6,5},{7,6},{9,8},{10,9},{11,10},{13,12},{... | collective-permute-start | bytes 995336 | tf_op jit(solution)/shard_map/ppermute | solution.py:19
  80.6 9.1 %collective-permute-start.2 = (bf16[36,12,384]{2,1,0:T(8,128)(2,1)S(1)}, bf16[36,12,384]{2,1,0:T(8,128)(2,1)S(1)}, u32[]{:S(2)}, u32[]{:S(2)}) collective-permute-start(bf16[36,12,384]{2,1,0:T(8,128)(2,1)S(1)} %get-tuple-element.17), channel_id=1, source_target_pairs={{0,1},{1,2},{2,3},{4,5},{5,6},{6,7},{8,9},{9,10},{10,11},{12,13},{... | collective-permute-start | bytes 995336 | tf_op jit(solution)/shard_map/ppermute | solution.py:17
  105.8 1.4 copy-start.18
  107.2 3.6 %copy-start.11 = (bf16[12,160,256]{2,1,0:T(8,128)(2,1)S(1)}, bf16[12,160,256]{2,1,0:T(8,128)(2,1)}, u32[]{:S(2)}) copy-start(bf16[12,160,256]{2,1,0:T(8,128)(2,1)} %get-tuple-element.22) | copy-start | bytes 2949124
  107.2 4.0 %copy-start.2 = (f32[1920,256]{1,0:T(8,128)S(1)}, f32[1920,256]{1,0:T(8,128)}, u32[]{:S(2)}) copy-start(f32[1920,256]{1,0:T(8,128)} %fusion.49) | copy-start | bytes 5898244
  109.0 2.2 copy-start
  109.0 2.5 %copy-start.1 = (f32[1920,256]{1,0:T(8,128)S(1)}, f32[1920,256]{1,0:T(8,128)}, u32[]{:S(2)}) copy-start(f32[1920,256]{1,0:T(8,128)} %fusion.45) | copy-start | bytes 5898244
  111.5 1.9 copy-start.6
  111.5 1.9 copy-start.8
  111.5 1.9 copy-start.10
  113.5 1.2 copy-start.7
  113.5 1.5 copy-start.9
  113.5 1.8 copy-start.12
  115.3 1.3 copy-start.16
  115.3 1.9 copy-start.4
  116.6 1.7 copy-start.3
  116.6 1.8 copy-start.17
Sparse Core Ops, SparseCore 0:
  107.3 133.5 all-reduce.1
where the time goes:
time: 250 us
  waiting for transfers between devices  181 us (72%)
  matrix products  28.2 us (11%)
  between operations  14.4 us (6%)
  starting transfers between devices  11.3 us (5%)
  local copies, waits for them, and re-layouts  7.58 us (3%)
  other arithmetic  7.45 us (3%)
    psum x1, waiting for transfers between devices, body(): total_kernel = lax.psum(partial_kernel, ('rows', 'cols'))  121 us
    ppermute x2, waiting for transfers between devices, extended(): lax.ppermute(tail, axis, [(i, (i + 1) % count) for i in range(ends)])  31.8 us
    ppermute x2, waiting for transfers between devices, extended(): lax.ppermute(head, axis, [((i + 1) % count, i) for i in range(ends)])  28.4 us
    dot_general x9, matrix products, body(): jnp.dot(gpiece, tap_weight.T, preferred_element_type=jnp.float32)  12.8 us
    dot_general x9, matrix products, body(): jnp.dot(piece, tap_weight, preferred_element_type=jnp.float32)  11.1 us
    ppermute x2, starting transfers between devices, extended(): lax.ppermute(tail, axis, [(i, (i + 1) % count) for i in range(ends)])  8.64 us
  transfers between devices with their start and end apart: 5, of which 3 were waited for; matrix products, arithmetic and copies ran while one was open for 7% of the time, Pallas kernels for 0%

commit v1 on v0

v1 whole, which is shorter than its diff:
```python
import jax
import jax.numpy as jnp
from jax import lax
from jax.sharding import Mesh
from jax.sharding import PartitionSpec as P

DILATION_STEP = 12
COLS = ("x", "core")
ALL = ("rows", "x", "core")


def column_extended(cells, width):
    count = lax.axis_size("x") * lax.axis_size("core")
    head = cells[:, :width]
    tail = cells[:, cells.shape[1] - width :]
    left = lax.ppermute(tail, COLS, [(i, i + 1) for i in range(count - 1)])
    right = lax.ppermute(head, COLS, [(i + 1, i) for i in range(count - 1)])
    return left, right


def row_blocks(cells, odd):
    count = lax.axis_size("rows")
    partner = lax.ppermute(cells, "rows", [(i, i ^ 1) for i in range(count)])
    steps = [(i, i - 2 if i % 2 else i + 2) for i in range(count)]
    far = lax.ppermute(partner, "rows", [(i, j) for i, j in steps if 0 <= j < count])
    return partner, far


def stacked(partner, cells, far, odd):
    above = jnp.where(odd, partner, far)
    below = jnp.where(odd, far, partner)
    return jnp.concatenate([above, cells, below], axis=0)


def total(part):
    size = part.shape[0]
    half = size // 2
    core = lax.axis_index("core")
    keep = lax.dynamic_slice_in_dim(part, core * half, half, 0)
    give = lax.dynamic_slice_in_dim(part, (1 - core) * half, half, 0)
    keep = keep + lax.ppermute(give, "core", [(0, 1), (1, 0)])
    chips = lax.axis_size("rows") * lax.axis_size("x")
    pieces = keep.reshape(chips, half // chips, part.shape[1])
    mine = lax.all_to_all(pieces, ("rows", "x"), 0, 0).sum(axis=0)
    own = lax.all_gather(mine, ("rows", "x"), axis=0, tiled=True)
    other = lax.ppermute(own, "core", [(0, 1), (1, 0)])
    first = core == 0
    return jnp.concatenate([jnp.where(first, own, other), jnp.where(first, other, own)], axis=0)


def body(features, weight, cotangent):
    height, width, cin = features.shape
    cout = weight.shape[3]
    pixels = height * width
    step = DILATION_STEP
    odd = lax.axis_index("rows") % 2 == 1

    both = jnp.concatenate([features, cotangent], axis=2)
    left, right = column_extended(both, step)
    grads = jnp.concatenate([left[:, :, cin:], cotangent, right[:, :, cin:]], axis=1)
    cells = jnp.concatenate([left[:, :, :cin], features, right[:, :, :cin]], axis=1)

    grad_map = stacked(*((lambda p: (p[0], grads, p[1]))(row_blocks(grads, odd))), odd)
    flat = features.reshape(pixels, cin)
    kernels = []
    back = jnp.zeros((pixels, cin), jnp.float32)
    windows = []
    for a in range(3):
        for b in range(3):
            piece = grad_map[step * (2 - a) : step * (2 - a) + height, step * (2 - b) : step * (2 - b) + width]
            piece = piece.reshape(pixels, cout)
            windows.append(piece)
            kernels.append(jnp.dot(flat.T, piece, preferred_element_type=jnp.float32))
    part = jnp.stack(kernels).reshape(9 * cin, cout)
    count = pixels
    for axis in ALL:
        count = count * lax.axis_size(axis)
    weight_grad = (total(part) * (1.0 / jnp.sqrt(jnp.float32(count)))).reshape(weight.shape)

    for t in range(9):
        back = back + jnp.dot(windows[t], weight[t // 3, t % 3].T, preferred_element_type=jnp.float32)
    input_grad = back.reshape(height, width, cin).astype(jnp.bfloat16)

    cell_map = stacked(*((lambda p: (p[0], cells, p[1]))(row_blocks(cells, odd))), odd)
    out = jnp.zeros((pixels, cout), jnp.float32)
    for a in range(3):
        for b in range(3):
            piece = cell_map[step * a : step * a + height, step * b : step * b + width].reshape(pixels, cin)
            out = out + jnp.dot(piece, weight[a, b], preferred_element_type=jnp.float32)
    conv_out = out.reshape(height, width, cout).astype(jnp.bfloat16)
    return conv_out, input_grad, weight_grad


def solution(mesh):
    rows, cols = (mesh.shape["rows"], mesh.shape["cols"])
    fine = Mesh(mesh.devices.reshape(rows, cols // 2, 2), ALL)
    placed = P("rows", COLS, None)
    return jax.shard_map(
        body,
        mesh=fine,
        in_specs=(placed, P(), placed),
        out_specs=(placed, placed, P()),
        check_vma=False,
    )
```

time: 250 us -> 155 us (0.62)
  waiting for transfers between devices: 181 us -> 41.8 us
  blocking collectives: 0 us -> 44.2 us
  between operations: 14.4 us -> 0.98 us
  starting transfers between devices: 11.3 us -> 20.6 us
  local copies, waits for them, and re-layouts: 7.58 us -> 12.4 us
  matrix products: 28.2 us -> 24.8 us
    psum x1 -> x0, waiting for transfers between devices: 121 us -> none  [body(): total_kernel = lax.psum(partial_kernel, ('rows', 'cols'))]
    all_gather x0 -> x1, blocking collectives: none -> 44.2 us  [total(): own = lax.all_gather(mine, ('rows', 'x'), axis=0, tiled=True)]
    ppermute x4 -> x8, waiting for transfers between devices: 60.2 us -> 37.3 us  [the longest x2 24.8 us: row_blocks(): lax.ppermute(partner, 'rows', [(i, j) for i, j in steps if 0 <= j < count])]
    all_to_all x0 -> x1, starting transfers between devices: none -> 4.86 us  [total(): mine = lax.all_to_all(pieces, ('rows', 'x'), 0, 0).sum(axis=0)]
    all_to_all x0 -> x1, waiting for transfers between devices: none -> 4.5 us  [total(): mine = lax.all_to_all(pieces, ('rows', 'x'), 0, 0).sum(axis=0)]
    ppermute x4 -> x8, starting transfers between devices: 11.2 us -> 15.7 us  [the longest x2 7.97 us: row_blocks(): lax.ppermute(partner, 'rows', [(i, j) for i, j in steps if 0 <= j < count])]
    dot_general x27, matrix products: 28.2 us -> 24.8 us  [the longest x9 10 us: body(): out = out + jnp.dot(piece, weight[a, b], preferred_element_type=jnp.float32)]
    slice x3 -> x0, other arithmetic: 2.97 us -> none  [the longest x2 2.83 us: window(): border_padded[DILATION_STEP * row_offset_tap:DILATION_STEP * row_offset_t...]
  transfers between devices with their start and end apart: 5 -> 9, of which waited for: 3 -> 5; matrix products, arithmetic and copies ran while one was open for 7% -> 25% of each run, Pallas kernels for 0% -> 0%
where the time goes in v1:
time: 155 us; the launch traced here: 153 us
  blocking collectives  44.2 us (29%)
  waiting for transfers between devices  41.8 us (27%)
  matrix products  24.8 us (16%)
  starting transfers between devices  20.6 us (13%)
  local copies, waits for them, and re-layouts  12.4 us (8%)
  other arithmetic  8.62 us (6%)
    all_gather x1, blocking collectives, total(): own = lax.all_gather(mine, ('rows', 'x'), axis=0, tiled=True)  44.2 us
    ppermute x2, waiting for transfers between devices, row_blocks(): lax.ppermute(partner, 'rows', [(i, j) for i, j in steps if 0 <= j < count])  24.8 us
    dot_general x9, matrix products, body(): out = out + jnp.dot(piece, weight[a, b], preferred_element_type=jnp.float32)  10 us
    dot_general x9, matrix products, body(): kernels.append(jnp.dot(flat.T, piece, preferred_element_type=jnp.float32))  9.05 us
    ppermute x2, waiting for transfers between devices, row_blocks(): partner = lax.ppermute(cells, 'rows', [(i, i ^ 1) for i in range(count)])  8.47 us
    ppermute x2, starting transfers between devices, row_blocks(): lax.ppermute(partner, 'rows', [(i, j) for i, j in steps if 0 <= j < count])  7.97 us
    dot_general x9, matrix products, body(): jnp.dot(windows[t], weight[t // 3, t % 3].T, preferred_element_type=jnp.f...  5.72 us
    unnamed x35, local copies, waits for them, and re-layouts  5.22 us
  transfers between devices with their start and end apart: 9, of which 5 were waited for; matrix products, arithmetic and copies ran while one was open for 25% of the time, Pallas kernels for 0%

profile of v1, /device:TPU:0, one launch (start us, length us, event | category | flops | bytes accessed | tf_op | source)
XLA Modules:
  0.0 153.4 jit_solution(592612157679829164)
XLA Ops:
  0.6 1.3 constant_dynamic-update-slice_fusion.1
  2.2 2.5 %collective-permute-start = (bf16[12,12,384]{2,1,0:T(8,128)(2,1)S(1)}, bf16[12,12,384]{2,1,0:T(8,128)(2,1)S(1)}, u32[]{:S(2)}, u32[]{:S(2)}) collective-permute-start(bf16[12,12,384]{2,1,0:T(8,128)(2,1)S(1)} %get-tuple-element.5), channel_id=1, source_target_pairs={{0,1},{1,2},{2,3},{4,5},{5,6},{6,7},{8,9},{9,10},{10,11},{12,13},{... | collective-permute-start | bytes 331784 | tf_op jit(solution)/shard_map/ppermute | solution.py:16
  4.7 1.3 collective-permute-start.1
  6.0 4.0 %collective-permute-done.1 = bf16[12,12,384]{2,1,0:T(8,128)(2,1)S(1)} collective-permute-done((bf16[12,12,384]{2,1,0:T(8,128)(2,1)S(1)}, bf16[12,12,384]{2,1,0:T(8,128)(2,1)S(1)}, u32[]{:S(2)}, u32[]{:S(2)}) %collective-permute-start.1) | collective-permute-done | bytes 110624 | tf_op jit(solution)/shard_map/ppermute | solution.py:17
  10.2 1.6 %collective-permute-start.4 = (bf16[12,184,128]{2,1,0:T(8,128)(2,1)S(1)}, bf16[12,184,128]{2,1,0:T(8,128)(2,1)}, u32[]{:S(2)}, u32[]{:S(2)}) collective-permute-start(bf16[12,184,128]{2,1,0:T(8,128)(2,1)S(1)} %pad_maximum_fusion.3), channel_id=1, source_target_pairs={{0,4},{4,0},{8,12},{12,8},{16,20},{20,16},{24,28},{28,24},{1,5},{5... | collective-permute-start | bytes 1695752 | tf_op jit(solution)/shard_map/ppermute | solution.py:23
  11.8 1.3 pad_maximum_fusion
  13.1 1.3 pad_maximum_fusion.1
  14.4 8.5 %collective-permute-done.4 = bf16[12,184,128]{2,1,0:T(8,128)(2,1)} collective-permute-done((bf16[12,184,128]{2,1,0:T(8,128)(2,1)S(1)}, bf16[12,184,128]{2,1,0:T(8,128)(2,1)}, u32[]{:S(2)}, u32[]{:S(2)}) %collective-permute-start.4) | collective-permute-done | bytes 565280 | tf_op jit(solution)/shard_map/ppermute | solution.py:23
  22.9 3.5 %collective-permute-start.5 = (bf16[12,184,128]{2,1,0:T(8,128)(2,1)}, bf16[12,184,128]{2,1,0:T(8,128)(2,1)S(1)}, u32[]{:S(2)}, u32[]{:S(2)}) collective-permute-start(bf16[12,184,128]{2,1,0:T(8,128)(2,1)} %collective-permute-done.4), channel_id=1, source_target_pairs={{0,8},{8,16},{12,4},{16,24},{20,12},{28,20},{1,9},{9,17},{13,5},{1... | collective-permute-start | bytes 1695752 | tf_op jit(solution)/shard_map/ppermute | solution.py:25
  26.6 2.3 %fusion.35 = f32[1920,128]{1,0:T(8,128)} fusion(bf16[1920,256]{1,0:T(8,128)(2,1)S(1)} %bitcast.177, bf16[3,3,256,128]{3,2,1,0:T(8,128)(2,1)} %param.4), kind=kOutput, calls=%fused_computation.66 | convolution fusion | flops 125829120 | bytes 2031616 | tf_op jit(solution)/shard_map/dot_general | solution.py:89
  29.0 1.3 fusion.33
  30.2 7.5 %collective-permute-done.5 = bf16[12,184,128]{2,1,0:T(8,128)(2,1)S(1)} collective-permute-done((bf16[12,184,128]{2,1,0:T(8,128)(2,1)}, bf16[12,184,128]{2,1,0:T(8,128)(2,1)S(1)}, u32[]{:S(2)}, u32[]{:S(2)}) %collective-permute-start.5) | collective-permute-done | bytes 565280 | tf_op jit(solution)/shard_map/ppermute | solution.py:25
  37.7 1.1 broadcast_select_fusion.3
  38.9 1.0 fusion.18
  39.9 1.0 fusion.17
  40.9 1.0 fusion.16
  41.9 1.0 fusion.15
  42.9 1.0 fusion.14
  43.9 1.7 %fusion.74 = (bf16[12,160,128]{2,1,0:T(8,128)(2,1)}, bf16[12,160,128]{2,1,0:T(8,128)(2,1)}, bf16[12,160,128]{2,1,0:T(8,128)(2,1)}, bf16[12,160,128]{2,1,0:T(8,12...) fusion(bf16[12,184,128]{2,1,0:T(8,128)(2,1)S(1)} %get-tuple-element.10, ...), kind=kLoop, calls=%fused_computation.108 | loop fusion | bytes 5898240 | tf_op jit(solution)/shard_map/slice | solution.py:70
  45.6 1.0 fusion.13
  46.6 1.0 fusion.12
  47.6 1.0 fusion.11
  48.7 1.0 fusion.10
  49.7 2.7 %copy.8 = f32[9,256,128]{2,1,0:T(8,128)} copy(f32[9,256,128]{1,2,0:T(8,128)} %fusion.10) | data formatting | bytes 2359296 | tf_op jit(solution)/shard_map/stack | solution.py:74
  52.3 1.2 constant_dynamic-slice_fusion
  53.5 2.3 %collective-permute-start.6 = (f32[1152,128]{1,0:T(8,128)S(1)}, f32[1152,128]{1,0:T(8,128)S(1)}, u32[]{:S(2)}, u32[]{:S(2)}) collective-permute-start(f32[1152,128]{1,0:T(8,128)S(1)} %constant_dynamic-slice_fusion), channel_id=1, source_target_pairs={{0,1},{1,0},{2,3},{3,2},{4,5},{5,4},{6,7},{7,6},{8,9},{9,8},{10,11... | collective-permute-start | bytes 1769480 | tf_op jit(solution)/shard_map/ppermute | solution.py:41
  56.2 0.6 copy-done.14
  57.3 0.6 copy-done.13
  58.3 0.6 copy-done.16
  58.9 0.6 fusion.3
  60.0 0.6 copy-done.4
  61.0 4.5 %collective-permute-start.3 = (bf16[12,184,256]{2,1,0:T(8,128)(2,1)}, bf16[12,184,256]{2,1,0:T(8,128)(2,1)S(1)}, u32[]{:S(2)}, u32[]{:S(2)}) collective-permute-start(bf16[12,184,256]{2,1,0:T(8,128)(2,1)} %collective-permute-done.2), channel_id=1, source_target_pairs={{0,8},{8,16},{12,4},{16,24},{20,12},{28,20},{1,9},{9,17},{13,5},{1... | collective-permute-start | bytes 3391496 | tf_op jit(solution)/shard_map/ppermute | solution.py:25
  65.9 0.6 copy-done.11
  66.5 1.4 fusion.4
  67.9 0.9 dynamic-slice_add_fusion
  68.8 4.9 %all-to-all-start = ((f32[16,72,128]{2,1,0:T(8,128)}), f32[16,72,128]{2,1,0:T(8,128)}, u32[]{:S(2)}, u32[]{:S(2)}) async-start(f32[16,72,128]{2,1,0:T(8,128)} %bitcast.56), calls=%async_computation | async-start | bytes 1179648 | tf_op jit(solution)/shard_map/all_to_all | solution.py:44
  73.7 17.3 %collective-permute-done.3 = bf16[12,184,256]{2,1,0:T(8,128)(2,1)S(1)} collective-permute-done((bf16[12,184,256]{2,1,0:T(8,128)(2,1)}, bf16[12,184,256]{2,1,0:T(8,128)(2,1)S(1)}, u32[]{:S(2)}, u32[]{:S(2)}) %collective-permute-start.3) | collective-permute-done | bytes 1130528 | tf_op jit(solution)/shard_map/ppermute | solution.py:25
  91.0 1.4 broadcast_select_fusion.1
  92.4 1.4 fusion.72
  94.7 1.4 fusion.21
  96.9 0.8 copy-done.6
  97.7 1.4 convolution_add_fusion.5
  99.1 4.5 %all-to-all-done = f32[16,72,128]{2,1,0:T(8,128)} async-done(((f32[16,72,128]{2,1,0:T(8,128)}), f32[16,72,128]{2,1,0:T(8,128)}, u32[]{:S(2)}, u32[]{:S(2)}) %all-to-all-start) | async-done | bytes 589856 | tf_op jit(solution)/shard_map/all_to_all | solution.py:44
  103.6 1.1 reduce_sum.9
  104.7 44.2 %all_gather.3 = f32[1152,128]{1,0:T(8,128)S(1)} all-gather(f32[72,128]{1,0:T(8,128)S(1)} %reduce_sum.9), channel_id=1, replica_groups=mesh['rows'=8,'x'=2,'core'=2] {'rows','x'}, dimensions={0}, use_global_device_ids=true | all-gather | bytes 626688 | tf_op jit(solution)/shard_map/all_gather | solution.py:45
  148.9 1.2 fusion.25
  150.2 2.0 %fusion.9 = bf16[1920,128]{1,0:T(8,128)(2,1)} fusion(f32[1920,128]{1,0:T(8,128)S(1)} %copy-done.7, f32[1920,128]{1,0:T(8,128)S(1)} %fusion.25, f32[1920,128]{1,0:T(8,128)S(1)} %copy-done.8, bf16[1920,256]{1,0:T(8,128)(2,1)S(1)} %bitcast.175, bf16[3,3,256,128]{3,2,1,0:T(8,128)(2,1)} %param.4), kind=kOutput, calls=%fused_computation.17 | convolution fusion | flops 126812160 | bytes 4489216 | tf_op jit(solution)/shard_map/dot_general | solution.py:89
  152.3 1.1 maximum_multiply_fusion
  (53 shorter events, 4.9 us)
Async XLA Ops:
  0.6 1.3 copy-start.1
  2.1 9.7 %copy-start = (bf16[12,160,256]{2,1,0:T(8,128)(2,1)S(1)}, bf16[12,160,256]{2,1,0:T(8,128)(2,1)}, u32[]{:S(2)}) copy-start(bf16[12,160,256]{2,1,0:T(8,128)(2,1)} %param.3) | copy-start | bytes 2949124
  2.2 3.8 %collective-permute-start = (bf16[12,12,384]{2,1,0:T(8,128)(2,1)S(1)}, bf16[12,12,384]{2,1,0:T(8,128)(2,1)S(1)}, u32[]{:S(2)}, u32[]{:S(2)}) collective-permute-start(bf16[12,12,384]{2,1,0:T(8,128)(2,1)S(1)} %get-tuple-element.5), channel_id=1, source_target_pairs={{0,1},{1,2},{2,3},{4,5},{5,6},{6,7},{8,9},{9,10},{10,11},{12,13},{... | collective-permute-start | bytes 331784 | tf_op jit(solution)/shard_map/ppermute | solution.py:16
  4.7 5.4 %collective-permute-start.1 = (bf16[12,12,384]{2,1,0:T(8,128)(2,1)S(1)}, bf16[12,12,384]{2,1,0:T(8,128)(2,1)S(1)}, u32[]{:S(2)}, u32[]{:S(2)}) collective-permute-start(bf16[12,12,384]{2,1,0:T(8,128)(2,1)S(1)} %get-tuple-element.6), channel_id=1, source_target_pairs={{1,0},{2,1},{3,2},{5,4},{6,5},{7,6},{9,8},{10,9},{11,10},{13,12},{... | collective-permute-start | bytes 331784 | tf_op jit(solution)/shard_map/ppermute | solution.py:17
  10.2 12.7 %collective-permute-start.4 = (bf16[12,184,128]{2,1,0:T(8,128)(2,1)S(1)}, bf16[12,184,128]{2,1,0:T(8,128)(2,1)}, u32[]{:S(2)}, u32[]{:S(2)}) collective-permute-start(bf16[12,184,128]{2,1,0:T(8,128)(2,1)S(1)} %pad_maximum_fusion.3), channel_id=1, source_target_pairs={{0,4},{4,0},{8,12},{12,8},{16,20},{20,16},{24,28},{28,24},{1,5},{5... | collective-permute-start | bytes 1695752 | tf_op jit(solution)/shard_map/ppermute | solution.py:23
  22.9 14.9 %collective-permute-start.5 = (bf16[12,184,128]{2,1,0:T(8,128)(2,1)}, bf16[12,184,128]{2,1,0:T(8,128)(2,1)S(1)}, u32[]{:S(2)}, u32[]{:S(2)}) collective-permute-start(bf16[12,184,128]{2,1,0:T(8,128)(2,1)} %collective-permute-done.4), channel_id=1, source_target_pairs={{0,8},{8,16},{12,4},{16,24},{20,12},{28,20},{1,9},{9,17},{13,5},{1... | collective-permute-start | bytes 1695752 | tf_op jit(solution)/shard_map/ppermute | solution.py:25
  26.5 19.1 %copy-start.3 = (bf16[12,160,128]{2,1,0:T(8,128)(2,1)}, bf16[12,160,128]{2,1,0:T(8,128)(2,1)S(1)}, u32[]{:S(2)}) copy-start(bf16[12,160,128]{2,1,0:T(8,128)(2,1)S(1)} %get-tuple-element.25) | copy-start | bytes 1474564
  26.6 34.4 %collective-permute-start.2 = (bf16[12,184,256]{2,1,0:T(8,128)(2,1)}, bf16[12,184,256]{2,1,0:T(8,128)(2,1)}, u32[]{:S(2)}, u32[]{:S(2)}) collective-permute-start(bf16[12,184,256]{2,1,0:T(8,128)(2,1)} %pad_maximum_fusion), channel_id=1, source_target_pairs={{0,4},{4,0},{8,12},{12,8},{16,20},{20,16},{24,28},{28,24},{1,5},{5... | collective-permute-start | bytes 3391496 | tf_op jit(solution)/shard_map/ppermute | solution.py:23
  52.3 3.5 %copy-start.9 = (bf16[3,3,256,128]{3,2,1,0:T(8,128)(2,1)S(1)}, bf16[3,3,256,128]{3,2,1,0:T(8,128)(2,1)}, u32[]{:S(2)}) copy-start(bf16[3,3,256,128]{3,2,1,0:T(8,128)(2,1)} %param.4) | copy-start | bytes 1769476
  52.3 3.5 %copy-start.15 = (bf16[12,160,128]{2,1,0:T(8,128)(2,1)S(1)}, bf16[12,160,128]{2,1,0:T(8,128)(2,1)}, u32[]{:S(2)}) copy-start(bf16[12,160,128]{2,1,0:T(8,128)(2,1)} %get-tuple-element.31) | copy-start | bytes 1474564
  53.5 14.4 %collective-permute-start.6 = (f32[1152,128]{1,0:T(8,128)S(1)}, f32[1152,128]{1,0:T(8,128)S(1)}, u32[]{:S(2)}, u32[]{:S(2)}) collective-permute-start(f32[1152,128]{1,0:T(8,128)S(1)} %constant_dynamic-slice_fusion), channel_id=1, source_target_pairs={{0,1},{1,0},{2,3},{3,2},{4,5},{5,4},{6,7},{7,6},{8,9},{9,8},{10,11... | collective-permute-start | bytes 1769480 | tf_op jit(solution)/shard_map/ppermute | solution.py:41
  55.8 1.0 copy-start.14
  56.8 1.0 copy-start.13
  57.9 1.0 copy-start.16
  59.5 1.0 copy-start.4
  60.6 4.9 %copy-start.12 = (bf16[12,160,128]{2,1,0:T(8,128)(2,1)S(1)}, bf16[12,160,128]{2,1,0:T(8,128)(2,1)}, u32[]{:S(2)}) copy-start(bf16[12,160,128]{2,1,0:T(8,128)(2,1)} %get-tuple-element.21) | copy-start | bytes 1474564
  61.0 30.0 %collective-permute-start.3 = (bf16[12,184,256]{2,1,0:T(8,128)(2,1)}, bf16[12,184,256]{2,1,0:T(8,128)(2,1)S(1)}, u32[]{:S(2)}, u32[]{:S(2)}) collective-permute-start(bf16[12,184,256]{2,1,0:T(8,128)(2,1)} %collective-permute-done.2), channel_id=1, source_target_pairs={{0,8},{8,16},{12,4},{16,24},{20,12},{28,20},{1,9},{9,17},{13,5},{1... | collective-permute-start | bytes 3391496 | tf_op jit(solution)/shard_map/ppermute | solution.py:25
  65.5 1.0 copy-start.11
  66.5 1.4 copy-start.2
  68.8 34.8 %all-to-all-start = ((f32[16,72,128]{2,1,0:T(8,128)}), f32[16,72,128]{2,1,0:T(8,128)}, u32[]{:S(2)}, u32[]{:S(2)}) async-start(f32[16,72,128]{2,1,0:T(8,128)} %bitcast.56), calls=%async_computation | async-start | bytes 1179648 | tf_op jit(solution)/shard_map/all_to_all | solution.py:44
  92.4 1.5 copy-start.10
  94.7 1.4 copy-start.5
  96.5 1.2 copy-start.6
  104.7 45.5 %copy-start.7 = (f32[1920,128]{1,0:T(8,128)S(1)}, f32[1920,128]{1,0:T(8,128)}, u32[]{:S(2)}) copy-start(f32[1920,128]{1,0:T(8,128)} %fusion.21) | copy-start | bytes 2949124
  104.7 45.5 %copy-start.8 = (f32[1920,128]{1,0:T(8,128)S(1)}, f32[1920,128]{1,0:T(8,128)}, u32[]{:S(2)}) copy-start(f32[1920,128]{1,0:T(8,128)} %convolution_add_fusion.5) | copy-start | bytes 2949124
  148.9 3.3 %collective-permute-start.7 = (f32[1152,128]{1,0:T(8,128)S(1)}, f32[1152,128]{1,0:T(8,128)S(1)}, u32[]{:S(2)}, u32[]{:S(2)}) collective-permute-start(f32[1152,128]{1,0:T(8,128)S(1)} %all_gather.3), channel_id=1, source_target_pairs={{0,1},{1,0},{2,3},{3,2},{4,5},{5,4},{6,7},{7,6},{8,9},{9,8},{10,11... | collective-permute-start | bytes 1769480 | tf_op jit(solution)/shard_map/ppermute | solution.py:46

commit v2 on v0

v2 whole, which is shorter than its diff:
```python
import functools
import math

import jax
import jax.numpy as jnp
from jax import lax
from jax.experimental import pallas as pl
from jax.experimental.pallas import tpu as pltpu
from jax.sharding import Mesh
from jax.sharding import PartitionSpec as P

DILATION_STEP = 12
STRIP = 16
TOP = 14
ALL = ("rows", "cols")
VMEM = pltpu.VMEM


def slots(odd):
    return (1 + odd, 2 - odd, 3 * (1 - odd), 3 * odd)


def gather_map(odd, blocks, left, right, ext):
    width = blocks[0].shape[1]
    for place, (block, slot) in enumerate(zip(blocks, slots(odd))):
        ext[slot, :, pl.ds(STRIP, width), :] = block[...]
        ext[slot, :, pl.ds(0, STRIP), :] = left[place]
        ext[slot, :, pl.ds(STRIP + width, STRIP), :] = right[place]


def shift_columns(ext, shifted, width):
    cout = ext.shape[3]
    for slot in range(4):
        whole = ext[slot].astype(jnp.float32)
        for q in range(3):
            start = STRIP + DILATION_STEP * (q - 1)
            shifted[slot, :, :, pl.ds(q * cout, cout)] = whole[:, start : start + width].astype(jnp.bfloat16)


def kernel_grad(chunk, par, f_own, f_par, d_own, d_par, d_near, d_far, left, right, out, ext, shifted, acc):
    odd = par[0]
    half, width, cin = f_par.shape
    cout = d_own.shape[2]
    pixels = half * width
    gather_map(odd, (d_own, d_par, d_near, d_far), left, right, ext)
    shift_columns(ext, shifted, width)
    own, partner = slots(odd)[:2]
    top = jnp.zeros((8, cout), jnp.float32)
    for a in range(3):
        total = None
        for block, slot in ((f_own, own), (f_par, partner)):
            lhs = block[...].reshape(pixels, cin)
            rhs = shifted[slot + 1 - a].reshape(pixels, 3 * cout)
            term = lax.dot_general(lhs, rhs, (((0,), (0,)), ((), ())), preferred_element_type=jnp.float32)
            total = term if total is None else total + term
        for b in range(3):
            piece = total[:, (2 - b) * cout : (3 - b) * cout]
            acc[pl.ds((3 * a + b) * cin, cin), :] = piece
            top = jnp.maximum(top, jnp.max(jnp.abs(piece).reshape(cin // 8, 8, cout), axis=0))
    most = jnp.max(jnp.max(top, axis=0, keepdims=True), axis=1, keepdims=True)
    level = jnp.ceil(jnp.log2(jnp.maximum(jnp.broadcast_to(most, (8, cout)), 2.0**-110)))
    scale = jnp.exp2(TOP - level)[:1]
    for c in range(out.shape[0]):
        out[c, pl.ds(0, chunk), :] = acc[pl.ds(c * chunk, chunk), :] * scale
        out[c, pl.ds(chunk, out.shape[1] - chunk), :] = jnp.broadcast_to(level[:1], (out.shape[1] - chunk, cout))


def kernel_back(par, w, d_own, d_par, d_near, d_far, left, right, out_own, out_par, ext, shifted):
    odd = par[0]
    half, width, cout = d_own.shape
    cin = w.shape[2]
    pixels = half * width
    gather_map(odd, (d_own, d_par, d_near, d_far), left, right, ext)
    shift_columns(ext, shifted, width)
    own, partner = slots(odd)[:2]
    for out, slot in ((out_own, own), (out_par, partner)):
        total = None
        for a in range(3):
            lhs = shifted[slot + 1 - a].reshape(pixels, 3 * cout)
            rhs = jnp.concatenate([w[a, 2 - q] for q in range(3)], axis=1)
            term = lax.dot_general(lhs, rhs, (((1,), (1,)), ((), ())), preferred_element_type=jnp.float32)
            total = term if total is None else total + term
        out[...] = total.astype(jnp.bfloat16).reshape(half, width, cin)


def kernel_out(par, w, f_own, f_par, f_near, f_far, left, right, out_own, out_par, ext):
    odd = par[0]
    half, width, cin = f_own.shape
    cout = w.shape[3]
    wide = width + 2 * STRIP
    gather_map(odd, (f_own, f_par, f_near, f_far), left, right, ext)
    own, partner = slots(odd)[:2]
    for out, slot in ((out_own, own), (out_par, partner)):
        total = None
        for a in range(3):
            lhs = ext[slot + a - 1].reshape(half * wide, cin)
            rhs = jnp.concatenate([w[a, b] for b in range(3)], axis=1)
            term = jnp.dot(lhs, rhs, preferred_element_type=jnp.float32)
            total = term if total is None else total + term
        total = total.reshape(half, wide, 3 * cout)
        result = None
        for b in range(3):
            start = STRIP + DILATION_STEP * (b - 1)
            term = total[:, start : start + width, b * cout : (b + 1) * cout]
            result = term if result is None else result + term
        out[...] = result.astype(jnp.bfloat16)


def call(kernel, operands, outs, scratch, flops):
    whole = pl.BlockSpec(memory_space=VMEM)
    size = sum(x.size * x.dtype.itemsize for x in operands) + sum(math.prod(o.shape) * o.dtype.itemsize for o in outs)
    return pl.pallas_call(
        kernel,
        out_shape=outs,
        in_specs=[pl.BlockSpec(memory_space=pltpu.SMEM)] + [whole] * (len(operands) - 1),
        out_specs=[whole] * len(outs),
        scratch_shapes=scratch,
        compiler_params=pltpu.CompilerParams(vmem_limit_bytes=48 * 1024 * 1024),
        cost_estimate=pl.CostEstimate(flops=flops, bytes_accessed=size, transcendentals=0),
    )(*operands)


def strips(blocks, count):
    width = blocks[0].shape[1]
    tails = jnp.stack([x[:, width - STRIP :] for x in blocks])
    heads = jnp.stack([x[:, :STRIP] for x in blocks])
    left = lax.ppermute(tails, "cols", [(i, i + 1) for i in range(count - 1)])
    right = lax.ppermute(heads, "cols", [(i + 1, i) for i in range(count - 1)])
    return left, right


def joined(odd, own, other):
    low = jnp.where(odd == 1, other, own)
    high = jnp.where(odd == 1, own, other)
    return jnp.concatenate([low, high], axis=0)


def body(features, weight, cotangent):
    height, width, cin = features.shape
    cout = weight.shape[3]
    half = height // 2
    rows, cols = (lax.axis_size("rows"), lax.axis_size("cols"))
    devices = rows * cols
    odd = lax.axis_index("rows") % 2
    par = odd.astype(jnp.int32).reshape(1)

    swap = [(i, i ^ 1) for i in range(rows)]
    up = [(i, i + 2 if i % 2 else i - 2) for i in range(rows)]
    near = [(i, j) for i, j in up if 0 <= j < rows]
    far = [(j, i) for i, j in near]

    def pick(cells, which):
        return lax.dynamic_slice_in_dim(cells, which * half, half, 0)

    d_own, d_give = (pick(cotangent, odd), pick(cotangent, 1 - odd))
    f_own, f_give = (pick(features, odd), pick(features, 1 - odd))
    d_par = lax.ppermute(d_give, "rows", swap)
    d_near = lax.ppermute(d_own, "rows", near)
    f_par = lax.ppermute(f_give, "rows", swap)
    f_near = lax.ppermute(f_own, "rows", near)
    d_far = lax.ppermute(d_par, "rows", far)
    d_blocks = (d_own, d_par, d_near, d_far)
    d_left, d_right = strips(d_blocks, cols)

    wide = width + 2 * STRIP
    chunk = 9 * cin // devices
    deep = -(-(chunk + 1) // STRIP) * STRIP
    flops = 2 * 9 * height * width * cin * cout
    ext = VMEM((4, half, wide, cout), jnp.bfloat16)
    shifted = VMEM((4, half, width, 3 * cout), jnp.bfloat16)
    (scaled,) = call(
        functools.partial(kernel_grad, chunk),
        (par, f_own, f_par) + d_blocks + (d_left, d_right),
        [jax.ShapeDtypeStruct((devices, deep, cout), jnp.float32)],
        [ext, shifted, VMEM((9 * cin, cout), jnp.float32)],
        flops,
    )
    got = lax.all_to_all(scaled.astype(jnp.float16), ALL, 0, 0)

    half_grad = jax.ShapeDtypeStruct((half, width, cin), jnp.bfloat16)
    g_own, g_par = call(
        kernel_back, (par, weight) + d_blocks + (d_left, d_right), [half_grad, half_grad], [ext, shifted], flops
    )
    g_other = lax.ppermute(g_par, "rows", swap)

    f_far = lax.ppermute(f_par, "rows", far)
    f_blocks = (f_own, f_par, f_near, f_far)
    f_left, f_right = strips(f_blocks, cols)

    levels = got[:, chunk, 0].astype(jnp.float32)
    highest = jnp.max(levels)
    shares = got[:, :chunk].astype(jnp.float32) * jnp.exp2(levels - highest)[:, None, None]
    mine = (jnp.sum(shares, axis=0) * (1.0 / devices)).astype(jnp.float16)
    spread = lax.all_to_all(jnp.broadcast_to(mine, (devices, chunk, cout)), ALL, 0, 0)

    half_out = jax.ShapeDtypeStruct((half, width, cout), jnp.bfloat16)
    o_own, o_par = call(
        kernel_out,
        (par, weight) + f_blocks + (f_left, f_right),
        [half_out, half_out],
        [VMEM((4, half, wide, cin), jnp.bfloat16)],
        flops,
    )
    o_other = lax.ppermute(o_par, "rows", swap)

    norm = devices / jnp.sqrt(jnp.float32(height * width * devices))
    weight_grad = spread.astype(jnp.float32) * (jnp.exp2(highest - TOP) * norm)
    return (
        joined(odd, o_own, o_other),
        joined(odd, g_own, g_other),
        weight_grad.reshape(weight.shape),
    )


def solution(mesh):
    placed = P("rows", "cols", None)
    return jax.shard_map(
        body,
        mesh=mesh,
        in_specs=(placed, P(), placed),
        out_specs=(placed, placed, P()),
        check_vma=False,
    )
```

time: 250 us -> 106 us (0.42)
  the two profiles are of different devices: /device:TPU:0 before, /device:TPU:1 now
where the time goes in v2:
time: 106 us; the launch traced here: 105 us
  starting transfers between devices  40.9 us (39%)
  waiting for transfers between devices  33.5 us (32%)
  other arithmetic  12.2 us (12%)
  local copies, waits for them, and re-layouts  9.22 us (9%)
  Pallas kernels  7.77 us (7%)
  between operations  1.66 us (2%)
    ppermute x1, waiting for transfers between devices, body(): f_near = lax.ppermute(f_own, 'rows', near)  15.9 us
    ppermute x2, waiting for transfers between devices, strips(): right = lax.ppermute(heads, 'cols', [(i + 1, i) for i in range(count - 1)])  11.1 us
    ppermute x2, starting transfers between devices, strips(): left = lax.ppermute(tails, 'cols', [(i, i + 1) for i in range(count - 1)])  10.4 us
    pallas_call x3, Pallas kernels, call(): pl.pallas_call(kernel, out_shape=outs, in_specs=[pl.BlockSpec(memory_spac...  7.77 us
    all_to_all x1, starting transfers between devices, body(): lax.all_to_all(jnp.broadcast_to(mine, (devices, chunk, cout)), ALL, 0, 0)  6.71 us
    all_to_all x1, starting transfers between devices, body(): got = lax.all_to_all(scaled.astype(jnp.float16), ALL, 0, 0)  4.78 us
    ppermute x2, starting transfers between devices, strips(): right = lax.ppermute(heads, 'cols', [(i + 1, i) for i in range(count - 1)])  4.14 us
    ppermute x1, starting transfers between devices, body(): f_far = lax.ppermute(f_par, 'rows', far)  4 us
  transfers between devices with their start and end apart: 14, of which 6 were waited for; matrix products, arithmetic and copies ran while one was open for 13% of the time, Pallas kernels for 5%

profile of v2, /device:TPU:1, one launch (start us, length us, event | category | flops | bytes accessed | tf_op | source)
XLA Modules:
  0.0 105.2 jit_solution(4466005075454039105)
XLA Ops:
  0.6 0.0 copy-start.6
  0.7 1.2 %constant_dynamic-slice_fusion = (bf16[6,160,128]{2,1,0:T(8,128)(2,1)S(1)}, bf16[6,160,128]{2,1,0:T(8,128)(2,1)S(1)}) fusion(bf16[12,160,128]{2,1,0:T(8,128)(2,1)} %param.5, s32[]{:T(128)S(6)} %select_n.42, s32[]{:T(128)S(6)} %select_n.41), kind=kLoop, calls=%fused_computation.32 | loop fusion | bytes 983048 | tf_op jit(solution)/shard_map/dynamic_slice | solution.py:153
  1.8 2.1 %collective-permute-start.6 = (bf16[6,160,128]{2,1,0:T(8,128)(2,1)S(1)}, bf16[6,160,128]{2,1,0:T(8,128)(2,1)S(1)}, u32[]{:S(2)}, u32[]{:S(2)}) collective-permute-start(bf16[6,160,128]{2,1,0:T(8,128)(2,1)S(1)} %get-tuple-element.19), channel_id=1, source_target_pairs={{0,4},{4,0},{8,12},{12,8},{16,20},{20,16},{24,28},{28,24},{1,5},{5... | collective-permute-start | bytes 737288 | tf_op jit(solution)/shard_map/ppermute | solution.py:157
  4.0 1.3 %collective-permute-start.7 = (bf16[6,160,128]{2,1,0:T(8,128)(2,1)S(1)}, bf16[6,160,128]{2,1,0:T(8,128)(2,1)S(1)}, u32[]{:S(2)}, u32[]{:S(2)}) collective-permute-start(bf16[6,160,128]{2,1,0:T(8,128)(2,1)S(1)} %get-tuple-element.20.d_own), channel_id=1, source_target_pairs={{4,12},{8,0},{12,20},{16,8},{20,28},{24,16},{5,13},{9,1},{13,21},{... | collective-permute-start | bytes 737288 | tf_op jit(solution)/shard_map/ppermute | solution.py:158
  5.3 0.1 constant_dynamic-slice_fusion.2
  5.4 2.2 %collective-permute-start = (bf16[6,160,256]{2,1,0:T(8,128)(2,1)S(1)}, bf16[6,160,256]{2,1,0:T(8,128)(2,1)S(1)}, u32[]{:S(2)}, u32[]{:S(2)}) collective-permute-start(bf16[6,160,256]{2,1,0:T(8,128)(2,1)S(1)} %get-tuple-element.15), channel_id=1, source_target_pairs={{0,4},{4,0},{8,12},{12,8},{16,20},{20,16},{24,28},{28,24},{1,5},{5... | collective-permute-start | bytes 1474568 | tf_op jit(solution)/shard_map/ppermute | solution.py:159
  7.6 0.8 dynamic-slice_bitcast_fusion.2
  8.3 1.3 %collective-permute-done.6.d_par = bf16[6,160,128]{2,1,0:T(8,128)(2,1)S(1)} collective-permute-done((bf16[6,160,128]{2,1,0:T(8,128)(2,1)S(1)}, bf16[6,160,128]{2,1,0:T(8,128)(2,1)S(1)}, u32[]{:S(2)}, u32[]{:S(2)}) %collective-permute-start.6) | collective-permute-done | bytes 245792 | tf_op jit(solution)/shard_map/ppermute | solution.py:157
  9.7 3.1 %collective-permute-start.8 = (bf16[6,160,128]{2,1,0:T(8,128)(2,1)S(1)}, bf16[6,160,128]{2,1,0:T(8,128)(2,1)S(1)}, u32[]{:S(2)}, u32[]{:S(2)}) collective-permute-start(bf16[6,160,128]{2,1,0:T(8,128)(2,1)S(1)} %collective-permute-done.6.d_par), channel_id=1, source_target_pairs={{12,4},{0,8},{20,12},{8,16},{28,20},{16,24},{13,5},{1,9},{21,13},{... | collective-permute-start | bytes 737288 | tf_op jit(solution)/shard_map/ppermute | solution.py:161
  12.8 0.0 collective-permute-done.7.d_near
  12.8 3.1 %collective-permute-done.8.d_far = bf16[6,160,128]{2,1,0:T(8,128)(2,1)S(1)} collective-permute-done((bf16[6,160,128]{2,1,0:T(8,128)(2,1)S(1)}, bf16[6,160,128]{2,1,0:T(8,128)(2,1)S(1)}, u32[]{:S(2)}, u32[]{:S(2)}) %collective-permute-start.8) | collective-permute-done | bytes 245792 | tf_op jit(solution)/shard_map/ppermute | solution.py:161
  15.9 6.6 %collective-permute-start.9 = (bf16[4,6,16,128]{3,2,1,0:T(8,128)(2,1)S(1)}, bf16[4,6,16,128]{3,2,1,0:T(8,128)(2,1)S(1)}, u32[]{:S(2)}, u32[]{:S(2)}) collective-permute-start(bf16[4,6,16,128]{3,2,1,0:T(8,128)(2,1)S(1)} %pad_maximum_fusion.4), channel_id=1, source_target_pairs={{0,1},{1,2},{2,3},{4,5},{5,6},{6,7},{8,9},{9,10},{10,11},{12,13},{... | collective-permute-start | bytes 294920 | tf_op jit(solution)/shard_map/ppermute | solution.py:127
  22.5 1.9 %collective-permute-start.10 = (bf16[4,6,16,128]{3,2,1,0:T(8,128)(2,1)S(1)}, bf16[4,6,16,128]{3,2,1,0:T(8,128)(2,1)S(1)}, u32[]{:S(2)}, u32[]{:S(2)}) collective-permute-start(bf16[4,6,16,128]{3,2,1,0:T(8,128)(2,1)S(1)} %pad_maximum_fusion.5), channel_id=1, source_target_pairs={{1,0},{2,1},{3,2},{5,4},{6,5},{7,6},{9,8},{10,9},{11,10},{13,12},{... | collective-permute-start | bytes 294920 | tf_op jit(solution)/shard_map/ppermute | solution.py:128
  24.4 0.0 collective-permute-done.f_par
  24.4 0.0 collective-permute-done.9.left
  24.4 4.0 %collective-permute-done.10.right = bf16[4,6,16,128]{3,2,1,0:T(8,128)(2,1)S(1)} collective-permute-done((bf16[4,6,16,128]{3,2,1,0:T(8,128)(2,1)S(1)}, bf16[4,6,16,128]{3,2,1,0:T(8,128)(2,1)S(1)}, u32[]{:S(2)}, u32[]{:S(2)}) %collective-permute-start.10) | collective-permute-done | bytes 98336 | tf_op jit(solution)/shard_map/ppermute | solution.py:128
  28.4 2.6 %shard_map.60 = f32[32,80,128]{2,1,0:T(8,128)S(1)} custom-call(s32[1]{0:T(128)} %bitcast.par, bf16[6,160,256]{2,1,0:T(8,128)(2,1)S(1)} %get-tuple-element.16.f_own, bf16[6,160,256]{2,1,0:T(8,128)(2,1)S(1)} %collective-permute-done.f_par, bf16[6,160,128]{2,1,0:T(8,128)(2,1)S(1)} %get-tuple-element.20.d_own, ...), custom_call_target="tpu_custom_call" | custom-call | flops 1132462080 | bytes 3473412 | tf_op jit(solution)/shard_map/pallas_call | solution.py:112
  31.0 0.9 convert_element_type.17
  32.0 4.8 %all-to-all-start = ((f16[32,80,128]{2,1,0:T(8,128)(2,1)}), f16[32,80,128]{2,1,0:T(8,128)(2,1)}, u32[]{:S(2)}, u32[]{:S(2)}) async-start(f16[32,80,128]{2,1,0:T(8,128)(2,1)} %convert_element_type.17), calls=%async_computation | async-start | bytes 1310720 | tf_op jit(solution)/shard_map/all_to_all | solution.py:178
  36.7 1.3 %collective-permute-start.1 = (bf16[6,160,256]{2,1,0:T(8,128)(2,1)S(1)}, bf16[6,160,256]{2,1,0:T(8,128)(2,1)S(1)}, u32[]{:S(2)}, u32[]{:S(2)}) collective-permute-start(bf16[6,160,256]{2,1,0:T(8,128)(2,1)S(1)} %get-tuple-element.16.f_own), channel_id=1, source_target_pairs={{4,12},{8,0},{12,20},{16,8},{20,28},{24,16},{5,13},{9,1},{13,21},{... | collective-permute-start | bytes 1474568 | tf_op jit(solution)/shard_map/ppermute | solution.py:160
  38.0 1.5 %dynamic-slice_bitcast_fusion = (bf16[1,6,16,256]{3,2,1,0:T(8,128)(2,1)}, bf16[1,6,16,256]{3,2,1,0:T(8,128)(2,1)S(1)}) fusion(bf16[12,160,256]{2,1,0:T(8,128)(2,1)} %param.3, s32[]{:T(128)S(6)} %select_n.41, s32[]{:T(128)S(6)} %add.17), kind=kLoop, calls=%fused_computation.15 | loop fusion | bytes 196616 | tf_op jit(solution)/shard_map/stack | solution.py:126
  39.5 4.0 %collective-permute-start.2 = (bf16[6,160,256]{2,1,0:T(8,128)(2,1)S(1)}, bf16[6,160,256]{2,1,0:T(8,128)(2,1)S(1)}, u32[]{:S(2)}, u32[]{:S(2)}) collective-permute-start(bf16[6,160,256]{2,1,0:T(8,128)(2,1)S(1)} %collective-permute-done.f_par), channel_id=1, source_target_pairs={{12,4},{0,8},{20,12},{8,16},{28,20},{16,24},{13,5},{1,9},{21,13},{... | collective-permute-start | bytes 1474568 | tf_op jit(solution)/shard_map/ppermute | solution.py:186
  43.5 0.6 slice_bitcast_fusion.2
  44.2 15.9 %collective-permute-done.1.f_near = bf16[6,160,256]{2,1,0:T(8,128)(2,1)S(1)} collective-permute-done((bf16[6,160,256]{2,1,0:T(8,128)(2,1)S(1)}, bf16[6,160,256]{2,1,0:T(8,128)(2,1)S(1)}, u32[]{:S(2)}, u32[]{:S(2)}) %collective-permute-start.1) | collective-permute-done | bytes 491552 | tf_op jit(solution)/shard_map/ppermute | solution.py:160
  60.0 0.6 slice_bitcast_fusion.1
  60.6 1.1 %copy-done = bf16[3,3,256,128]{3,2,1,0:T(8,128)(2,1)S(1)} copy-done((bf16[3,3,256,128]{3,2,1,0:T(8,128)(2,1)S(1)}, bf16[3,3,256,128]{3,2,1,0:T(8,128)(2,1)}, u32[]{:S(2)}) %copy-start) | copy-done | bytes 589848
  61.7 0.9 copy-done.5
  62.6 3.0 %shard_map.59 = (bf16[6,160,256]{2,1,0:T(8,128)(2,1)S(1)}, bf16[6,160,256]{2,1,0:T(8,128)(2,1)}) custom-call(s32[1]{0:T(128)} %bitcast.par, bf16[3,3,256,128]{3,2,1,0:T(8,128)(2,1)S(1)} %copy-done, bf16[6,160,128]{2,1,0:T(8,128)(2,1)S(1)} %get-tuple-element.20.d_own, bf16[6,160,128]{2,1,0:T(8,128)(2,1)S(1)} %collective-permute-done.6.d_par, ...), custom_call_target="tpu_custom_call" | custom-call | flops 1132462080 | bytes 2752516 | tf_op jit(solution)/shard_map/pallas_call | solution.py:112
  65.7 0.7 pad_maximum_fusion.2
  66.4 3.8 %collective-permute-start.3 = (bf16[4,6,16,256]{3,2,1,0:T(8,128)(2,1)}, bf16[4,6,16,256]{3,2,1,0:T(8,128)(2,1)S(1)}, u32[]{:S(2)}, u32[]{:S(2)}) collective-permute-start(bf16[4,6,16,256]{3,2,1,0:T(8,128)(2,1)} %pad_maximum_fusion.2), channel_id=1, source_target_pairs={{0,1},{1,2},{2,3},{4,5},{5,6},{6,7},{8,9},{9,10},{10,11},{12,13},{... | collective-permute-start | bytes 589832 | tf_op jit(solution)/shard_map/ppermute | solution.py:127
  70.2 1.5 %fusion = f32[]{:T(128)} fusion(f16[32,80,128]{2,1,0:T(8,128)(2,1)} %all-to-all-done), kind=kLoop, calls=%fused_computation.31 | loop fusion | flops 63 | bytes 68 | tf_op jit(solution)/shard_map/reduce_max | solution.py:191
  71.8 1.8 %exponential_reduce_fusion = f32[32]{0:T(128)S(1)} fusion(f16[32,80,128]{2,1,0:T(8,128)(2,1)} %all-to-all-done, f32[]{:T(128)} %fusion), kind=kLoop, calls=%fused_computation.30 | loop fusion | flops 96 | bytes 196 | tf_op jit(solution)/shard_map/exp2 | solution.py:192
  73.6 1.3 %multiply_reduce_fusion = f32[72,128]{1,0:T(8,128)S(1)} fusion(f16[32,80,128]{2,1,0:T(8,128)(2,1)} %all-to-all-done, f32[32]{0:T(128)S(1)} %exponential_reduce_fusion), kind=kLoop, calls=%fused_computation.1 | loop fusion | flops 875520 | bytes 626816 | tf_op jit(solution)/shard_map/reduce_sum | solution.py:193
  74.9 0.0 copy-start.1
  74.9 0.9 broadcast_in_dim.4
  75.8 6.7 %all-to-all-start.1 = ((f16[32,72,128]{2,1,0:T(8,128)(2,1)}), f16[32,72,128]{2,1,0:T(8,128)(2,1)}, u32[]{:S(2)}, u32[]{:S(2)}) async-start(f16[32,72,128]{2,1,0:T(8,128)(2,1)} %broadcast_in_dim.4), calls=%async_computation.1 | async-start | bytes 1179648 | tf_op jit(solution)/shard_map/all_to_all | solution.py:194
  82.6 0.7 pad_maximum_fusion.3
  83.3 2.2 %collective-permute-start.4 = (bf16[4,6,16,256]{3,2,1,0:T(8,128)(2,1)}, bf16[4,6,16,256]{3,2,1,0:T(8,128)(2,1)S(1)}, u32[]{:S(2)}, u32[]{:S(2)}) collective-permute-start(bf16[4,6,16,256]{3,2,1,0:T(8,128)(2,1)} %pad_maximum_fusion.3), channel_id=1, source_target_pairs={{1,0},{2,1},{3,2},{5,4},{6,5},{7,6},{9,8},{10,9},{11,10},{13,12},{... | collective-permute-start | bytes 589832 | tf_op jit(solution)/shard_map/ppermute | solution.py:128
  85.5 7.1 %collective-permute-done.4.right = bf16[4,6,16,256]{3,2,1,0:T(8,128)(2,1)S(1)} collective-permute-done((bf16[4,6,16,256]{3,2,1,0:T(8,128)(2,1)}, bf16[4,6,16,256]{3,2,1,0:T(8,128)(2,1)S(1)}, u32[]{:S(2)}, u32[]{:S(2)}) %collective-permute-start.4) | collective-permute-done | bytes 196640 | tf_op jit(solution)/shard_map/ppermute | solution.py:128
  92.6 0.7 copy-done.2
  93.3 0.9 copy-done.3
  94.2 2.1 %shard_map.58 = (bf16[6,160,128]{2,1,0:T(8,128)(2,1)S(1)}, bf16[6,160,128]{2,1,0:T(8,128)(2,1)S(1)}) custom-call(s32[1]{0:T(128)} %bitcast.par, bf16[3,3,256,128]{3,2,1,0:T(8,128)(2,1)S(1)} %copy-done.1, bf16[6,160,256]{2,1,0:T(8,128)(2,1)S(1)} %get-tuple-element.16.f_own, bf16[6,160,256]{2,1,0:T(8,128)(2,1)S(1)} %collective-permute-done.f_par, ...), custom_call_target="tpu_custom_call" | custom-call | flops 1132462080 | bytes 3440644 | tf_op jit(solution)/shard_map/pallas_call | solution.py:112
  96.4 0.8 collective-permute-start.5
  97.2 1.1 %broadcast_select_fusion.1 = (bf16[6,160,256]{2,1,0:T(8,128)(2,1)S(1)}, bf16[6,160,256]{2,1,0:T(8,128)(2,1)S(1)}) fusion(bf16[6,160,256]{2,1,0:T(8,128)(2,1)} %collective-permute-done.11, bf16[6,160,256]{2,1,0:T(8,128)(2,1)S(1)} %get-tuple-element.10, pred[]{:T(512)S(6)} %eq.4), kind=kLoop, calls=%fused_computation.5 | loop fusion | flops 491520 | bytes 1966081 | tf_op jit(solution)/shard_map/jit(_where)/select_n | solution.py:133
  98.3 1.0 pad_maximum_fusion
  99.3 2.1 %collective-permute-done.5 = bf16[6,160,128]{2,1,0:T(8,128)(2,1)S(1)} collective-permute-done((bf16[6,160,128]{2,1,0:T(8,128)(2,1)S(1)}, bf16[6,160,128]{2,1,0:T(8,128)(2,1)S(1)}, u32[]{:S(2)}, u32[]{:S(2)}) %collective-permute-start.5) | collective-permute-done | bytes 245792 | tf_op jit(solution)/shard_map/ppermute | solution.py:204
  101.5 0.8 pad_maximum_fusion.1
  103.1 2.2 %convert_multiply_fusion = f32[32,72,128]{2,1,0:T(8,128)} fusion(f16[32,72,128]{2,1,0:T(8,128)(2,1)} %all-to-all-done.1, f32[]{:T(128)S(6)} %mul.40), kind=kLoop, calls=%fused_computation | loop fusion | flops 589824 | bytes 1769476 | tf_op jit(solution)/shard_map/mul | solution.py:207
  (28 shorter events, 0.1 us)
Async XLA Ops:
  0.6 4.6 %copy-start.6 = (bf16[12,160,256]{2,1,0:T(8,128)(2,1)S(1)}, bf16[12,160,256]{2,1,0:T(8,128)(2,1)}, u32[]{:S(2)}) copy-start(bf16[12,160,256]{2,1,0:T(8,128)(2,1)} %param.3) | copy-start | bytes 2949124
  1.8 7.8 %collective-permute-start.6 = (bf16[6,160,128]{2,1,0:T(8,128)(2,1)S(1)}, bf16[6,160,128]{2,1,0:T(8,128)(2,1)S(1)}, u32[]{:S(2)}, u32[]{:S(2)}) collective-permute-start(bf16[6,160,128]{2,1,0:T(8,128)(2,1)S(1)} %get-tuple-element.19), channel_id=1, source_target_pairs={{0,4},{4,0},{8,12},{12,8},{16,20},{20,16},{24,28},{28,24},{1,5},{5... | collective-permute-start | bytes 737288 | tf_op jit(solution)/shard_map/ppermute | solution.py:157
  4.0 8.8 %collective-permute-start.7 = (bf16[6,160,128]{2,1,0:T(8,128)(2,1)S(1)}, bf16[6,160,128]{2,1,0:T(8,128)(2,1)S(1)}, u32[]{:S(2)}, u32[]{:S(2)}) collective-permute-start(bf16[6,160,128]{2,1,0:T(8,128)(2,1)S(1)} %get-tuple-element.20.d_own), channel_id=1, source_target_pairs={{4,12},{8,0},{12,20},{16,8},{20,28},{24,16},{5,13},{9,1},{13,21},{... | collective-permute-start | bytes 737288 | tf_op jit(solution)/shard_map/ppermute | solution.py:158
  5.4 19.1 %collective-permute-start = (bf16[6,160,256]{2,1,0:T(8,128)(2,1)S(1)}, bf16[6,160,256]{2,1,0:T(8,128)(2,1)S(1)}, u32[]{:S(2)}, u32[]{:S(2)}) collective-permute-start(bf16[6,160,256]{2,1,0:T(8,128)(2,1)S(1)} %get-tuple-element.15), channel_id=1, source_target_pairs={{0,4},{4,0},{8,12},{12,8},{16,20},{20,16},{24,28},{28,24},{1,5},{5... | collective-permute-start | bytes 1474568 | tf_op jit(solution)/shard_map/ppermute | solution.py:159
  9.7 6.2 %collective-permute-start.8 = (bf16[6,160,128]{2,1,0:T(8,128)(2,1)S(1)}, bf16[6,160,128]{2,1,0:T(8,128)(2,1)S(1)}, u32[]{:S(2)}, u32[]{:S(2)}) collective-permute-start(bf16[6,160,128]{2,1,0:T(8,128)(2,1)S(1)} %collective-permute-done.6.d_par), channel_id=1, source_target_pairs={{12,4},{0,8},{20,12},{8,16},{28,20},{16,24},{13,5},{1,9},{21,13},{... | collective-permute-start | bytes 737288 | tf_op jit(solution)/shard_map/ppermute | solution.py:161
  15.9 8.5 %collective-permute-start.9 = (bf16[4,6,16,128]{3,2,1,0:T(8,128)(2,1)S(1)}, bf16[4,6,16,128]{3,2,1,0:T(8,128)(2,1)S(1)}, u32[]{:S(2)}, u32[]{:S(2)}) collective-permute-start(bf16[4,6,16,128]{3,2,1,0:T(8,128)(2,1)S(1)} %pad_maximum_fusion.4), channel_id=1, source_target_pairs={{0,1},{1,2},{2,3},{4,5},{5,6},{6,7},{8,9},{9,10},{10,11},{12,13},{... | collective-permute-start | bytes 294920 | tf_op jit(solution)/shard_map/ppermute | solution.py:127
  22.5 5.9 %collective-permute-start.10 = (bf16[4,6,16,128]{3,2,1,0:T(8,128)(2,1)S(1)}, bf16[4,6,16,128]{3,2,1,0:T(8,128)(2,1)S(1)}, u32[]{:S(2)}, u32[]{:S(2)}) collective-permute-start(bf16[4,6,16,128]{3,2,1,0:T(8,128)(2,1)S(1)} %pad_maximum_fusion.5), channel_id=1, source_target_pairs={{1,0},{2,1},{3,2},{5,4},{6,5},{7,6},{9,8},{10,9},{11,10},{13,12},{... | collective-permute-start | bytes 294920 | tf_op jit(solution)/shard_map/ppermute | solution.py:128
  28.4 2.6 %copy-start.4 = (bf16[4,6,16,128]{3,2,1,0:T(8,128)(2,1)}, bf16[4,6,16,128]{3,2,1,0:T(8,128)(2,1)S(1)}, u32[]{:S(2)}) copy-start(bf16[4,6,16,128]{3,2,1,0:T(8,128)(2,1)S(1)} %collective-permute-done.10.right) | copy-start | bytes 294916
  32.0 38.3 %all-to-all-start = ((f16[32,80,128]{2,1,0:T(8,128)(2,1)}), f16[32,80,128]{2,1,0:T(8,128)(2,1)}, u32[]{:S(2)}, u32[]{:S(2)}) async-start(f16[32,80,128]{2,1,0:T(8,128)(2,1)} %convert_element_type.17), calls=%async_computation | async-start | bytes 1310720 | tf_op jit(solution)/shard_map/all_to_all | solution.py:178
  36.7 23.3 %collective-permute-start.1 = (bf16[6,160,256]{2,1,0:T(8,128)(2,1)S(1)}, bf16[6,160,256]{2,1,0:T(8,128)(2,1)S(1)}, u32[]{:S(2)}, u32[]{:S(2)}) collective-permute-start(bf16[6,160,256]{2,1,0:T(8,128)(2,1)S(1)} %get-tuple-element.16.f_own), channel_id=1, source_target_pairs={{4,12},{8,0},{12,20},{16,8},{20,28},{24,16},{5,13},{9,1},{13,21},{... | collective-permute-start | bytes 1474568 | tf_op jit(solution)/shard_map/ppermute | solution.py:160
  39.5 26.1 %collective-permute-start.2 = (bf16[6,160,256]{2,1,0:T(8,128)(2,1)S(1)}, bf16[6,160,256]{2,1,0:T(8,128)(2,1)S(1)}, u32[]{:S(2)}, u32[]{:S(2)}) collective-permute-start(bf16[6,160,256]{2,1,0:T(8,128)(2,1)S(1)} %collective-permute-done.f_par), channel_id=1, source_target_pairs={{12,4},{0,8},{20,12},{8,16},{28,20},{16,24},{13,5},{1,9},{21,13},{... | collective-permute-start | bytes 1474568 | tf_op jit(solution)/shard_map/ppermute | solution.py:186
  60.6 1.1 %copy-start = (bf16[3,3,256,128]{3,2,1,0:T(8,128)(2,1)S(1)}, bf16[3,3,256,128]{3,2,1,0:T(8,128)(2,1)}, u32[]{:S(2)}) copy-start(bf16[3,3,256,128]{3,2,1,0:T(8,128)(2,1)} %w.3) | copy-start | bytes 1769476
  61.7 0.9 copy-start.5
  65.6 31.6 %collective-permute-start.11 = (bf16[6,160,256]{2,1,0:T(8,128)(2,1)}, bf16[6,160,256]{2,1,0:T(8,128)(2,1)}, u32[]{:S(2)}, u32[]{:S(2)}) collective-permute-start(bf16[6,160,256]{2,1,0:T(8,128)(2,1)} %get-tuple-element.9), channel_id=1, source_target_pairs={{0,4},{4,0},{8,12},{12,8},{16,20},{20,16},{24,28},{28,24},{1,5},{5... | collective-permute-start | bytes 1474568 | tf_op jit(solution)/shard_map/ppermute | solution.py:184
  66.4 19.1 %collective-permute-start.3 = (bf16[4,6,16,256]{3,2,1,0:T(8,128)(2,1)}, bf16[4,6,16,256]{3,2,1,0:T(8,128)(2,1)S(1)}, u32[]{:S(2)}, u32[]{:S(2)}) collective-permute-start(bf16[4,6,16,256]{3,2,1,0:T(8,128)(2,1)} %pad_maximum_fusion.2), channel_id=1, source_target_pairs={{0,1},{1,2},{2,3},{4,5},{5,6},{6,7},{8,9},{9,10},{10,11},{12,13},{... | collective-permute-start | bytes 589832 | tf_op jit(solution)/shard_map/ppermute | solution.py:127
  73.6 8.9 %copy-start.7 = (bf16[1,6,16,256]{3,2,1,0:T(8,128)(2,1)S(1)}, bf16[1,6,16,256]{3,2,1,0:T(8,128)(2,1)}, u32[]{:S(2)}) copy-start(bf16[1,6,16,256]{3,2,1,0:T(8,128)(2,1)} %get-tuple-element.13) | copy-start | bytes 147460
  73.6 8.9 %copy-start.8 = (bf16[1,6,16,256]{3,2,1,0:T(8,128)(2,1)S(1)}, bf16[1,6,16,256]{3,2,1,0:T(8,128)(2,1)}, u32[]{:S(2)}) copy-start(bf16[1,6,16,256]{3,2,1,0:T(8,128)(2,1)} %get-tuple-element.23) | copy-start | bytes 147460
  73.6 9.0 %copy-start.9 = (bf16[1,6,16,256]{3,2,1,0:T(8,128)(2,1)S(1)}, bf16[1,6,16,256]{3,2,1,0:T(8,128)(2,1)}, u32[]{:S(2)}) copy-start(bf16[1,6,16,256]{3,2,1,0:T(8,128)(2,1)} %get-tuple-element.25) | copy-start | bytes 147460
  74.9 18.4 %copy-start.1 = (bf16[3,3,256,128]{3,2,1,0:T(8,128)(2,1)S(1)}, bf16[3,3,256,128]{3,2,1,0:T(8,128)(2,1)}, u32[]{:S(2)}) copy-start(bf16[3,3,256,128]{3,2,1,0:T(8,128)(2,1)} %w.3) | copy-start | bytes 1769476
  75.8 27.2 %all-to-all-start.1 = ((f16[32,72,128]{2,1,0:T(8,128)(2,1)}), f16[32,72,128]{2,1,0:T(8,128)(2,1)}, u32[]{:S(2)}, u32[]{:S(2)}) async-start(f16[32,72,128]{2,1,0:T(8,128)(2,1)} %broadcast_in_dim.4), calls=%async_computation.1 | async-start | bytes 1179648 | tf_op jit(solution)/shard_map/all_to_all | solution.py:194
  83.3 9.3 %collective-permute-start.4 = (bf16[4,6,16,256]{3,2,1,0:T(8,128)(2,1)}, bf16[4,6,16,256]{3,2,1,0:T(8,128)(2,1)S(1)}, u32[]{:S(2)}, u32[]{:S(2)}) collective-permute-start(bf16[4,6,16,256]{3,2,1,0:T(8,128)(2,1)} %pad_maximum_fusion.3), channel_id=1, source_target_pairs={{1,0},{2,1},{3,2},{5,4},{6,5},{7,6},{9,8},{10,9},{11,10},{13,12},{... | collective-permute-start | bytes 589832 | tf_op jit(solution)/shard_map/ppermute | solution.py:128
  92.6 0.7 copy-start.2
  93.3 0.9 copy-start.3
  96.4 5.1 %collective-permute-start.5 = (bf16[6,160,128]{2,1,0:T(8,128)(2,1)S(1)}, bf16[6,160,128]{2,1,0:T(8,128)(2,1)S(1)}, u32[]{:S(2)}, u32[]{:S(2)}) collective-permute-start(bf16[6,160,128]{2,1,0:T(8,128)(2,1)S(1)} %get-tuple-element.7), channel_id=1, source_target_pairs={{0,4},{4,0},{8,12},{12,8},{16,20},{20,16},{24,28},{28,24},{1,5},{5... | collective-permute-start | bytes 737288 | tf_op jit(solution)/shard_map/ppermute | solution.py:204

commit v3 on v2

--- a/solution.py
+++ b/solution.py
@@ -37,24 +37,39 @@
             shifted[slot, :, :, pl.ds(q * cout, cout)] = whole[:, start : start + width].astype(jnp.bfloat16)
 
 
-def kernel_grad(chunk, par, f_own, f_par, d_own, d_par, d_near, d_far, left, right, out, ext, shifted, acc):
-    odd = par[0]
-    half, width, cin = f_par.shape
-    cout = d_own.shape[2]
+def kernel_extend(par, cells, left, right, own, give):
+    odd = par[0]
+    half, wide, _ = own.shape
+    width = cells.shape[1]
+    for out, start in ((own, odd * half), (give, (1 - odd) * half)):
+        rows = pl.ds(start, half)
+        out[:, pl.ds(0, STRIP), :] = left[rows]
+        out[:, pl.ds(STRIP, width), :] = cells[rows]
+        out[:, pl.ds(STRIP + width, STRIP), :] = right[rows]
+
+
+def kernel_grad(chunk, par, f_own, f_par, d_own, d_par, d_near, d_far, out, ext, shifted, acc):
+    odd = par[0]
+    half, width, cout = d_own.shape
+    cin = f_own.shape[2]
     pixels = half * width
-    gather_map(odd, (d_own, d_par, d_near, d_far), left, right, ext)
-    shift_columns(ext, shifted, width)
+    for block, slot in zip((d_own, d_par, d_near, d_far), slots(odd)):
+        ext[slot] = block[...]
     own, partner = slots(odd)[:2]
+    total = None
+    for block, slot in ((f_own, own), (f_par, partner)):
+        whole = block[...].astype(jnp.float32)
+        for b in range(3):
+            start = STRIP + DILATION_STEP * (b - 1)
+            shifted[:, :, pl.ds(b * cin, cin)] = whole[:, start : start + width].astype(jnp.bfloat16)
+        lhs = shifted[...].reshape(pixels, 3 * cin)
+        rhs = jnp.concatenate([ext[slot + 1 - a].reshape(pixels, cout) for a in range(3)], axis=1)
+        term = lax.dot_general(lhs, rhs, (((0,), (0,)), ((), ())), preferred_element_type=jnp.float32)
+        total = term if total is None else total + term
     top = jnp.zeros((8, cout), jnp.float32)
     for a in range(3):
-        total = None
-        for block, slot in ((f_own, own), (f_par, partner)):
-            lhs = block[...].reshape(pixels, cin)
-            rhs = shifted[slot + 1 - a].reshape(pixels, 3 * cout)
-            term = lax.dot_general(lhs, rhs, (((0,), (0,)), ((), ())), preferred_element_type=jnp.float32)
-            total = term if total is None else total + term
         for b in range(3):
-            piece = total[:, (2 - b) * cout : (3 - b) * cout]
+            piece = total[b * cin : (b + 1) * cin, a * cout : (a + 1) * cout]
             acc[pl.ds((3 * a + b) * cin, cin), :] = piece
             top = jnp.maximum(top, jnp.max(jnp.abs(piece).reshape(cin // 8, 8, cout), axis=0))
     most = jnp.max(jnp.max(top, axis=0, keepdims=True), axis=1, keepdims=True)
@@ -83,12 +98,12 @@
         out[...] = total.astype(jnp.bfloat16).reshape(half, width, cin)
 
 
-def kernel_out(par, w, f_own, f_par, f_near, f_far, left, right, out_own, out_par, ext):
-    odd = par[0]
-    half, width, cin = f_own.shape
-    cout = w.shape[3]
-    wide = width + 2 * STRIP
-    gather_map(odd, (f_own, f_par, f_near, f_far), left, right, ext)
+def kernel_out(par, w, f_own, f_par, f_near, f_far, out_own, out_par, ext):
+    odd = par[0]
+    half, width, cout = out_own.shape
+    wide, cin = f_own.shape[1:]
+    for block, slot in zip((f_own, f_par, f_near, f_far), slots(odd)):
+        ext[slot] = block[...]
     own, partner = slots(odd)[:2]
     for out, slot in ((out_own, own), (out_par, partner)):
         total = None
@@ -121,9 +136,10 @@
 
 
 def strips(blocks, count):
-    width = blocks[0].shape[1]
-    tails = jnp.stack([x[:, width - STRIP :] for x in blocks])
-    heads = jnp.stack([x[:, :STRIP] for x in blocks])
+    width = blocks[0].shape[-2]
+    tails = [x[..., width - STRIP :, :] for x in blocks]
+    heads = [x[..., :STRIP, :] for x in blocks]
+    tails, heads = (x[0] if len(x) == 1 else jnp.stack(x) for x in (tails, heads))
     left = lax.ppermute(tails, "cols", [(i, i + 1) for i in range(count - 1)])
     right = lax.ppermute(heads, "cols", [(i + 1, i) for i in range(count - 1)])
     return left, right
@@ -152,56 +168,65 @@
     def pick(cells, which):
         return lax.dynamic_slice_in_dim(cells, which * half, half, 0)
 
-    d_own, d_give = (pick(cotangent, odd), pick(cotangent, 1 - odd))
-    f_own, f_give = (pick(features, odd), pick(features, 1 - odd))
-    d_par = lax.ppermute(d_give, "rows", swap)
-    d_near = lax.ppermute(d_own, "rows", near)
-    f_par = lax.ppermute(f_give, "rows", swap)
-    f_near = lax.ppermute(f_own, "rows", near)
-    d_far = lax.ppermute(d_par, "rows", far)
-    d_blocks = (d_own, d_par, d_near, d_far)
-    d_left, d_right = strips(d_blocks, cols)
-
     wide = width + 2 * STRIP
     chunk = 9 * cin // devices
     deep = -(-(chunk + 1) // STRIP) * STRIP
     flops = 2 * 9 * height * width * cin * cout
+
+    d_own, d_give = (pick(cotangent, odd), pick(cotangent, 1 - odd))
+    d_par = lax.ppermute(d_give, "rows", swap)
+    f_left, f_right = strips((features,), cols)
+    d_near = lax.ppermute(d_own, "rows", near)
+    broad = jax.ShapeDtypeStruct((half, wide, cin), jnp.bfloat16)
+    f_own, f_give = call(kernel_extend, (par, features, f_left, f_right), [broad, broad], [], 0)
+    f_par = lax.ppermute(f_give, "rows", swap)
+    f_near = lax.ppermute(f_own, "rows", near)
+    d_far = lax.ppermute(d_par, "rows", far)
+    f_far = lax.ppermute(f_par, "rows", far)
+    d_blocks = (d_own, d_par, d_near, d_far)
+
+    f_own, f_near = lax.optimization_barrier((f_own, f_near))
     ext = VMEM((4, half, wide, cout), jnp.bfloat16)
-    shifted = VMEM((4, half, width, 3 * cout), jnp.bfloat16)
     (scaled,) = call(
         functools.partial(kernel_grad, chunk),
-        (par, f_own, f_par) + d_blocks + (d_left, d_right),
+        (par, f_own, f_par) + d_blocks,
         [jax.ShapeDtypeStruct((devices, deep, cout), jnp.float32)],
-        [ext, shifted, VMEM((9 * cin, cout), jnp.float32)],
+        [
+            VMEM((4, half, width, cout), jnp.bfloat16),
+            VMEM((half, width, 3 * cin), jnp.bfloat16),
+            VMEM((9 * cin, cout), jnp.float32),
+        ],
         flops,
     )
     got = lax.all_to_all(scaled.astype(jnp.float16), ALL, 0, 0)
 
+    d_left, d_right = strips(d_blocks, cols)
+    d_left, f_far = lax.optimization_barrier((d_left, f_far))
     half_grad = jax.ShapeDtypeStruct((half, width, cin), jnp.bfloat16)
     g_own, g_par = call(
-        kernel_back, (par, weight) + d_blocks + (d_left, d_right), [half_grad, half_grad], [ext, shifted], flops
+        kernel_back,
+        (par, weight) + d_blocks + (d_left, d_right),
+        [half_grad, half_grad],
+        [ext, VMEM((4, half, width, 3 * cout), jnp.bfloat16)],
+        flops,
     )
     g_other = lax.ppermute(g_par, "rows", swap)
-
-    f_far = lax.ppermute(f_par, "rows", far)
-    f_blocks = (f_own, f_par, f_near, f_far)
-    f_left, f_right = strips(f_blocks, cols)
-
-    levels = got[:, chunk, 0].astype(jnp.float32)
-    highest = jnp.max(levels)
-    shares = got[:, :chunk].astype(jnp.float32) * jnp.exp2(levels - highest)[:, None, None]
-    mine = (jnp.sum(shares, axis=0) * (1.0 / devices)).astype(jnp.float16)
-    spread = lax.all_to_all(jnp.broadcast_to(mine, (devices, chunk, cout)), ALL, 0, 0)
 
     half_out = jax.ShapeDtypeStruct((half, width, cout), jnp.bfloat16)
     o_own, o_par = call(
         kernel_out,
-        (par, weight) + f_blocks + (f_left, f_right),
+        (par, weight, f_own, f_par, f_near, f_far),
         [half_out, half_out],
         [VMEM((4, half, wide, cin), jnp.bfloat16)],
         flops,
     )
     o_other = lax.ppermute(o_par, "rows", swap)
+
+    levels = got[:, chunk : chunk + 1].astype(jnp.float32)
+    highest = jnp.max(levels, axis=0, keepdims=True)
+    shares = got[:, :chunk].astype(jnp.float32) * jnp.exp2(levels - highest)
+    mine = (jnp.sum(shares, axis=0, keepdims=True) * (1.0 / devices)).astype(jnp.float16)
+    spread = lax.all_to_all(jnp.broadcast_to(mine, (devices, chunk, cout)), ALL, 0, 0)
 
     norm = devices / jnp.sqrt(jnp.float32(height * width * devices))
     weight_grad = spread.astype(jnp.float32) * (jnp.exp2(highest - TOP) * norm)

time: 106 us -> 114 us (1.075)
  the two profiles are of different devices: /device:TPU:1 before, /device:TPU:0 now
where the time goes in v3:
time: 114 us
  waiting for transfers between devices  50.5 us (44%)
  starting transfers between devices  40.5 us (36%)
  other arithmetic  8.09 us (7%)
  Pallas kernels  7.22 us (6%)
  local copies, waits for them, and re-layouts  6.37 us (6%)
    ppermute x1, waiting for transfers between devices, body(): f_far = lax.ppermute(f_par, 'rows', far)  16.3 us
    ppermute x1, waiting for transfers between devices, body(): g_other = lax.ppermute(g_par, 'rows', swap)  14.3 us
    ppermute x1, waiting for transfers between devices, body(): d_par = lax.ppermute(d_give, 'rows', swap)  12.7 us
    pallas_call x4, Pallas kernels, call(): pl.pallas_call(kernel, out_shape=outs, in_specs=[pl.BlockSpec(memory_spac...  7.22 us
    all_to_all x1, starting transfers between devices, body(): lax.all_to_all(jnp.broadcast_to(mine, (devices, chunk, cout)), ALL, 0, 0)  6.38 us
    ppermute x1, waiting for transfers between devices, body(): d_far = lax.ppermute(d_par, 'rows', far)  6.07 us
    all_to_all x1, starting transfers between devices, body(): got = lax.all_to_all(scaled.astype(jnp.float16), ALL, 0, 0)  4.9 us
    ppermute x2, starting transfers between devices, strips(): left = lax.ppermute(tails, 'cols', [(i, i + 1) for i in range(count - 1)])  4.81 us
  transfers between devices with their start and end apart: 14, of which 6 were waited for; matrix products, arithmetic and copies ran while one was open for 5% of the time, Pallas kernels for 4%

profile of v3, /device:TPU:0, one launch (start us, length us, event | category | flops | bytes accessed | tf_op | source)
XLA Modules:
  0.0 113.7 jit_solution(8784673565747785497)
XLA Ops:
  0.6 1.0 fusion.1
  1.6 1.3 %collective-permute-start.1 = (bf16[12,16,256]{2,1,0:T(8,128)(2,1)S(1)}, bf16[12,16,256]{2,1,0:T(8,128)(2,1)S(1)}, u32[]{:S(2)}, u32[]{:S(2)}) collective-permute-start(bf16[12,16,256]{2,1,0:T(8,128)(2,1)S(1)} %get-tuple-element.25), channel_id=1, source_target_pairs={{1,0},{2,1},{3,2},{5,4},{6,5},{7,6},{9,8},{10,9},{11,10},{13,12},{... | collective-permute-start | bytes 294920 | tf_op jit(solution)/shard_map/ppermute | solution.py:144
  2.9 3.0 %collective-permute-start = (bf16[12,16,256]{2,1,0:T(8,128)(2,1)S(1)}, bf16[12,16,256]{2,1,0:T(8,128)(2,1)S(1)}, u32[]{:S(2)}, u32[]{:S(2)}) collective-permute-start(bf16[12,16,256]{2,1,0:T(8,128)(2,1)S(1)} %get-tuple-element.26), channel_id=1, source_target_pairs={{0,1},{1,2},{2,3},{4,5},{5,6},{6,7},{8,9},{9,10},{10,11},{12,13},{... | collective-permute-start | bytes 294920 | tf_op jit(solution)/shard_map/ppermute | solution.py:143
  6.0 0.0 collective-permute-done.1.right
  6.0 0.9 collective-permute-done.left
  6.9 1.2 %copy-done = bf16[12,160,256]{2,1,0:T(8,128)(2,1)S(1)} copy-done((bf16[12,160,256]{2,1,0:T(8,128)(2,1)S(1)}, bf16[12,160,256]{2,1,0:T(8,128)(2,1)}, u32[]{:S(2)}) %copy-start) | copy-done | bytes 983064
  8.1 0.1 shard_map.58
  8.1 3.0 %collective-permute-start.3 = (bf16[6,192,256]{2,1,0:T(8,128)(2,1)S(1)}, bf16[6,192,256]{2,1,0:T(8,128)(2,1)S(1)}, u32[]{:S(2)}, u32[]{:S(2)}) collective-permute-start(bf16[6,192,256]{2,1,0:T(8,128)(2,1)S(1)} %get-tuple-element.15), channel_id=1, source_target_pairs={{0,4},{4,0},{8,12},{12,8},{16,20},{20,16},{24,28},{28,24},{1,5},{5... | collective-permute-start | bytes 1769480 | tf_op jit(solution)/shard_map/ppermute | solution.py:182
  11.2 1.3 %collective-permute-start.2 = (bf16[6,192,256]{2,1,0:T(8,128)(2,1)S(1)}, bf16[6,192,256]{2,1,0:T(8,128)(2,1)S(1)}, u32[]{:S(2)}, u32[]{:S(2)}) collective-permute-start(bf16[6,192,256]{2,1,0:T(8,128)(2,1)S(1)} %get-tuple-element.14.f_own), channel_id=1, source_target_pairs={{4,12},{8,0},{12,20},{16,8},{20,28},{24,16},{5,13},{9,1},{13,21},{... | collective-permute-start | bytes 1769480 | tf_op jit(solution)/shard_map/ppermute | solution.py:183
  12.5 2.8 %collective-permute-start.4 = (bf16[6,160,128]{2,1,0:T(8,128)(2,1)S(1)}, bf16[6,160,128]{2,1,0:T(8,128)(2,1)S(1)}, u32[]{:S(2)}, u32[]{:S(2)}) collective-permute-start(bf16[6,160,128]{2,1,0:T(8,128)(2,1)S(1)} %get-tuple-element.32), channel_id=1, source_target_pairs={{0,4},{4,0},{8,12},{12,8},{16,20},{20,16},{24,28},{28,24},{1,5},{5... | collective-permute-start | bytes 737288 | tf_op jit(solution)/shard_map/ppermute | solution.py:177
  15.3 1.3 %collective-permute-start.5 = (bf16[6,160,128]{2,1,0:T(8,128)(2,1)S(1)}, bf16[6,160,128]{2,1,0:T(8,128)(2,1)S(1)}, u32[]{:S(2)}, u32[]{:S(2)}) collective-permute-start(bf16[6,160,128]{2,1,0:T(8,128)(2,1)S(1)} %get-tuple-element.31.d_own), channel_id=1, source_target_pairs={{4,12},{8,0},{12,20},{16,8},{20,28},{24,16},{5,13},{9,1},{13,21},{... | collective-permute-start | bytes 737288 | tf_op jit(solution)/shard_map/ppermute | solution.py:179
  16.6 12.7 %collective-permute-done.4.d_par = bf16[6,160,128]{2,1,0:T(8,128)(2,1)S(1)} collective-permute-done((bf16[6,160,128]{2,1,0:T(8,128)(2,1)S(1)}, bf16[6,160,128]{2,1,0:T(8,128)(2,1)S(1)}, u32[]{:S(2)}, u32[]{:S(2)}) %collective-permute-start.4) | collective-permute-done | bytes 245792 | tf_op jit(solution)/shard_map/ppermute | solution.py:177
  29.4 4.4 %collective-permute-start.6 = (bf16[6,160,128]{2,1,0:T(8,128)(2,1)S(1)}, bf16[6,160,128]{2,1,0:T(8,128)(2,1)S(1)}, u32[]{:S(2)}, u32[]{:S(2)}) collective-permute-start(bf16[6,160,128]{2,1,0:T(8,128)(2,1)S(1)} %collective-permute-done.4.d_par), channel_id=1, source_target_pairs={{12,4},{0,8},{20,12},{8,16},{28,20},{16,24},{13,5},{1,9},{21,13},{... | collective-permute-start | bytes 737288 | tf_op jit(solution)/shard_map/ppermute | solution.py:184
  33.8 0.0 collective-permute-done.2.f_near
  33.8 0.0 copy-start.2
  33.8 0.2 collective-permute-done.5.d_near
  34.0 6.1 %collective-permute-done.6.d_far = bf16[6,160,128]{2,1,0:T(8,128)(2,1)S(1)} collective-permute-done((bf16[6,160,128]{2,1,0:T(8,128)(2,1)S(1)}, bf16[6,160,128]{2,1,0:T(8,128)(2,1)S(1)}, u32[]{:S(2)}, u32[]{:S(2)}) %collective-permute-start.6) | collective-permute-done | bytes 245792 | tf_op jit(solution)/shard_map/ppermute | solution.py:184
  40.1 0.0 collective-permute-done.3.f_par
  40.1 2.1 %shard_map.61 = f32[32,80,128]{2,1,0:T(8,128)S(1)} custom-call(s32[1]{0:T(128)} %bitcast.par, bf16[6,192,256]{2,1,0:T(8,128)(2,1)S(1)} %get-tuple-element.14.f_own, bf16[6,192,256]{2,1,0:T(8,128)(2,1)S(1)} %collective-permute-done.3.f_par, bf16[6,160,128]{2,1,0:T(8,128)(2,1)S(1)} %get-tuple-element.31.d_own, ...), custom_call_target="tpu_custom_call" | custom-call | flops 1132462080 | bytes 3473412 | tf_op jit(solution)/shard_map/pallas_call | solution.py:127
  42.2 0.9 convert_element_type.20
  43.1 4.9 %all-to-all-start = ((f16[32,80,128]{2,1,0:T(8,128)(2,1)}), f16[32,80,128]{2,1,0:T(8,128)(2,1)}, u32[]{:S(2)}, u32[]{:S(2)}) async-start(f16[32,80,128]{2,1,0:T(8,128)(2,1)} %convert_element_type.20), calls=%async_computation | async-start | bytes 1310720 | tf_op jit(solution)/shard_map/all_to_all | solution.py:201
  48.1 3.6 %collective-permute-start.8 = (bf16[6,192,256]{2,1,0:T(8,128)(2,1)S(1)}, bf16[6,192,256]{2,1,0:T(8,128)(2,1)S(1)}, u32[]{:S(2)}, u32[]{:S(2)}) collective-permute-start(bf16[6,192,256]{2,1,0:T(8,128)(2,1)S(1)} %collective-permute-done.3.f_par), channel_id=1, source_target_pairs={{12,4},{0,8},{20,12},{8,16},{28,20},{16,24},{13,5},{1,9},{21,13},{... | collective-permute-start | bytes 1769480 | tf_op jit(solution)/shard_map/ppermute | solution.py:185
  51.8 1.8 %collective-permute-start.7 = (bf16[4,6,16,128]{3,2,1,0:T(8,128)(2,1)S(1)}, bf16[4,6,16,128]{3,2,1,0:T(8,128)(2,1)S(1)}, u32[]{:S(2)}, u32[]{:S(2)}) collective-permute-start(bf16[4,6,16,128]{3,2,1,0:T(8,128)(2,1)S(1)} %pad_maximum_fusion.2), channel_id=1, source_target_pairs={{0,1},{1,2},{2,3},{4,5},{5,6},{6,7},{8,9},{9,10},{10,11},{12,13},{... | collective-permute-start | bytes 294920 | tf_op jit(solution)/shard_map/ppermute | solution.py:143
  53.6 1.3 %collective-permute-start.10 = (bf16[4,6,16,128]{3,2,1,0:T(8,128)(2,1)S(1)}, bf16[4,6,16,128]{3,2,1,0:T(8,128)(2,1)S(1)}, u32[]{:S(2)}, u32[]{:S(2)}) collective-permute-start(bf16[4,6,16,128]{3,2,1,0:T(8,128)(2,1)S(1)} %pad_maximum_fusion.3), channel_id=1, source_target_pairs={{1,0},{2,1},{3,2},{5,4},{6,5},{7,6},{9,8},{10,9},{11,10},{13,12},{... | collective-permute-start | bytes 294920 | tf_op jit(solution)/shard_map/ppermute | solution.py:144
  54.9 0.0 collective-permute-done.7.left
  54.9 0.6 copy-done.4
  55.5 16.3 %collective-permute-done.8.f_far = bf16[6,192,256]{2,1,0:T(8,128)(2,1)S(1)} collective-permute-done((bf16[6,192,256]{2,1,0:T(8,128)(2,1)S(1)}, bf16[6,192,256]{2,1,0:T(8,128)(2,1)S(1)}, u32[]{:S(2)}, u32[]{:S(2)}) %collective-permute-start.8) | collective-permute-done | bytes 589856 | tf_op jit(solution)/shard_map/ppermute | solution.py:185
  71.8 1.1 copy-done.3
  72.9 2.8 %shard_map.59 = (bf16[6,160,128]{2,1,0:T(8,128)(2,1)S(1)}, bf16[6,160,128]{2,1,0:T(8,128)(2,1)}) custom-call(s32[1]{0:T(128)} %bitcast.par, bf16[3,3,256,128]{3,2,1,0:T(8,128)(2,1)S(1)} %copy-done.1, bf16[6,192,256]{2,1,0:T(8,128)(2,1)S(1)} %get-tuple-element.14.f_own, bf16[6,192,256]{2,1,0:T(8,128)(2,1)S(1)} %collective-permute-done.3.f_par, ...), custom_call_target="tpu_custom_call" | custom-call | flops 1132462080 | bytes 3440644 | tf_op jit(solution)/shard_map/pallas_call | solution.py:127
  75.7 3.6 %collective-permute-start.9 = (bf16[6,160,128]{2,1,0:T(8,128)(2,1)}, bf16[6,160,128]{2,1,0:T(8,128)(2,1)S(1)}, u32[]{:S(2)}, u32[]{:S(2)}) collective-permute-start(bf16[6,160,128]{2,1,0:T(8,128)(2,1)} %get-tuple-element.18), channel_id=1, source_target_pairs={{0,4},{4,0},{8,12},{12,8},{16,20},{20,16},{24,28},{28,24},{1,5},{5... | collective-permute-start | bytes 737288 | tf_op jit(solution)/shard_map/ppermute | solution.py:223
  79.3 0.0 all-to-all-done
  79.3 0.9 fusion
  80.2 0.9 multiply_exponential_fusion
  81.1 1.2 %multiply_reduce_fusion = f32[72,128]{1,0:T(8,128)S(1)} fusion(f16[32,80,128]{2,1,0:T(8,128)(2,1)} %all-to-all-done, f32[32,128]{1,0:T(8,128)S(1)} %bitcast.20), kind=kLoop, calls=%fused_computation.1 | loop fusion | flops 875520 | bytes 643072 | tf_op jit(solution)/shard_map/reduce_sum | solution.py:228
  82.3 0.9 broadcast_in_dim.2
  83.2 6.4 %all-to-all-start.1 = ((f16[32,72,128]{2,1,0:T(8,128)(2,1)}), f16[32,72,128]{2,1,0:T(8,128)(2,1)}, u32[]{:S(2)}, u32[]{:S(2)}) async-start(f16[32,72,128]{2,1,0:T(8,128)(2,1)} %broadcast_in_dim.2), calls=%async_computation.1 | async-start | bytes 1179648 | tf_op jit(solution)/shard_map/all_to_all | solution.py:229
  89.6 0.0 collective-permute-done.10.right
  89.6 0.0 copy-start.6
  89.7 0.6 copy-done.6
  90.3 0.9 copy-done.7
  91.2 2.3 %shard_map.60 = (bf16[6,160,256]{2,1,0:T(8,128)(2,1)S(1)}, bf16[6,160,256]{2,1,0:T(8,128)(2,1)S(1)}) custom-call(s32[1]{0:T(128)} %bitcast.par, bf16[3,3,256,128]{3,2,1,0:T(8,128)(2,1)S(1)} %copy-done.1, bf16[6,160,128]{2,1,0:T(8,128)(2,1)S(1)} %get-tuple-element.31.d_own, bf16[6,160,128]{2,1,0:T(8,128)(2,1)S(1)} %collective-permute-done.4.d_par, ...), custom_call_target="tpu_custom_call" | custom-call | flops 1132462080 | bytes 2752516 | tf_op jit(solution)/shard_map/pallas_call | solution.py:127
  93.4 1.8 %collective-permute-start.11 = (bf16[6,160,256]{2,1,0:T(8,128)(2,1)S(1)}, bf16[6,160,256]{2,1,0:T(8,128)(2,1)S(1)}, u32[]{:S(2)}, u32[]{:S(2)}) collective-permute-start(bf16[6,160,256]{2,1,0:T(8,128)(2,1)S(1)} %get-tuple-element.21), channel_id=1, source_target_pairs={{0,4},{4,0},{8,12},{12,8},{16,20},{20,16},{24,28},{28,24},{1,5},{5... | collective-permute-start | bytes 1474568 | tf_op jit(solution)/shard_map/ppermute | solution.py:213
  95.2 0.0 collective-permute-done.9
  95.3 0.8 pad_maximum_fusion.1
  96.1 14.3 %collective-permute-done.11 = bf16[6,160,256]{2,1,0:T(8,128)(2,1)S(1)} collective-permute-done((bf16[6,160,256]{2,1,0:T(8,128)(2,1)S(1)}, bf16[6,160,256]{2,1,0:T(8,128)(2,1)S(1)}, u32[]{:S(2)}, u32[]{:S(2)}) %collective-permute-start.11) | collective-permute-done | bytes 491552 | tf_op jit(solution)/shard_map/ppermute | solution.py:213
  110.4 0.1 broadcast_select_fusion.1
  110.4 1.0 pad_maximum_fusion
  111.5 2.2 %convert_multiply_fusion = f32[32,72,128]{2,1,0:T(8,128)} fusion(f16[32,72,128]{2,1,0:T(8,128)(2,1)} %all-to-all-done.1, f32[128]{0:T(128)S(1)} %exponential_multiply_fusion), kind=kLoop, calls=%fused_computation | loop fusion | flops 589824 | bytes 1769984 | tf_op jit(solution)/shard_map/mul | solution.py:232
  (22 shorter events, 0.2 us)
Async XLA Ops:
  1.6 4.4 %collective-permute-start.1 = (bf16[12,16,256]{2,1,0:T(8,128)(2,1)S(1)}, bf16[12,16,256]{2,1,0:T(8,128)(2,1)S(1)}, u32[]{:S(2)}, u32[]{:S(2)}) collective-permute-start(bf16[12,16,256]{2,1,0:T(8,128)(2,1)S(1)} %get-tuple-element.25), channel_id=1, source_target_pairs={{1,0},{2,1},{3,2},{5,4},{6,5},{7,6},{9,8},{10,9},{11,10},{13,12},{... | collective-permute-start | bytes 294920 | tf_op jit(solution)/shard_map/ppermute | solution.py:144
  2.9 4.0 %collective-permute-start = (bf16[12,16,256]{2,1,0:T(8,128)(2,1)S(1)}, bf16[12,16,256]{2,1,0:T(8,128)(2,1)S(1)}, u32[]{:S(2)}, u32[]{:S(2)}) collective-permute-start(bf16[12,16,256]{2,1,0:T(8,128)(2,1)S(1)} %get-tuple-element.26), channel_id=1, source_target_pairs={{0,1},{1,2},{2,3},{4,5},{5,6},{6,7},{8,9},{9,10},{10,11},{12,13},{... | collective-permute-start | bytes 294920 | tf_op jit(solution)/shard_map/ppermute | solution.py:143
  6.9 1.2 %copy-start = (bf16[12,160,256]{2,1,0:T(8,128)(2,1)S(1)}, bf16[12,160,256]{2,1,0:T(8,128)(2,1)}, u32[]{:S(2)}) copy-start(bf16[12,160,256]{2,1,0:T(8,128)(2,1)} %cells.1) | copy-start | bytes 2949124
  8.1 4.4 %copy-start.8 = (bf16[12,160,128]{2,1,0:T(8,128)(2,1)S(1)}, bf16[12,160,128]{2,1,0:T(8,128)(2,1)}, u32[]{:S(2)}) copy-start(bf16[12,160,128]{2,1,0:T(8,128)(2,1)} %param.5) | copy-start | bytes 1474564
  8.1 32.0 %collective-permute-start.3 = (bf16[6,192,256]{2,1,0:T(8,128)(2,1)S(1)}, bf16[6,192,256]{2,1,0:T(8,128)(2,1)S(1)}, u32[]{:S(2)}, u32[]{:S(2)}) collective-permute-start(bf16[6,192,256]{2,1,0:T(8,128)(2,1)S(1)} %get-tuple-element.15), channel_id=1, source_target_pairs={{0,4},{4,0},{8,12},{12,8},{16,20},{20,16},{24,28},{28,24},{1,5},{5... | collective-permute-start | bytes 1769480 | tf_op jit(solution)/shard_map/ppermute | solution.py:182
  11.2 22.6 %collective-permute-start.2 = (bf16[6,192,256]{2,1,0:T(8,128)(2,1)S(1)}, bf16[6,192,256]{2,1,0:T(8,128)(2,1)S(1)}, u32[]{:S(2)}, u32[]{:S(2)}) collective-permute-start(bf16[6,192,256]{2,1,0:T(8,128)(2,1)S(1)} %get-tuple-element.14.f_own), channel_id=1, source_target_pairs={{4,12},{8,0},{12,20},{16,8},{20,28},{24,16},{5,13},{9,1},{13,21},{... | collective-permute-start | bytes 1769480 | tf_op jit(solution)/shard_map/ppermute | solution.py:183
  12.5 16.8 %collective-permute-start.4 = (bf16[6,160,128]{2,1,0:T(8,128)(2,1)S(1)}, bf16[6,160,128]{2,1,0:T(8,128)(2,1)S(1)}, u32[]{:S(2)}, u32[]{:S(2)}) collective-permute-start(bf16[6,160,128]{2,1,0:T(8,128)(2,1)S(1)} %get-tuple-element.32), channel_id=1, source_target_pairs={{0,4},{4,0},{8,12},{12,8},{16,20},{20,16},{24,28},{28,24},{1,5},{5... | collective-permute-start | bytes 737288 | tf_op jit(solution)/shard_map/ppermute | solution.py:177
  15.3 18.7 %collective-permute-start.5 = (bf16[6,160,128]{2,1,0:T(8,128)(2,1)S(1)}, bf16[6,160,128]{2,1,0:T(8,128)(2,1)S(1)}, u32[]{:S(2)}, u32[]{:S(2)}) collective-permute-start(bf16[6,160,128]{2,1,0:T(8,128)(2,1)S(1)} %get-tuple-element.31.d_own), channel_id=1, source_target_pairs={{4,12},{8,0},{12,20},{16,8},{20,28},{24,16},{5,13},{9,1},{13,21},{... | collective-permute-start | bytes 737288 | tf_op jit(solution)/shard_map/ppermute | solution.py:179
  29.4 10.8 %collective-permute-start.6 = (bf16[6,160,128]{2,1,0:T(8,128)(2,1)S(1)}, bf16[6,160,128]{2,1,0:T(8,128)(2,1)S(1)}, u32[]{:S(2)}, u32[]{:S(2)}) collective-permute-start(bf16[6,160,128]{2,1,0:T(8,128)(2,1)S(1)} %collective-permute-done.4.d_par), channel_id=1, source_target_pairs={{12,4},{0,8},{20,12},{8,16},{28,20},{16,24},{13,5},{1,9},{21,13},{... | collective-permute-start | bytes 737288 | tf_op jit(solution)/shard_map/ppermute | solution.py:184
  33.8 8.4 %copy-start.2 = (bf16[6,192,256]{2,1,0:T(8,128)(2,1)}, bf16[6,192,256]{2,1,0:T(8,128)(2,1)S(1)}, u32[]{:S(2)}) copy-start(bf16[6,192,256]{2,1,0:T(8,128)(2,1)S(1)} %collective-permute-done.2.f_near) | copy-start | bytes 1769476
  43.1 28.7 %copy-start.1 = (bf16[3,3,256,128]{3,2,1,0:T(8,128)(2,1)S(1)}, bf16[3,3,256,128]{3,2,1,0:T(8,128)(2,1)}, u32[]{:S(2)}) copy-start(bf16[3,3,256,128]{3,2,1,0:T(8,128)(2,1)} %w.3) | copy-start | bytes 1769476
  43.1 36.2 %all-to-all-start = ((f16[32,80,128]{2,1,0:T(8,128)(2,1)}), f16[32,80,128]{2,1,0:T(8,128)(2,1)}, u32[]{:S(2)}, u32[]{:S(2)}) async-start(f16[32,80,128]{2,1,0:T(8,128)(2,1)} %convert_element_type.20), calls=%async_computation | async-start | bytes 1310720 | tf_op jit(solution)/shard_map/all_to_all | solution.py:201
  48.1 23.8 %collective-permute-start.8 = (bf16[6,192,256]{2,1,0:T(8,128)(2,1)S(1)}, bf16[6,192,256]{2,1,0:T(8,128)(2,1)S(1)}, u32[]{:S(2)}, u32[]{:S(2)}) collective-permute-start(bf16[6,192,256]{2,1,0:T(8,128)(2,1)S(1)} %collective-permute-done.3.f_par), channel_id=1, source_target_pairs={{12,4},{0,8},{20,12},{8,16},{28,20},{16,24},{13,5},{1,9},{21,13},{... | collective-permute-start | bytes 1769480 | tf_op jit(solution)/shard_map/ppermute | solution.py:185
  51.8 3.1 %collective-permute-start.7 = (bf16[4,6,16,128]{3,2,1,0:T(8,128)(2,1)S(1)}, bf16[4,6,16,128]{3,2,1,0:T(8,128)(2,1)S(1)}, u32[]{:S(2)}, u32[]{:S(2)}) collective-permute-start(bf16[4,6,16,128]{3,2,1,0:T(8,128)(2,1)S(1)} %pad_maximum_fusion.2), channel_id=1, source_target_pairs={{0,1},{1,2},{2,3},{4,5},{5,6},{6,7},{8,9},{9,10},{10,11},{12,13},{... | collective-permute-start | bytes 294920 | tf_op jit(solution)/shard_map/ppermute | solution.py:143
  53.6 36.1 %collective-permute-start.10 = (bf16[4,6,16,128]{3,2,1,0:T(8,128)(2,1)S(1)}, bf16[4,6,16,128]{3,2,1,0:T(8,128)(2,1)S(1)}, u32[]{:S(2)}, u32[]{:S(2)}) collective-permute-start(bf16[4,6,16,128]{3,2,1,0:T(8,128)(2,1)S(1)} %pad_maximum_fusion.3), channel_id=1, source_target_pairs={{1,0},{2,1},{3,2},{5,4},{6,5},{7,6},{9,8},{10,9},{11,10},{13,12},{... | collective-permute-start | bytes 294920 | tf_op jit(solution)/shard_map/ppermute | solution.py:144
  54.9 0.6 copy-start.4
  71.8 1.1 copy-start.3
  75.7 19.5 %collective-permute-start.9 = (bf16[6,160,128]{2,1,0:T(8,128)(2,1)}, bf16[6,160,128]{2,1,0:T(8,128)(2,1)S(1)}, u32[]{:S(2)}, u32[]{:S(2)}) collective-permute-start(bf16[6,160,128]{2,1,0:T(8,128)(2,1)} %get-tuple-element.18), channel_id=1, source_target_pairs={{0,4},{4,0},{8,12},{12,8},{16,20},{20,16},{24,28},{28,24},{1,5},{5... | collective-permute-start | bytes 737288 | tf_op jit(solution)/shard_map/ppermute | solution.py:223
  81.1 9.2 %copy-start.5 = (bf16[4,6,16,128]{3,2,1,0:T(8,128)(2,1)S(1)}, bf16[4,6,16,128]{3,2,1,0:T(8,128)(2,1)}, u32[]{:S(2)}) copy-start(bf16[4,6,16,128]{3,2,1,0:T(8,128)(2,1)} %copy-done.4) | copy-start | bytes 294916
  83.2 28.2 %all-to-all-start.1 = ((f16[32,72,128]{2,1,0:T(8,128)(2,1)}), f16[32,72,128]{2,1,0:T(8,128)(2,1)}, u32[]{:S(2)}, u32[]{:S(2)}) async-start(f16[32,72,128]{2,1,0:T(8,128)(2,1)} %broadcast_in_dim.2), calls=%async_computation.1 | async-start | bytes 1179648 | tf_op jit(solution)/shard_map/all_to_all | solution.py:229
  89.6 0.6 copy-start.6
  90.3 0.9 copy-start.7
  93.4 16.9 %collective-permute-start.11 = (bf16[6,160,256]{2,1,0:T(8,128)(2,1)S(1)}, bf16[6,160,256]{2,1,0:T(8,128)(2,1)S(1)}, u32[]{:S(2)}, u32[]{:S(2)}) collective-permute-start(bf16[6,160,256]{2,1,0:T(8,128)(2,1)S(1)} %get-tuple-element.21), channel_id=1, source_target_pairs={{0,4},{4,0},{8,12},{12,8},{16,20},{20,16},{24,28},{28,24},{1,5},{5... | collective-permute-start | bytes 1474568 | tf_op jit(solution)/shard_map/ppermute | solution.py:213

commit v4 on v3

--- a/solution.py
+++ b/solution.py
@@ -12,7 +12,8 @@
 DILATION_STEP = 12
 STRIP = 16
 TOP = 14
-ALL = ("rows", "cols")
+COLS = ("x", "core")
+CHIPS = ("rows", "x")
 VMEM = pltpu.VMEM
 
 
@@ -48,8 +49,8 @@
         out[:, pl.ds(STRIP + width, STRIP), :] = right[rows]
 
 
-def kernel_grad(chunk, par, f_own, f_par, d_own, d_par, d_near, d_far, out, ext, shifted, acc):
-    odd = par[0]
+def kernel_grad(par, f_own, f_par, d_own, d_par, d_near, d_far, keep, give, ext, shifted, acc):
+    odd, core = (par[0], par[1])
     half, width, cout = d_own.shape
     cin = f_own.shape[2]
     pixels = half * width
@@ -66,17 +67,24 @@
         rhs = jnp.concatenate([ext[slot + 1 - a].reshape(pixels, cout) for a in range(3)], axis=1)
         term = lax.dot_general(lhs, rhs, (((0,), (0,)), ((), ())), preferred_element_type=jnp.float32)
         total = term if total is None else total + term
-    top = jnp.zeros((8, cout), jnp.float32)
     for a in range(3):
         for b in range(3):
             piece = total[b * cin : (b + 1) * cin, a * cout : (a + 1) * cout]
             acc[pl.ds((3 * a + b) * cin, cin), :] = piece
-            top = jnp.maximum(top, jnp.max(jnp.abs(piece).reshape(cin // 8, 8, cout), axis=0))
+    size = keep.shape[0]
+    keep[...] = acc[pl.ds(core * size, size), :]
+    give[...] = acc[pl.ds((1 - core) * size, size), :]
+
+
+def kernel_scale(chunk, par, keep, given, out):
+    total = keep[...] + given[...]
+    size, cout = keep.shape
+    top = jnp.max(jnp.abs(total).reshape(size // 8, 8, cout), axis=0)
     most = jnp.max(jnp.max(top, axis=0, keepdims=True), axis=1, keepdims=True)
     level = jnp.ceil(jnp.log2(jnp.maximum(jnp.broadcast_to(most, (8, cout)), 2.0**-110)))
-    scale = jnp.exp2(TOP - level)[:1]
+    scaled = total * jnp.exp2(TOP - level)[:1]
     for c in range(out.shape[0]):
-        out[c, pl.ds(0, chunk), :] = acc[pl.ds(c * chunk, chunk), :] * scale
+        out[c, pl.ds(0, chunk), :] = scaled[c * chunk : (c + 1) * chunk]
         out[c, pl.ds(chunk, out.shape[1] - chunk), :] = jnp.broadcast_to(level[:1], (out.shape[1] - chunk, cout))
 
 
@@ -140,8 +148,8 @@
     tails = [x[..., width - STRIP :, :] for x in blocks]
     heads = [x[..., :STRIP, :] for x in blocks]
     tails, heads = (x[0] if len(x) == 1 else jnp.stack(x) for x in (tails, heads))
-    left = lax.ppermute(tails, "cols", [(i, i + 1) for i in range(count - 1)])
-    right = lax.ppermute(heads, "cols", [(i + 1, i) for i in range(count - 1)])
+    left = lax.ppermute(tails, COLS, [(i, i + 1) for i in range(count - 1)])
+    right = lax.ppermute(heads, COLS, [(i + 1, i) for i in range(count - 1)])
     return left, right
 
 
@@ -155,21 +163,26 @@
     height, width, cin = features.shape
     cout = weight.shape[3]
     half = height // 2
-    rows, cols = (lax.axis_size("rows"), lax.axis_size("cols"))
-    devices = rows * cols
+    rows = lax.axis_size("rows")
+    cols = lax.axis_size("x") * lax.axis_size("core")
+    chips = rows * lax.axis_size("x")
     odd = lax.axis_index("rows") % 2
-    par = odd.astype(jnp.int32).reshape(1)
+    core = lax.axis_index("core")
+    par = jnp.stack([odd, core]).astype(jnp.int32)
 
     swap = [(i, i ^ 1) for i in range(rows)]
+    other_core = [(0, 1), (1, 0)]
     up = [(i, i + 2 if i % 2 else i - 2) for i in range(rows)]
     near = [(i, j) for i, j in up if 0 <= j < rows]
     far = [(j, i) for i, j in near]
+    fence = lax.optimization_barrier
 
     def pick(cells, which):
         return lax.dynamic_slice_in_dim(cells, which * half, half, 0)
 
     wide = width + 2 * STRIP
-    chunk = 9 * cin // devices
+    share = 9 * cin // 2
+    chunk = share // chips
     deep = -(-(chunk + 1) // STRIP) * STRIP
     flops = 2 * 9 * height * width * cin * cout
 
@@ -179,18 +192,20 @@
     d_near = lax.ppermute(d_own, "rows", near)
     broad = jax.ShapeDtypeStruct((half, wide, cin), jnp.bfloat16)
     f_own, f_give = call(kernel_extend, (par, features, f_left, f_right), [broad, broad], [], 0)
+    f_give, d_par = fence((f_give, d_par))
+    d_far = lax.ppermute(d_par, "rows", far)
     f_par = lax.ppermute(f_give, "rows", swap)
     f_near = lax.ppermute(f_own, "rows", near)
-    d_far = lax.ppermute(d_par, "rows", far)
     f_far = lax.ppermute(f_par, "rows", far)
     d_blocks = (d_own, d_par, d_near, d_far)
-
-    f_own, f_near = lax.optimization_barrier((f_own, f_near))
-    ext = VMEM((4, half, wide, cout), jnp.bfloat16)
-    (scaled,) = call(
-        functools.partial(kernel_grad, chunk),
+    d_left, d_right = strips(d_blocks, cols)
+
+    f_own, f_near = fence((f_own, f_near))
+    part = jax.ShapeDtypeStruct((share, cout), jnp.float32)
+    keep, give = call(
+        kernel_grad,
         (par, f_own, f_par) + d_blocks,
-        [jax.ShapeDtypeStruct((devices, deep, cout), jnp.float32)],
+        [part, part],
         [
             VMEM((4, half, width, cout), jnp.bfloat16),
             VMEM((half, width, 3 * cin), jnp.bfloat16),
@@ -198,19 +213,28 @@
         ],
         flops,
     )
-    got = lax.all_to_all(scaled.astype(jnp.float16), ALL, 0, 0)
-
-    d_left, d_right = strips(d_blocks, cols)
-    d_left, f_far = lax.optimization_barrier((d_left, f_far))
+    given = lax.ppermute(give, "core", other_core)
+
     half_grad = jax.ShapeDtypeStruct((half, width, cin), jnp.bfloat16)
     g_own, g_par = call(
         kernel_back,
         (par, weight) + d_blocks + (d_left, d_right),
         [half_grad, half_grad],
-        [ext, VMEM((4, half, width, 3 * cout), jnp.bfloat16)],
+        [VMEM((4, half, wide, cout), jnp.bfloat16), VMEM((4, half, width, 3 * cout), jnp.bfloat16)],
         flops,
     )
+    given, g_par = fence((given, g_par))
     g_other = lax.ppermute(g_par, "rows", swap)
+
+    (scaled,) = call(
+        functools.partial(kernel_scale, chunk),
+        (par, keep, given),
+        [jax.ShapeDtypeStruct((chips, deep, cout), jnp.float32)],
+        [],
+        0,
+    )
+    scaled, f_far = fence((scaled.astype(jnp.float16), f_far))
+    got = lax.all_to_all(scaled, CHIPS, 0, 0)
 
     half_out = jax.ShapeDtypeStruct((half, width, cout), jnp.bfloat16)
     o_own, o_par = call(
@@ -220,16 +244,26 @@
         [VMEM((4, half, wide, cin), jnp.bfloat16)],
         flops,
     )
+    got, o_par = fence((got, o_par))
     o_other = lax.ppermute(o_par, "rows", swap)
 
     levels = got[:, chunk : chunk + 1].astype(jnp.float32)
     highest = jnp.max(levels, axis=0, keepdims=True)
-    shares = got[:, :chunk].astype(jnp.float32) * jnp.exp2(levels - highest)
-    mine = (jnp.sum(shares, axis=0, keepdims=True) * (1.0 / devices)).astype(jnp.float16)
-    spread = lax.all_to_all(jnp.broadcast_to(mine, (devices, chunk, cout)), ALL, 0, 0)
-
-    norm = devices / jnp.sqrt(jnp.float32(height * width * devices))
-    weight_grad = spread.astype(jnp.float32) * (jnp.exp2(highest - TOP) * norm)
+    shares = got.astype(jnp.float32) * jnp.exp2(levels - highest)
+    mine = jnp.sum(shares, axis=0, keepdims=True) * (1.0 / chips)
+    place = lax.broadcasted_iota(jnp.int32, mine.shape, 1)
+    mine = jnp.where(place < chunk, mine, highest).astype(jnp.float16)
+    spread = lax.all_to_all(jnp.broadcast_to(mine, (chips, deep, cout)), CHIPS, 0, 0)
+    other = lax.ppermute(spread, "core", other_core)
+
+    norm = chips / jnp.sqrt(jnp.float32(height * width * chips * 2))
+
+    def restored(low, high):
+        picked = jnp.where(core == 0, low, high)
+        factor = jnp.exp2(picked[:1, chunk : chunk + 1].astype(jnp.float32) - TOP) * norm
+        return (picked[:, :chunk].astype(jnp.float32) * factor).reshape(share, cout)
+
+    weight_grad = jnp.concatenate([restored(spread, other), restored(other, spread)], axis=0)
     return (
         joined(odd, o_own, o_other),
         joined(odd, g_own, g_other),
@@ -238,10 +272,12 @@
 
 
 def solution(mesh):
-    placed = P("rows", "cols", None)
+    rows, cols = (mesh.shape["rows"], mesh.shape["cols"])
+    fine = Mesh(mesh.devices.reshape(rows, cols // 2, 2), ("rows",) + COLS)
+    placed = P("rows", COLS, None)
     return jax.shard_map(
         body,
-        mesh=mesh,
+        mesh=fine,
         in_specs=(placed, P(), placed),
         out_specs=(placed, placed, P()),
         check_vma=False,

time: 114 us -> 94.4 us (0.83)
  waiting for transfers between devices: 50.5 us -> 29 us
  Pallas kernels: 7.22 us -> 12 us
  starting transfers between devices: 40.5 us -> 38 us
    ppermute x1, waiting for transfers between devices: 14.3 us -> 0.01 us  [body(): g_other = lax.ppermute(g_par, 'rows', swap)]
    ppermute x1, waiting for transfers between devices: 16.3 us -> 2.61 us  [body(): f_far = lax.ppermute(f_par, 'rows', far)]
    ppermute x1, waiting for transfers between devices: 12.7 us -> 0.01 us  [body(): d_par = lax.ppermute(d_give, 'rows', swap)]
    all_to_all x2, waiting for transfers between devices: 0.01 us -> 11 us  [the longest x1 6.33 us: body(): lax.all_to_all(jnp.broadcast_to(mine, (chips, deep, cout)), CHIPS, 0, 0)]
    ppermute x1, waiting for transfers between devices: 0.21 us -> 10.3 us  [body(): d_near = lax.ppermute(d_own, 'rows', near)]
    ppermute x1, waiting for transfers between devices: 6.07 us -> 0.01 us  [body(): d_far = lax.ppermute(d_par, 'rows', far)]
    pallas_call x4 -> x5, Pallas kernels: 7.22 us -> 12 us  [call(): pl.pallas_call(kernel, out_shape=outs, in_specs=[pl.BlockSpec(memory_spac...]
    ppermute x4 -> x6, waiting for transfers between devices: 0.9 us -> 5.04 us  [the longest x2 3.37 us: strips(): right = lax.ppermute(heads, COLS, [(i + 1, i) for i in range(count - 1)])]
  transfers between devices with their start and end apart: 14 -> 16, of which waited for: 6 -> 7; matrix products, arithmetic and copies ran while one was open for 5% -> 10% of each run, Pallas kernels for 4% -> 10%
where the time goes in v4:
time: 94.4 us; the launch traced here: 93.5 us
  starting transfers between devices  38 us (40%)
  waiting for transfers between devices  29 us (31%)
  Pallas kernels  12 us (13%)
  other arithmetic  7.93 us (8%)
  local copies, waits for them, and re-layouts  5.58 us (6%)
    pallas_call x5, Pallas kernels, call(): pl.pallas_call(kernel, out_shape=outs, in_specs=[pl.BlockSpec(memory_spac...  12 us
    ppermute x1, waiting for transfers between devices, body(): d_near = lax.ppermute(d_own, 'rows', near)  10.3 us
    all_to_all x1, waiting for transfers between devices, body(): lax.all_to_all(jnp.broadcast_to(mine, (chips, deep, cout)), CHIPS, 0, 0)  6.33 us
    all_to_all x1, starting transfers between devices, body(): got = lax.all_to_all(scaled, CHIPS, 0, 0)  4.81 us
    all_to_all x1, waiting for transfers between devices, body(): got = lax.all_to_all(scaled, CHIPS, 0, 0)  4.71 us
    ppermute x1, starting transfers between devices, body(): d_far = lax.ppermute(d_par, 'rows', far)  4.55 us
    ppermute x2, starting transfers between devices, strips(): left = lax.ppermute(tails, COLS, [(i, i + 1) for i in range(count - 1)])  4.5 us
    all_to_all x1, starting transfers between devices, body(): lax.all_to_all(jnp.broadcast_to(mine, (chips, deep, cout)), CHIPS, 0, 0)  3.59 us
  transfers between devices with their start and end apart: 16, of which 7 were waited for; matrix products, arithmetic and copies ran while one was open for 10% of the time, Pallas kernels for 10%

profile of v4, /device:TPU:0, one launch (start us, length us, event | category | flops | bytes accessed | tf_op | source)
XLA Modules:
  0.0 93.5 jit_solution(14531842498247349428)
XLA Ops:
  0.6 0.0 copy-start
  0.7 1.2 %constant_dynamic-slice_fusion = (bf16[6,160,128]{2,1,0:T(8,128)(2,1)S(1)}, bf16[6,160,128]{2,1,0:T(8,128)(2,1)S(1)}) fusion(bf16[12,160,128]{2,1,0:T(8,128)(2,1)} %param.5, s32[]{:T(128)S(6)} %select_n.61, s32[]{:T(128)S(6)} %select_n.60), kind=kLoop, calls=%fused_computation.25 | loop fusion | bytes 983048 | tf_op jit(solution)/shard_map/dynamic_slice | solution.py:181
  1.8 3.0 %collective-permute-start.3 = (bf16[6,160,128]{2,1,0:T(8,128)(2,1)S(1)}, bf16[6,160,128]{2,1,0:T(8,128)(2,1)S(1)}, u32[]{:S(2)}, u32[]{:S(2)}) collective-permute-start(bf16[6,160,128]{2,1,0:T(8,128)(2,1)S(1)} %get-tuple-element.50), channel_id=1, source_target_pairs={{0,4},{4,0},{8,12},{12,8},{16,20},{20,16},{24,28},{28,24},{1,5},{5... | collective-permute-start | bytes 737288 | tf_op jit(solution)/shard_map/ppermute | solution.py:190
  4.9 1.0 %fusion.10 = (bf16[12,16,256]{2,1,0:T(8,128)(2,1)S(1)}, bf16[12,16,256]{2,1,0:T(8,128)(2,1)S(1)}) fusion(bf16[12,160,256]{2,1,0:T(8,128)(2,1)} %cells.1), kind=kLoop, calls=%fused_computation.41 | loop fusion | bytes 393216 | tf_op jit(solution)/shard_map/slice | solution.py:149
  5.8 1.5 %collective-permute-start = (bf16[12,16,256]{2,1,0:T(8,128)(2,1)S(1)}, bf16[12,16,256]{2,1,0:T(8,128)(2,1)S(1)}, u32[]{:S(2)}, u32[]{:S(2)}) collective-permute-start(bf16[12,16,256]{2,1,0:T(8,128)(2,1)S(1)} %get-tuple-element.42), channel_id=1, source_target_pairs={{0,1},{1,2},{2,3},{4,5},{5,6},{6,7},{8,9},{9,10},{10,11},{12,13},{... | collective-permute-start | bytes 294920 | tf_op jit(solution)/shard_map/ppermute | solution.py:151
  7.3 1.3 %collective-permute-start.1 = (bf16[12,16,256]{2,1,0:T(8,128)(2,1)S(1)}, bf16[12,16,256]{2,1,0:T(8,128)(2,1)S(1)}, u32[]{:S(2)}, u32[]{:S(2)}) collective-permute-start(bf16[12,16,256]{2,1,0:T(8,128)(2,1)S(1)} %get-tuple-element.41), channel_id=1, source_target_pairs={{1,0},{2,1},{3,2},{5,4},{6,5},{7,6},{9,8},{10,9},{11,10},{13,12},{... | collective-permute-start | bytes 294920 | tf_op jit(solution)/shard_map/ppermute | solution.py:152
  8.6 0.1 pad_add_fusion.par
  8.7 0.0 collective-permute-done.left
  8.7 3.4 %collective-permute-done.1.right = bf16[12,16,256]{2,1,0:T(8,128)(2,1)S(1)} collective-permute-done((bf16[12,16,256]{2,1,0:T(8,128)(2,1)S(1)}, bf16[12,16,256]{2,1,0:T(8,128)(2,1)S(1)}, u32[]{:S(2)}, u32[]{:S(2)}) %collective-permute-start.1) | collective-permute-done | bytes 98336 | tf_op jit(solution)/shard_map/ppermute | solution.py:152
  12.1 1.4 %shard_map.58 = (bf16[6,192,256]{2,1,0:T(8,128)(2,1)S(1)}, bf16[6,192,256]{2,1,0:T(8,128)(2,1)}) custom-call(s32[2]{0:T(128)S(1)} %pad_add_fusion.par, bf16[12,160,256]{2,1,0:T(8,128)(2,1)S(1)} %copy-done, bf16[12,16,256]{2,1,0:T(8,128)(2,1)S(1)} %collective-permute-done.left, bf16[12,16,256]{2,1,0:T(8,128)(2,1)S(1)} %collective-permute-done.1.right), custom_call_target="tpu_custom_call" | custom-call | bytes 2359304 | tf_op jit(solution)/shard_map/pallas_call | solution.py:135
  13.5 1.3 %collective-permute-start.2 = (bf16[6,192,256]{2,1,0:T(8,128)(2,1)S(1)}, bf16[6,192,256]{2,1,0:T(8,128)(2,1)S(1)}, u32[]{:S(2)}, u32[]{:S(2)}) collective-permute-start(bf16[6,192,256]{2,1,0:T(8,128)(2,1)S(1)} %get-tuple-element.22.f_own), channel_id=1, source_target_pairs={{4,12},{8,0},{12,20},{16,8},{20,28},{24,16},{5,13},{9,1},{13,21},{... | collective-permute-start | bytes 1769480 | tf_op jit(solution)/shard_map/ppermute | solution.py:198
  14.8 2.8 %collective-permute-start.4 = (bf16[6,192,256]{2,1,0:T(8,128)(2,1)}, bf16[6,192,256]{2,1,0:T(8,128)(2,1)}, u32[]{:S(2)}, u32[]{:S(2)}) collective-permute-start(bf16[6,192,256]{2,1,0:T(8,128)(2,1)} %get-tuple-element.24), channel_id=1, source_target_pairs={{0,4},{4,0},{8,12},{12,8},{16,20},{20,16},{24,28},{28,24},{1,5},{5... | collective-permute-start | bytes 1769480 | tf_op jit(solution)/shard_map/ppermute | solution.py:197
  17.6 1.3 %collective-permute-start.5 = (bf16[6,160,128]{2,1,0:T(8,128)(2,1)S(1)}, bf16[6,160,128]{2,1,0:T(8,128)(2,1)S(1)}, u32[]{:S(2)}, u32[]{:S(2)}) collective-permute-start(bf16[6,160,128]{2,1,0:T(8,128)(2,1)S(1)} %get-tuple-element.49.d_own), channel_id=1, source_target_pairs={{4,12},{8,0},{12,20},{16,8},{20,28},{24,16},{5,13},{9,1},{13,21},{... | collective-permute-start | bytes 737288 | tf_op jit(solution)/shard_map/ppermute | solution.py:192
  18.9 0.8 dynamic-slice_bitcast_fusion
  19.7 4.5 %collective-permute-start.6 = (bf16[6,160,128]{2,1,0:T(8,128)(2,1)S(1)}, bf16[6,160,128]{2,1,0:T(8,128)(2,1)S(1)}, u32[]{:S(2)}, u32[]{:S(2)}) collective-permute-start(bf16[6,160,128]{2,1,0:T(8,128)(2,1)S(1)} %collective-permute-done.3.d_par), channel_id=1, source_target_pairs={{12,4},{0,8},{20,12},{8,16},{28,20},{16,24},{13,5},{1,9},{21,13},{... | collective-permute-start | bytes 737288 | tf_op jit(solution)/shard_map/ppermute | solution.py:196
  24.2 10.3 %collective-permute-done.5.d_near = bf16[6,160,128]{2,1,0:T(8,128)(2,1)S(1)} collective-permute-done((bf16[6,160,128]{2,1,0:T(8,128)(2,1)S(1)}, bf16[6,160,128]{2,1,0:T(8,128)(2,1)S(1)}, u32[]{:S(2)}, u32[]{:S(2)}) %collective-permute-start.5) | collective-permute-done | bytes 245792 | tf_op jit(solution)/shard_map/ppermute | solution.py:192
  34.5 0.0 collective-permute-done.2.f_near
  34.5 3.1 %shard_map.59 = (f32[1152,128]{1,0:T(8,128)S(1)}, f32[1152,128]{1,0:T(8,128)S(1)}) custom-call(s32[2]{0:T(128)S(1)} %pad_add_fusion.par, bf16[6,192,256]{2,1,0:T(8,128)(2,1)S(1)} %get-tuple-element.22.f_own, bf16[6,192,256]{2,1,0:T(8,128)(2,1)} %collective-permute-done.4.f_par, bf16[6,160,128]{2,1,0:T(8,128)(2,1)S(1)} %get-tuple-element.49.d_own, ...), custom_call_target="tpu_custom_call" | custom-call | flops 1132462080 | bytes 3342344 | tf_op jit(solution)/shard_map/pallas_call | solution.py:135
  37.6 2.2 %collective-permute-start.7 = (f32[1152,128]{1,0:T(8,128)S(1)}, f32[1152,128]{1,0:T(8,128)S(1)}, u32[]{:S(2)}, u32[]{:S(2)}) collective-permute-start(f32[1152,128]{1,0:T(8,128)S(1)} %get-tuple-element.27), channel_id=1, source_target_pairs={{0,1},{1,0},{2,3},{3,2},{4,5},{5,4},{6,7},{7,6},{8,9},{9,8},{10,11... | collective-permute-start | bytes 1769480 | tf_op jit(solution)/shard_map/ppermute | solution.py:216
  39.9 3.5 %collective-permute-start.10 = (bf16[6,192,256]{2,1,0:T(8,128)(2,1)}, bf16[6,192,256]{2,1,0:T(8,128)(2,1)S(1)}, u32[]{:S(2)}, u32[]{:S(2)}) collective-permute-start(bf16[6,192,256]{2,1,0:T(8,128)(2,1)} %collective-permute-done.4.f_par), channel_id=1, source_target_pairs={{12,4},{0,8},{20,12},{8,16},{28,20},{16,24},{13,5},{1,9},{21,13},{... | collective-permute-start | bytes 1769480 | tf_op jit(solution)/shard_map/ppermute | solution.py:199
  43.4 1.3 %collective-permute-start.9 = (bf16[4,6,16,128]{3,2,1,0:T(8,128)(2,1)S(1)}, bf16[4,6,16,128]{3,2,1,0:T(8,128)(2,1)S(1)}, u32[]{:S(2)}, u32[]{:S(2)}) collective-permute-start(bf16[4,6,16,128]{3,2,1,0:T(8,128)(2,1)S(1)} %pad_maximum_fusion.4), channel_id=1, source_target_pairs={{1,0},{2,1},{3,2},{5,4},{6,5},{7,6},{9,8},{10,9},{11,10},{13,12},{... | collective-permute-start | bytes 294920 | tf_op jit(solution)/shard_map/ppermute | solution.py:152
  44.7 3.0 %collective-permute-start.8 = (bf16[4,6,16,128]{3,2,1,0:T(8,128)(2,1)S(1)}, bf16[4,6,16,128]{3,2,1,0:T(8,128)(2,1)S(1)}, u32[]{:S(2)}, u32[]{:S(2)}) collective-permute-start(bf16[4,6,16,128]{3,2,1,0:T(8,128)(2,1)S(1)} %pad_maximum_fusion.3), channel_id=1, source_target_pairs={{0,1},{1,2},{2,3},{4,5},{5,6},{6,7},{8,9},{9,10},{10,11},{12,13},{... | collective-permute-start | bytes 294920 | tf_op jit(solution)/shard_map/ppermute | solution.py:151
  47.8 0.9 collective-permute-done.8.left
  48.7 3.6 %shard_map.60 = (bf16[6,160,256]{2,1,0:T(8,128)(2,1)S(1)}, bf16[6,160,256]{2,1,0:T(8,128)(2,1)}) custom-call(s32[2]{0:T(128)S(1)} %pad_add_fusion.par, bf16[3,3,256,128]{3,2,1,0:T(8,128)(2,1)S(1)} %copy-done.1, bf16[6,160,128]{2,1,0:T(8,128)(2,1)S(1)} %get-tuple-element.49.d_own, bf16[6,160,128]{2,1,0:T(8,128)(2,1)S(1)} %collective-permute-done.3.d_par, ...), custom_call_target="tpu_custom_call" | custom-call | flops 1132462080 | bytes 2752520 | tf_op jit(solution)/shard_map/pallas_call | solution.py:135
  52.3 0.7 shard_map.61
  53.0 0.8 convert_element_type.29
  53.8 2.6 %collective-permute-done.10.f_far = bf16[6,192,256]{2,1,0:T(8,128)(2,1)S(1)} collective-permute-done((bf16[6,192,256]{2,1,0:T(8,128)(2,1)}, bf16[6,192,256]{2,1,0:T(8,128)(2,1)S(1)}, u32[]{:S(2)}, u32[]{:S(2)}) %collective-permute-start.10) | collective-permute-done | bytes 589856 | tf_op jit(solution)/shard_map/ppermute | solution.py:199
  56.4 0.8 copy-done.2
  57.2 4.8 %all-to-all-start = ((f16[16,80,128]{2,1,0:T(8,128)(2,1)}), f16[16,80,128]{2,1,0:T(8,128)(2,1)}, u32[]{:S(2)}, u32[]{:S(2)}) async-start(f16[16,80,128]{2,1,0:T(8,128)(2,1)} %convert_element_type.29), calls=%async_computation | async-start | bytes 655360 | tf_op jit(solution)/shard_map/all_to_all | solution.py:237
  62.1 1.9 %collective-permute-start.12 = (bf16[6,160,256]{2,1,0:T(8,128)(2,1)}, bf16[6,160,256]{2,1,0:T(8,128)(2,1)}, u32[]{:S(2)}, u32[]{:S(2)}) collective-permute-start(bf16[6,160,256]{2,1,0:T(8,128)(2,1)} %get-tuple-element.36), channel_id=1, source_target_pairs={{0,4},{4,0},{8,12},{12,8},{16,20},{20,16},{24,28},{28,24},{1,5},{5... | collective-permute-start | bytes 1474568 | tf_op jit(solution)/shard_map/ppermute | solution.py:227
  64.0 1.1 %copy-done.3 = bf16[6,192,256]{2,1,0:T(8,128)(2,1)S(1)} copy-done((bf16[6,192,256]{2,1,0:T(8,128)(2,1)S(1)}, bf16[6,192,256]{2,1,0:T(8,128)(2,1)}, u32[]{:S(2)}) %copy-start.3) | copy-done | bytes 589848
  65.1 3.2 %shard_map.62 = (bf16[6,160,128]{2,1,0:T(8,128)(2,1)S(1)}, bf16[6,160,128]{2,1,0:T(8,128)(2,1)S(1)}) custom-call(s32[2]{0:T(128)S(1)} %pad_add_fusion.par, bf16[3,3,256,128]{3,2,1,0:T(8,128)(2,1)S(1)} %copy-done.1, bf16[6,192,256]{2,1,0:T(8,128)(2,1)S(1)} %get-tuple-element.22.f_own, bf16[6,192,256]{2,1,0:T(8,128)(2,1)} %collective-permute-done.4.f_par, ...), custom_call_target="tpu_custom_call" | custom-call | flops 1132462080 | bytes 3440648 | tf_op jit(solution)/shard_map/pallas_call | solution.py:135
  68.3 4.7 %all-to-all-done = f16[16,80,128]{2,1,0:T(8,128)(2,1)} async-done(((f16[16,80,128]{2,1,0:T(8,128)(2,1)}), f16[16,80,128]{2,1,0:T(8,128)(2,1)}, u32[]{:S(2)}, u32[]{:S(2)}) %all-to-all-start) | async-done | bytes 327712 | tf_op jit(solution)/shard_map/all_to_all | solution.py:237
  73.0 0.8 convert_reduce_fusion
  73.8 0.8 multiply_exponential_fusion
  74.6 1.1 %multiply_reduce_fusion = f32[80,128]{1,0:T(8,128)S(1)} fusion(f16[16,80,128]{2,1,0:T(8,128)(2,1)} %all-to-all-done, f32[16,128]{1,0:T(8,128)S(1)} %bitcast.29), kind=kLoop, calls=%fused_computation.2 | loop fusion | flops 481280 | bytes 376832 | tf_op jit(solution)/shard_map/reduce_sum | solution.py:253
  75.6 0.1 select_convert_fusion
  75.7 0.8 broadcast_in_dim.16
  76.5 3.6 %all-to-all-start.1 = ((f16[16,80,128]{2,1,0:T(8,128)(2,1)}), f16[16,80,128]{2,1,0:T(8,128)(2,1)S(1)}, u32[]{:S(2)}, u32[]{:S(2)}) async-start(f16[16,80,128]{2,1,0:T(8,128)(2,1)} %broadcast_in_dim.16), calls=%async_computation.1 | async-start | bytes 655360 | tf_op jit(solution)/shard_map/all_to_all | solution.py:256
  80.1 1.9 %collective-permute-start.11 = (bf16[6,160,128]{2,1,0:T(8,128)(2,1)S(1)}, bf16[6,160,128]{2,1,0:T(8,128)(2,1)S(1)}, u32[]{:S(2)}, u32[]{:S(2)}) collective-permute-start(bf16[6,160,128]{2,1,0:T(8,128)(2,1)S(1)} %get-tuple-element.34), channel_id=1, source_target_pairs={{0,4},{4,0},{8,12},{12,8},{16,20},{20,16},{24,28},{28,24},{1,5},{5... | collective-permute-start | bytes 737288 | tf_op jit(solution)/shard_map/ppermute | solution.py:248
  82.0 1.1 %broadcast_select_fusion.1 = (bf16[6,160,256]{2,1,0:T(8,128)(2,1)S(1)}, bf16[6,160,256]{2,1,0:T(8,128)(2,1)S(1)}) fusion(bf16[6,160,256]{2,1,0:T(8,128)(2,1)} %collective-permute-done.12, bf16[6,160,256]{2,1,0:T(8,128)(2,1)S(1)} %get-tuple-element.37, pred[]{:T(512)S(6)} %eq.6), kind=kLoop, calls=%fused_computation.7 | loop fusion | flops 491520 | bytes 1966081 | tf_op jit(solution)/shard_map/jit(_where)/select_n | solution.py:157
  83.1 1.0 %pad_maximum_fusion.1 = bf16[12,160,256]{2,1,0:T(8,128)(2,1)} fusion(bf16[6,160,256]{2,1,0:T(8,128)(2,1)S(1)} %get-tuple-element.40, bf16[6,160,256]{2,1,0:T(8,128)(2,1)S(1)} %get-tuple-element.39), kind=kLoop, calls=%fused_computation.1 | loop fusion | flops 491520 | bytes 1966080 | tf_op jit(solution)/shard_map/concatenate | solution.py:159
  84.1 6.3 %all-to-all-done.1 = f16[16,80,128]{2,1,0:T(8,128)(2,1)S(1)} async-done(((f16[16,80,128]{2,1,0:T(8,128)(2,1)}), f16[16,80,128]{2,1,0:T(8,128)(2,1)S(1)}, u32[]{:S(2)}, u32[]{:S(2)}) %all-to-all-start.1) | async-done | bytes 327712 | tf_op jit(solution)/shard_map/all_to_all | solution.py:256
  90.5 0.8 pad_maximum_fusion.2
  91.3 0.8 collective-permute-done.13
  92.1 0.2 broadcast_select_fusion.3
  92.3 0.1 convert_multiply_fusion
  92.4 1.1 %pad_maximum_fusion = f32[2304,128]{1,0:T(8,128)} fusion(f32[1152,128]{1,0:T(8,128)S(1)} %bitcast.26, f32[1152,128]{1,0:T(8,128)S(1)} %bitcast.27), kind=kLoop, calls=%fused_computation | loop fusion | flops 294912 | bytes 2359296 | tf_op jit(solution)/shard_map/concatenate | solution.py:266
  (22 shorter events, 0.1 us)
Async XLA Ops:
  0.6 11.4 %copy-start = (bf16[12,160,256]{2,1,0:T(8,128)(2,1)S(1)}, bf16[12,160,256]{2,1,0:T(8,128)(2,1)}, u32[]{:S(2)}) copy-start(bf16[12,160,256]{2,1,0:T(8,128)(2,1)} %cells.1) | copy-start | bytes 2949124
  1.8 12.9 %collective-permute-start.3 = (bf16[6,160,128]{2,1,0:T(8,128)(2,1)S(1)}, bf16[6,160,128]{2,1,0:T(8,128)(2,1)S(1)}, u32[]{:S(2)}, u32[]{:S(2)}) collective-permute-start(bf16[6,160,128]{2,1,0:T(8,128)(2,1)S(1)} %get-tuple-element.50), channel_id=1, source_target_pairs={{0,4},{4,0},{8,12},{12,8},{16,20},{20,16},{24,28},{28,24},{1,5},{5... | collective-permute-start | bytes 737288 | tf_op jit(solution)/shard_map/ppermute | solution.py:190
  5.8 2.9 %collective-permute-start = (bf16[12,16,256]{2,1,0:T(8,128)(2,1)S(1)}, bf16[12,16,256]{2,1,0:T(8,128)(2,1)S(1)}, u32[]{:S(2)}, u32[]{:S(2)}) collective-permute-start(bf16[12,16,256]{2,1,0:T(8,128)(2,1)S(1)} %get-tuple-element.42), channel_id=1, source_target_pairs={{0,1},{1,2},{2,3},{4,5},{5,6},{6,7},{8,9},{9,10},{10,11},{12,13},{... | collective-permute-start | bytes 294920 | tf_op jit(solution)/shard_map/ppermute | solution.py:151
  7.3 4.7 %collective-permute-start.1 = (bf16[12,16,256]{2,1,0:T(8,128)(2,1)S(1)}, bf16[12,16,256]{2,1,0:T(8,128)(2,1)S(1)}, u32[]{:S(2)}, u32[]{:S(2)}) collective-permute-start(bf16[12,16,256]{2,1,0:T(8,128)(2,1)S(1)} %get-tuple-element.41), channel_id=1, source_target_pairs={{1,0},{2,1},{3,2},{5,4},{6,5},{7,6},{9,8},{10,9},{11,10},{13,12},{... | collective-permute-start | bytes 294920 | tf_op jit(solution)/shard_map/ppermute | solution.py:152
  13.5 21.0 %collective-permute-start.2 = (bf16[6,192,256]{2,1,0:T(8,128)(2,1)S(1)}, bf16[6,192,256]{2,1,0:T(8,128)(2,1)S(1)}, u32[]{:S(2)}, u32[]{:S(2)}) collective-permute-start(bf16[6,192,256]{2,1,0:T(8,128)(2,1)S(1)} %get-tuple-element.22.f_own), channel_id=1, source_target_pairs={{4,12},{8,0},{12,20},{16,8},{20,28},{24,16},{5,13},{9,1},{13,21},{... | collective-permute-start | bytes 1769480 | tf_op jit(solution)/shard_map/ppermute | solution.py:198
  14.8 19.7 %collective-permute-start.4 = (bf16[6,192,256]{2,1,0:T(8,128)(2,1)}, bf16[6,192,256]{2,1,0:T(8,128)(2,1)}, u32[]{:S(2)}, u32[]{:S(2)}) collective-permute-start(bf16[6,192,256]{2,1,0:T(8,128)(2,1)} %get-tuple-element.24), channel_id=1, source_target_pairs={{0,4},{4,0},{8,12},{12,8},{16,20},{20,16},{24,28},{28,24},{1,5},{5... | collective-permute-start | bytes 1769480 | tf_op jit(solution)/shard_map/ppermute | solution.py:197
  17.6 16.9 %collective-permute-start.5 = (bf16[6,160,128]{2,1,0:T(8,128)(2,1)S(1)}, bf16[6,160,128]{2,1,0:T(8,128)(2,1)S(1)}, u32[]{:S(2)}, u32[]{:S(2)}) collective-permute-start(bf16[6,160,128]{2,1,0:T(8,128)(2,1)S(1)} %get-tuple-element.49.d_own), channel_id=1, source_target_pairs={{4,12},{8,0},{12,20},{16,8},{20,28},{24,16},{5,13},{9,1},{13,21},{... | collective-permute-start | bytes 737288 | tf_op jit(solution)/shard_map/ppermute | solution.py:192
  19.7 14.9 %collective-permute-start.6 = (bf16[6,160,128]{2,1,0:T(8,128)(2,1)S(1)}, bf16[6,160,128]{2,1,0:T(8,128)(2,1)S(1)}, u32[]{:S(2)}, u32[]{:S(2)}) collective-permute-start(bf16[6,160,128]{2,1,0:T(8,128)(2,1)S(1)} %collective-permute-done.3.d_par), channel_id=1, source_target_pairs={{12,4},{0,8},{20,12},{8,16},{28,20},{16,24},{13,5},{1,9},{21,13},{... | collective-permute-start | bytes 737288 | tf_op jit(solution)/shard_map/ppermute | solution.py:196
  34.5 14.2 %copy-start.1 = (bf16[3,3,256,128]{3,2,1,0:T(8,128)(2,1)S(1)}, bf16[3,3,256,128]{3,2,1,0:T(8,128)(2,1)}, u32[]{:S(2)}) copy-start(bf16[3,3,256,128]{3,2,1,0:T(8,128)(2,1)} %w.3) | copy-start | bytes 1769476
  37.6 14.7 %collective-permute-start.7 = (f32[1152,128]{1,0:T(8,128)S(1)}, f32[1152,128]{1,0:T(8,128)S(1)}, u32[]{:S(2)}, u32[]{:S(2)}) collective-permute-start(f32[1152,128]{1,0:T(8,128)S(1)} %get-tuple-element.27), channel_id=1, source_target_pairs={{0,1},{1,0},{2,3},{3,2},{4,5},{5,4},{6,7},{7,6},{8,9},{9,8},{10,11... | collective-permute-start | bytes 1769480 | tf_op jit(solution)/shard_map/ppermute | solution.py:216
  39.9 16.6 %collective-permute-start.10 = (bf16[6,192,256]{2,1,0:T(8,128)(2,1)}, bf16[6,192,256]{2,1,0:T(8,128)(2,1)S(1)}, u32[]{:S(2)}, u32[]{:S(2)}) collective-permute-start(bf16[6,192,256]{2,1,0:T(8,128)(2,1)} %collective-permute-done.4.f_par), channel_id=1, source_target_pairs={{12,4},{0,8},{20,12},{8,16},{28,20},{16,24},{13,5},{1,9},{21,13},{... | collective-permute-start | bytes 1769480 | tf_op jit(solution)/shard_map/ppermute | solution.py:199
  43.4 4.4 %collective-permute-start.9 = (bf16[4,6,16,128]{3,2,1,0:T(8,128)(2,1)S(1)}, bf16[4,6,16,128]{3,2,1,0:T(8,128)(2,1)S(1)}, u32[]{:S(2)}, u32[]{:S(2)}) collective-permute-start(bf16[4,6,16,128]{3,2,1,0:T(8,128)(2,1)S(1)} %pad_maximum_fusion.4), channel_id=1, source_target_pairs={{1,0},{2,1},{3,2},{5,4},{6,5},{7,6},{9,8},{10,9},{11,10},{13,12},{... | collective-permute-start | bytes 294920 | tf_op jit(solution)/shard_map/ppermute | solution.py:152
  44.7 4.0 %collective-permute-start.8 = (bf16[4,6,16,128]{3,2,1,0:T(8,128)(2,1)S(1)}, bf16[4,6,16,128]{3,2,1,0:T(8,128)(2,1)S(1)}, u32[]{:S(2)}, u32[]{:S(2)}) collective-permute-start(bf16[4,6,16,128]{3,2,1,0:T(8,128)(2,1)S(1)} %pad_maximum_fusion.3), channel_id=1, source_target_pairs={{0,1},{1,2},{2,3},{4,5},{5,6},{6,7},{8,9},{9,10},{10,11},{12,13},{... | collective-permute-start | bytes 294920 | tf_op jit(solution)/shard_map/ppermute | solution.py:151
  56.4 0.8 copy-start.2
  57.2 15.8 %all-to-all-start = ((f16[16,80,128]{2,1,0:T(8,128)(2,1)}), f16[16,80,128]{2,1,0:T(8,128)(2,1)}, u32[]{:S(2)}, u32[]{:S(2)}) async-start(f16[16,80,128]{2,1,0:T(8,128)(2,1)} %convert_element_type.29), calls=%async_computation | async-start | bytes 655360 | tf_op jit(solution)/shard_map/all_to_all | solution.py:237
  62.1 19.9 %collective-permute-start.12 = (bf16[6,160,256]{2,1,0:T(8,128)(2,1)}, bf16[6,160,256]{2,1,0:T(8,128)(2,1)}, u32[]{:S(2)}, u32[]{:S(2)}) collective-permute-start(bf16[6,160,256]{2,1,0:T(8,128)(2,1)} %get-tuple-element.36), channel_id=1, source_target_pairs={{0,4},{4,0},{8,12},{12,8},{16,20},{20,16},{24,28},{28,24},{1,5},{5... | collective-permute-start | bytes 1474568 | tf_op jit(solution)/shard_map/ppermute | solution.py:227
  64.0 1.1 %copy-start.3 = (bf16[6,192,256]{2,1,0:T(8,128)(2,1)S(1)}, bf16[6,192,256]{2,1,0:T(8,128)(2,1)}, u32[]{:S(2)}) copy-start(bf16[6,192,256]{2,1,0:T(8,128)(2,1)} %copy-done.2) | copy-start | bytes 1769476
  76.5 14.0 %all-to-all-start.1 = ((f16[16,80,128]{2,1,0:T(8,128)(2,1)}), f16[16,80,128]{2,1,0:T(8,128)(2,1)S(1)}, u32[]{:S(2)}, u32[]{:S(2)}) async-start(f16[16,80,128]{2,1,0:T(8,128)(2,1)} %broadcast_in_dim.16), calls=%async_computation.1 | async-start | bytes 655360 | tf_op jit(solution)/shard_map/all_to_all | solution.py:256
  80.1 10.4 %collective-permute-start.11 = (bf16[6,160,128]{2,1,0:T(8,128)(2,1)S(1)}, bf16[6,160,128]{2,1,0:T(8,128)(2,1)S(1)}, u32[]{:S(2)}, u32[]{:S(2)}) collective-permute-start(bf16[6,160,128]{2,1,0:T(8,128)(2,1)S(1)} %get-tuple-element.34), channel_id=1, source_target_pairs={{0,4},{4,0},{8,12},{12,8},{16,20},{20,16},{24,28},{28,24},{1,5},{5... | collective-permute-start | bytes 737288 | tf_op jit(solution)/shard_map/ppermute | solution.py:248
  90.5 1.6 %collective-permute-start.13 = (f16[16,80,128]{2,1,0:T(8,128)(2,1)S(1)}, f16[16,80,128]{2,1,0:T(8,128)(2,1)S(1)}, u32[]{:S(2)}, u32[]{:S(2)}) collective-permute-start(f16[16,80,128]{2,1,0:T(8,128)(2,1)S(1)} %all-to-all-done.1), channel_id=1, source_target_pairs={{0,1},{1,0},{2,3},{3,2},{4,5},{5,4},{6,7},{7,6},{8,9},{9,8},{10,11... | collective-permute-start | bytes 983048 | tf_op jit(solution)/shard_map/ppermute | solution.py:257

commit v5 on v4

--- a/solution.py
+++ b/solution.py
@@ -38,39 +38,24 @@
             shifted[slot, :, :, pl.ds(q * cout, cout)] = whole[:, start : start + width].astype(jnp.bfloat16)
 
 
-def kernel_extend(par, cells, left, right, own, give):
-    odd = par[0]
-    half, wide, _ = own.shape
-    width = cells.shape[1]
-    for out, start in ((own, odd * half), (give, (1 - odd) * half)):
-        rows = pl.ds(start, half)
-        out[:, pl.ds(0, STRIP), :] = left[rows]
-        out[:, pl.ds(STRIP, width), :] = cells[rows]
-        out[:, pl.ds(STRIP + width, STRIP), :] = right[rows]
-
-
-def kernel_grad(par, f_own, f_par, d_own, d_par, d_near, d_far, keep, give, ext, shifted, acc):
+def kernel_grad(par, f_own, f_par, d_own, d_par, d_near, d_far, left, right, keep, give, ext, shifted, acc):
     odd, core = (par[0], par[1])
     half, width, cout = d_own.shape
     cin = f_own.shape[2]
     pixels = half * width
-    for block, slot in zip((d_own, d_par, d_near, d_far), slots(odd)):
-        ext[slot] = block[...]
+    gather_map(odd, (d_own, d_par, d_near, d_far), left, right, ext)
+    shift_columns(ext, shifted, width)
     own, partner = slots(odd)[:2]
     total = None
     for block, slot in ((f_own, own), (f_par, partner)):
-        whole = block[...].astype(jnp.float32)
-        for b in range(3):
-            start = STRIP + DILATION_STEP * (b - 1)
-            shifted[:, :, pl.ds(b * cin, cin)] = whole[:, start : start + width].astype(jnp.bfloat16)
-        lhs = shifted[...].reshape(pixels, 3 * cin)
-        rhs = jnp.concatenate([ext[slot + 1 - a].reshape(pixels, cout) for a in range(3)], axis=1)
+        lhs = block[...].reshape(pixels, cin)
+        rhs = jnp.concatenate([shifted[slot + 1 - a].reshape(pixels, 3 * cout) for a in range(3)], axis=1)
         term = lax.dot_general(lhs, rhs, (((0,), (0,)), ((), ())), preferred_element_type=jnp.float32)
         total = term if total is None else total + term
     for a in range(3):
         for b in range(3):
-            piece = total[b * cin : (b + 1) * cin, a * cout : (a + 1) * cout]
-            acc[pl.ds((3 * a + b) * cin, cin), :] = piece
+            start = (3 * a + 2 - b) * cout
+            acc[pl.ds((3 * a + b) * cin, cin), :] = total[:, start : start + cout]
     size = keep.shape[0]
     keep[...] = acc[pl.ds(core * size, size), :]
     give[...] = acc[pl.ds((1 - core) * size, size), :]
@@ -106,12 +91,12 @@
         out[...] = total.astype(jnp.bfloat16).reshape(half, width, cin)
 
 
-def kernel_out(par, w, f_own, f_par, f_near, f_far, out_own, out_par, ext):
+def kernel_out(par, w, f_own, f_par, f_near, f_far, left, right, out_own, out_par, ext):
     odd = par[0]
     half, width, cout = out_own.shape
-    wide, cin = f_own.shape[1:]
-    for block, slot in zip((f_own, f_par, f_near, f_far), slots(odd)):
-        ext[slot] = block[...]
+    cin = f_own.shape[2]
+    wide = width + 2 * STRIP
+    gather_map(odd, (f_own, f_par, f_near, f_far), left, right, ext)
     own, partner = slots(odd)[:2]
     for out, slot in ((out_own, own), (out_par, partner)):
         total = None
@@ -139,15 +124,18 @@
         out_specs=[whole] * len(outs),
         scratch_shapes=scratch,
         compiler_params=pltpu.CompilerParams(vmem_limit_bytes=48 * 1024 * 1024),
-        cost_estimate=pl.CostEstimate(flops=flops, bytes_accessed=size, transcendentals=0),
+        cost_estimate=pl.CostEstimate(flops=flops, bytes_accessed=size if flops else 0, transcendentals=0),
     )(*operands)
 
 
-def strips(blocks, count):
-    width = blocks[0].shape[-2]
-    tails = [x[..., width - STRIP :, :] for x in blocks]
-    heads = [x[..., :STRIP, :] for x in blocks]
-    tails, heads = (x[0] if len(x) == 1 else jnp.stack(x) for x in (tails, heads))
+def edges(blocks):
+    width = blocks[0].shape[1]
+    tails = jnp.stack([x[:, width - STRIP :] for x in blocks])
+    heads = jnp.stack([x[:, :STRIP] for x in blocks])
+    return tails, heads
+
+
+def exchanged(tails, heads, count):
     left = lax.ppermute(tails, COLS, [(i, i + 1) for i in range(count - 1)])
     right = lax.ppermute(heads, COLS, [(i + 1, i) for i in range(count - 1)])
     return left, right
@@ -187,44 +175,32 @@
     flops = 2 * 9 * height * width * cin * cout
 
     d_own, d_give = (pick(cotangent, odd), pick(cotangent, 1 - odd))
+    f_own, f_give = (pick(features, odd), pick(features, 1 - odd))
     d_par = lax.ppermute(d_give, "rows", swap)
-    f_left, f_right = strips((features,), cols)
     d_near = lax.ppermute(d_own, "rows", near)
-    broad = jax.ShapeDtypeStruct((half, wide, cin), jnp.bfloat16)
-    f_own, f_give = call(kernel_extend, (par, features, f_left, f_right), [broad, broad], [], 0)
     f_give, d_par = fence((f_give, d_par))
+    f_par = lax.ppermute(f_give, "rows", swap)
     d_far = lax.ppermute(d_par, "rows", far)
-    f_par = lax.ppermute(f_give, "rows", swap)
-    f_near = lax.ppermute(f_own, "rows", near)
+    f_first, d_near = fence((f_own, d_near))
+    f_near = lax.ppermute(f_first, "rows", near)
     f_far = lax.ppermute(f_par, "rows", far)
     d_blocks = (d_own, d_par, d_near, d_far)
-    d_left, d_right = strips(d_blocks, cols)
-
-    f_own, f_near = fence((f_own, f_near))
+    f_blocks = (f_own, f_par, f_near, f_far)
+    d_left, d_right = exchanged(*edges(d_blocks), cols)
+
     part = jax.ShapeDtypeStruct((share, cout), jnp.float32)
+    d_maps = [VMEM((4, half, wide, cout), jnp.bfloat16), VMEM((4, half, width, 3 * cout), jnp.bfloat16)]
     keep, give = call(
         kernel_grad,
-        (par, f_own, f_par) + d_blocks,
+        (par, f_own, f_par) + d_blocks + (d_left, d_right),
         [part, part],
-        [
-            VMEM((4, half, width, cout), jnp.bfloat16),
-            VMEM((half, width, 3 * cin), jnp.bfloat16),
-            VMEM((9 * cin, cout), jnp.float32),
-        ],
-        flops,
+        d_maps + [VMEM((9 * cin, cout), jnp.float32)],
+        30 * flops,
     )
     given = lax.ppermute(give, "core", other_core)
-
-    half_grad = jax.ShapeDtypeStruct((half, width, cin), jnp.bfloat16)
-    g_own, g_par = call(
-        kernel_back,
-        (par, weight) + d_blocks + (d_left, d_right),
-        [half_grad, half_grad],
-        [VMEM((4, half, wide, cout), jnp.bfloat16), VMEM((4, half, width, 3 * cout), jnp.bfloat16)],
-        flops,
-    )
-    given, g_par = fence((given, g_par))
-    g_other = lax.ppermute(g_par, "rows", swap)
+    f_first, f_near = fence((f_own, f_near))
+    f_tails, f_heads = edges((f_first, f_par, f_near, f_far))
+    given, f_tails, f_heads = fence((given, f_tails, f_heads))
 
     (scaled,) = call(
         functools.partial(kernel_scale, chunk),
@@ -233,16 +209,26 @@
         [],
         0,
     )
-    scaled, f_far = fence((scaled.astype(jnp.float16), f_far))
+    scaled, f_tails, f_heads = fence((scaled.astype(jnp.float16), f_tails, f_heads))
+    f_blocks = (f_own, f_par, f_near, f_far)
     got = lax.all_to_all(scaled, CHIPS, 0, 0)
+
+    d_left, _ = fence((d_left, scaled))
+    half_grad = jax.ShapeDtypeStruct((half, width, cin), jnp.bfloat16)
+    g_own, g_par = call(
+        kernel_back, (par, weight) + d_blocks + (d_left, d_right), [half_grad, half_grad], d_maps, 0
+    )
+    g_other = lax.ppermute(g_par, "rows", swap)
+
+    f_left, f_right = exchanged(f_tails, f_heads, cols)
 
     half_out = jax.ShapeDtypeStruct((half, width, cout), jnp.bfloat16)
     o_own, o_par = call(
         kernel_out,
-        (par, weight, f_own, f_par, f_near, f_far),
+        (par, weight) + f_blocks + (f_left, f_right),
         [half_out, half_out],
         [VMEM((4, half, wide, cin), jnp.bfloat16)],
-        flops,
+        0,
     )
     got, o_par = fence((got, o_par))
     o_other = lax.ppermute(o_par, "rows", swap)
@@ -253,6 +239,7 @@
     mine = jnp.sum(shares, axis=0, keepdims=True) * (1.0 / chips)
     place = lax.broadcasted_iota(jnp.int32, mine.shape, 1)
     mine = jnp.where(place < chunk, mine, highest).astype(jnp.float16)
+    mine, g_other = fence((mine, g_other))
     spread = lax.all_to_all(jnp.broadcast_to(mine, (chips, deep, cout)), CHIPS, 0, 0)
     other = lax.ppermute(spread, "core", other_core)
 

time: 94.4 us -> 100 us (1.059)
  starting transfers between devices: 38 us -> 43.1 us
  Pallas kernels: 12 us -> 9.74 us
  waiting for transfers between devices: 29 us -> 30 us
    ppermute x1, waiting for transfers between devices: 10.3 us -> 0.01 us  [body(): d_near = lax.ppermute(d_own, 'rows', near)]
    ppermute x1, waiting for transfers between devices: 0.01 us -> 6.69 us  [body(): g_other = lax.ppermute(g_par, 'rows', swap)]
    ppermute x1, waiting for transfers between devices: 0.01 us -> 4.83 us  [body(): d_par = lax.ppermute(d_give, 'rows', swap)]
    all_to_all x1, waiting for transfers between devices: 4.71 us -> 0.01 us  [body(): got = lax.all_to_all(scaled, CHIPS, 0, 0)]
    all_to_all x1, starting transfers between devices: 3.59 us -> 6.29 us  [body(): lax.all_to_all(jnp.broadcast_to(mine, (chips, deep, cout)), CHIPS, 0, 0)]
    ppermute x1, waiting for transfers between devices: 2.61 us -> 5.13 us  [body(): f_far = lax.ppermute(f_par, 'rows', far)]
    pallas_call x5 -> x4, Pallas kernels: 12 us -> 9.74 us  [call(): pl.pallas_call(kernel, out_shape=outs, in_specs=[pl.BlockSpec(memory_spac...]
    ppermute x1, starting transfers between devices: 3.03 us -> 5.24 us  [body(): d_par = lax.ppermute(d_give, 'rows', swap)]
  transfers between devices with their start and end apart: 16 -> 16, of which waited for: 7 -> 7; matrix products, arithmetic and copies ran while one was open for 10% -> 8% of each run, Pallas kernels for 10% -> 9%
where the time goes in v5:
time: 100 us; the launch traced here: 99.1 us
  starting transfers between devices  43.1 us (43%)
  waiting for transfers between devices  30 us (30%)
  Pallas kernels  9.74 us (10%)
  other arithmetic  8.74 us (9%)
  local copies, waits for them, and re-layouts  6.53 us (7%)
  between operations  1.01 us (1%)
    pallas_call x4, Pallas kernels, call(): pl.pallas_call(kernel, out_shape=outs, in_specs=[pl.BlockSpec(memory_spac...  9.74 us
    all_to_all x1, waiting for transfers between devices, body(): lax.all_to_all(jnp.broadcast_to(mine, (chips, deep, cout)), CHIPS, 0, 0)  7.54 us
    ppermute x1, waiting for transfers between devices, body(): g_other = lax.ppermute(g_par, 'rows', swap)  6.69 us
    all_to_all x1, starting transfers between devices, body(): got = lax.all_to_all(scaled, CHIPS, 0, 0)  6.38 us
    all_to_all x1, starting transfers between devices, body(): lax.all_to_all(jnp.broadcast_to(mine, (chips, deep, cout)), CHIPS, 0, 0)  6.29 us
    ppermute x2, starting transfers between devices, exchanged(): left = lax.ppermute(tails, COLS, [(i, i + 1) for i in range(count - 1)])  6.08 us
    ppermute x1, starting transfers between devices, body(): d_par = lax.ppermute(d_give, 'rows', swap)  5.24 us
    ppermute x1, waiting for transfers between devices, body(): f_far = lax.ppermute(f_par, 'rows', far)  5.13 us
  transfers between devices with their start and end apart: 16, of which 7 were waited for; matrix products, arithmetic and copies ran while one was open for 8% of the time, Pallas kernels for 9%

profile of v5, /device:TPU:0, one launch (start us, length us, event | category | flops | bytes accessed | tf_op | source)
XLA Modules:
  0.0 99.1 jit_solution(13426469323222807953)
XLA Ops:
  0.7 1.2 %constant_dynamic-slice_fusion = (bf16[6,160,128]{2,1,0:T(8,128)(2,1)S(1)}, bf16[6,160,128]{2,1,0:T(8,128)(2,1)S(1)}) fusion(bf16[12,160,128]{2,1,0:T(8,128)(2,1)} %param.5, s32[]{:T(128)S(6)} %select_n.65, s32[]{:T(128)S(6)} %select_n.66), kind=kLoop, calls=%fused_computation.36 | loop fusion | bytes 983048 | tf_op jit(solution)/shard_map/dynamic_slice | solution.py:169
  1.8 1.3 %collective-permute-start.2 = (bf16[6,160,128]{2,1,0:T(8,128)(2,1)S(1)}, bf16[6,160,128]{2,1,0:T(8,128)(2,1)S(1)}, u32[]{:S(2)}, u32[]{:S(2)}) collective-permute-start(bf16[6,160,128]{2,1,0:T(8,128)(2,1)S(1)} %get-tuple-element.67.d_own), channel_id=1, source_target_pairs={{4,12},{8,0},{12,20},{16,8},{20,28},{24,16},{5,13},{9,1},{13,21},{... | collective-permute-start | bytes 737288 | tf_op jit(solution)/shard_map/ppermute | solution.py:180
  3.1 5.2 %collective-permute-start = (bf16[6,160,128]{2,1,0:T(8,128)(2,1)S(1)}, bf16[6,160,128]{2,1,0:T(8,128)(2,1)S(1)}, u32[]{:S(2)}, u32[]{:S(2)}) collective-permute-start(bf16[6,160,128]{2,1,0:T(8,128)(2,1)S(1)} %get-tuple-element.68), channel_id=1, source_target_pairs={{0,4},{4,0},{8,12},{12,8},{16,20},{20,16},{24,28},{28,24},{1,5},{5... | collective-permute-start | bytes 737288 | tf_op jit(solution)/shard_map/ppermute | solution.py:179
  8.4 0.1 constant_dynamic-slice_fusion.2
  8.5 0.8 dynamic-slice_bitcast_fusion
  9.2 4.8 %collective-permute-done.d_par = bf16[6,160,128]{2,1,0:T(8,128)(2,1)S(1)} collective-permute-done((bf16[6,160,128]{2,1,0:T(8,128)(2,1)S(1)}, bf16[6,160,128]{2,1,0:T(8,128)(2,1)S(1)}, u32[]{:S(2)}, u32[]{:S(2)}) %collective-permute-start) | collective-permute-done | bytes 245792 | tf_op jit(solution)/shard_map/ppermute | solution.py:179
  14.1 3.5 %collective-permute-start.3 = (bf16[6,160,128]{2,1,0:T(8,128)(2,1)S(1)}, bf16[6,160,128]{2,1,0:T(8,128)(2,1)S(1)}, u32[]{:S(2)}, u32[]{:S(2)}) collective-permute-start(bf16[6,160,128]{2,1,0:T(8,128)(2,1)S(1)} %collective-permute-done.d_par), channel_id=1, source_target_pairs={{12,4},{0,8},{20,12},{8,16},{28,20},{16,24},{13,5},{1,9},{21,13},{... | collective-permute-start | bytes 737288 | tf_op jit(solution)/shard_map/ppermute | solution.py:183
  17.6 1.3 %collective-permute-start.7 = (bf16[6,160,256]{2,1,0:T(8,128)(2,1)S(1)}, bf16[6,160,256]{2,1,0:T(8,128)(2,1)S(1)}, u32[]{:S(2)}, u32[]{:S(2)}) collective-permute-start(bf16[6,160,256]{2,1,0:T(8,128)(2,1)S(1)} %get-tuple-element.32.f_own), channel_id=1, source_target_pairs={{4,12},{8,0},{12,20},{16,8},{20,28},{24,16},{5,13},{9,1},{13,21},{... | collective-permute-start | bytes 1474568 | tf_op jit(solution)/shard_map/ppermute | solution.py:185
  18.9 2.9 %collective-permute-start.1 = (bf16[6,160,256]{2,1,0:T(8,128)(2,1)S(1)}, bf16[6,160,256]{2,1,0:T(8,128)(2,1)S(1)}, u32[]{:S(2)}, u32[]{:S(2)}) collective-permute-start(bf16[6,160,256]{2,1,0:T(8,128)(2,1)S(1)} %get-tuple-element.26), channel_id=1, source_target_pairs={{0,4},{4,0},{8,12},{12,8},{16,20},{20,16},{24,28},{28,24},{1,5},{5... | collective-permute-start | bytes 1474568 | tf_op jit(solution)/shard_map/ppermute | solution.py:182
  21.8 0.1 collective-permute-done.3.d_far
  21.9 1.3 %collective-permute-start.5 = (bf16[4,6,16,128]{3,2,1,0:T(8,128)(2,1)S(1)}, bf16[4,6,16,128]{3,2,1,0:T(8,128)(2,1)S(1)}, u32[]{:S(2)}, u32[]{:S(2)}) collective-permute-start(bf16[4,6,16,128]{3,2,1,0:T(8,128)(2,1)S(1)} %pad_maximum_fusion.6), channel_id=1, source_target_pairs={{1,0},{2,1},{3,2},{5,4},{6,5},{7,6},{9,8},{10,9},{11,10},{13,12},{... | collective-permute-start | bytes 294920 | tf_op jit(solution)/shard_map/ppermute | solution.py:140
  23.2 3.0 %collective-permute-start.4 = (bf16[4,6,16,128]{3,2,1,0:T(8,128)(2,1)S(1)}, bf16[4,6,16,128]{3,2,1,0:T(8,128)(2,1)S(1)}, u32[]{:S(2)}, u32[]{:S(2)}) collective-permute-start(bf16[4,6,16,128]{3,2,1,0:T(8,128)(2,1)S(1)} %pad_maximum_fusion.5), channel_id=1, source_target_pairs={{0,1},{1,2},{2,3},{4,5},{5,6},{6,7},{8,9},{9,10},{10,11},{12,13},{... | collective-permute-start | bytes 294920 | tf_op jit(solution)/shard_map/ppermute | solution.py:139
  26.2 0.1 pad_add_fusion.par
  26.3 4.9 %collective-permute-done.7.f_near = bf16[6,160,256]{2,1,0:T(8,128)(2,1)S(1)} collective-permute-done((bf16[6,160,256]{2,1,0:T(8,128)(2,1)S(1)}, bf16[6,160,256]{2,1,0:T(8,128)(2,1)S(1)}, u32[]{:S(2)}, u32[]{:S(2)}) %collective-permute-start.7) | collective-permute-done | bytes 491552 | tf_op jit(solution)/shard_map/ppermute | solution.py:185
  31.3 3.8 %collective-permute-start.8 = (bf16[6,160,256]{2,1,0:T(8,128)(2,1)S(1)}, bf16[6,160,256]{2,1,0:T(8,128)(2,1)S(1)}, u32[]{:S(2)}, u32[]{:S(2)}) collective-permute-start(bf16[6,160,256]{2,1,0:T(8,128)(2,1)S(1)} %collective-permute-done.1.f_par), channel_id=1, source_target_pairs={{12,4},{0,8},{20,12},{8,16},{28,20},{16,24},{13,5},{1,9},{21,13},{... | collective-permute-start | bytes 1474568 | tf_op jit(solution)/shard_map/ppermute | solution.py:186
  35.1 2.7 %shard_map.58 = (f32[1152,128]{1,0:T(8,128)S(1)}, f32[1152,128]{1,0:T(8,128)S(1)}) custom-call(s32[2]{0:T(128)S(1)} %pad_add_fusion.par, bf16[6,160,256]{2,1,0:T(8,128)(2,1)S(1)} %get-tuple-element.32.f_own, bf16[6,160,256]{2,1,0:T(8,128)(2,1)S(1)} %collective-permute-done.1.f_par, bf16[6,160,128]{2,1,0:T(8,128)(2,1)S(1)} %get-tuple-element.67.d_own, ...), custom_call_target="tpu_custom_call" | custom-call | flops 33973862400 | bytes 3342344 | tf_op jit(solution)/shard_map/pallas_call | solution.py:120
  37.9 0.1 collective-permute-start.6
  38.0 5.1 %collective-permute-done.8.f_far = bf16[6,160,256]{2,1,0:T(8,128)(2,1)S(1)} collective-permute-done((bf16[6,160,256]{2,1,0:T(8,128)(2,1)S(1)}, bf16[6,160,256]{2,1,0:T(8,128)(2,1)S(1)}, u32[]{:S(2)}, u32[]{:S(2)}) %collective-permute-start.8) | collective-permute-done | bytes 491552 | tf_op jit(solution)/shard_map/ppermute | solution.py:186
  43.1 0.8 pad_maximum_fusion.3
  43.9 0.7 shard_map.59
  44.7 0.0 copy-start
  44.7 0.8 convert_element_type.32
  45.5 6.4 %all-to-all-start = ((f16[16,80,128]{2,1,0:T(8,128)(2,1)}), f16[16,80,128]{2,1,0:T(8,128)(2,1)}, u32[]{:S(2)}, u32[]{:S(2)}) async-start(f16[16,80,128]{2,1,0:T(8,128)(2,1)} %convert_element_type.32), calls=%async_computation | async-start | bytes 655360 | tf_op jit(solution)/shard_map/all_to_all | solution.py:214
  51.9 1.3 %collective-permute-start.10 = (bf16[4,6,16,256]{3,2,1,0:T(8,128)(2,1)}, bf16[4,6,16,256]{3,2,1,0:T(8,128)(2,1)S(1)}, u32[]{:S(2)}, u32[]{:S(2)}) collective-permute-start(bf16[4,6,16,256]{3,2,1,0:T(8,128)(2,1)} %get-tuple-element.39), channel_id=1, source_target_pairs={{1,0},{2,1},{3,2},{5,4},{6,5},{7,6},{9,8},{10,9},{11,10},{13,12},{... | collective-permute-start | bytes 589832 | tf_op jit(solution)/shard_map/ppermute | solution.py:140
  53.2 3.0 %collective-permute-start.9 = (bf16[4,6,16,256]{3,2,1,0:T(8,128)(2,1)}, bf16[4,6,16,256]{3,2,1,0:T(8,128)(2,1)S(1)}, u32[]{:S(2)}, u32[]{:S(2)}) collective-permute-start(bf16[4,6,16,256]{3,2,1,0:T(8,128)(2,1)} %get-tuple-element.38), channel_id=1, source_target_pairs={{0,1},{1,2},{2,3},{4,5},{5,6},{6,7},{8,9},{9,10},{10,11},{12,13},{... | collective-permute-start | bytes 589832 | tf_op jit(solution)/shard_map/ppermute | solution.py:139
  56.2 0.0 copy-start.2
  56.2 0.9 copy-done.2
  57.2 0.9 copy-done.4
  58.1 0.9 copy-done.6
  59.0 0.9 copy-done.8
  59.9 3.6 %shard_map.61 = (bf16[6,160,256]{2,1,0:T(8,128)(2,1)S(1)}, bf16[6,160,256]{2,1,0:T(8,128)(2,1)}) custom-call(s32[2]{0:T(128)S(1)} %pad_add_fusion.par, bf16[3,3,256,128]{3,2,1,0:T(8,128)(2,1)S(1)} %copy-done, bf16[6,160,128]{2,1,0:T(8,128)(2,1)S(1)} %get-tuple-element.67.d_own, bf16[6,160,128]{2,1,0:T(8,128)(2,1)S(1)} %copy-done.2, ...), custom_call_target="tpu_custom_call" | custom-call | tf_op jit(solution)/shard_map/pallas_call | solution.py:120
  63.5 1.9 %collective-permute-start.12 = (bf16[6,160,256]{2,1,0:T(8,128)(2,1)}, bf16[6,160,256]{2,1,0:T(8,128)(2,1)}, u32[]{:S(2)}, u32[]{:S(2)}) collective-permute-start(bf16[6,160,256]{2,1,0:T(8,128)(2,1)} %get-tuple-element.45), channel_id=1, source_target_pairs={{0,4},{4,0},{8,12},{12,8},{16,20},{20,16},{24,28},{28,24},{1,5},{5... | collective-permute-start | bytes 1474568 | tf_op jit(solution)/shard_map/ppermute | solution.py:221
  65.4 2.7 %shard_map.60 = (bf16[6,160,128]{2,1,0:T(8,128)(2,1)S(1)}, bf16[6,160,128]{2,1,0:T(8,128)(2,1)S(1)}) custom-call(s32[2]{0:T(128)S(1)} %pad_add_fusion.par, bf16[3,3,256,128]{3,2,1,0:T(8,128)(2,1)S(1)} %copy-done, bf16[6,160,256]{2,1,0:T(8,128)(2,1)S(1)} %get-tuple-element.32.f_own, bf16[6,160,256]{2,1,0:T(8,128)(2,1)S(1)} %collective-permute-done.1.f_par, ...), custom_call_target="tpu_custom_call" | custom-call | tf_op jit(solution)/shard_map/pallas_call | solution.py:120
  68.0 0.8 convert_reduce_fusion
  68.8 0.8 multiply_exponential_fusion
  69.6 1.1 %multiply_reduce_fusion = f32[80,128]{1,0:T(8,128)S(1)} fusion(f16[16,80,128]{2,1,0:T(8,128)(2,1)} %all-to-all-done, f32[16,128]{1,0:T(8,128)S(1)} %bitcast.51), kind=kLoop, calls=%fused_computation.2 | loop fusion | flops 481280 | bytes 376832 | tf_op jit(solution)/shard_map/reduce_sum | solution.py:239
  70.7 0.1 fusion
  70.8 6.7 %collective-permute-done.12 = bf16[6,160,256]{2,1,0:T(8,128)(2,1)} collective-permute-done((bf16[6,160,256]{2,1,0:T(8,128)(2,1)}, bf16[6,160,256]{2,1,0:T(8,128)(2,1)}, u32[]{:S(2)}, u32[]{:S(2)}) %collective-permute-start.12) | collective-permute-done | bytes 491552 | tf_op jit(solution)/shard_map/ppermute | solution.py:221
  77.5 0.8 broadcast_in_dim.19
  78.2 6.3 %all-to-all-start.1 = ((f16[16,80,128]{2,1,0:T(8,128)(2,1)}), f16[16,80,128]{2,1,0:T(8,128)(2,1)S(1)}, u32[]{:S(2)}, u32[]{:S(2)}) async-start(f16[16,80,128]{2,1,0:T(8,128)(2,1)} %broadcast_in_dim.19), calls=%async_computation.1 | async-start | bytes 655360 | tf_op jit(solution)/shard_map/all_to_all | solution.py:243
  84.5 1.9 %collective-permute-start.11 = (bf16[6,160,128]{2,1,0:T(8,128)(2,1)S(1)}, bf16[6,160,128]{2,1,0:T(8,128)(2,1)S(1)}, u32[]{:S(2)}, u32[]{:S(2)}) collective-permute-start(bf16[6,160,128]{2,1,0:T(8,128)(2,1)S(1)} %get-tuple-element.41), channel_id=1, source_target_pairs={{0,4},{4,0},{8,12},{12,8},{16,20},{20,16},{24,28},{28,24},{1,5},{5... | collective-permute-start | bytes 737288 | tf_op jit(solution)/shard_map/ppermute | solution.py:234
  86.4 1.1 %broadcast_select_fusion.1 = (bf16[6,160,256]{2,1,0:T(8,128)(2,1)S(1)}, bf16[6,160,256]{2,1,0:T(8,128)(2,1)S(1)}) fusion(bf16[6,160,256]{2,1,0:T(8,128)(2,1)} %collective-permute-done.12, bf16[6,160,256]{2,1,0:T(8,128)(2,1)S(1)} %get-tuple-element.47, pred[]{:T(512)S(6)} %eq.6), kind=kLoop, calls=%fused_computation.7 | loop fusion | flops 491520 | bytes 1966081 | tf_op jit(solution)/shard_map/jit(_where)/select_n | solution.py:145
  87.5 1.0 %pad_maximum_fusion.1 = bf16[12,160,256]{2,1,0:T(8,128)(2,1)} fusion(bf16[6,160,256]{2,1,0:T(8,128)(2,1)S(1)} %get-tuple-element.50, bf16[6,160,256]{2,1,0:T(8,128)(2,1)S(1)} %get-tuple-element.49), kind=kLoop, calls=%fused_computation.1 | loop fusion | flops 491520 | bytes 1966080 | tf_op jit(solution)/shard_map/concatenate | solution.py:147
  88.6 7.5 %all-to-all-done.1 = f16[16,80,128]{2,1,0:T(8,128)(2,1)S(1)} async-done(((f16[16,80,128]{2,1,0:T(8,128)(2,1)}), f16[16,80,128]{2,1,0:T(8,128)(2,1)S(1)}, u32[]{:S(2)}, u32[]{:S(2)}) %all-to-all-start.1) | async-done | bytes 327712 | tf_op jit(solution)/shard_map/all_to_all | solution.py:243
  96.2 0.8 pad_maximum_fusion.2
  97.0 0.8 collective-permute-done.13
  97.7 0.2 broadcast_select_fusion.3
  98.1 1.1 %pad_maximum_fusion = f32[2304,128]{1,0:T(8,128)} fusion(f32[1152,128]{1,0:T(8,128)S(1)} %bitcast.48, f32[1152,128]{1,0:T(8,128)S(1)} %bitcast.47), kind=kLoop, calls=%fused_computation | loop fusion | flops 294912 | bytes 2359296 | tf_op jit(solution)/shard_map/concatenate | solution.py:253
  (39 shorter events, 0.3 us)
Async XLA Ops:
  0.6 7.8 %copy-start.9 = (bf16[12,160,256]{2,1,0:T(8,128)(2,1)S(1)}, bf16[12,160,256]{2,1,0:T(8,128)(2,1)}, u32[]{:S(2)}) copy-start(bf16[12,160,256]{2,1,0:T(8,128)(2,1)} %param.3) | copy-start | bytes 2949124
  1.8 15.7 %collective-permute-start.2 = (bf16[6,160,128]{2,1,0:T(8,128)(2,1)S(1)}, bf16[6,160,128]{2,1,0:T(8,128)(2,1)S(1)}, u32[]{:S(2)}, u32[]{:S(2)}) collective-permute-start(bf16[6,160,128]{2,1,0:T(8,128)(2,1)S(1)} %get-tuple-element.67.d_own), channel_id=1, source_target_pairs={{4,12},{8,0},{12,20},{16,8},{20,28},{24,16},{5,13},{9,1},{13,21},{... | collective-permute-start | bytes 737288 | tf_op jit(solution)/shard_map/ppermute | solution.py:180
  3.1 10.9 %collective-permute-start = (bf16[6,160,128]{2,1,0:T(8,128)(2,1)S(1)}, bf16[6,160,128]{2,1,0:T(8,128)(2,1)S(1)}, u32[]{:S(2)}, u32[]{:S(2)}) collective-permute-start(bf16[6,160,128]{2,1,0:T(8,128)(2,1)S(1)} %get-tuple-element.68), channel_id=1, source_target_pairs={{0,4},{4,0},{8,12},{12,8},{16,20},{20,16},{24,28},{28,24},{1,5},{5... | collective-permute-start | bytes 737288 | tf_op jit(solution)/shard_map/ppermute | solution.py:179
  14.1 23.8 %copy-start.1 = (bf16[6,160,128]{2,1,0:T(8,128)(2,1)}, bf16[6,160,128]{2,1,0:T(8,128)(2,1)S(1)}, u32[]{:S(2)}) copy-start(bf16[6,160,128]{2,1,0:T(8,128)(2,1)S(1)} %collective-permute-done.d_par) | copy-start | bytes 737284
  14.1 7.8 %collective-permute-start.3 = (bf16[6,160,128]{2,1,0:T(8,128)(2,1)S(1)}, bf16[6,160,128]{2,1,0:T(8,128)(2,1)S(1)}, u32[]{:S(2)}, u32[]{:S(2)}) collective-permute-start(bf16[6,160,128]{2,1,0:T(8,128)(2,1)S(1)} %collective-permute-done.d_par), channel_id=1, source_target_pairs={{12,4},{0,8},{20,12},{8,16},{28,20},{16,24},{13,5},{1,9},{21,13},{... | collective-permute-start | bytes 737288 | tf_op jit(solution)/shard_map/ppermute | solution.py:183
  17.6 13.7 %collective-permute-start.7 = (bf16[6,160,256]{2,1,0:T(8,128)(2,1)S(1)}, bf16[6,160,256]{2,1,0:T(8,128)(2,1)S(1)}, u32[]{:S(2)}, u32[]{:S(2)}) collective-permute-start(bf16[6,160,256]{2,1,0:T(8,128)(2,1)S(1)} %get-tuple-element.32.f_own), channel_id=1, source_target_pairs={{4,12},{8,0},{12,20},{16,8},{20,28},{24,16},{5,13},{9,1},{13,21},{... | collective-permute-start | bytes 1474568 | tf_op jit(solution)/shard_map/ppermute | solution.py:185
  18.9 12.4 %collective-permute-start.1 = (bf16[6,160,256]{2,1,0:T(8,128)(2,1)S(1)}, bf16[6,160,256]{2,1,0:T(8,128)(2,1)S(1)}, u32[]{:S(2)}, u32[]{:S(2)}) collective-permute-start(bf16[6,160,256]{2,1,0:T(8,128)(2,1)S(1)} %get-tuple-element.26), channel_id=1, source_target_pairs={{0,4},{4,0},{8,12},{12,8},{16,20},{20,16},{24,28},{28,24},{1,5},{5... | collective-permute-start | bytes 1474568 | tf_op jit(solution)/shard_map/ppermute | solution.py:182
  21.8 16.0 %copy-start.3 = (bf16[6,160,128]{2,1,0:T(8,128)(2,1)}, bf16[6,160,128]{2,1,0:T(8,128)(2,1)S(1)}, u32[]{:S(2)}) copy-start(bf16[6,160,128]{2,1,0:T(8,128)(2,1)S(1)} %collective-permute-done.3.d_far) | copy-start | bytes 737284
  21.9 13.2 %collective-permute-start.5 = (bf16[4,6,16,128]{3,2,1,0:T(8,128)(2,1)S(1)}, bf16[4,6,16,128]{3,2,1,0:T(8,128)(2,1)S(1)}, u32[]{:S(2)}, u32[]{:S(2)}) collective-permute-start(bf16[4,6,16,128]{3,2,1,0:T(8,128)(2,1)S(1)} %pad_maximum_fusion.6), channel_id=1, source_target_pairs={{1,0},{2,1},{3,2},{5,4},{6,5},{7,6},{9,8},{10,9},{11,10},{13,12},{... | collective-permute-start | bytes 294920 | tf_op jit(solution)/shard_map/ppermute | solution.py:140
  23.2 11.9 %collective-permute-start.4 = (bf16[4,6,16,128]{3,2,1,0:T(8,128)(2,1)S(1)}, bf16[4,6,16,128]{3,2,1,0:T(8,128)(2,1)S(1)}, u32[]{:S(2)}, u32[]{:S(2)}) collective-permute-start(bf16[4,6,16,128]{3,2,1,0:T(8,128)(2,1)S(1)} %pad_maximum_fusion.5), channel_id=1, source_target_pairs={{0,1},{1,2},{2,3},{4,5},{5,6},{6,7},{8,9},{9,10},{10,11},{12,13},{... | collective-permute-start | bytes 294920 | tf_op jit(solution)/shard_map/ppermute | solution.py:139
  31.3 11.9 %collective-permute-start.8 = (bf16[6,160,256]{2,1,0:T(8,128)(2,1)S(1)}, bf16[6,160,256]{2,1,0:T(8,128)(2,1)S(1)}, u32[]{:S(2)}, u32[]{:S(2)}) collective-permute-start(bf16[6,160,256]{2,1,0:T(8,128)(2,1)S(1)} %collective-permute-done.1.f_par), channel_id=1, source_target_pairs={{12,4},{0,8},{20,12},{8,16},{28,20},{16,24},{13,5},{1,9},{21,13},{... | collective-permute-start | bytes 1474568 | tf_op jit(solution)/shard_map/ppermute | solution.py:186
  35.0 2.8 %copy-start.5 = (bf16[4,6,16,128]{3,2,1,0:T(8,128)(2,1)}, bf16[4,6,16,128]{3,2,1,0:T(8,128)(2,1)S(1)}, u32[]{:S(2)}) copy-start(bf16[4,6,16,128]{3,2,1,0:T(8,128)(2,1)S(1)} %collective-permute-done.5.right) | copy-start | bytes 294916
  35.1 2.8 %copy-start.7 = (bf16[4,6,16,128]{3,2,1,0:T(8,128)(2,1)}, bf16[4,6,16,128]{3,2,1,0:T(8,128)(2,1)S(1)}, u32[]{:S(2)}) copy-start(bf16[4,6,16,128]{3,2,1,0:T(8,128)(2,1)S(1)} %collective-permute-done.4.left) | copy-start | bytes 294916
  37.9 6.1 %collective-permute-start.6 = (f32[1152,128]{1,0:T(8,128)S(1)}, f32[1152,128]{1,0:T(8,128)S(1)}, u32[]{:S(2)}, u32[]{:S(2)}) collective-permute-start(f32[1152,128]{1,0:T(8,128)S(1)} %get-tuple-element.30), channel_id=1, source_target_pairs={{0,1},{1,0},{2,3},{3,2},{4,5},{5,4},{6,7},{7,6},{8,9},{9,8},{10,11... | collective-permute-start | bytes 1769480 | tf_op jit(solution)/shard_map/ppermute | solution.py:200
  44.7 11.5 %copy-start = (bf16[3,3,256,128]{3,2,1,0:T(8,128)(2,1)S(1)}, bf16[3,3,256,128]{3,2,1,0:T(8,128)(2,1)}, u32[]{:S(2)}) copy-start(bf16[3,3,256,128]{3,2,1,0:T(8,128)(2,1)} %w.3) | copy-start | bytes 1769476
  45.5 22.6 %all-to-all-start = ((f16[16,80,128]{2,1,0:T(8,128)(2,1)}), f16[16,80,128]{2,1,0:T(8,128)(2,1)}, u32[]{:S(2)}, u32[]{:S(2)}) async-start(f16[16,80,128]{2,1,0:T(8,128)(2,1)} %convert_element_type.32), calls=%async_computation | async-start | bytes 655360 | tf_op jit(solution)/shard_map/all_to_all | solution.py:214
  51.9 13.5 %collective-permute-start.10 = (bf16[4,6,16,256]{3,2,1,0:T(8,128)(2,1)}, bf16[4,6,16,256]{3,2,1,0:T(8,128)(2,1)S(1)}, u32[]{:S(2)}, u32[]{:S(2)}) collective-permute-start(bf16[4,6,16,256]{3,2,1,0:T(8,128)(2,1)} %get-tuple-element.39), channel_id=1, source_target_pairs={{1,0},{2,1},{3,2},{5,4},{6,5},{7,6},{9,8},{10,9},{11,10},{13,12},{... | collective-permute-start | bytes 589832 | tf_op jit(solution)/shard_map/ppermute | solution.py:140
  53.2 12.2 %collective-permute-start.9 = (bf16[4,6,16,256]{3,2,1,0:T(8,128)(2,1)}, bf16[4,6,16,256]{3,2,1,0:T(8,128)(2,1)S(1)}, u32[]{:S(2)}, u32[]{:S(2)}) collective-permute-start(bf16[4,6,16,256]{3,2,1,0:T(8,128)(2,1)} %get-tuple-element.38), channel_id=1, source_target_pairs={{0,1},{1,2},{2,3},{4,5},{5,6},{6,7},{8,9},{9,10},{10,11},{12,13},{... | collective-permute-start | bytes 589832 | tf_op jit(solution)/shard_map/ppermute | solution.py:139
  56.2 0.9 copy-start.2
  57.2 0.9 copy-start.4
  58.1 0.9 copy-start.6
  59.0 0.9 copy-start.8
  63.5 14.0 %collective-permute-start.12 = (bf16[6,160,256]{2,1,0:T(8,128)(2,1)}, bf16[6,160,256]{2,1,0:T(8,128)(2,1)}, u32[]{:S(2)}, u32[]{:S(2)}) collective-permute-start(bf16[6,160,256]{2,1,0:T(8,128)(2,1)} %get-tuple-element.45), channel_id=1, source_target_pairs={{0,4},{4,0},{8,12},{12,8},{16,20},{20,16},{24,28},{28,24},{1,5},{5... | collective-permute-start | bytes 1474568 | tf_op jit(solution)/shard_map/ppermute | solution.py:221
  78.2 17.9 %all-to-all-start.1 = ((f16[16,80,128]{2,1,0:T(8,128)(2,1)}), f16[16,80,128]{2,1,0:T(8,128)(2,1)S(1)}, u32[]{:S(2)}, u32[]{:S(2)}) async-start(f16[16,80,128]{2,1,0:T(8,128)(2,1)} %broadcast_in_dim.19), calls=%async_computation.1 | async-start | bytes 655360 | tf_op jit(solution)/shard_map/all_to_all | solution.py:243
  84.5 11.6 %collective-permute-start.11 = (bf16[6,160,128]{2,1,0:T(8,128)(2,1)S(1)}, bf16[6,160,128]{2,1,0:T(8,128)(2,1)S(1)}, u32[]{:S(2)}, u32[]{:S(2)}) collective-permute-start(bf16[6,160,128]{2,1,0:T(8,128)(2,1)S(1)} %get-tuple-element.41), channel_id=1, source_target_pairs={{0,4},{4,0},{8,12},{12,8},{16,20},{20,16},{24,28},{28,24},{1,5},{5... | collective-permute-start | bytes 737288 | tf_op jit(solution)/shard_map/ppermute | solution.py:234
  96.1 1.6 %collective-permute-start.13 = (f16[16,80,128]{2,1,0:T(8,128)(2,1)S(1)}, f16[16,80,128]{2,1,0:T(8,128)(2,1)S(1)}, u32[]{:S(2)}, u32[]{:S(2)}) collective-permute-start(f16[16,80,128]{2,1,0:T(8,128)(2,1)S(1)} %all-to-all-done.1), channel_id=1, source_target_pairs={{0,1},{1,0},{2,3},{3,2},{4,5},{5,4},{6,7},{7,6},{8,9},{9,8},{10,11... | collective-permute-start | bytes 983048 | tf_op jit(solution)/shard_map/ppermute | solution.py:244

commit v6 on v5

--- a/solution.py
+++ b/solution.py
@@ -23,8 +23,10 @@
 
 def gather_map(odd, blocks, left, right, ext):
     width = blocks[0].shape[1]
+    depth = ext.shape[3]
     for place, (block, slot) in enumerate(zip(blocks, slots(odd))):
-        ext[slot, :, pl.ds(STRIP, width), :] = block[...]
+        first = 0 if depth > block.shape[2] // 2 else block.shape[2] - depth
+        ext[slot, :, pl.ds(STRIP, width), :] = block[:, :, first : first + depth]
         ext[slot, :, pl.ds(0, STRIP), :] = left[place]
         ext[slot, :, pl.ds(STRIP + width, STRIP), :] = right[place]
 
@@ -123,15 +125,16 @@
         in_specs=[pl.BlockSpec(memory_space=pltpu.SMEM)] + [whole] * (len(operands) - 1),
         out_specs=[whole] * len(outs),
         scratch_shapes=scratch,
-        compiler_params=pltpu.CompilerParams(vmem_limit_bytes=48 * 1024 * 1024),
+        compiler_params=pltpu.CompilerParams(vmem_limit_bytes=20 * 1024 * 1024),
         cost_estimate=pl.CostEstimate(flops=flops, bytes_accessed=size if flops else 0, transcendentals=0),
     )(*operands)
 
 
-def edges(blocks):
+def edges(blocks, first, depth):
     width = blocks[0].shape[1]
-    tails = jnp.stack([x[:, width - STRIP :] for x in blocks])
-    heads = jnp.stack([x[:, :STRIP] for x in blocks])
+    parts = [x if x.shape[2] == depth else x[:, :, first : first + depth] for x in blocks]
+    tails = jnp.stack([x[:, width - STRIP :] for x in parts])
+    heads = jnp.stack([x[:, :STRIP] for x in parts])
     return tails, heads
 
 
@@ -176,17 +179,15 @@
 
     d_own, d_give = (pick(cotangent, odd), pick(cotangent, 1 - odd))
     f_own, f_give = (pick(features, odd), pick(features, 1 - odd))
+    both = lax.ppermute(jnp.concatenate([f_own, d_own], axis=2), "rows", near)
     d_par = lax.ppermute(d_give, "rows", swap)
-    d_near = lax.ppermute(d_own, "rows", near)
     f_give, d_par = fence((f_give, d_par))
     f_par = lax.ppermute(f_give, "rows", swap)
     d_far = lax.ppermute(d_par, "rows", far)
-    f_first, d_near = fence((f_own, d_near))
-    f_near = lax.ppermute(f_first, "rows", near)
     f_far = lax.ppermute(f_par, "rows", far)
-    d_blocks = (d_own, d_par, d_near, d_far)
-    f_blocks = (f_own, f_par, f_near, f_far)
-    d_left, d_right = exchanged(*edges(d_blocks), cols)
+    d_blocks = (d_own, d_par, both, d_far)
+    f_blocks = (f_own, f_par, both, f_far)
+    d_left, d_right = exchanged(*edges(d_blocks, cin, cout), cols)
 
     part = jax.ShapeDtypeStruct((share, cout), jnp.float32)
     d_maps = [VMEM((4, half, wide, cout), jnp.bfloat16), VMEM((4, half, width, 3 * cout), jnp.bfloat16)]
@@ -198,9 +199,13 @@
         30 * flops,
     )
     given = lax.ppermute(give, "core", other_core)
-    f_first, f_near = fence((f_own, f_near))
-    f_tails, f_heads = edges((f_first, f_par, f_near, f_far))
-    given, f_tails, f_heads = fence((given, f_tails, f_heads))
+    f_tails, f_heads = edges(f_blocks, 0, cin)
+    half_grad = jax.ShapeDtypeStruct((half, width, cin), jnp.bfloat16)
+    g_own, g_par = call(
+        kernel_back, (par, weight) + d_blocks + (d_left, d_right), [half_grad, half_grad], d_maps, 0
+    )
+    g_other = lax.ppermute(g_par, "rows", swap)
+    given, f_tails, f_heads, g_par = fence((given, f_tails, f_heads, g_par))
 
     (scaled,) = call(
         functools.partial(kernel_scale, chunk),
@@ -210,17 +215,10 @@
         0,
     )
     scaled, f_tails, f_heads = fence((scaled.astype(jnp.float16), f_tails, f_heads))
-    f_blocks = (f_own, f_par, f_near, f_far)
     got = lax.all_to_all(scaled, CHIPS, 0, 0)
 
-    d_left, _ = fence((d_left, scaled))
-    half_grad = jax.ShapeDtypeStruct((half, width, cin), jnp.bfloat16)
-    g_own, g_par = call(
-        kernel_back, (par, weight) + d_blocks + (d_left, d_right), [half_grad, half_grad], d_maps, 0
-    )
-    g_other = lax.ppermute(g_par, "rows", swap)
-
     f_left, f_right = exchanged(f_tails, f_heads, cols)
+    f_left, g_other = fence((f_left, g_other))
 
     half_out = jax.ShapeDtypeStruct((half, width, cout), jnp.bfloat16)
     o_own, o_par = call(
@@ -239,7 +237,6 @@
     mine = jnp.sum(shares, axis=0, keepdims=True) * (1.0 / chips)
     place = lax.broadcasted_iota(jnp.int32, mine.shape, 1)
     mine = jnp.where(place < chunk, mine, highest).astype(jnp.float16)
-    mine, g_other = fence((mine, g_other))
     spread = lax.all_to_all(jnp.broadcast_to(mine, (chips, deep, cout)), CHIPS, 0, 0)
     other = lax.ppermute(spread, "core", other_core)
 

time: 100 us -> 95.6 us (0.956)
  starting transfers between devices: 43.1 us -> 37.3 us
  waiting for transfers between devices: 30 us -> 31.2 us
  local copies, waits for them, and re-layouts: 6.53 us -> 7.67 us
    ppermute x1, waiting for transfers between devices: 5.13 us -> 0.01 us  [body(): f_far = lax.ppermute(f_par, 'rows', far)]
    ppermute x2, starting transfers between devices: 6.08 us -> 2.58 us  [exchanged(): left = lax.ppermute(tails, COLS, [(i, i + 1) for i in range(count - 1)])]
    ppermute x1, waiting for transfers between devices: 0.08 us -> 3.53 us  [body(): d_far = lax.ppermute(d_par, 'rows', far)]
    ppermute x1, waiting for transfers between devices: 6.69 us -> 10 us  [body(): g_other = lax.ppermute(g_par, 'rows', swap)]
    ppermute x1, starting transfers between devices: 0.07 us -> 3.17 us  [body(): given = lax.ppermute(give, 'core', other_core)]
    ppermute x1, starting transfers between devices: 2.9 us -> 0.01 us  [body(): f_par = lax.ppermute(f_give, 'rows', swap)]
    ppermute x2 -> x1, waiting for transfers between devices: 4.95 us -> 7.84 us  [body(): both = lax.ppermute(jnp.concatenate([f_own, d_own], axis=2), 'rows', near)]
    ppermute x1, waiting for transfers between devices: 4.83 us -> 2.22 us  [body(): d_par = lax.ppermute(d_give, 'rows', swap)]
  transfers between devices with their start and end apart: 16 -> 15, of which waited for: 7 -> 6; matrix products, arithmetic and copies ran while one was open for 8% -> 6% of each run, Pallas kernels for 9% -> 9%
where the time goes in v6:
time: 95.6 us; the launch traced here: 94.9 us
  starting transfers between devices  37.3 us (39%)
  waiting for transfers between devices  31.2 us (33%)
  Pallas kernels  9.02 us (9%)
  other arithmetic  8.7 us (9%)
  local copies, waits for them, and re-layouts  7.67 us (8%)
  between operations  0.99 us (1%)
    ppermute x1, waiting for transfers between devices, body(): g_other = lax.ppermute(g_par, 'rows', swap)  10 us
    pallas_call x4, Pallas kernels, call(): pl.pallas_call(kernel, out_shape=outs, in_specs=[pl.BlockSpec(memory_spac...  9.02 us
    ppermute x1, waiting for transfers between devices, body(): both = lax.ppermute(jnp.concatenate([f_own, d_own], axis=2), 'rows', near)  7.84 us
    all_to_all x1, starting transfers between devices, body(): got = lax.all_to_all(scaled, CHIPS, 0, 0)  7.36 us
    all_to_all x1, waiting for transfers between devices, body(): lax.all_to_all(jnp.broadcast_to(mine, (chips, deep, cout)), CHIPS, 0, 0)  6.84 us
    all_to_all x1, starting transfers between devices, body(): lax.all_to_all(jnp.broadcast_to(mine, (chips, deep, cout)), CHIPS, 0, 0)  6.07 us
    ppermute x1, starting transfers between devices, body(): d_far = lax.ppermute(d_par, 'rows', far)  3.7 us
    ppermute x1, starting transfers between devices, body(): f_far = lax.ppermute(f_par, 'rows', far)  3.63 us
  transfers between devices with their start and end apart: 15, of which 6 were waited for; matrix products, arithmetic and copies ran while one was open for 6% of the time, Pallas kernels for 9%

profile of v6, /device:TPU:0, one launch (start us, length us, event | category | flops | bytes accessed | tf_op | source)
XLA Modules:
  0.0 94.9 jit_solution(7586479171129599968)
XLA Ops:
  0.7 1.2 %constant_dynamic-slice_fusion = (bf16[6,160,128]{2,1,0:T(8,128)(2,1)S(1)}, bf16[6,160,128]{2,1,0:T(8,128)(2,1)S(1)}) fusion(bf16[12,160,128]{2,1,0:T(8,128)(2,1)} %param.5, s32[]{:T(128)S(6)} %select_n.62, s32[]{:T(128)S(6)} %select_n.63), kind=kLoop, calls=%fused_computation.36 | loop fusion | bytes 983048 | tf_op jit(solution)/shard_map/dynamic_slice | solution.py:172
  1.8 3.0 %collective-permute-start = (bf16[6,160,128]{2,1,0:T(8,128)(2,1)S(1)}, bf16[6,160,128]{2,1,0:T(8,128)(2,1)S(1)}, u32[]{:S(2)}, u32[]{:S(2)}) collective-permute-start(bf16[6,160,128]{2,1,0:T(8,128)(2,1)S(1)} %get-tuple-element.60), channel_id=1, source_target_pairs={{0,4},{4,0},{8,12},{12,8},{16,20},{20,16},{24,28},{28,24},{1,5},{5... | collective-permute-start | bytes 737288 | tf_op jit(solution)/shard_map/ppermute | solution.py:183
  4.9 0.8 constant_dynamic-slice_fusion.2
  5.7 0.9 pad_maximum_fusion.2
  6.7 1.3 %collective-permute-start.2 = (bf16[6,160,384]{2,1,0:T(8,128)(2,1)}, bf16[6,160,384]{2,1,0:T(8,128)(2,1)S(1)}, u32[]{:S(2)}, u32[]{:S(2)}) collective-permute-start(bf16[6,160,384]{2,1,0:T(8,128)(2,1)} %pad_maximum_fusion.2), channel_id=1, source_target_pairs={{4,12},{8,0},{12,20},{16,8},{20,28},{24,16},{5,13},{9,1},{13,21},{... | collective-permute-start | bytes 2211848 | tf_op jit(solution)/shard_map/ppermute | solution.py:182
  8.0 0.7 dynamic-slice_bitcast_fusion
  8.6 2.2 %collective-permute-done.d_par = bf16[6,160,128]{2,1,0:T(8,128)(2,1)S(1)} collective-permute-done((bf16[6,160,128]{2,1,0:T(8,128)(2,1)S(1)}, bf16[6,160,128]{2,1,0:T(8,128)(2,1)S(1)}, u32[]{:S(2)}, u32[]{:S(2)}) %collective-permute-start) | collective-permute-done | bytes 245792 | tf_op jit(solution)/shard_map/ppermute | solution.py:183
  10.8 3.7 %collective-permute-start.3 = (bf16[6,160,128]{2,1,0:T(8,128)(2,1)S(1)}, bf16[6,160,128]{2,1,0:T(8,128)(2,1)S(1)}, u32[]{:S(2)}, u32[]{:S(2)}) collective-permute-start(bf16[6,160,128]{2,1,0:T(8,128)(2,1)S(1)} %collective-permute-done.d_par), channel_id=1, source_target_pairs={{12,4},{0,8},{20,12},{8,16},{28,20},{16,24},{13,5},{1,9},{21,13},{... | collective-permute-start | bytes 737288 | tf_op jit(solution)/shard_map/ppermute | solution.py:186
  14.5 0.8 dynamic-slice_bitcast_fusion.2
  15.3 0.0 collective-permute-start.1
  15.3 3.5 %collective-permute-done.3.d_far = bf16[6,160,128]{2,1,0:T(8,128)(2,1)S(1)} collective-permute-done((bf16[6,160,128]{2,1,0:T(8,128)(2,1)S(1)}, bf16[6,160,128]{2,1,0:T(8,128)(2,1)S(1)}, u32[]{:S(2)}, u32[]{:S(2)}) %collective-permute-start.3) | collective-permute-done | bytes 245792 | tf_op jit(solution)/shard_map/ppermute | solution.py:186
  18.9 7.8 %collective-permute-done.2.d_near.f_near = bf16[6,160,384]{2,1,0:T(8,128)(2,1)S(1)} collective-permute-done((bf16[6,160,384]{2,1,0:T(8,128)(2,1)}, bf16[6,160,384]{2,1,0:T(8,128)(2,1)S(1)}, u32[]{:S(2)}, u32[]{:S(2)}) %collective-permute-start.2) | collective-permute-done | bytes 737312 | tf_op jit(solution)/shard_map/ppermute | solution.py:182
  26.7 1.3 %collective-permute-start.4 = (bf16[4,6,16,128]{3,2,1,0:T(8,128)(2,1)S(1)}, bf16[4,6,16,128]{3,2,1,0:T(8,128)(2,1)S(1)}, u32[]{:S(2)}, u32[]{:S(2)}) collective-permute-start(bf16[4,6,16,128]{3,2,1,0:T(8,128)(2,1)S(1)} %pad_maximum_fusion.6), channel_id=1, source_target_pairs={{0,1},{1,2},{2,3},{4,5},{5,6},{6,7},{8,9},{9,10},{10,11},{12,13},{... | collective-permute-start | bytes 294920 | tf_op jit(solution)/shard_map/ppermute | solution.py:142
  28.1 1.3 %collective-permute-start.5 = (bf16[4,6,16,128]{3,2,1,0:T(8,128)(2,1)S(1)}, bf16[4,6,16,128]{3,2,1,0:T(8,128)(2,1)S(1)}, u32[]{:S(2)}, u32[]{:S(2)}) collective-permute-start(bf16[4,6,16,128]{3,2,1,0:T(8,128)(2,1)S(1)} %pad_maximum_fusion.7), channel_id=1, source_target_pairs={{1,0},{2,1},{3,2},{5,4},{6,5},{7,6},{9,8},{10,9},{11,10},{13,12},{... | collective-permute-start | bytes 294920 | tf_op jit(solution)/shard_map/ppermute | solution.py:143
  29.4 0.1 pad_add_fusion.par
  29.5 3.6 %collective-permute-start.7 = (bf16[6,160,256]{2,1,0:T(8,128)(2,1)S(1)}, bf16[6,160,256]{2,1,0:T(8,128)(2,1)S(1)}, u32[]{:S(2)}, u32[]{:S(2)}) collective-permute-start(bf16[6,160,256]{2,1,0:T(8,128)(2,1)S(1)} %collective-permute-done.1.f_par), channel_id=1, source_target_pairs={{12,4},{0,8},{20,12},{8,16},{28,20},{16,24},{13,5},{1,9},{21,13},{... | collective-permute-start | bytes 1474568 | tf_op jit(solution)/shard_map/ppermute | solution.py:187
  33.1 2.8 %shard_map.58 = (f32[1152,128]{1,0:T(8,128)S(1)}, f32[1152,128]{1,0:T(8,128)S(1)}) custom-call(s32[2]{0:T(128)S(1)} %pad_add_fusion.par, bf16[6,160,256]{2,1,0:T(8,128)(2,1)S(1)} %get-tuple-element.44.f_own, bf16[6,160,256]{2,1,0:T(8,128)(2,1)S(1)} %collective-permute-done.1.f_par, bf16[6,160,128]{2,1,0:T(8,128)(2,1)S(1)} %get-tuple-element.59.d_own, ...), custom_call_target="tpu_custom_call" | custom-call | flops 33973862400 | bytes 3833864 | tf_op jit(solution)/shard_map/pallas_call | solution.py:122
  35.9 3.2 %collective-permute-start.6 = (f32[1152,128]{1,0:T(8,128)S(1)}, f32[1152,128]{1,0:T(8,128)S(1)}, u32[]{:S(2)}, u32[]{:S(2)}) collective-permute-start(f32[1152,128]{1,0:T(8,128)S(1)} %get-tuple-element.24), channel_id=1, source_target_pairs={{0,1},{1,0},{2,3},{3,2},{4,5},{5,4},{6,7},{7,6},{8,9},{9,8},{10,11... | collective-permute-start | bytes 1769480 | tf_op jit(solution)/shard_map/ppermute | solution.py:201
  39.1 0.0 copy-start.2
  39.1 0.9 copy-done.2
  40.1 0.9 copy-done.4
  41.0 2.8 %shard_map.59 = (bf16[6,160,256]{2,1,0:T(8,128)(2,1)S(1)}, bf16[6,160,256]{2,1,0:T(8,128)(2,1)S(1)}) custom-call(s32[2]{0:T(128)S(1)} %pad_add_fusion.par, bf16[3,3,256,128]{3,2,1,0:T(8,128)(2,1)S(1)} %copy-done, bf16[6,160,128]{2,1,0:T(8,128)(2,1)S(1)} %get-tuple-element.59.d_own, bf16[6,160,128]{2,1,0:T(8,128)(2,1)S(1)} %copy-done.2, ...), custom_call_target="tpu_custom_call" | custom-call | tf_op jit(solution)/shard_map/pallas_call | solution.py:122
  43.9 0.0 copy-start.5
  43.9 0.8 pad_maximum_fusion.4
  44.7 0.7 shard_map.60
  45.4 0.8 convert_element_type.29
  46.2 7.4 %all-to-all-start = ((f16[16,80,128]{2,1,0:T(8,128)(2,1)}), f16[16,80,128]{2,1,0:T(8,128)(2,1)}, u32[]{:S(2)}, u32[]{:S(2)}) async-start(f16[16,80,128]{2,1,0:T(8,128)(2,1)} %convert_element_type.29), calls=%async_computation | async-start | bytes 655360 | tf_op jit(solution)/shard_map/all_to_all | solution.py:218
  53.6 1.9 %collective-permute-start.9 = (bf16[6,160,256]{2,1,0:T(8,128)(2,1)}, bf16[6,160,256]{2,1,0:T(8,128)(2,1)S(1)}, u32[]{:S(2)}, u32[]{:S(2)}) collective-permute-start(bf16[6,160,256]{2,1,0:T(8,128)(2,1)} %copy-done.5), channel_id=1, source_target_pairs={{0,4},{4,0},{8,12},{12,8},{16,20},{20,16},{24,28},{28,24},{1,5},{5... | collective-permute-start | bytes 1474568 | tf_op jit(solution)/shard_map/ppermute | solution.py:207
  55.5 1.3 %collective-permute-start.8 = (bf16[4,6,16,256]{3,2,1,0:T(8,128)(2,1)}, bf16[4,6,16,256]{3,2,1,0:T(8,128)(2,1)S(1)}, u32[]{:S(2)}, u32[]{:S(2)}) collective-permute-start(bf16[4,6,16,256]{3,2,1,0:T(8,128)(2,1)} %get-tuple-element.30), channel_id=1, source_target_pairs={{0,1},{1,2},{2,3},{4,5},{5,6},{6,7},{8,9},{9,10},{10,11},{12,13},{... | collective-permute-start | bytes 589832 | tf_op jit(solution)/shard_map/ppermute | solution.py:142
  56.8 1.3 %collective-permute-start.10 = (bf16[4,6,16,256]{3,2,1,0:T(8,128)(2,1)S(1)}, bf16[4,6,16,256]{3,2,1,0:T(8,128)(2,1)S(1)}, u32[]{:S(2)}, u32[]{:S(2)}) collective-permute-start(bf16[4,6,16,256]{3,2,1,0:T(8,128)(2,1)S(1)} %get-tuple-element.32), channel_id=1, source_target_pairs={{1,0},{2,1},{3,2},{5,4},{6,5},{7,6},{9,8},{10,9},{11,10},{13,12},{... | collective-permute-start | bytes 589832 | tf_op jit(solution)/shard_map/ppermute | solution.py:143
  58.1 10.0 %collective-permute-done.9 = bf16[6,160,256]{2,1,0:T(8,128)(2,1)S(1)} collective-permute-done((bf16[6,160,256]{2,1,0:T(8,128)(2,1)}, bf16[6,160,256]{2,1,0:T(8,128)(2,1)S(1)}, u32[]{:S(2)}, u32[]{:S(2)}) %collective-permute-start.9) | collective-permute-done | bytes 491552 | tf_op jit(solution)/shard_map/ppermute | solution.py:207
  68.1 0.8 copy-done.9
  68.9 2.7 %shard_map.61 = (bf16[6,160,128]{2,1,0:T(8,128)(2,1)S(1)}, bf16[6,160,128]{2,1,0:T(8,128)(2,1)S(1)}) custom-call(s32[2]{0:T(128)S(1)} %pad_add_fusion.par, bf16[3,3,256,128]{3,2,1,0:T(8,128)(2,1)S(1)} %copy-done, bf16[6,160,256]{2,1,0:T(8,128)(2,1)S(1)} %get-tuple-element.44.f_own, bf16[6,160,256]{2,1,0:T(8,128)(2,1)S(1)} %collective-permute-done.1.f_par, ...), custom_call_target="tpu_custom_call" | custom-call | tf_op jit(solution)/shard_map/pallas_call | solution.py:122
  71.6 0.7 copy-done.6
  72.3 0.9 convert_reduce_fusion
  73.2 0.8 multiply_exponential_fusion
  73.9 1.1 %multiply_reduce_fusion = f32[80,128]{1,0:T(8,128)S(1)} fusion(f16[16,80,128]{2,1,0:T(8,128)(2,1)} %all-to-all-done, f32[16,128]{1,0:T(8,128)S(1)} %bitcast.45), kind=kLoop, calls=%fused_computation.3 | loop fusion | flops 481280 | bytes 376832 | tf_op jit(solution)/shard_map/reduce_sum | solution.py:237
  75.0 0.1 select_convert_fusion
  75.1 0.8 broadcast_in_dim.16
  75.9 6.1 %all-to-all-start.1 = ((f16[16,80,128]{2,1,0:T(8,128)(2,1)}), f16[16,80,128]{2,1,0:T(8,128)(2,1)S(1)}, u32[]{:S(2)}, u32[]{:S(2)}) async-start(f16[16,80,128]{2,1,0:T(8,128)(2,1)} %broadcast_in_dim.16), calls=%async_computation.1 | async-start | bytes 655360 | tf_op jit(solution)/shard_map/all_to_all | solution.py:240
  82.0 2.0 %collective-permute-start.11 = (bf16[6,160,128]{2,1,0:T(8,128)(2,1)S(1)}, bf16[6,160,128]{2,1,0:T(8,128)(2,1)S(1)}, u32[]{:S(2)}, u32[]{:S(2)}) collective-permute-start(bf16[6,160,128]{2,1,0:T(8,128)(2,1)S(1)} %copy-done.7), channel_id=1, source_target_pairs={{0,4},{4,0},{8,12},{12,8},{16,20},{20,16},{24,28},{28,24},{1,5},{5... | collective-permute-start | bytes 737288 | tf_op jit(solution)/shard_map/ppermute | solution.py:232
  83.9 0.1 broadcast_select_fusion.1
  84.0 1.0 %pad_maximum_fusion.1 = bf16[12,160,256]{2,1,0:T(8,128)(2,1)} fusion(bf16[6,160,256]{2,1,0:T(8,128)(2,1)S(1)} %get-tuple-element.40, bf16[6,160,256]{2,1,0:T(8,128)(2,1)S(1)} %get-tuple-element.39), kind=kLoop, calls=%fused_computation.1 | loop fusion | flops 491520 | bytes 1966080 | tf_op jit(solution)/shard_map/concatenate | solution.py:150
  85.0 6.8 %all-to-all-done.1 = f16[16,80,128]{2,1,0:T(8,128)(2,1)S(1)} async-done(((f16[16,80,128]{2,1,0:T(8,128)(2,1)}), f16[16,80,128]{2,1,0:T(8,128)(2,1)S(1)}, u32[]{:S(2)}, u32[]{:S(2)}) %all-to-all-start.1) | async-done | bytes 327712 | tf_op jit(solution)/shard_map/all_to_all | solution.py:240
  91.9 0.8 pad_maximum_fusion.3
  92.7 0.8 collective-permute-done.12
  93.5 0.2 broadcast_select_fusion.3
  93.8 1.1 %pad_maximum_fusion = f32[2304,128]{1,0:T(8,128)} fusion(f32[1152,128]{1,0:T(8,128)S(1)} %bitcast.42, f32[1152,128]{1,0:T(8,128)S(1)} %bitcast.43), kind=kLoop, calls=%fused_computation | loop fusion | flops 294912 | bytes 2359296 | tf_op jit(solution)/shard_map/concatenate | solution.py:250
  (44 shorter events, 0.3 us)
Async XLA Ops:
  0.6 4.3 %copy-start.8 = (bf16[12,160,256]{2,1,0:T(8,128)(2,1)S(1)}, bf16[12,160,256]{2,1,0:T(8,128)(2,1)}, u32[]{:S(2)}) copy-start(bf16[12,160,256]{2,1,0:T(8,128)(2,1)} %param.3) | copy-start | bytes 2949124
  1.8 9.0 %collective-permute-start = (bf16[6,160,128]{2,1,0:T(8,128)(2,1)S(1)}, bf16[6,160,128]{2,1,0:T(8,128)(2,1)S(1)}, u32[]{:S(2)}, u32[]{:S(2)}) collective-permute-start(bf16[6,160,128]{2,1,0:T(8,128)(2,1)S(1)} %get-tuple-element.60), channel_id=1, source_target_pairs={{0,4},{4,0},{8,12},{12,8},{16,20},{20,16},{24,28},{28,24},{1,5},{5... | collective-permute-start | bytes 737288 | tf_op jit(solution)/shard_map/ppermute | solution.py:183
  6.7 20.0 %collective-permute-start.2 = (bf16[6,160,384]{2,1,0:T(8,128)(2,1)}, bf16[6,160,384]{2,1,0:T(8,128)(2,1)S(1)}, u32[]{:S(2)}, u32[]{:S(2)}) collective-permute-start(bf16[6,160,384]{2,1,0:T(8,128)(2,1)} %pad_maximum_fusion.2), channel_id=1, source_target_pairs={{4,12},{8,0},{12,20},{16,8},{20,28},{24,16},{5,13},{9,1},{13,21},{... | collective-permute-start | bytes 2211848 | tf_op jit(solution)/shard_map/ppermute | solution.py:182
  10.8 25.1 %copy-start.1 = (bf16[6,160,128]{2,1,0:T(8,128)(2,1)}, bf16[6,160,128]{2,1,0:T(8,128)(2,1)S(1)}, u32[]{:S(2)}) copy-start(bf16[6,160,128]{2,1,0:T(8,128)(2,1)S(1)} %collective-permute-done.d_par) | copy-start | bytes 737284
  10.8 8.0 %collective-permute-start.3 = (bf16[6,160,128]{2,1,0:T(8,128)(2,1)S(1)}, bf16[6,160,128]{2,1,0:T(8,128)(2,1)S(1)}, u32[]{:S(2)}, u32[]{:S(2)}) collective-permute-start(bf16[6,160,128]{2,1,0:T(8,128)(2,1)S(1)} %collective-permute-done.d_par), channel_id=1, source_target_pairs={{12,4},{0,8},{20,12},{8,16},{28,20},{16,24},{13,5},{1,9},{21,13},{... | collective-permute-start | bytes 737288 | tf_op jit(solution)/shard_map/ppermute | solution.py:186
  15.3 14.1 %collective-permute-start.1 = (bf16[6,160,256]{2,1,0:T(8,128)(2,1)}, bf16[6,160,256]{2,1,0:T(8,128)(2,1)S(1)}, u32[]{:S(2)}, u32[]{:S(2)}) collective-permute-start(bf16[6,160,256]{2,1,0:T(8,128)(2,1)} %get-tuple-element.21), channel_id=1, source_target_pairs={{0,4},{4,0},{8,12},{12,8},{16,20},{20,16},{24,28},{28,24},{1,5},{5... | collective-permute-start | bytes 1474568 | tf_op jit(solution)/shard_map/ppermute | solution.py:185
  18.9 17.1 %copy-start.3 = (bf16[6,160,128]{2,1,0:T(8,128)(2,1)}, bf16[6,160,128]{2,1,0:T(8,128)(2,1)S(1)}, u32[]{:S(2)}) copy-start(bf16[6,160,128]{2,1,0:T(8,128)(2,1)S(1)} %collective-permute-done.3.d_far) | copy-start | bytes 737284
  26.7 6.4 %collective-permute-start.4 = (bf16[4,6,16,128]{3,2,1,0:T(8,128)(2,1)S(1)}, bf16[4,6,16,128]{3,2,1,0:T(8,128)(2,1)S(1)}, u32[]{:S(2)}, u32[]{:S(2)}) collective-permute-start(bf16[4,6,16,128]{3,2,1,0:T(8,128)(2,1)S(1)} %pad_maximum_fusion.6), channel_id=1, source_target_pairs={{0,1},{1,2},{2,3},{4,5},{5,6},{6,7},{8,9},{9,10},{10,11},{12,13},{... | collective-permute-start | bytes 294920 | tf_op jit(solution)/shard_map/ppermute | solution.py:142
  28.1 5.0 %collective-permute-start.5 = (bf16[4,6,16,128]{3,2,1,0:T(8,128)(2,1)S(1)}, bf16[4,6,16,128]{3,2,1,0:T(8,128)(2,1)S(1)}, u32[]{:S(2)}, u32[]{:S(2)}) collective-permute-start(bf16[4,6,16,128]{3,2,1,0:T(8,128)(2,1)S(1)} %pad_maximum_fusion.7), channel_id=1, source_target_pairs={{1,0},{2,1},{3,2},{5,4},{6,5},{7,6},{9,8},{10,9},{11,10},{13,12},{... | collective-permute-start | bytes 294920 | tf_op jit(solution)/shard_map/ppermute | solution.py:143
  29.4 9.7 %copy-start = (bf16[3,3,256,128]{3,2,1,0:T(8,128)(2,1)S(1)}, bf16[3,3,256,128]{3,2,1,0:T(8,128)(2,1)}, u32[]{:S(2)}) copy-start(bf16[3,3,256,128]{3,2,1,0:T(8,128)(2,1)} %w.3) | copy-start | bytes 1769476
  29.5 14.4 %collective-permute-start.7 = (bf16[6,160,256]{2,1,0:T(8,128)(2,1)S(1)}, bf16[6,160,256]{2,1,0:T(8,128)(2,1)S(1)}, u32[]{:S(2)}, u32[]{:S(2)}) collective-permute-start(bf16[6,160,256]{2,1,0:T(8,128)(2,1)S(1)} %collective-permute-done.1.f_par), channel_id=1, source_target_pairs={{12,4},{0,8},{20,12},{8,16},{28,20},{16,24},{13,5},{1,9},{21,13},{... | collective-permute-start | bytes 1474568 | tf_op jit(solution)/shard_map/ppermute | solution.py:187
  35.9 8.8 %collective-permute-start.6 = (f32[1152,128]{1,0:T(8,128)S(1)}, f32[1152,128]{1,0:T(8,128)S(1)}, u32[]{:S(2)}, u32[]{:S(2)}) collective-permute-start(f32[1152,128]{1,0:T(8,128)S(1)} %get-tuple-element.24), channel_id=1, source_target_pairs={{0,1},{1,0},{2,3},{3,2},{4,5},{5,4},{6,7},{7,6},{8,9},{9,8},{10,11... | collective-permute-start | bytes 1769480 | tf_op jit(solution)/shard_map/ppermute | solution.py:201
  39.1 0.9 copy-start.2
  40.1 0.9 copy-start.4
  41.0 2.9 %copy-start.11 = (bf16[1,6,16,256]{3,2,1,0:T(8,128)(2,1)S(1)}, bf16[1,6,16,256]{3,2,1,0:T(8,128)(2,1)}, u32[]{:S(2)}) copy-start(bf16[1,6,16,256]{3,2,1,0:T(8,128)(2,1)} %get-tuple-element.41) | copy-start | bytes 147460
  41.0 2.9 %copy-start.12 = (bf16[1,6,16,256]{3,2,1,0:T(8,128)(2,1)S(1)}, bf16[1,6,16,256]{3,2,1,0:T(8,128)(2,1)}, u32[]{:S(2)}) copy-start(bf16[1,6,16,256]{3,2,1,0:T(8,128)(2,1)} %get-tuple-element.42) | copy-start | bytes 147460
  43.9 1.6 %copy-start.5 = (bf16[6,160,256]{2,1,0:T(8,128)(2,1)}, bf16[6,160,256]{2,1,0:T(8,128)(2,1)S(1)}, u32[]{:S(2)}) copy-start(bf16[6,160,256]{2,1,0:T(8,128)(2,1)S(1)} %get-tuple-element.25) | copy-start | bytes 1474564
  46.2 26.1 %all-to-all-start = ((f16[16,80,128]{2,1,0:T(8,128)(2,1)}), f16[16,80,128]{2,1,0:T(8,128)(2,1)}, u32[]{:S(2)}, u32[]{:S(2)}) async-start(f16[16,80,128]{2,1,0:T(8,128)(2,1)} %convert_element_type.29), calls=%async_computation | async-start | bytes 655360 | tf_op jit(solution)/shard_map/all_to_all | solution.py:218
  53.6 14.5 %collective-permute-start.9 = (bf16[6,160,256]{2,1,0:T(8,128)(2,1)}, bf16[6,160,256]{2,1,0:T(8,128)(2,1)S(1)}, u32[]{:S(2)}, u32[]{:S(2)}) collective-permute-start(bf16[6,160,256]{2,1,0:T(8,128)(2,1)} %copy-done.5), channel_id=1, source_target_pairs={{0,4},{4,0},{8,12},{12,8},{16,20},{20,16},{24,28},{28,24},{1,5},{5... | collective-permute-start | bytes 1474568 | tf_op jit(solution)/shard_map/ppermute | solution.py:207
  55.5 12.7 %collective-permute-start.8 = (bf16[4,6,16,256]{3,2,1,0:T(8,128)(2,1)}, bf16[4,6,16,256]{3,2,1,0:T(8,128)(2,1)S(1)}, u32[]{:S(2)}, u32[]{:S(2)}) collective-permute-start(bf16[4,6,16,256]{3,2,1,0:T(8,128)(2,1)} %get-tuple-element.30), channel_id=1, source_target_pairs={{0,1},{1,2},{2,3},{4,5},{5,6},{6,7},{8,9},{9,10},{10,11},{12,13},{... | collective-permute-start | bytes 589832 | tf_op jit(solution)/shard_map/ppermute | solution.py:142
  56.8 12.1 %collective-permute-start.10 = (bf16[4,6,16,256]{3,2,1,0:T(8,128)(2,1)S(1)}, bf16[4,6,16,256]{3,2,1,0:T(8,128)(2,1)S(1)}, u32[]{:S(2)}, u32[]{:S(2)}) collective-permute-start(bf16[4,6,16,256]{3,2,1,0:T(8,128)(2,1)S(1)} %get-tuple-element.32), channel_id=1, source_target_pairs={{1,0},{2,1},{3,2},{5,4},{6,5},{7,6},{9,8},{10,9},{11,10},{13,12},{... | collective-permute-start | bytes 589832 | tf_op jit(solution)/shard_map/ppermute | solution.py:143
  68.1 0.8 copy-start.9
  71.6 0.7 copy-start.6
  72.3 11.6 %copy-start.10 = (bf16[6,160,256]{2,1,0:T(8,128)(2,1)S(1)}, bf16[6,160,256]{2,1,0:T(8,128)(2,1)}, u32[]{:S(2)}) copy-start(bf16[6,160,256]{2,1,0:T(8,128)(2,1)} %copy-done.9) | copy-start | bytes 1474564
  72.3 9.6 %copy-start.7 = (bf16[6,160,128]{2,1,0:T(8,128)(2,1)S(1)}, bf16[6,160,128]{2,1,0:T(8,128)(2,1)}, u32[]{:S(2)}) copy-start(bf16[6,160,128]{2,1,0:T(8,128)(2,1)} %copy-done.6) | copy-start | bytes 737284
  75.9 16.0 %all-to-all-start.1 = ((f16[16,80,128]{2,1,0:T(8,128)(2,1)}), f16[16,80,128]{2,1,0:T(8,128)(2,1)S(1)}, u32[]{:S(2)}, u32[]{:S(2)}) async-start(f16[16,80,128]{2,1,0:T(8,128)(2,1)} %broadcast_in_dim.16), calls=%async_computation.1 | async-start | bytes 655360 | tf_op jit(solution)/shard_map/all_to_all | solution.py:240
  82.0 9.9 %collective-permute-start.11 = (bf16[6,160,128]{2,1,0:T(8,128)(2,1)S(1)}, bf16[6,160,128]{2,1,0:T(8,128)(2,1)S(1)}, u32[]{:S(2)}, u32[]{:S(2)}) collective-permute-start(bf16[6,160,128]{2,1,0:T(8,128)(2,1)S(1)} %copy-done.7), channel_id=1, source_target_pairs={{0,4},{4,0},{8,12},{12,8},{16,20},{20,16},{24,28},{28,24},{1,5},{5... | collective-permute-start | bytes 737288 | tf_op jit(solution)/shard_map/ppermute | solution.py:232
  91.9 1.6 %collective-permute-start.12 = (f16[16,80,128]{2,1,0:T(8,128)(2,1)S(1)}, f16[16,80,128]{2,1,0:T(8,128)(2,1)S(1)}, u32[]{:S(2)}, u32[]{:S(2)}) collective-permute-start(f16[16,80,128]{2,1,0:T(8,128)(2,1)S(1)} %all-to-all-done.1), channel_id=1, source_target_pairs={{0,1},{1,0},{2,3},{3,2},{4,5},{5,4},{6,7},{7,6},{8,9},{9,8},{10,11... | collective-permute-start | bytes 983048 | tf_op jit(solution)/shard_map/ppermute | solution.py:241

commit v7 on v5

--- a/solution.py
+++ b/solution.py
@@ -123,7 +123,7 @@
         in_specs=[pl.BlockSpec(memory_space=pltpu.SMEM)] + [whole] * (len(operands) - 1),
         out_specs=[whole] * len(outs),
         scratch_shapes=scratch,
-        compiler_params=pltpu.CompilerParams(vmem_limit_bytes=48 * 1024 * 1024),
+        compiler_params=pltpu.CompilerParams(vmem_limit_bytes=12 * 1024 * 1024),
         cost_estimate=pl.CostEstimate(flops=flops, bytes_accessed=size if flops else 0, transcendentals=0),
     )(*operands)
 
@@ -181,7 +181,7 @@
     f_give, d_par = fence((f_give, d_par))
     f_par = lax.ppermute(f_give, "rows", swap)
     d_far = lax.ppermute(d_par, "rows", far)
-    f_first, d_near = fence((f_own, d_near))
+    f_first, d_far = fence((f_own, d_far))
     f_near = lax.ppermute(f_first, "rows", near)
     f_far = lax.ppermute(f_par, "rows", far)
     d_blocks = (d_own, d_par, d_near, d_far)
@@ -198,9 +198,13 @@
         30 * flops,
     )
     given = lax.ppermute(give, "core", other_core)
-    f_first, f_near = fence((f_own, f_near))
-    f_tails, f_heads = edges((f_first, f_par, f_near, f_far))
-    given, f_tails, f_heads = fence((given, f_tails, f_heads))
+    f_tails, f_heads = edges(f_blocks)
+    half_grad = jax.ShapeDtypeStruct((half, width, cin), jnp.bfloat16)
+    g_own, g_par = call(
+        kernel_back, (par, weight) + d_blocks + (d_left, d_right), [half_grad, half_grad], d_maps, 0
+    )
+    g_other = lax.ppermute(g_par, "rows", swap)
+    given, f_tails, f_heads, g_par = fence((given, f_tails, f_heads, g_par))
 
     (scaled,) = call(
         functools.partial(kernel_scale, chunk),
@@ -210,15 +214,8 @@
         0,
     )
     scaled, f_tails, f_heads = fence((scaled.astype(jnp.float16), f_tails, f_heads))
-    f_blocks = (f_own, f_par, f_near, f_far)
     got = lax.all_to_all(scaled, CHIPS, 0, 0)
-
-    d_left, _ = fence((d_left, scaled))
-    half_grad = jax.ShapeDtypeStruct((half, width, cin), jnp.bfloat16)
-    g_own, g_par = call(
-        kernel_back, (par, weight) + d_blocks + (d_left, d_right), [half_grad, half_grad], d_maps, 0
-    )
-    g_other = lax.ppermute(g_par, "rows", swap)
+    g_own, _ = fence((g_own, scaled))
 
     f_left, f_right = exchanged(f_tails, f_heads, cols)
 
@@ -239,7 +236,6 @@
     mine = jnp.sum(shares, axis=0, keepdims=True) * (1.0 / chips)
     place = lax.broadcasted_iota(jnp.int32, mine.shape, 1)
     mine = jnp.where(place < chunk, mine, highest).astype(jnp.float16)
-    mine, g_other = fence((mine, g_other))
     spread = lax.all_to_all(jnp.broadcast_to(mine, (chips, deep, cout)), CHIPS, 0, 0)
     other = lax.ppermute(spread, "core", other_core)
 

time: 100 us -> 91.8 us (0.918)
  waiting for transfers between devices: 30 us -> 21.7 us
    ppermute x1, waiting for transfers between devices: 6.69 us -> 0.01 us  [body(): g_other = lax.ppermute(g_par, 'rows', swap)]
    ppermute x1, waiting for transfers between devices: 4.95 us -> 0.01 us  [body(): f_near = lax.ppermute(f_first, 'rows', near)]
    ppermute x2, waiting for transfers between devices: 0.01 us -> 4.42 us  [exchanged(): right = lax.ppermute(heads, COLS, [(i + 1, i) for i in range(count - 1)])]
    ppermute x1, waiting for transfers between devices: 0.08 us -> 4.18 us  [body(): d_far = lax.ppermute(d_par, 'rows', far)]
    ppermute x2, starting transfers between devices: 6.08 us -> 2.6 us  [exchanged(): left = lax.ppermute(tails, COLS, [(i, i + 1) for i in range(count - 1)])]
    ppermute x1, starting transfers between devices: 0.07 us -> 3.32 us  [body(): given = lax.ppermute(give, 'core', other_core)]
    ppermute x1, waiting for transfers between devices: 4.83 us -> 1.58 us  [body(): d_par = lax.ppermute(d_give, 'rows', swap)]
    ppermute x1, waiting for transfers between devices: 5.13 us -> 1.88 us  [body(): f_far = lax.ppermute(f_par, 'rows', far)]
  transfers between devices with their start and end apart: 16 -> 16, of which waited for: 7 -> 9; matrix products, arithmetic and copies ran while one was open for 8% -> 12% of each run, Pallas kernels for 9% -> 9%
where the time goes in v7:
time: 91.8 us; the launch traced here: 91 us
  starting transfers between devices  43.1 us (47%)
  waiting for transfers between devices  21.7 us (24%)
  Pallas kernels  8.95 us (10%)
  other arithmetic  8.77 us (10%)
  local copies, waits for them, and re-layouts  7.5 us (8%)
  between operations  1 us (1%)
    pallas_call x4, Pallas kernels, call(): pl.pallas_call(kernel, out_shape=outs, in_specs=[pl.BlockSpec(memory_spac...  8.95 us
    all_to_all x1, starting transfers between devices, body(): got = lax.all_to_all(scaled, CHIPS, 0, 0)  8.92 us
    all_to_all x1, waiting for transfers between devices, body(): lax.all_to_all(jnp.broadcast_to(mine, (chips, deep, cout)), CHIPS, 0, 0)  7.96 us
    all_to_all x1, starting transfers between devices, body(): lax.all_to_all(jnp.broadcast_to(mine, (chips, deep, cout)), CHIPS, 0, 0)  7.95 us
    ppermute x2, waiting for transfers between devices, exchanged(): right = lax.ppermute(heads, COLS, [(i + 1, i) for i in range(count - 1)])  4.42 us
    ppermute x1, starting transfers between devices, body(): f_far = lax.ppermute(f_par, 'rows', far)  4.4 us
    ppermute x1, waiting for transfers between devices, body(): d_far = lax.ppermute(d_par, 'rows', far)  4.18 us
    ppermute x1, starting transfers between devices, body(): d_far = lax.ppermute(d_par, 'rows', far)  3.7 us
  transfers between devices with their start and end apart: 16, of which 9 were waited for; matrix products, arithmetic and copies ran while one was open for 12% of the time, Pallas kernels for 9%

profile of v7, /device:TPU:0, one launch (start us, length us, event | category | flops | bytes accessed | tf_op | source)
XLA Modules:
  0.0 91.0 jit_solution(5328756814006234245)
XLA Ops:
  0.7 1.2 %constant_dynamic-slice_fusion = (bf16[6,160,128]{2,1,0:T(8,128)(2,1)S(1)}, bf16[6,160,128]{2,1,0:T(8,128)(2,1)S(1)}) fusion(bf16[12,160,128]{2,1,0:T(8,128)(2,1)} %param.5, s32[]{:T(128)S(6)} %select_n.62, s32[]{:T(128)S(6)} %select_n.63), kind=kLoop, calls=%fused_computation.35 | loop fusion | bytes 983048 | tf_op jit(solution)/shard_map/dynamic_slice | solution.py:169
  1.8 3.0 %collective-permute-start = (bf16[6,160,128]{2,1,0:T(8,128)(2,1)S(1)}, bf16[6,160,128]{2,1,0:T(8,128)(2,1)S(1)}, u32[]{:S(2)}, u32[]{:S(2)}) collective-permute-start(bf16[6,160,128]{2,1,0:T(8,128)(2,1)S(1)} %get-tuple-element.60), channel_id=1, source_target_pairs={{0,4},{4,0},{8,12},{12,8},{16,20},{20,16},{24,28},{28,24},{1,5},{5... | collective-permute-start | bytes 737288 | tf_op jit(solution)/shard_map/ppermute | solution.py:179
  4.9 1.3 %collective-permute-start.2 = (bf16[6,160,128]{2,1,0:T(8,128)(2,1)S(1)}, bf16[6,160,128]{2,1,0:T(8,128)(2,1)S(1)}, u32[]{:S(2)}, u32[]{:S(2)}) collective-permute-start(bf16[6,160,128]{2,1,0:T(8,128)(2,1)S(1)} %get-tuple-element.59.d_own), channel_id=1, source_target_pairs={{4,12},{8,0},{12,20},{16,8},{20,28},{24,16},{5,13},{9,1},{13,21},{... | collective-permute-start | bytes 737288 | tf_op jit(solution)/shard_map/ppermute | solution.py:180
  6.2 1.5 %dynamic-slice_bitcast_fusion = (bf16[1,6,16,256]{3,2,1,0:T(8,128)(2,1)}, bf16[1,6,16,256]{3,2,1,0:T(8,128)(2,1)}) fusion(bf16[12,160,256]{2,1,0:T(8,128)(2,1)} %param.3, s32[]{:T(128)S(6)} %select_n.62, s32[]{:T(128)S(6)} %add.18), kind=kLoop, calls=%fused_computation.19 | loop fusion | bytes 196616 | tf_op jit(solution)/shard_map/stack | solution.py:134
  7.7 0.8 constant_dynamic-slice_fusion.2
  8.5 0.8 dynamic-slice_bitcast_fusion.2
  9.3 1.6 %collective-permute-done.d_par = bf16[6,160,128]{2,1,0:T(8,128)(2,1)S(1)} collective-permute-done((bf16[6,160,128]{2,1,0:T(8,128)(2,1)S(1)}, bf16[6,160,128]{2,1,0:T(8,128)(2,1)S(1)}, u32[]{:S(2)}, u32[]{:S(2)}) %collective-permute-start) | collective-permute-done | bytes 245792 | tf_op jit(solution)/shard_map/ppermute | solution.py:179
  10.8 3.7 %collective-permute-start.3 = (bf16[6,160,128]{2,1,0:T(8,128)(2,1)S(1)}, bf16[6,160,128]{2,1,0:T(8,128)(2,1)S(1)}, u32[]{:S(2)}, u32[]{:S(2)}) collective-permute-start(bf16[6,160,128]{2,1,0:T(8,128)(2,1)S(1)} %collective-permute-done.d_par), channel_id=1, source_target_pairs={{12,4},{0,8},{20,12},{8,16},{28,20},{16,24},{13,5},{1,9},{21,13},{... | collective-permute-start | bytes 737288 | tf_op jit(solution)/shard_map/ppermute | solution.py:183
  14.6 0.1 collective-permute-start.1
  14.7 4.2 %collective-permute-done.3.d_far = bf16[6,160,128]{2,1,0:T(8,128)(2,1)S(1)} collective-permute-done((bf16[6,160,128]{2,1,0:T(8,128)(2,1)S(1)}, bf16[6,160,128]{2,1,0:T(8,128)(2,1)S(1)}, u32[]{:S(2)}, u32[]{:S(2)}) %collective-permute-start.3) | collective-permute-done | bytes 245792 | tf_op jit(solution)/shard_map/ppermute | solution.py:183
  18.9 1.3 %collective-permute-start.4 = (bf16[4,6,16,128]{3,2,1,0:T(8,128)(2,1)S(1)}, bf16[4,6,16,128]{3,2,1,0:T(8,128)(2,1)S(1)}, u32[]{:S(2)}, u32[]{:S(2)}) collective-permute-start(bf16[4,6,16,128]{3,2,1,0:T(8,128)(2,1)S(1)} %pad_maximum_fusion.5), channel_id=1, source_target_pairs={{0,1},{1,2},{2,3},{4,5},{5,6},{6,7},{8,9},{9,10},{10,11},{12,13},{... | collective-permute-start | bytes 294920 | tf_op jit(solution)/shard_map/ppermute | solution.py:139
  20.2 1.3 %collective-permute-start.5 = (bf16[4,6,16,128]{3,2,1,0:T(8,128)(2,1)S(1)}, bf16[4,6,16,128]{3,2,1,0:T(8,128)(2,1)S(1)}, u32[]{:S(2)}, u32[]{:S(2)}) collective-permute-start(bf16[4,6,16,128]{3,2,1,0:T(8,128)(2,1)S(1)} %pad_maximum_fusion.6), channel_id=1, source_target_pairs={{1,0},{2,1},{3,2},{5,4},{6,5},{7,6},{9,8},{10,9},{11,10},{13,12},{... | collective-permute-start | bytes 294920 | tf_op jit(solution)/shard_map/ppermute | solution.py:140
  21.5 0.1 pad_add_fusion.par
  21.6 1.3 %collective-permute-start.7 = (bf16[6,160,256]{2,1,0:T(8,128)(2,1)S(1)}, bf16[6,160,256]{2,1,0:T(8,128)(2,1)S(1)}, u32[]{:S(2)}, u32[]{:S(2)}) collective-permute-start(bf16[6,160,256]{2,1,0:T(8,128)(2,1)S(1)} %get-tuple-element.27.f_own), channel_id=1, source_target_pairs={{4,12},{8,0},{12,20},{16,8},{20,28},{24,16},{5,13},{9,1},{13,21},{... | collective-permute-start | bytes 1474568 | tf_op jit(solution)/shard_map/ppermute | solution.py:185
  22.9 2.2 %collective-permute-done.5.right = bf16[4,6,16,128]{3,2,1,0:T(8,128)(2,1)S(1)} collective-permute-done((bf16[4,6,16,128]{3,2,1,0:T(8,128)(2,1)S(1)}, bf16[4,6,16,128]{3,2,1,0:T(8,128)(2,1)S(1)}, u32[]{:S(2)}, u32[]{:S(2)}) %collective-permute-start.5) | collective-permute-done | bytes 98336 | tf_op jit(solution)/shard_map/ppermute | solution.py:140
  25.1 2.8 %shard_map.59 = (bf16[6,160,256]{2,1,0:T(8,128)(2,1)S(1)}, bf16[6,160,256]{2,1,0:T(8,128)(2,1)S(1)}) custom-call(s32[2]{0:T(128)S(1)} %pad_add_fusion.par, bf16[3,3,256,128]{3,2,1,0:T(8,128)(2,1)S(1)} %copy-done, bf16[6,160,128]{2,1,0:T(8,128)(2,1)S(1)} %get-tuple-element.59.d_own, bf16[6,160,128]{2,1,0:T(8,128)(2,1)S(1)} %collective-permute-done.d_par, ...), custom_call_target="tpu_custom_call" | custom-call | tf_op jit(solution)/shard_map/pallas_call | solution.py:120
  28.0 0.8 copy-done.3
  28.7 4.4 %collective-permute-start.8 = (bf16[6,160,256]{2,1,0:T(8,128)(2,1)S(1)}, bf16[6,160,256]{2,1,0:T(8,128)(2,1)S(1)}, u32[]{:S(2)}, u32[]{:S(2)}) collective-permute-start(bf16[6,160,256]{2,1,0:T(8,128)(2,1)S(1)} %collective-permute-done.1.f_par), channel_id=1, source_target_pairs={{12,4},{0,8},{20,12},{8,16},{28,20},{16,24},{13,5},{1,9},{21,13},{... | collective-permute-start | bytes 1474568 | tf_op jit(solution)/shard_map/ppermute | solution.py:186
  33.2 0.9 %copy-done.2 = bf16[6,160,128]{2,1,0:T(8,128)(2,1)S(1)} copy-done((bf16[6,160,128]{2,1,0:T(8,128)(2,1)S(1)}, bf16[6,160,128]{2,1,0:T(8,128)(2,1)}, u32[]{:S(2)}) %copy-start.2) | copy-done | bytes 245784
  34.1 2.7 %shard_map.58 = (f32[1152,128]{1,0:T(8,128)S(1)}, f32[1152,128]{1,0:T(8,128)S(1)}) custom-call(s32[2]{0:T(128)S(1)} %pad_add_fusion.par, bf16[6,160,256]{2,1,0:T(8,128)(2,1)S(1)} %get-tuple-element.27.f_own, bf16[6,160,256]{2,1,0:T(8,128)(2,1)S(1)} %collective-permute-done.1.f_par, bf16[6,160,128]{2,1,0:T(8,128)(2,1)S(1)} %get-tuple-element.59.d_own, ...), custom_call_target="tpu_custom_call" | custom-call | flops 33973862400 | bytes 3342344 | tf_op jit(solution)/shard_map/pallas_call | solution.py:120
  36.8 3.3 %collective-permute-start.6 = (f32[1152,128]{1,0:T(8,128)S(1)}, f32[1152,128]{1,0:T(8,128)S(1)}, u32[]{:S(2)}, u32[]{:S(2)}) collective-permute-start(f32[1152,128]{1,0:T(8,128)S(1)} %get-tuple-element.26), channel_id=1, source_target_pairs={{0,1},{1,0},{2,3},{3,2},{4,5},{5,4},{6,7},{7,6},{8,9},{9,8},{10,11... | collective-permute-start | bytes 1769480 | tf_op jit(solution)/shard_map/ppermute | solution.py:200
  40.2 1.9 %collective-permute-done.8.f_far = bf16[6,160,256]{2,1,0:T(8,128)(2,1)S(1)} collective-permute-done((bf16[6,160,256]{2,1,0:T(8,128)(2,1)S(1)}, bf16[6,160,256]{2,1,0:T(8,128)(2,1)S(1)}, u32[]{:S(2)}, u32[]{:S(2)}) %collective-permute-start.8) | collective-permute-done | bytes 491552 | tf_op jit(solution)/shard_map/ppermute | solution.py:186
  42.1 0.8 pad_maximum_fusion.3
  42.9 0.7 shard_map.60
  43.6 0.8 convert_element_type.29
  44.4 8.9 %all-to-all-start = ((f16[16,80,128]{2,1,0:T(8,128)(2,1)}), f16[16,80,128]{2,1,0:T(8,128)(2,1)}, u32[]{:S(2)}, u32[]{:S(2)}) async-start(f16[16,80,128]{2,1,0:T(8,128)(2,1)} %convert_element_type.29), calls=%async_computation | async-start | bytes 655360 | tf_op jit(solution)/shard_map/all_to_all | solution.py:217
  53.3 1.3 %collective-permute-start.9 = (bf16[4,6,16,256]{3,2,1,0:T(8,128)(2,1)}, bf16[4,6,16,256]{3,2,1,0:T(8,128)(2,1)S(1)}, u32[]{:S(2)}, u32[]{:S(2)}) collective-permute-start(bf16[4,6,16,256]{3,2,1,0:T(8,128)(2,1)} %get-tuple-element.33), channel_id=1, source_target_pairs={{0,1},{1,2},{2,3},{4,5},{5,6},{6,7},{8,9},{9,10},{10,11},{12,13},{... | collective-permute-start | bytes 589832 | tf_op jit(solution)/shard_map/ppermute | solution.py:139
  54.7 1.3 %collective-permute-start.10 = (bf16[4,6,16,256]{3,2,1,0:T(8,128)(2,1)S(1)}, bf16[4,6,16,256]{3,2,1,0:T(8,128)(2,1)S(1)}, u32[]{:S(2)}, u32[]{:S(2)}) collective-permute-start(bf16[4,6,16,256]{3,2,1,0:T(8,128)(2,1)S(1)} %copy-done.9), channel_id=1, source_target_pairs={{1,0},{2,1},{3,2},{5,4},{6,5},{7,6},{9,8},{10,9},{11,10},{13,12},{... | collective-permute-start | bytes 589832 | tf_op jit(solution)/shard_map/ppermute | solution.py:140
  56.0 1.9 %collective-permute-start.12 = (bf16[6,160,256]{2,1,0:T(8,128)(2,1)}, bf16[6,160,256]{2,1,0:T(8,128)(2,1)}, u32[]{:S(2)}, u32[]{:S(2)}) collective-permute-start(bf16[6,160,256]{2,1,0:T(8,128)(2,1)} %copy-done.3), channel_id=1, source_target_pairs={{0,4},{4,0},{8,12},{12,8},{16,20},{20,16},{24,28},{28,24},{1,5},{5... | collective-permute-start | bytes 1474568 | tf_op jit(solution)/shard_map/ppermute | solution.py:206
  57.9 2.2 %collective-permute-done.10.right = bf16[4,6,16,256]{3,2,1,0:T(8,128)(2,1)S(1)} collective-permute-done((bf16[4,6,16,256]{3,2,1,0:T(8,128)(2,1)S(1)}, bf16[4,6,16,256]{3,2,1,0:T(8,128)(2,1)S(1)}, u32[]{:S(2)}, u32[]{:S(2)}) %collective-permute-start.10) | collective-permute-done | bytes 196640 | tf_op jit(solution)/shard_map/ppermute | solution.py:140
  60.1 2.7 %shard_map.61 = (bf16[6,160,128]{2,1,0:T(8,128)(2,1)S(1)}, bf16[6,160,128]{2,1,0:T(8,128)(2,1)S(1)}) custom-call(s32[2]{0:T(128)S(1)} %pad_add_fusion.par, bf16[3,3,256,128]{3,2,1,0:T(8,128)(2,1)S(1)} %copy-done, bf16[6,160,256]{2,1,0:T(8,128)(2,1)S(1)} %get-tuple-element.27.f_own, bf16[6,160,256]{2,1,0:T(8,128)(2,1)S(1)} %collective-permute-done.1.f_par, ...), custom_call_target="tpu_custom_call" | custom-call | tf_op jit(solution)/shard_map/pallas_call | solution.py:120
  62.8 0.7 copy-done.4
  63.5 0.9 all-to-all-done
  64.4 0.8 convert_reduce_fusion
  65.2 0.8 multiply_exponential_fusion
  66.0 1.1 %multiply_reduce_fusion = f32[80,128]{1,0:T(8,128)S(1)} fusion(f16[16,80,128]{2,1,0:T(8,128)(2,1)} %all-to-all-done, f32[16,128]{1,0:T(8,128)S(1)} %bitcast.45), kind=kLoop, calls=%fused_computation.2 | loop fusion | flops 481280 | bytes 376832 | tf_op jit(solution)/shard_map/reduce_sum | solution.py:236
  67.0 0.1 select_convert_fusion
  67.1 0.8 broadcast_in_dim.16
  67.9 8.0 %all-to-all-start.1 = ((f16[16,80,128]{2,1,0:T(8,128)(2,1)}), f16[16,80,128]{2,1,0:T(8,128)(2,1)S(1)}, u32[]{:S(2)}, u32[]{:S(2)}) async-start(f16[16,80,128]{2,1,0:T(8,128)(2,1)} %broadcast_in_dim.16), calls=%async_computation.1 | async-start | bytes 655360 | tf_op jit(solution)/shard_map/all_to_all | solution.py:239
  75.9 2.0 %collective-permute-start.11 = (bf16[6,160,128]{2,1,0:T(8,128)(2,1)S(1)}, bf16[6,160,128]{2,1,0:T(8,128)(2,1)S(1)}, u32[]{:S(2)}, u32[]{:S(2)}) collective-permute-start(bf16[6,160,128]{2,1,0:T(8,128)(2,1)S(1)} %copy-done.5), channel_id=1, source_target_pairs={{0,4},{4,0},{8,12},{12,8},{16,20},{20,16},{24,28},{28,24},{1,5},{5... | collective-permute-start | bytes 737288 | tf_op jit(solution)/shard_map/ppermute | solution.py:231
  77.9 1.1 %broadcast_select_fusion.1 = (bf16[6,160,256]{2,1,0:T(8,128)(2,1)S(1)}, bf16[6,160,256]{2,1,0:T(8,128)(2,1)S(1)}) fusion(bf16[6,160,256]{2,1,0:T(8,128)(2,1)} %collective-permute-done.12, bf16[6,160,256]{2,1,0:T(8,128)(2,1)S(1)} %get-tuple-element.39, pred[]{:T(512)S(6)} %eq.6), kind=kLoop, calls=%fused_computation.7 | loop fusion | flops 491520 | bytes 1966081 | tf_op jit(solution)/shard_map/jit(_where)/select_n | solution.py:145
  79.0 1.0 %pad_maximum_fusion.1 = bf16[12,160,256]{2,1,0:T(8,128)(2,1)} fusion(bf16[6,160,256]{2,1,0:T(8,128)(2,1)S(1)} %get-tuple-element.42, bf16[6,160,256]{2,1,0:T(8,128)(2,1)S(1)} %get-tuple-element.41), kind=kLoop, calls=%fused_computation.1 | loop fusion | flops 491520 | bytes 1966080 | tf_op jit(solution)/shard_map/concatenate | solution.py:147
  80.0 8.0 %all-to-all-done.1 = f16[16,80,128]{2,1,0:T(8,128)(2,1)S(1)} async-done(((f16[16,80,128]{2,1,0:T(8,128)(2,1)}), f16[16,80,128]{2,1,0:T(8,128)(2,1)S(1)}, u32[]{:S(2)}, u32[]{:S(2)}) %all-to-all-start.1) | async-done | bytes 327712 | tf_op jit(solution)/shard_map/all_to_all | solution.py:239
  88.0 0.3 collective-permute-done.11
  88.3 0.8 pad_maximum_fusion.2
  89.2 0.4 collective-permute-done.13
  89.6 0.2 broadcast_select_fusion.3
  89.9 1.1 %pad_maximum_fusion = f32[2304,128]{1,0:T(8,128)} fusion(f32[1152,128]{1,0:T(8,128)S(1)} %bitcast.42, f32[1152,128]{1,0:T(8,128)S(1)} %bitcast.43), kind=kLoop, calls=%fused_computation | loop fusion | flops 294912 | bytes 2359296 | tf_op jit(solution)/shard_map/concatenate | solution.py:249
  (39 shorter events, 0.3 us)
Async XLA Ops:
  0.6 7.0 %copy-start.6 = (bf16[12,160,256]{2,1,0:T(8,128)(2,1)S(1)}, bf16[12,160,256]{2,1,0:T(8,128)(2,1)}, u32[]{:S(2)}) copy-start(bf16[12,160,256]{2,1,0:T(8,128)(2,1)} %param.3) | copy-start | bytes 2949124
  1.8 9.0 %collective-permute-start = (bf16[6,160,128]{2,1,0:T(8,128)(2,1)S(1)}, bf16[6,160,128]{2,1,0:T(8,128)(2,1)S(1)}, u32[]{:S(2)}, u32[]{:S(2)}) collective-permute-start(bf16[6,160,128]{2,1,0:T(8,128)(2,1)S(1)} %get-tuple-element.60), channel_id=1, source_target_pairs={{0,4},{4,0},{8,12},{12,8},{16,20},{20,16},{24,28},{28,24},{1,5},{5... | collective-permute-start | bytes 737288 | tf_op jit(solution)/shard_map/ppermute | solution.py:179
  4.9 9.8 %collective-permute-start.2 = (bf16[6,160,128]{2,1,0:T(8,128)(2,1)S(1)}, bf16[6,160,128]{2,1,0:T(8,128)(2,1)S(1)}, u32[]{:S(2)}, u32[]{:S(2)}) collective-permute-start(bf16[6,160,128]{2,1,0:T(8,128)(2,1)S(1)} %get-tuple-element.59.d_own), channel_id=1, source_target_pairs={{4,12},{8,0},{12,20},{16,8},{20,28},{24,16},{5,13},{9,1},{13,21},{... | collective-permute-start | bytes 737288 | tf_op jit(solution)/shard_map/ppermute | solution.py:180
  7.6 17.5 %copy-start = (bf16[3,3,256,128]{3,2,1,0:T(8,128)(2,1)S(1)}, bf16[3,3,256,128]{3,2,1,0:T(8,128)(2,1)}, u32[]{:S(2)}) copy-start(bf16[3,3,256,128]{3,2,1,0:T(8,128)(2,1)} %w.3) | copy-start | bytes 1769476
  10.8 8.0 %collective-permute-start.3 = (bf16[6,160,128]{2,1,0:T(8,128)(2,1)S(1)}, bf16[6,160,128]{2,1,0:T(8,128)(2,1)S(1)}, u32[]{:S(2)}, u32[]{:S(2)}) collective-permute-start(bf16[6,160,128]{2,1,0:T(8,128)(2,1)S(1)} %collective-permute-done.d_par), channel_id=1, source_target_pairs={{12,4},{0,8},{20,12},{8,16},{28,20},{16,24},{13,5},{1,9},{21,13},{... | collective-permute-start | bytes 737288 | tf_op jit(solution)/shard_map/ppermute | solution.py:183
  14.6 14.2 %collective-permute-start.1 = (bf16[6,160,256]{2,1,0:T(8,128)(2,1)}, bf16[6,160,256]{2,1,0:T(8,128)(2,1)S(1)}, u32[]{:S(2)}, u32[]{:S(2)}) collective-permute-start(bf16[6,160,256]{2,1,0:T(8,128)(2,1)} %get-tuple-element.22), channel_id=1, source_target_pairs={{0,4},{4,0},{8,12},{12,8},{16,20},{20,16},{24,28},{28,24},{1,5},{5... | collective-permute-start | bytes 1474568 | tf_op jit(solution)/shard_map/ppermute | solution.py:182
  14.6 13.3 %copy-start.1 = (bf16[6,160,128]{2,1,0:T(8,128)(2,1)}, bf16[6,160,128]{2,1,0:T(8,128)(2,1)S(1)}, u32[]{:S(2)}) copy-start(bf16[6,160,128]{2,1,0:T(8,128)(2,1)S(1)} %collective-permute-done.2.d_near) | copy-start | bytes 737284
  18.9 4.0 %collective-permute-start.4 = (bf16[4,6,16,128]{3,2,1,0:T(8,128)(2,1)S(1)}, bf16[4,6,16,128]{3,2,1,0:T(8,128)(2,1)S(1)}, u32[]{:S(2)}, u32[]{:S(2)}) collective-permute-start(bf16[4,6,16,128]{3,2,1,0:T(8,128)(2,1)S(1)} %pad_maximum_fusion.5), channel_id=1, source_target_pairs={{0,1},{1,2},{2,3},{4,5},{5,6},{6,7},{8,9},{9,10},{10,11},{12,13},{... | collective-permute-start | bytes 294920 | tf_op jit(solution)/shard_map/ppermute | solution.py:139
  20.2 4.9 %collective-permute-start.5 = (bf16[4,6,16,128]{3,2,1,0:T(8,128)(2,1)S(1)}, bf16[4,6,16,128]{3,2,1,0:T(8,128)(2,1)S(1)}, u32[]{:S(2)}, u32[]{:S(2)}) collective-permute-start(bf16[4,6,16,128]{3,2,1,0:T(8,128)(2,1)S(1)} %pad_maximum_fusion.6), channel_id=1, source_target_pairs={{1,0},{2,1},{3,2},{5,4},{6,5},{7,6},{9,8},{10,9},{11,10},{13,12},{... | collective-permute-start | bytes 294920 | tf_op jit(solution)/shard_map/ppermute | solution.py:140
  21.6 18.6 %collective-permute-start.7 = (bf16[6,160,256]{2,1,0:T(8,128)(2,1)S(1)}, bf16[6,160,256]{2,1,0:T(8,128)(2,1)S(1)}, u32[]{:S(2)}, u32[]{:S(2)}) collective-permute-start(bf16[6,160,256]{2,1,0:T(8,128)(2,1)S(1)} %get-tuple-element.27.f_own), channel_id=1, source_target_pairs={{4,12},{8,0},{12,20},{16,8},{20,28},{24,16},{5,13},{9,1},{13,21},{... | collective-permute-start | bytes 1474568 | tf_op jit(solution)/shard_map/ppermute | solution.py:185
  25.1 17.0 %copy-start.7 = (bf16[1,6,16,256]{3,2,1,0:T(8,128)(2,1)S(1)}, bf16[1,6,16,256]{3,2,1,0:T(8,128)(2,1)}, u32[]{:S(2)}) copy-start(bf16[1,6,16,256]{3,2,1,0:T(8,128)(2,1)} %get-tuple-element.43) | copy-start | bytes 147460
  25.1 17.0 %copy-start.8 = (bf16[1,6,16,256]{3,2,1,0:T(8,128)(2,1)S(1)}, bf16[1,6,16,256]{3,2,1,0:T(8,128)(2,1)}, u32[]{:S(2)}) copy-start(bf16[1,6,16,256]{3,2,1,0:T(8,128)(2,1)} %get-tuple-element.44) | copy-start | bytes 147460
  27.9 0.8 copy-start.3
  28.7 13.3 %collective-permute-start.8 = (bf16[6,160,256]{2,1,0:T(8,128)(2,1)S(1)}, bf16[6,160,256]{2,1,0:T(8,128)(2,1)S(1)}, u32[]{:S(2)}, u32[]{:S(2)}) collective-permute-start(bf16[6,160,256]{2,1,0:T(8,128)(2,1)S(1)} %collective-permute-done.1.f_par), channel_id=1, source_target_pairs={{12,4},{0,8},{20,12},{8,16},{28,20},{16,24},{13,5},{1,9},{21,13},{... | collective-permute-start | bytes 1474568 | tf_op jit(solution)/shard_map/ppermute | solution.py:186
  33.1 0.9 %copy-start.2 = (bf16[6,160,128]{2,1,0:T(8,128)(2,1)S(1)}, bf16[6,160,128]{2,1,0:T(8,128)(2,1)}, u32[]{:S(2)}) copy-start(bf16[6,160,128]{2,1,0:T(8,128)(2,1)} %copy-done.1) | copy-start | bytes 737284
  36.8 6.1 %collective-permute-start.6 = (f32[1152,128]{1,0:T(8,128)S(1)}, f32[1152,128]{1,0:T(8,128)S(1)}, u32[]{:S(2)}, u32[]{:S(2)}) collective-permute-start(f32[1152,128]{1,0:T(8,128)S(1)} %get-tuple-element.26), channel_id=1, source_target_pairs={{0,1},{1,0},{2,3},{3,2},{4,5},{5,4},{6,7},{7,6},{8,9},{9,8},{10,11... | collective-permute-start | bytes 1769480 | tf_op jit(solution)/shard_map/ppermute | solution.py:200
  43.6 11.0 %copy-start.9 = (bf16[4,6,16,256]{3,2,1,0:T(8,128)(2,1)S(1)}, bf16[4,6,16,256]{3,2,1,0:T(8,128)(2,1)}, u32[]{:S(2)}) copy-start(bf16[4,6,16,256]{3,2,1,0:T(8,128)(2,1)} %get-tuple-element.34) | copy-start | bytes 589828
  44.4 20.0 %all-to-all-start = ((f16[16,80,128]{2,1,0:T(8,128)(2,1)}), f16[16,80,128]{2,1,0:T(8,128)(2,1)}, u32[]{:S(2)}, u32[]{:S(2)}) async-start(f16[16,80,128]{2,1,0:T(8,128)(2,1)} %convert_element_type.29), calls=%async_computation | async-start | bytes 655360 | tf_op jit(solution)/shard_map/all_to_all | solution.py:217
  53.3 4.6 %collective-permute-start.9 = (bf16[4,6,16,256]{3,2,1,0:T(8,128)(2,1)}, bf16[4,6,16,256]{3,2,1,0:T(8,128)(2,1)S(1)}, u32[]{:S(2)}, u32[]{:S(2)}) collective-permute-start(bf16[4,6,16,256]{3,2,1,0:T(8,128)(2,1)} %get-tuple-element.33), channel_id=1, source_target_pairs={{0,1},{1,2},{2,3},{4,5},{5,6},{6,7},{8,9},{9,10},{10,11},{12,13},{... | collective-permute-start | bytes 589832 | tf_op jit(solution)/shard_map/ppermute | solution.py:139
  54.7 5.4 %collective-permute-start.10 = (bf16[4,6,16,256]{3,2,1,0:T(8,128)(2,1)S(1)}, bf16[4,6,16,256]{3,2,1,0:T(8,128)(2,1)S(1)}, u32[]{:S(2)}, u32[]{:S(2)}) collective-permute-start(bf16[4,6,16,256]{3,2,1,0:T(8,128)(2,1)S(1)} %copy-done.9), channel_id=1, source_target_pairs={{1,0},{2,1},{3,2},{5,4},{6,5},{7,6},{9,8},{10,9},{11,10},{13,12},{... | collective-permute-start | bytes 589832 | tf_op jit(solution)/shard_map/ppermute | solution.py:140
  56.0 21.9 %collective-permute-start.12 = (bf16[6,160,256]{2,1,0:T(8,128)(2,1)}, bf16[6,160,256]{2,1,0:T(8,128)(2,1)}, u32[]{:S(2)}, u32[]{:S(2)}) collective-permute-start(bf16[6,160,256]{2,1,0:T(8,128)(2,1)} %copy-done.3), channel_id=1, source_target_pairs={{0,4},{4,0},{8,12},{12,8},{16,20},{20,16},{24,28},{28,24},{1,5},{5... | collective-permute-start | bytes 1474568 | tf_op jit(solution)/shard_map/ppermute | solution.py:206
  62.8 0.7 copy-start.4
  64.4 11.5 %copy-start.5 = (bf16[6,160,128]{2,1,0:T(8,128)(2,1)S(1)}, bf16[6,160,128]{2,1,0:T(8,128)(2,1)}, u32[]{:S(2)}) copy-start(bf16[6,160,128]{2,1,0:T(8,128)(2,1)} %copy-done.4) | copy-start | bytes 737284
  67.9 20.1 %all-to-all-start.1 = ((f16[16,80,128]{2,1,0:T(8,128)(2,1)}), f16[16,80,128]{2,1,0:T(8,128)(2,1)S(1)}, u32[]{:S(2)}, u32[]{:S(2)}) async-start(f16[16,80,128]{2,1,0:T(8,128)(2,1)} %broadcast_in_dim.16), calls=%async_computation.1 | async-start | bytes 655360 | tf_op jit(solution)/shard_map/all_to_all | solution.py:239
  75.9 12.4 %collective-permute-start.11 = (bf16[6,160,128]{2,1,0:T(8,128)(2,1)S(1)}, bf16[6,160,128]{2,1,0:T(8,128)(2,1)S(1)}, u32[]{:S(2)}, u32[]{:S(2)}) collective-permute-start(bf16[6,160,128]{2,1,0:T(8,128)(2,1)S(1)} %copy-done.5), channel_id=1, source_target_pairs={{0,4},{4,0},{8,12},{12,8},{16,20},{20,16},{24,28},{28,24},{1,5},{5... | collective-permute-start | bytes 737288 | tf_op jit(solution)/shard_map/ppermute | solution.py:231
  88.0 1.6 %collective-permute-start.13 = (f16[16,80,128]{2,1,0:T(8,128)(2,1)S(1)}, f16[16,80,128]{2,1,0:T(8,128)(2,1)S(1)}, u32[]{:S(2)}, u32[]{:S(2)}) collective-permute-start(f16[16,80,128]{2,1,0:T(8,128)(2,1)S(1)} %all-to-all-done.1), channel_id=1, source_target_pairs={{0,1},{1,0},{2,3},{3,2},{4,5},{5,4},{6,7},{7,6},{8,9},{9,8},{10,11... | collective-permute-start | bytes 983048 | tf_op jit(solution)/shard_map/ppermute | solution.py:240

commit v8 on v5

--- a/solution.py
+++ b/solution.py
@@ -73,6 +73,18 @@
         out[c, pl.ds(chunk, out.shape[1] - chunk), :] = jnp.broadcast_to(level[:1], (out.shape[1] - chunk, cout))
 
 
+def kernel_sum(chunk, par, got, out):
+    chips, deep, cout = got.shape
+    levels = [got[i, pl.ds(chunk, 1), :] for i in range(chips)]
+    highest = functools.reduce(jnp.maximum, levels)
+    total = None
+    for i in range(chips):
+        term = got[i, pl.ds(0, chunk), :] * jnp.exp2(levels[i] - highest)
+        total = term if total is None else total + term
+    out[pl.ds(0, chunk), :] = total * (1.0 / chips)
+    out[pl.ds(chunk, deep - chunk), :] = jnp.broadcast_to(highest, (deep - chunk, cout))
+
+
 def kernel_back(par, w, d_own, d_par, d_near, d_far, left, right, out_own, out_par, ext, shifted):
     odd = par[0]
     half, width, cout = d_own.shape
@@ -123,7 +135,7 @@
         in_specs=[pl.BlockSpec(memory_space=pltpu.SMEM)] + [whole] * (len(operands) - 1),
         out_specs=[whole] * len(outs),
         scratch_shapes=scratch,
-        compiler_params=pltpu.CompilerParams(vmem_limit_bytes=48 * 1024 * 1024),
+        compiler_params=pltpu.CompilerParams(vmem_limit_bytes=12 * 1024 * 1024),
         cost_estimate=pl.CostEstimate(flops=flops, bytes_accessed=size if flops else 0, transcendentals=0),
     )(*operands)
 
@@ -181,7 +193,7 @@
     f_give, d_par = fence((f_give, d_par))
     f_par = lax.ppermute(f_give, "rows", swap)
     d_far = lax.ppermute(d_par, "rows", far)
-    f_first, d_near = fence((f_own, d_near))
+    f_first, d_far = fence((f_own, d_far))
     f_near = lax.ppermute(f_first, "rows", near)
     f_far = lax.ppermute(f_par, "rows", far)
     d_blocks = (d_own, d_par, d_near, d_far)
@@ -198,8 +210,7 @@
         30 * flops,
     )
     given = lax.ppermute(give, "core", other_core)
-    f_first, f_near = fence((f_own, f_near))
-    f_tails, f_heads = edges((f_first, f_par, f_near, f_far))
+    f_tails, f_heads = edges(f_blocks)
     given, f_tails, f_heads = fence((given, f_tails, f_heads))
 
     (scaled,) = call(
@@ -210,17 +221,28 @@
         0,
     )
     scaled, f_tails, f_heads = fence((scaled.astype(jnp.float16), f_tails, f_heads))
-    f_blocks = (f_own, f_par, f_near, f_far)
     got = lax.all_to_all(scaled, CHIPS, 0, 0)
-
     d_left, _ = fence((d_left, scaled))
     half_grad = jax.ShapeDtypeStruct((half, width, cin), jnp.bfloat16)
     g_own, g_par = call(
         kernel_back, (par, weight) + d_blocks + (d_left, d_right), [half_grad, half_grad], d_maps, 0
     )
     g_other = lax.ppermute(g_par, "rows", swap)
+    got, g_par = fence((got, g_par))
 
     f_left, f_right = exchanged(f_tails, f_heads, cols)
+
+    (mine,) = call(
+        functools.partial(kernel_sum, chunk),
+        (par, got.astype(jnp.float32)),
+        [jax.ShapeDtypeStruct((deep, cout), jnp.float32)],
+        [],
+        0,
+    )
+    mine = mine.astype(jnp.float16)
+    f_left, copies = fence((f_left, jnp.broadcast_to(mine[None], (chips, deep, cout))))
+    spread = lax.all_to_all(copies, CHIPS, 0, 0)
+    other = lax.ppermute(spread, "core", other_core)
 
     half_out = jax.ShapeDtypeStruct((half, width, cout), jnp.bfloat16)
     o_own, o_par = call(
@@ -230,18 +252,7 @@
         [VMEM((4, half, wide, cin), jnp.bfloat16)],
         0,
     )
-    got, o_par = fence((got, o_par))
     o_other = lax.ppermute(o_par, "rows", swap)
-
-    levels = got[:, chunk : chunk + 1].astype(jnp.float32)
-    highest = jnp.max(levels, axis=0, keepdims=True)
-    shares = got.astype(jnp.float32) * jnp.exp2(levels - highest)
-    mine = jnp.sum(shares, axis=0, keepdims=True) * (1.0 / chips)
-    place = lax.broadcasted_iota(jnp.int32, mine.shape, 1)
-    mine = jnp.where(place < chunk, mine, highest).astype(jnp.float16)
-    mine, g_other = fence((mine, g_other))
-    spread = lax.all_to_all(jnp.broadcast_to(mine, (chips, deep, cout)), CHIPS, 0, 0)
-    other = lax.ppermute(spread, "core", other_core)
 
     norm = chips / jnp.sqrt(jnp.float32(height * width * chips * 2))
 

time: 100 us -> 95.1 us (0.951); the launches traced: 99.1 us -> 93.2 us
  waiting for transfers between devices: 30 us -> 21.7 us
  local copies, waits for them, and re-layouts: 6.53 us -> 8.98 us
  Pallas kernels: 9.74 us -> 11.1 us
    all_to_all x1, waiting for transfers between devices: 7.54 us -> 0.01 us  [body(): spread = lax.all_to_all(copies, CHIPS, 0, 0)]
    ppermute x1, waiting for transfers between devices: 6.69 us -> 0.01 us  [body(): g_other = lax.ppermute(g_par, 'rows', swap)]
    ppermute x1, starting transfers between devices: 0.01 us -> 4.35 us  [body(): other = lax.ppermute(spread, 'core', other_core)]
    ppermute x1, waiting for transfers between devices: 0.08 us -> 4.18 us  [body(): d_far = lax.ppermute(d_par, 'rows', far)]
    ppermute x1, waiting for transfers between devices: 0.01 us -> 3.56 us  [body(): f_par = lax.ppermute(f_give, 'rows', swap)]
    ppermute x2, starting transfers between devices: 6.08 us -> 2.58 us  [exchanged(): left = lax.ppermute(tails, COLS, [(i, i + 1) for i in range(count - 1)])]
    all_to_all x1, starting transfers between devices: 6.29 us -> 9.58 us  [body(): spread = lax.all_to_all(copies, CHIPS, 0, 0)]
    ppermute x1, starting transfers between devices: 2.9 us -> 0.07 us  [body(): f_par = lax.ppermute(f_give, 'rows', swap)]
  transfers between devices with their start and end apart: 16 -> 16, of which waited for: 7 -> 8; matrix products, arithmetic and copies ran while one was open for 8% -> 8% of each run, Pallas kernels for 9% -> 11%
where the time goes in v8:
time: 95.1 us; the launch traced here: 93.2 us
  starting transfers between devices  42.3 us (44%)
  waiting for transfers between devices  21.7 us (23%)
  Pallas kernels  11.1 us (12%)
  local copies, waits for them, and re-layouts  8.98 us (9%)
  other arithmetic  8.1 us (9%)
  between operations  1 us (1%)
    pallas_call x5, Pallas kernels, call(): pl.pallas_call(kernel, out_shape=outs, in_specs=[pl.BlockSpec(memory_spac...  11.1 us
    all_to_all x1, starting transfers between devices, body(): spread = lax.all_to_all(copies, CHIPS, 0, 0)  9.58 us
    all_to_all x1, starting transfers between devices, body(): got = lax.all_to_all(scaled, CHIPS, 0, 0)  5.98 us
    ppermute x1, waiting for transfers between devices, body(): f_far = lax.ppermute(f_par, 'rows', far)  5.57 us
    unnamed x24, local copies, waits for them, and re-layouts  5.3 us
    ppermute x1, starting transfers between devices, body(): other = lax.ppermute(spread, 'core', other_core)  4.35 us
    ppermute x1, waiting for transfers between devices, body(): d_far = lax.ppermute(d_par, 'rows', far)  4.18 us
    ppermute x1, starting transfers between devices, body(): d_far = lax.ppermute(d_par, 'rows', far)  3.7 us
  transfers between devices with their start and end apart: 16, of which 8 were waited for; matrix products, arithmetic and copies ran while one was open for 8% of the time, Pallas kernels for 11%

profile of v8, /device:TPU:0, one launch (start us, length us, event | category | flops | bytes accessed | tf_op | source)
XLA Modules:
  0.0 93.2 jit_solution(12519749292869955641)
XLA Ops:
  0.7 1.2 %constant_dynamic-slice_fusion = (bf16[6,160,128]{2,1,0:T(8,128)(2,1)S(1)}, bf16[6,160,128]{2,1,0:T(8,128)(2,1)S(1)}) fusion(bf16[12,160,128]{2,1,0:T(8,128)(2,1)} %param.5, s32[]{:T(128)S(6)} %select_n.53, s32[]{:T(128)S(6)} %select_n.54), kind=kLoop, calls=%fused_computation.31 | loop fusion | bytes 983048 | tf_op jit(solution)/shard_map/dynamic_slice | solution.py:181
  1.8 3.0 %collective-permute-start = (bf16[6,160,128]{2,1,0:T(8,128)(2,1)S(1)}, bf16[6,160,128]{2,1,0:T(8,128)(2,1)S(1)}, u32[]{:S(2)}, u32[]{:S(2)}) collective-permute-start(bf16[6,160,128]{2,1,0:T(8,128)(2,1)S(1)} %get-tuple-element.62), channel_id=1, source_target_pairs={{0,4},{4,0},{8,12},{12,8},{16,20},{20,16},{24,28},{28,24},{1,5},{5... | collective-permute-start | bytes 737288 | tf_op jit(solution)/shard_map/ppermute | solution.py:191
  4.9 1.3 %collective-permute-start.5 = (bf16[6,160,128]{2,1,0:T(8,128)(2,1)S(1)}, bf16[6,160,128]{2,1,0:T(8,128)(2,1)S(1)}, u32[]{:S(2)}, u32[]{:S(2)}) collective-permute-start(bf16[6,160,128]{2,1,0:T(8,128)(2,1)S(1)} %get-tuple-element.61.d_own), channel_id=1, source_target_pairs={{4,12},{8,0},{12,20},{16,8},{20,28},{24,16},{5,13},{9,1},{13,21},{... | collective-permute-start | bytes 737288 | tf_op jit(solution)/shard_map/ppermute | solution.py:192
  6.2 0.8 dynamic-slice_bitcast_fusion
  7.0 0.1 constant_dynamic-slice_fusion.2
  7.1 0.8 dynamic-slice_bitcast_fusion.2
  7.9 3.0 %collective-permute-done.d_par = bf16[6,160,128]{2,1,0:T(8,128)(2,1)S(1)} collective-permute-done((bf16[6,160,128]{2,1,0:T(8,128)(2,1)S(1)}, bf16[6,160,128]{2,1,0:T(8,128)(2,1)S(1)}, u32[]{:S(2)}, u32[]{:S(2)}) %collective-permute-start) | collective-permute-done | bytes 245792 | tf_op jit(solution)/shard_map/ppermute | solution.py:191
  10.8 3.7 %collective-permute-start.2 = (bf16[6,160,128]{2,1,0:T(8,128)(2,1)S(1)}, bf16[6,160,128]{2,1,0:T(8,128)(2,1)S(1)}, u32[]{:S(2)}, u32[]{:S(2)}) collective-permute-start(bf16[6,160,128]{2,1,0:T(8,128)(2,1)S(1)} %collective-permute-done.d_par), channel_id=1, source_target_pairs={{12,4},{0,8},{20,12},{8,16},{28,20},{16,24},{13,5},{1,9},{21,13},{... | collective-permute-start | bytes 737288 | tf_op jit(solution)/shard_map/ppermute | solution.py:195
  14.7 4.2 %collective-permute-done.2.d_far = bf16[6,160,128]{2,1,0:T(8,128)(2,1)S(1)} collective-permute-done((bf16[6,160,128]{2,1,0:T(8,128)(2,1)S(1)}, bf16[6,160,128]{2,1,0:T(8,128)(2,1)S(1)}, u32[]{:S(2)}, u32[]{:S(2)}) %collective-permute-start.2) | collective-permute-done | bytes 245792 | tf_op jit(solution)/shard_map/ppermute | solution.py:195
  18.9 1.3 %collective-permute-start.6 = (bf16[4,6,16,128]{3,2,1,0:T(8,128)(2,1)S(1)}, bf16[4,6,16,128]{3,2,1,0:T(8,128)(2,1)S(1)}, u32[]{:S(2)}, u32[]{:S(2)}) collective-permute-start(bf16[4,6,16,128]{3,2,1,0:T(8,128)(2,1)S(1)} %pad_maximum_fusion.5), channel_id=1, source_target_pairs={{0,1},{1,2},{2,3},{4,5},{5,6},{6,7},{8,9},{9,10},{10,11},{12,13},{... | collective-permute-start | bytes 294920 | tf_op jit(solution)/shard_map/ppermute | solution.py:151
  20.2 1.3 %collective-permute-start.7 = (bf16[4,6,16,128]{3,2,1,0:T(8,128)(2,1)S(1)}, bf16[4,6,16,128]{3,2,1,0:T(8,128)(2,1)S(1)}, u32[]{:S(2)}, u32[]{:S(2)}) collective-permute-start(bf16[4,6,16,128]{3,2,1,0:T(8,128)(2,1)S(1)} %pad_maximum_fusion.6), channel_id=1, source_target_pairs={{1,0},{2,1},{3,2},{5,4},{6,5},{7,6},{9,8},{10,9},{11,10},{13,12},{... | collective-permute-start | bytes 294920 | tf_op jit(solution)/shard_map/ppermute | solution.py:152
  21.5 0.1 pad_add_fusion.par
  21.6 1.3 %collective-permute-start.3 = (bf16[6,160,256]{2,1,0:T(8,128)(2,1)S(1)}, bf16[6,160,256]{2,1,0:T(8,128)(2,1)S(1)}, u32[]{:S(2)}, u32[]{:S(2)}) collective-permute-start(bf16[6,160,256]{2,1,0:T(8,128)(2,1)S(1)} %get-tuple-element.25.f_own), channel_id=1, source_target_pairs={{4,12},{8,0},{12,20},{16,8},{20,28},{24,16},{5,13},{9,1},{13,21},{... | collective-permute-start | bytes 1474568 | tf_op jit(solution)/shard_map/ppermute | solution.py:197
  22.9 3.6 %collective-permute-done.1.f_par = bf16[6,160,256]{2,1,0:T(8,128)(2,1)S(1)} collective-permute-done((bf16[6,160,256]{2,1,0:T(8,128)(2,1)S(1)}, bf16[6,160,256]{2,1,0:T(8,128)(2,1)S(1)}, u32[]{:S(2)}, u32[]{:S(2)}) %collective-permute-start.1) | collective-permute-done | bytes 491552 | tf_op jit(solution)/shard_map/ppermute | solution.py:194
  26.4 3.5 %collective-permute-start.4 = (bf16[6,160,256]{2,1,0:T(8,128)(2,1)S(1)}, bf16[6,160,256]{2,1,0:T(8,128)(2,1)S(1)}, u32[]{:S(2)}, u32[]{:S(2)}) collective-permute-start(bf16[6,160,256]{2,1,0:T(8,128)(2,1)S(1)} %collective-permute-done.1.f_par), channel_id=1, source_target_pairs={{12,4},{0,8},{20,12},{8,16},{28,20},{16,24},{13,5},{1,9},{21,13},{... | collective-permute-start | bytes 1474568 | tf_op jit(solution)/shard_map/ppermute | solution.py:198
  30.0 2.8 %shard_map.58 = (f32[1152,128]{1,0:T(8,128)S(1)}, f32[1152,128]{1,0:T(8,128)S(1)}) custom-call(s32[2]{0:T(128)S(1)} %pad_add_fusion.par, bf16[6,160,256]{2,1,0:T(8,128)(2,1)S(1)} %get-tuple-element.25.f_own, bf16[6,160,256]{2,1,0:T(8,128)(2,1)S(1)} %collective-permute-done.1.f_par, bf16[6,160,128]{2,1,0:T(8,128)(2,1)S(1)} %get-tuple-element.61.d_own, ...), custom_call_target="tpu_custom_call" | custom-call | flops 33973862400 | bytes 3342344 | tf_op jit(solution)/shard_map/pallas_call | solution.py:132
  32.8 0.6 collective-permute-start.8
  33.4 2.4 %collective-permute-done.3.f_near = bf16[6,160,256]{2,1,0:T(8,128)(2,1)S(1)} collective-permute-done((bf16[6,160,256]{2,1,0:T(8,128)(2,1)S(1)}, bf16[6,160,256]{2,1,0:T(8,128)(2,1)S(1)}, u32[]{:S(2)}, u32[]{:S(2)}) %collective-permute-start.3) | collective-permute-done | bytes 491552 | tf_op jit(solution)/shard_map/ppermute | solution.py:197
  35.8 5.6 %collective-permute-done.4.f_far = bf16[6,160,256]{2,1,0:T(8,128)(2,1)S(1)} collective-permute-done((bf16[6,160,256]{2,1,0:T(8,128)(2,1)S(1)}, bf16[6,160,256]{2,1,0:T(8,128)(2,1)S(1)}, u32[]{:S(2)}, u32[]{:S(2)}) %collective-permute-start.4) | collective-permute-done | bytes 491552 | tf_op jit(solution)/shard_map/ppermute | solution.py:198
  41.4 0.8 pad_maximum_fusion.3
  42.2 0.7 shard_map.59
  43.0 0.8 convert_element_type.21
  43.7 6.0 %all-to-all-start = ((f16[16,80,128]{2,1,0:T(8,128)(2,1)}), f16[16,80,128]{2,1,0:T(8,128)(2,1)}, u32[]{:S(2)}, u32[]{:S(2)}) async-start(f16[16,80,128]{2,1,0:T(8,128)(2,1)} %convert_element_type.21), calls=%async_computation | async-start | bytes 655360 | tf_op jit(solution)/shard_map/all_to_all | solution.py:224
  49.7 0.9 %copy-done.2 = bf16[6,160,128]{2,1,0:T(8,128)(2,1)S(1)} copy-done((bf16[6,160,128]{2,1,0:T(8,128)(2,1)S(1)}, bf16[6,160,128]{2,1,0:T(8,128)(2,1)}, u32[]{:S(2)}) %copy-start.2) | copy-done | bytes 245784
  50.7 0.9 %copy-done.4 = bf16[6,160,128]{2,1,0:T(8,128)(2,1)S(1)} copy-done((bf16[6,160,128]{2,1,0:T(8,128)(2,1)S(1)}, bf16[6,160,128]{2,1,0:T(8,128)(2,1)}, u32[]{:S(2)}) %copy-start.4) | copy-done | bytes 245784
  51.6 0.9 copy-done.8
  52.5 0.9 copy-done.10
  53.4 3.6 %shard_map.60 = (bf16[6,160,256]{2,1,0:T(8,128)(2,1)S(1)}, bf16[6,160,256]{2,1,0:T(8,128)(2,1)}) custom-call(s32[2]{0:T(128)S(1)} %pad_add_fusion.par, bf16[3,3,256,128]{3,2,1,0:T(8,128)(2,1)S(1)} %copy-done, bf16[6,160,128]{2,1,0:T(8,128)(2,1)S(1)} %get-tuple-element.61.d_own, bf16[6,160,128]{2,1,0:T(8,128)(2,1)S(1)} %collective-permute-done.d_par, ...), custom_call_target="tpu_custom_call" | custom-call | tf_op jit(solution)/shard_map/pallas_call | solution.py:132
  57.0 1.9 %collective-permute-start.12 = (bf16[6,160,256]{2,1,0:T(8,128)(2,1)}, bf16[6,160,256]{2,1,0:T(8,128)(2,1)}, u32[]{:S(2)}, u32[]{:S(2)}) collective-permute-start(bf16[6,160,256]{2,1,0:T(8,128)(2,1)} %get-tuple-element.35), channel_id=1, source_target_pairs={{0,4},{4,0},{8,12},{12,8},{16,20},{20,16},{24,28},{28,24},{1,5},{5... | collective-permute-start | bytes 1474568 | tf_op jit(solution)/shard_map/ppermute | solution.py:230
  58.9 1.3 %collective-permute-start.9 = (bf16[4,6,16,256]{3,2,1,0:T(8,128)(2,1)}, bf16[4,6,16,256]{3,2,1,0:T(8,128)(2,1)S(1)}, u32[]{:S(2)}, u32[]{:S(2)}) collective-permute-start(bf16[4,6,16,256]{3,2,1,0:T(8,128)(2,1)} %get-tuple-element.32), channel_id=1, source_target_pairs={{0,1},{1,2},{2,3},{4,5},{5,6},{6,7},{8,9},{9,10},{10,11},{12,13},{... | collective-permute-start | bytes 589832 | tf_op jit(solution)/shard_map/ppermute | solution.py:151
  60.2 0.2 all-to-all-done
  60.4 1.0 %convert_element_type.22.got = f32[16,80,128]{2,1,0:T(8,128)S(1)} convert(f16[16,80,128]{2,1,0:T(8,128)(2,1)} %all-to-all-done) | non-fusion elementwise | flops 163840 | bytes 983040 | tf_op jit(solution)/shard_map/convert_element_type | solution.py:237
  61.4 0.6 shard_map.61
  62.1 0.8 broadcast_in_dim.2
  62.8 9.6 %all-to-all-start.1 = ((f16[16,80,128]{2,1,0:T(8,128)(2,1)}), f16[16,80,128]{2,1,0:T(8,128)(2,1)}, u32[]{:S(2)}, u32[]{:S(2)}) async-start(f16[16,80,128]{2,1,0:T(8,128)(2,1)} %broadcast_in_dim.2), calls=%async_computation.1 | async-start | bytes 655360 | tf_op jit(solution)/shard_map/all_to_all | solution.py:244
  72.4 1.3 %collective-permute-start.10 = (bf16[4,6,16,256]{3,2,1,0:T(8,128)(2,1)}, bf16[4,6,16,256]{3,2,1,0:T(8,128)(2,1)S(1)}, u32[]{:S(2)}, u32[]{:S(2)}) collective-permute-start(bf16[4,6,16,256]{3,2,1,0:T(8,128)(2,1)} %get-tuple-element.38), channel_id=1, source_target_pairs={{1,0},{2,1},{3,2},{5,4},{6,5},{7,6},{9,8},{10,9},{11,10},{13,12},{... | collective-permute-start | bytes 589832 | tf_op jit(solution)/shard_map/ppermute | solution.py:152
  73.7 2.2 %collective-permute-done.10.right = bf16[4,6,16,256]{3,2,1,0:T(8,128)(2,1)S(1)} collective-permute-done((bf16[4,6,16,256]{3,2,1,0:T(8,128)(2,1)}, bf16[4,6,16,256]{3,2,1,0:T(8,128)(2,1)S(1)}, u32[]{:S(2)}, u32[]{:S(2)}) %collective-permute-start.10) | collective-permute-done | bytes 196640 | tf_op jit(solution)/shard_map/ppermute | solution.py:152
  76.0 0.7 copy-done.5
  76.6 0.9 copy-done.6
  77.6 3.4 %shard_map.62 = (bf16[6,160,128]{2,1,0:T(8,128)(2,1)S(1)}, bf16[6,160,128]{2,1,0:T(8,128)(2,1)}) custom-call(s32[2]{0:T(128)S(1)} %pad_add_fusion.par, bf16[3,3,256,128]{3,2,1,0:T(8,128)(2,1)S(1)} %copy-done, bf16[6,160,256]{2,1,0:T(8,128)(2,1)S(1)} %get-tuple-element.25.f_own, bf16[6,160,256]{2,1,0:T(8,128)(2,1)S(1)} %collective-permute-done.1.f_par, ...), custom_call_target="tpu_custom_call" | custom-call | tf_op jit(solution)/shard_map/pallas_call | solution.py:132
  81.0 1.9 %collective-permute-start.11 = (bf16[6,160,128]{2,1,0:T(8,128)(2,1)}, bf16[6,160,128]{2,1,0:T(8,128)(2,1)S(1)}, u32[]{:S(2)}, u32[]{:S(2)}) collective-permute-start(bf16[6,160,128]{2,1,0:T(8,128)(2,1)} %get-tuple-element.39), channel_id=1, source_target_pairs={{0,4},{4,0},{8,12},{12,8},{16,20},{20,16},{24,28},{28,24},{1,5},{5... | collective-permute-start | bytes 737288 | tf_op jit(solution)/shard_map/ppermute | solution.py:255
  82.8 1.2 %broadcast_select_fusion.1 = (bf16[6,160,256]{2,1,0:T(8,128)(2,1)S(1)}, bf16[6,160,256]{2,1,0:T(8,128)(2,1)S(1)}) fusion(bf16[6,160,256]{2,1,0:T(8,128)(2,1)} %collective-permute-done.12, bf16[6,160,256]{2,1,0:T(8,128)(2,1)S(1)} %get-tuple-element.41, pred[]{:T(512)S(6)} %eq.6), kind=kLoop, calls=%fused_computation.6 | loop fusion | flops 491520 | bytes 1966081 | tf_op jit(solution)/shard_map/jit(_where)/select_n | solution.py:157
  84.0 1.0 %pad_maximum_fusion.1 = bf16[12,160,256]{2,1,0:T(8,128)(2,1)} fusion(bf16[6,160,256]{2,1,0:T(8,128)(2,1)S(1)} %get-tuple-element.44, bf16[6,160,256]{2,1,0:T(8,128)(2,1)S(1)} %get-tuple-element.43), kind=kLoop, calls=%fused_computation.1 | loop fusion | flops 491520 | bytes 1966080 | tf_op jit(solution)/shard_map/concatenate | solution.py:159
  85.0 4.3 %collective-permute-start.13 = (f16[16,80,128]{2,1,0:T(8,128)(2,1)}, f16[16,80,128]{2,1,0:T(8,128)(2,1)S(1)}, u32[]{:S(2)}, u32[]{:S(2)}) collective-permute-start(f16[16,80,128]{2,1,0:T(8,128)(2,1)} %all-to-all-done.1), channel_id=1, source_target_pairs={{0,1},{1,0},{2,3},{3,2},{4,5},{5,4},{6,7},{7,6},{8,9},{9,8},{10,11... | collective-permute-start | bytes 983048 | tf_op jit(solution)/shard_map/ppermute | solution.py:245
  89.4 0.8 pad_maximum_fusion.2
  90.2 0.6 collective-permute-done.13
  90.8 1.1 %broadcast_select_fusion.3 = (f16[16,80,128]{2,1,0:T(8,128)(2,1)S(1)}, f16[16,80,128]{2,1,0:T(8,128)(2,1)S(1)}) fusion(f16[16,80,128]{2,1,0:T(8,128)(2,1)} %all-to-all-done.1, f16[16,80,128]{2,1,0:T(8,128)(2,1)S(1)} %collective-permute-done.13, pred[]{:T(512)S(6)} %eq.7), kind=kLoop, calls=%fused_computation.8 | loop fusion | flops 327680 | bytes 1310721 | tf_op jit(solution)/shard_map/jit(_where)/select_n | solution.py:260
  92.1 1.1 %pad_maximum_fusion = f32[2304,128]{1,0:T(8,128)} fusion(f32[1152,128]{1,0:T(8,128)S(1)} %bitcast.41, f32[1152,128]{1,0:T(8,128)S(1)} %bitcast.42), kind=kLoop, calls=%fused_computation | loop fusion | flops 294912 | bytes 2359296 | tf_op jit(solution)/shard_map/concatenate | solution.py:264
  (41 shorter events, 0.4 us)
Async XLA Ops:
  0.6 6.4 %copy-start.11 = (bf16[12,160,256]{2,1,0:T(8,128)(2,1)S(1)}, bf16[12,160,256]{2,1,0:T(8,128)(2,1)}, u32[]{:S(2)}) copy-start(bf16[12,160,256]{2,1,0:T(8,128)(2,1)} %param.3) | copy-start | bytes 2949124
  1.8 9.0 %collective-permute-start = (bf16[6,160,128]{2,1,0:T(8,128)(2,1)S(1)}, bf16[6,160,128]{2,1,0:T(8,128)(2,1)S(1)}, u32[]{:S(2)}, u32[]{:S(2)}) collective-permute-start(bf16[6,160,128]{2,1,0:T(8,128)(2,1)S(1)} %get-tuple-element.62), channel_id=1, source_target_pairs={{0,4},{4,0},{8,12},{12,8},{16,20},{20,16},{24,28},{28,24},{1,5},{5... | collective-permute-start | bytes 737288 | tf_op jit(solution)/shard_map/ppermute | solution.py:191
  4.9 9.8 %collective-permute-start.5 = (bf16[6,160,128]{2,1,0:T(8,128)(2,1)S(1)}, bf16[6,160,128]{2,1,0:T(8,128)(2,1)S(1)}, u32[]{:S(2)}, u32[]{:S(2)}) collective-permute-start(bf16[6,160,128]{2,1,0:T(8,128)(2,1)S(1)} %get-tuple-element.61.d_own), channel_id=1, source_target_pairs={{4,12},{8,0},{12,20},{16,8},{20,28},{24,16},{5,13},{9,1},{13,21},{... | collective-permute-start | bytes 737288 | tf_op jit(solution)/shard_map/ppermute | solution.py:192
  10.8 8.0 %collective-permute-start.2 = (bf16[6,160,128]{2,1,0:T(8,128)(2,1)S(1)}, bf16[6,160,128]{2,1,0:T(8,128)(2,1)S(1)}, u32[]{:S(2)}, u32[]{:S(2)}) collective-permute-start(bf16[6,160,128]{2,1,0:T(8,128)(2,1)S(1)} %collective-permute-done.d_par), channel_id=1, source_target_pairs={{12,4},{0,8},{20,12},{8,16},{28,20},{16,24},{13,5},{1,9},{21,13},{... | collective-permute-start | bytes 737288 | tf_op jit(solution)/shard_map/ppermute | solution.py:195
  14.6 11.9 %collective-permute-start.1 = (bf16[6,160,256]{2,1,0:T(8,128)(2,1)S(1)}, bf16[6,160,256]{2,1,0:T(8,128)(2,1)S(1)}, u32[]{:S(2)}, u32[]{:S(2)}) collective-permute-start(bf16[6,160,256]{2,1,0:T(8,128)(2,1)S(1)} %get-tuple-element.23), channel_id=1, source_target_pairs={{0,4},{4,0},{8,12},{12,8},{16,20},{20,16},{24,28},{28,24},{1,5},{5... | collective-permute-start | bytes 1474568 | tf_op jit(solution)/shard_map/ppermute | solution.py:194
  14.6 18.1 %copy-start.1 = (bf16[6,160,128]{2,1,0:T(8,128)(2,1)}, bf16[6,160,128]{2,1,0:T(8,128)(2,1)S(1)}, u32[]{:S(2)}) copy-start(bf16[6,160,128]{2,1,0:T(8,128)(2,1)S(1)} %collective-permute-done.5.d_near) | copy-start | bytes 737284
  18.9 13.9 %copy-start.3 = (bf16[6,160,128]{2,1,0:T(8,128)(2,1)}, bf16[6,160,128]{2,1,0:T(8,128)(2,1)S(1)}, u32[]{:S(2)}) copy-start(bf16[6,160,128]{2,1,0:T(8,128)(2,1)S(1)} %collective-permute-done.2.d_far) | copy-start | bytes 737284
  18.9 11.1 %collective-permute-start.6 = (bf16[4,6,16,128]{3,2,1,0:T(8,128)(2,1)S(1)}, bf16[4,6,16,128]{3,2,1,0:T(8,128)(2,1)S(1)}, u32[]{:S(2)}, u32[]{:S(2)}) collective-permute-start(bf16[4,6,16,128]{3,2,1,0:T(8,128)(2,1)S(1)} %pad_maximum_fusion.5), channel_id=1, source_target_pairs={{0,1},{1,2},{2,3},{4,5},{5,6},{6,7},{8,9},{9,10},{10,11},{12,13},{... | collective-permute-start | bytes 294920 | tf_op jit(solution)/shard_map/ppermute | solution.py:151
  20.2 9.7 %collective-permute-start.7 = (bf16[4,6,16,128]{3,2,1,0:T(8,128)(2,1)S(1)}, bf16[4,6,16,128]{3,2,1,0:T(8,128)(2,1)S(1)}, u32[]{:S(2)}, u32[]{:S(2)}) collective-permute-start(bf16[4,6,16,128]{3,2,1,0:T(8,128)(2,1)S(1)} %pad_maximum_fusion.6), channel_id=1, source_target_pairs={{1,0},{2,1},{3,2},{5,4},{6,5},{7,6},{9,8},{10,9},{11,10},{13,12},{... | collective-permute-start | bytes 294920 | tf_op jit(solution)/shard_map/ppermute | solution.py:152
  21.6 14.2 %collective-permute-start.3 = (bf16[6,160,256]{2,1,0:T(8,128)(2,1)S(1)}, bf16[6,160,256]{2,1,0:T(8,128)(2,1)S(1)}, u32[]{:S(2)}, u32[]{:S(2)}) collective-permute-start(bf16[6,160,256]{2,1,0:T(8,128)(2,1)S(1)} %get-tuple-element.25.f_own), channel_id=1, source_target_pairs={{4,12},{8,0},{12,20},{16,8},{20,28},{24,16},{5,13},{9,1},{13,21},{... | collective-permute-start | bytes 1474568 | tf_op jit(solution)/shard_map/ppermute | solution.py:197
  26.4 14.9 %collective-permute-start.4 = (bf16[6,160,256]{2,1,0:T(8,128)(2,1)S(1)}, bf16[6,160,256]{2,1,0:T(8,128)(2,1)S(1)}, u32[]{:S(2)}, u32[]{:S(2)}) collective-permute-start(bf16[6,160,256]{2,1,0:T(8,128)(2,1)S(1)} %collective-permute-done.1.f_par), channel_id=1, source_target_pairs={{12,4},{0,8},{20,12},{8,16},{28,20},{16,24},{13,5},{1,9},{21,13},{... | collective-permute-start | bytes 1474568 | tf_op jit(solution)/shard_map/ppermute | solution.py:198
  29.9 2.8 %copy-start.7 = (bf16[4,6,16,128]{3,2,1,0:T(8,128)(2,1)}, bf16[4,6,16,128]{3,2,1,0:T(8,128)(2,1)S(1)}, u32[]{:S(2)}) copy-start(bf16[4,6,16,128]{3,2,1,0:T(8,128)(2,1)S(1)} %collective-permute-done.6.left) | copy-start | bytes 294916
  30.0 2.8 %copy-start.9 = (bf16[4,6,16,128]{3,2,1,0:T(8,128)(2,1)}, bf16[4,6,16,128]{3,2,1,0:T(8,128)(2,1)S(1)}, u32[]{:S(2)}) copy-start(bf16[4,6,16,128]{3,2,1,0:T(8,128)(2,1)S(1)} %collective-permute-done.7.right) | copy-start | bytes 294916
  32.8 9.4 %collective-permute-start.8 = (f32[1152,128]{1,0:T(8,128)S(1)}, f32[1152,128]{1,0:T(8,128)S(1)}, u32[]{:S(2)}, u32[]{:S(2)}) collective-permute-start(f32[1152,128]{1,0:T(8,128)S(1)} %get-tuple-element.28), channel_id=1, source_target_pairs={{0,1},{1,0},{2,3},{3,2},{4,5},{5,4},{6,7},{7,6},{8,9},{9,8},{10,11... | collective-permute-start | bytes 1769480 | tf_op jit(solution)/shard_map/ppermute | solution.py:212
  42.9 6.8 %copy-start = (bf16[3,3,256,128]{3,2,1,0:T(8,128)(2,1)S(1)}, bf16[3,3,256,128]{3,2,1,0:T(8,128)(2,1)}, u32[]{:S(2)}) copy-start(bf16[3,3,256,128]{3,2,1,0:T(8,128)(2,1)} %w.3) | copy-start | bytes 1769476
  43.7 16.7 %all-to-all-start = ((f16[16,80,128]{2,1,0:T(8,128)(2,1)}), f16[16,80,128]{2,1,0:T(8,128)(2,1)}, u32[]{:S(2)}, u32[]{:S(2)}) async-start(f16[16,80,128]{2,1,0:T(8,128)(2,1)} %convert_element_type.21), calls=%async_computation | async-start | bytes 655360 | tf_op jit(solution)/shard_map/all_to_all | solution.py:224
  49.7 0.9 %copy-start.2 = (bf16[6,160,128]{2,1,0:T(8,128)(2,1)S(1)}, bf16[6,160,128]{2,1,0:T(8,128)(2,1)}, u32[]{:S(2)}) copy-start(bf16[6,160,128]{2,1,0:T(8,128)(2,1)} %copy-done.1) | copy-start | bytes 737284
  50.7 0.9 %copy-start.4 = (bf16[6,160,128]{2,1,0:T(8,128)(2,1)S(1)}, bf16[6,160,128]{2,1,0:T(8,128)(2,1)}, u32[]{:S(2)}) copy-start(bf16[6,160,128]{2,1,0:T(8,128)(2,1)} %copy-done.3) | copy-start | bytes 737284
  51.6 0.9 copy-start.8
  52.5 0.9 copy-start.10
  57.0 25.8 %collective-permute-start.12 = (bf16[6,160,256]{2,1,0:T(8,128)(2,1)}, bf16[6,160,256]{2,1,0:T(8,128)(2,1)}, u32[]{:S(2)}, u32[]{:S(2)}) collective-permute-start(bf16[6,160,256]{2,1,0:T(8,128)(2,1)} %get-tuple-element.35), channel_id=1, source_target_pairs={{0,4},{4,0},{8,12},{12,8},{16,20},{20,16},{24,28},{28,24},{1,5},{5... | collective-permute-start | bytes 1474568 | tf_op jit(solution)/shard_map/ppermute | solution.py:230
  58.9 3.2 %collective-permute-start.9 = (bf16[4,6,16,256]{3,2,1,0:T(8,128)(2,1)}, bf16[4,6,16,256]{3,2,1,0:T(8,128)(2,1)S(1)}, u32[]{:S(2)}, u32[]{:S(2)}) collective-permute-start(bf16[4,6,16,256]{3,2,1,0:T(8,128)(2,1)} %get-tuple-element.32), channel_id=1, source_target_pairs={{0,1},{1,2},{2,3},{4,5},{5,6},{6,7},{8,9},{9,10},{10,11},{12,13},{... | collective-permute-start | bytes 589832 | tf_op jit(solution)/shard_map/ppermute | solution.py:151
  62.8 22.2 %all-to-all-start.1 = ((f16[16,80,128]{2,1,0:T(8,128)(2,1)}), f16[16,80,128]{2,1,0:T(8,128)(2,1)}, u32[]{:S(2)}, u32[]{:S(2)}) async-start(f16[16,80,128]{2,1,0:T(8,128)(2,1)} %broadcast_in_dim.2), calls=%async_computation.1 | async-start | bytes 655360 | tf_op jit(solution)/shard_map/all_to_all | solution.py:244
  72.4 3.5 %collective-permute-start.10 = (bf16[4,6,16,256]{3,2,1,0:T(8,128)(2,1)}, bf16[4,6,16,256]{3,2,1,0:T(8,128)(2,1)S(1)}, u32[]{:S(2)}, u32[]{:S(2)}) collective-permute-start(bf16[4,6,16,256]{3,2,1,0:T(8,128)(2,1)} %get-tuple-element.38), channel_id=1, source_target_pairs={{1,0},{2,1},{3,2},{5,4},{6,5},{7,6},{9,8},{10,9},{11,10},{13,12},{... | collective-permute-start | bytes 589832 | tf_op jit(solution)/shard_map/ppermute | solution.py:152
  76.0 0.7 copy-start.5
  76.6 0.9 copy-start.6
  81.0 8.4 %collective-permute-start.11 = (bf16[6,160,128]{2,1,0:T(8,128)(2,1)}, bf16[6,160,128]{2,1,0:T(8,128)(2,1)S(1)}, u32[]{:S(2)}, u32[]{:S(2)}) collective-permute-start(bf16[6,160,128]{2,1,0:T(8,128)(2,1)} %get-tuple-element.39), channel_id=1, source_target_pairs={{0,4},{4,0},{8,12},{12,8},{16,20},{20,16},{24,28},{28,24},{1,5},{5... | collective-permute-start | bytes 737288 | tf_op jit(solution)/shard_map/ppermute | solution.py:255
  85.0 5.8 %collective-permute-start.13 = (f16[16,80,128]{2,1,0:T(8,128)(2,1)}, f16[16,80,128]{2,1,0:T(8,128)(2,1)S(1)}, u32[]{:S(2)}, u32[]{:S(2)}) collective-permute-start(f16[16,80,128]{2,1,0:T(8,128)(2,1)} %all-to-all-done.1), channel_id=1, source_target_pairs={{0,1},{1,0},{2,3},{3,2},{4,5},{5,4},{6,7},{7,6},{8,9},{9,8},{10,11... | collective-permute-start | bytes 983048 | tf_op jit(solution)/shard_map/ppermute | solution.py:245

commit v9 on v8

--- a/solution.py
+++ b/solution.py
@@ -38,7 +38,7 @@
             shifted[slot, :, :, pl.ds(q * cout, cout)] = whole[:, start : start + width].astype(jnp.bfloat16)
 
 
-def kernel_grad(par, f_own, f_par, d_own, d_par, d_near, d_far, left, right, keep, give, ext, shifted, acc):
+def kernel_grad(par, f_own, f_par, d_own, d_par, d_near, d_far, left, right, keep, give, shifted, ext, acc):
     odd, core = (par[0], par[1])
     half, width, cout = d_own.shape
     cin = f_own.shape[2]
@@ -85,18 +85,15 @@
     out[pl.ds(chunk, deep - chunk), :] = jnp.broadcast_to(highest, (deep - chunk, cout))
 
 
-def kernel_back(par, w, d_own, d_par, d_near, d_far, left, right, out_own, out_par, ext, shifted):
+def kernel_back(par, w, shifted, out_own, out_par):
     odd = par[0]
-    half, width, cout = d_own.shape
-    cin = w.shape[2]
-    pixels = half * width
-    gather_map(odd, (d_own, d_par, d_near, d_far), left, right, ext)
-    shift_columns(ext, shifted, width)
+    half, width, cin = out_own.shape
+    pixels, depth = (half * width, shifted.shape[3])
     own, partner = slots(odd)[:2]
     for out, slot in ((out_own, own), (out_par, partner)):
         total = None
         for a in range(3):
-            lhs = shifted[slot + 1 - a].reshape(pixels, 3 * cout)
+            lhs = shifted[slot + 1 - a].reshape(pixels, depth)
             rhs = jnp.concatenate([w[a, 2 - q] for q in range(3)], axis=1)
             term = lax.dot_general(lhs, rhs, (((1,), (1,)), ((), ())), preferred_element_type=jnp.float32)
             total = term if total is None else total + term
@@ -140,11 +137,17 @@
     )(*operands)
 
 
-def edges(blocks):
-    width = blocks[0].shape[1]
-    tails = jnp.stack([x[:, width - STRIP :] for x in blocks])
-    heads = jnp.stack([x[:, :STRIP] for x in blocks])
-    return tails, heads
+def kernel_edges(par, *refs):
+    blocks, (tails, heads) = (refs[:-2], refs[-2:])
+    for place, block in enumerate(blocks):
+        tails[place] = block[:, pl.ds(block.shape[1] - STRIP, STRIP), :]
+        heads[place] = block[:, pl.ds(0, STRIP), :]
+
+
+def edges(par, blocks, flops):
+    half, _, depth = blocks[0].shape
+    strip = jax.ShapeDtypeStruct((len(blocks), half, STRIP, depth), jnp.bfloat16)
+    return call(kernel_edges, (par,) + blocks, [strip, strip], [], flops)
 
 
 def exchanged(tails, heads, count):
@@ -190,7 +193,6 @@
     f_own, f_give = (pick(features, odd), pick(features, 1 - odd))
     d_par = lax.ppermute(d_give, "rows", swap)
     d_near = lax.ppermute(d_own, "rows", near)
-    f_give, d_par = fence((f_give, d_par))
     f_par = lax.ppermute(f_give, "rows", swap)
     d_far = lax.ppermute(d_par, "rows", far)
     f_first, d_far = fence((f_own, d_far))
@@ -198,19 +200,18 @@
     f_far = lax.ppermute(f_par, "rows", far)
     d_blocks = (d_own, d_par, d_near, d_far)
     f_blocks = (f_own, f_par, f_near, f_far)
-    d_left, d_right = exchanged(*edges(d_blocks), cols)
+    d_left, d_right = exchanged(*edges(par, d_blocks, flops), cols)
 
     part = jax.ShapeDtypeStruct((share, cout), jnp.float32)
-    d_maps = [VMEM((4, half, wide, cout), jnp.bfloat16), VMEM((4, half, width, 3 * cout), jnp.bfloat16)]
-    keep, give = call(
+    keep, give, shifted = call(
         kernel_grad,
         (par, f_own, f_par) + d_blocks + (d_left, d_right),
-        [part, part],
-        d_maps + [VMEM((9 * cin, cout), jnp.float32)],
+        [part, part, jax.ShapeDtypeStruct((4, half, width, 3 * cout), jnp.bfloat16)],
+        [VMEM((4, half, wide, cout), jnp.bfloat16), VMEM((9 * cin, cout), jnp.float32)],
         30 * flops,
     )
     given = lax.ppermute(give, "core", other_core)
-    f_tails, f_heads = edges(f_blocks)
+    f_tails, f_heads = edges(par, f_blocks, 2 * flops)
     given, f_tails, f_heads = fence((given, f_tails, f_heads))
 
     (scaled,) = call(
@@ -222,10 +223,10 @@
     )
     scaled, f_tails, f_heads = fence((scaled.astype(jnp.float16), f_tails, f_heads))
     got = lax.all_to_all(scaled, CHIPS, 0, 0)
-    d_left, _ = fence((d_left, scaled))
+    shifted, _ = fence((shifted, scaled))
     half_grad = jax.ShapeDtypeStruct((half, width, cin), jnp.bfloat16)
     g_own, g_par = call(
-        kernel_back, (par, weight) + d_blocks + (d_left, d_right), [half_grad, half_grad], d_maps, 0
+        kernel_back, (par, weight, shifted), [half_grad, half_grad], [], 0
     )
     g_other = lax.ppermute(g_par, "rows", swap)
     got, g_par = fence((got, g_par))
@@ -240,7 +241,7 @@
         0,
     )
     mine = mine.astype(jnp.float16)
-    f_left, copies = fence((f_left, jnp.broadcast_to(mine[None], (chips, deep, cout))))
+    f_left, f_right, copies = fence((f_left, f_right, jnp.broadcast_to(mine[None], (chips, deep, cout))))
     spread = lax.all_to_all(copies, CHIPS, 0, 0)
     other = lax.ppermute(spread, "core", other_core)
 

time: 95.1 us -> 92.4 us (0.972); the launches traced: 93.2 us -> 91.6 us
  starting transfers between devices: 42.3 us -> 45.1 us
  waiting for transfers between devices: 21.7 us -> 19.1 us
  Pallas kernels: 11.1 us -> 13.5 us
  local copies, waits for them, and re-layouts: 8.98 us -> 6.73 us
  other arithmetic: 8.1 us -> 6.2 us
    ppermute x1, waiting for transfers between devices: 5.57 us -> 0.77 us  [body(): f_far = lax.ppermute(f_par, 'rows', far)]
    ppermute x1, waiting for transfers between devices: 0.01 us -> 4.41 us  [body(): d_near = lax.ppermute(d_own, 'rows', near)]
    ppermute x1, starting transfers between devices: 4.35 us -> 0.01 us  [body(): other = lax.ppermute(spread, 'core', other_core)]
    ppermute x1, waiting for transfers between devices: 3.56 us -> 0.01 us  [body(): f_par = lax.ppermute(f_give, 'rows', swap)]
    ppermute x1, waiting for transfers between devices: 2.96 us -> 6.49 us  [body(): d_par = lax.ppermute(d_give, 'rows', swap)]
    all_to_all x1, waiting for transfers between devices: 0.01 us -> 3.32 us  [body(): spread = lax.all_to_all(copies, CHIPS, 0, 0)]
    all_to_all x1, starting transfers between devices: 5.98 us -> 8.94 us  [body(): got = lax.all_to_all(scaled, CHIPS, 0, 0)]
    pallas_call x5 -> x7, Pallas kernels: 11.1 us -> 13.5 us  [call(): pl.pallas_call(kernel, out_shape=outs, in_specs=[pl.BlockSpec(memory_spac...]
  transfers between devices with their start and end apart: 16 -> 16, of which waited for: 8 -> 6; matrix products, arithmetic and copies ran while one was open for 8% -> 4% of each run, Pallas kernels for 11% -> 14%
where the time goes in v9:
time: 92.4 us; the launch traced here: 91.6 us
  starting transfers between devices  45.1 us (49%)
  waiting for transfers between devices  19.1 us (21%)
  Pallas kernels  13.5 us (15%)
  local copies, waits for them, and re-layouts  6.73 us (7%)
  other arithmetic  6.2 us (7%)
  between operations  1 us (1%)
    pallas_call x7, Pallas kernels, call(): pl.pallas_call(kernel, out_shape=outs, in_specs=[pl.BlockSpec(memory_spac...  13.5 us
    all_to_all x1, starting transfers between devices, body(): got = lax.all_to_all(scaled, CHIPS, 0, 0)  8.94 us
    all_to_all x1, starting transfers between devices, body(): spread = lax.all_to_all(copies, CHIPS, 0, 0)  8.69 us
    ppermute x1, waiting for transfers between devices, body(): d_par = lax.ppermute(d_give, 'rows', swap)  6.49 us
    unnamed x36, local copies, waits for them, and re-layouts  4.71 us
    ppermute x1, starting transfers between devices, body(): f_far = lax.ppermute(f_par, 'rows', far)  4.58 us
    ppermute x1, waiting for transfers between devices, body(): d_near = lax.ppermute(d_own, 'rows', near)  4.41 us
    ppermute x2, starting transfers between devices, exchanged(): left = lax.ppermute(tails, COLS, [(i, i + 1) for i in range(count - 1)])  4.32 us
  transfers between devices with their start and end apart: 16, of which 6 were waited for; matrix products, arithmetic and copies ran while one was open for 4% of the time, Pallas kernels for 14%

profile of v9, /device:TPU:0, one launch (start us, length us, event | category | flops | bytes accessed | tf_op | source)
XLA Modules:
  0.0 91.6 jit_solution(7763435446686249591)
XLA Ops:
  0.7 1.2 %constant_dynamic-slice_fusion = (bf16[6,160,128]{2,1,0:T(8,128)(2,1)S(1)}, bf16[6,160,128]{2,1,0:T(8,128)(2,1)S(1)}) fusion(bf16[12,160,128]{2,1,0:T(8,128)(2,1)} %param.5, s32[]{:T(128)S(6)} %select_n.53, s32[]{:T(128)S(6)} %select_n.54), kind=kLoop, calls=%fused_computation.11 | loop fusion | bytes 983048 | tf_op jit(solution)/shard_map/dynamic_slice | solution.py:184
  1.8 0.0 copy-start.9
  1.9 3.0 %collective-permute-start.1 = (bf16[6,160,128]{2,1,0:T(8,128)(2,1)S(1)}, bf16[6,160,128]{2,1,0:T(8,128)(2,1)S(1)}, u32[]{:S(2)}, u32[]{:S(2)}) collective-permute-start(bf16[6,160,128]{2,1,0:T(8,128)(2,1)S(1)} %get-tuple-element.60), channel_id=1, source_target_pairs={{0,4},{4,0},{8,12},{12,8},{16,20},{20,16},{24,28},{28,24},{1,5},{5... | collective-permute-start | bytes 737288 | tf_op jit(solution)/shard_map/ppermute | solution.py:194
  4.9 0.1 constant_dynamic-slice_fusion.2
  5.0 0.2 collective-permute-start
  5.2 6.5 %collective-permute-done.1.refs_1_.d_par = bf16[6,160,128]{2,1,0:T(8,128)(2,1)S(1)} collective-permute-done((bf16[6,160,128]{2,1,0:T(8,128)(2,1)S(1)}, bf16[6,160,128]{2,1,0:T(8,128)(2,1)S(1)}, u32[]{:S(2)}, u32[]{:S(2)}) %collective-permute-start.1) | collective-permute-done | bytes 245792 | tf_op jit(solution)/shard_map/ppermute | solution.py:194
  11.7 4.0 %collective-permute-start.2 = (bf16[6,160,128]{2,1,0:T(8,128)(2,1)S(1)}, bf16[6,160,128]{2,1,0:T(8,128)(2,1)S(1)}, u32[]{:S(2)}, u32[]{:S(2)}) collective-permute-start(bf16[6,160,128]{2,1,0:T(8,128)(2,1)S(1)} %collective-permute-done.1.refs_1_.d_par), channel_id=1, source_target_pairs={{12,4},{0,8},{20,12},{8,16},{28,20},{16,24},{13,5},{1,9},{21,13},{... | collective-permute-start | bytes 737288 | tf_op jit(solution)/shard_map/ppermute | solution.py:197
  15.7 1.3 %collective-permute-start.5 = (bf16[6,160,128]{2,1,0:T(8,128)(2,1)S(1)}, bf16[6,160,128]{2,1,0:T(8,128)(2,1)S(1)}, u32[]{:S(2)}, u32[]{:S(2)}) collective-permute-start(bf16[6,160,128]{2,1,0:T(8,128)(2,1)S(1)} %get-tuple-element.59.refs_0_.d_own), channel_id=1, source_target_pairs={{4,12},{8,0},{12,20},{16,8},{20,28},{24,16},{5,13},{9,1},{13,21},{... | collective-permute-start | bytes 737288 | tf_op jit(solution)/shard_map/ppermute | solution.py:195
  17.0 0.1 pad_add_fusion.par
  17.1 2.3 %collective-permute-done.2.refs_3_.d_far = bf16[6,160,128]{2,1,0:T(8,128)(2,1)S(1)} collective-permute-done((bf16[6,160,128]{2,1,0:T(8,128)(2,1)S(1)}, bf16[6,160,128]{2,1,0:T(8,128)(2,1)S(1)}, u32[]{:S(2)}, u32[]{:S(2)}) %collective-permute-start.2) | collective-permute-done | bytes 245792 | tf_op jit(solution)/shard_map/ppermute | solution.py:197
  19.4 4.4 %collective-permute-done.5.refs_2_.d_near = bf16[6,160,128]{2,1,0:T(8,128)(2,1)S(1)} collective-permute-done((bf16[6,160,128]{2,1,0:T(8,128)(2,1)S(1)}, bf16[6,160,128]{2,1,0:T(8,128)(2,1)S(1)}, u32[]{:S(2)}, u32[]{:S(2)}) %collective-permute-start.5) | collective-permute-done | bytes 245792 | tf_op jit(solution)/shard_map/ppermute | solution.py:195
  23.8 0.6 shard_map.58
  24.4 0.1 copy-done.15
  24.5 1.3 %collective-permute-start.6 = (bf16[4,6,16,128]{3,2,1,0:T(8,128)(2,1)S(1)}, bf16[4,6,16,128]{3,2,1,0:T(8,128)(2,1)S(1)}, u32[]{:S(2)}, u32[]{:S(2)}) collective-permute-start(bf16[4,6,16,128]{3,2,1,0:T(8,128)(2,1)S(1)} %get-tuple-element.29), channel_id=1, source_target_pairs={{0,1},{1,2},{2,3},{4,5},{5,6},{6,7},{8,9},{9,10},{10,11},{12,13},{... | collective-permute-start | bytes 294920 | tf_op jit(solution)/shard_map/ppermute | solution.py:154
  25.8 1.3 %collective-permute-start.7 = (bf16[4,6,16,128]{3,2,1,0:T(8,128)(2,1)S(1)}, bf16[4,6,16,128]{3,2,1,0:T(8,128)(2,1)S(1)}, u32[]{:S(2)}, u32[]{:S(2)}) collective-permute-start(bf16[4,6,16,128]{3,2,1,0:T(8,128)(2,1)S(1)} %get-tuple-element.30), channel_id=1, source_target_pairs={{1,0},{2,1},{3,2},{5,4},{6,5},{7,6},{9,8},{10,9},{11,10},{13,12},{... | collective-permute-start | bytes 294920 | tf_op jit(solution)/shard_map/ppermute | solution.py:155
  27.1 1.3 %collective-permute-start.3 = (bf16[6,160,256]{2,1,0:T(8,128)(2,1)S(1)}, bf16[6,160,256]{2,1,0:T(8,128)(2,1)S(1)}, u32[]{:S(2)}, u32[]{:S(2)}) collective-permute-start(bf16[6,160,256]{2,1,0:T(8,128)(2,1)S(1)} %get-tuple-element.27.f_own.refs_0_), channel_id=1, source_target_pairs={{4,12},{8,0},{12,20},{16,8},{20,28},{24,16},{5,13},{9,1},{13,21},{... | collective-permute-start | bytes 1474568 | tf_op jit(solution)/shard_map/ppermute | solution.py:199
  28.4 4.6 %collective-permute-start.4 = (bf16[6,160,256]{2,1,0:T(8,128)(2,1)}, bf16[6,160,256]{2,1,0:T(8,128)(2,1)S(1)}, u32[]{:S(2)}, u32[]{:S(2)}) collective-permute-start(bf16[6,160,256]{2,1,0:T(8,128)(2,1)} %collective-permute-done.f_par.refs_1_), channel_id=1, source_target_pairs={{12,4},{0,8},{20,12},{8,16},{28,20},{16,24},{13,5},{1,9},{21,13},{... | collective-permute-start | bytes 1474568 | tf_op jit(solution)/shard_map/ppermute | solution.py:200
  33.0 0.9 %copy-done.10 = bf16[6,160,128]{2,1,0:T(8,128)(2,1)S(1)} copy-done((bf16[6,160,128]{2,1,0:T(8,128)(2,1)S(1)}, bf16[6,160,128]{2,1,0:T(8,128)(2,1)}, u32[]{:S(2)}) %copy-start.10) | copy-done | bytes 245784
  34.0 0.9 %copy-done.12 = bf16[6,160,128]{2,1,0:T(8,128)(2,1)S(1)} copy-done((bf16[6,160,128]{2,1,0:T(8,128)(2,1)S(1)}, bf16[6,160,128]{2,1,0:T(8,128)(2,1)}, u32[]{:S(2)}) %copy-start.12) | copy-done | bytes 245784
  34.9 0.9 %copy-done.14 = bf16[6,160,128]{2,1,0:T(8,128)(2,1)S(1)} copy-done((bf16[6,160,128]{2,1,0:T(8,128)(2,1)S(1)}, bf16[6,160,128]{2,1,0:T(8,128)(2,1)}, u32[]{:S(2)}) %copy-start.14) | copy-done | bytes 245784
  35.8 0.9 %copy-done.16 = bf16[6,160,128]{2,1,0:T(8,128)(2,1)S(1)} copy-done((bf16[6,160,128]{2,1,0:T(8,128)(2,1)S(1)}, bf16[6,160,128]{2,1,0:T(8,128)(2,1)}, u32[]{:S(2)}) %copy-start.16) | copy-done | bytes 245784
  36.8 3.3 %shard_map.59 = (f32[1152,128]{1,0:T(8,128)S(1)}, f32[1152,128]{1,0:T(8,128)S(1)}, bf16[4,6,160,384]{3,2,1,0:T(8,128)(2,1)S(1)}) custom-call(s32[2]{0:T(128)S(1)} %pad_add_fusion.par, bf16[6,160,256]{2,1,0:T(8,128)(2,1)S(1)} %get-tuple-element.27.f_own.refs_0_, bf16[6,160,256]{2,1,0:T(8,128)(2,1)} %collective-permute-done.f_par.refs_1_, ...), custom_call_target="tpu_custom_call" | custom-call | flops 33973862400 | bytes 6291464 | tf_op jit(solution)/shard_map/pallas_call | solution.py:129
  40.1 2.4 %collective-permute-start.8 = (f32[1152,128]{1,0:T(8,128)S(1)}, f32[1152,128]{1,0:T(8,128)S(1)}, u32[]{:S(2)}, u32[]{:S(2)}) collective-permute-start(f32[1152,128]{1,0:T(8,128)S(1)} %get-tuple-element.32), channel_id=1, source_target_pairs={{0,1},{1,0},{2,3},{3,2},{4,5},{5,4},{6,7},{7,6},{8,9},{9,8},{10,11... | collective-permute-start | bytes 1769480 | tf_op jit(solution)/shard_map/ppermute | solution.py:213
  42.4 0.8 collective-permute-done.4.refs_3_.f_far
  43.2 2.0 %shard_map.60 = (bf16[4,6,16,256]{3,2,1,0:T(8,128)(2,1)}, bf16[4,6,16,256]{3,2,1,0:T(8,128)(2,1)}) custom-call(s32[2]{0:T(128)S(1)} %pad_add_fusion.par, bf16[6,160,256]{2,1,0:T(8,128)(2,1)S(1)} %get-tuple-element.27.f_own.refs_0_, bf16[6,160,256]{2,1,0:T(8,128)(2,1)} %collective-permute-done.f_par.refs_1_, ...), custom_call_target="tpu_custom_call" | custom-call | flops 2264924160 | bytes 2359304 | tf_op jit(solution)/shard_map/pallas_call | solution.py:129
  45.2 0.7 shard_map.61
  46.0 0.8 convert_element_type.21
  46.7 8.9 %all-to-all-start = ((f16[16,80,128]{2,1,0:T(8,128)(2,1)}), f16[16,80,128]{2,1,0:T(8,128)(2,1)}, u32[]{:S(2)}, u32[]{:S(2)}) async-start(f16[16,80,128]{2,1,0:T(8,128)(2,1)} %convert_element_type.21), calls=%async_computation | async-start | bytes 655360 | tf_op jit(solution)/shard_map/all_to_all | solution.py:225
  55.7 3.1 %shard_map.62 = (bf16[6,160,256]{2,1,0:T(8,128)(2,1)S(1)}, bf16[6,160,256]{2,1,0:T(8,128)(2,1)}) custom-call(s32[2]{0:T(128)S(1)} %pad_add_fusion.par, bf16[3,3,256,128]{3,2,1,0:T(8,128)(2,1)S(1)} %copy-done, bf16[4,6,160,384]{3,2,1,0:T(8,128)(2,1)S(1)} %get-tuple-element.42.shifted), custom_call_target="tpu_custom_call" | custom-call | tf_op jit(solution)/shard_map/pallas_call | solution.py:129
  58.8 0.8 copy-done.7
  59.6 1.9 %collective-permute-start.12 = (bf16[6,160,256]{2,1,0:T(8,128)(2,1)}, bf16[6,160,256]{2,1,0:T(8,128)(2,1)S(1)}, u32[]{:S(2)}, u32[]{:S(2)}) collective-permute-start(bf16[6,160,256]{2,1,0:T(8,128)(2,1)} %get-tuple-element.43), channel_id=1, source_target_pairs={{0,4},{4,0},{8,12},{12,8},{16,20},{20,16},{24,28},{28,24},{1,5},{5... | collective-permute-start | bytes 1474568 | tf_op jit(solution)/shard_map/ppermute | solution.py:231
  61.4 1.3 %collective-permute-start.10 = (bf16[4,6,16,256]{3,2,1,0:T(8,128)(2,1)}, bf16[4,6,16,256]{3,2,1,0:T(8,128)(2,1)S(1)}, u32[]{:S(2)}, u32[]{:S(2)}) collective-permute-start(bf16[4,6,16,256]{3,2,1,0:T(8,128)(2,1)} %get-tuple-element.39), channel_id=1, source_target_pairs={{1,0},{2,1},{3,2},{5,4},{6,5},{7,6},{9,8},{10,9},{11,10},{13,12},{... | collective-permute-start | bytes 589832 | tf_op jit(solution)/shard_map/ppermute | solution.py:155
  62.7 3.0 %collective-permute-start.9 = (bf16[4,6,16,256]{3,2,1,0:T(8,128)(2,1)}, bf16[4,6,16,256]{3,2,1,0:T(8,128)(2,1)S(1)}, u32[]{:S(2)}, u32[]{:S(2)}) collective-permute-start(bf16[4,6,16,256]{3,2,1,0:T(8,128)(2,1)} %get-tuple-element.38), channel_id=1, source_target_pairs={{0,1},{1,2},{2,3},{4,5},{5,6},{6,7},{8,9},{9,10},{10,11},{12,13},{... | collective-permute-start | bytes 589832 | tf_op jit(solution)/shard_map/ppermute | solution.py:154
  65.8 1.0 %convert_element_type.22.got = f32[16,80,128]{2,1,0:T(8,128)S(1)} convert(f16[16,80,128]{2,1,0:T(8,128)(2,1)} %all-to-all-done) | non-fusion elementwise | flops 163840 | bytes 983040 | tf_op jit(solution)/shard_map/convert_element_type | solution.py:238
  66.8 0.6 shard_map.63
  67.4 0.8 broadcast_in_dim.2
  68.2 8.7 %all-to-all-start.1 = ((f16[16,80,128]{2,1,0:T(8,128)(2,1)}), f16[16,80,128]{2,1,0:T(8,128)(2,1)}, u32[]{:S(2)}, u32[]{:S(2)}) async-start(f16[16,80,128]{2,1,0:T(8,128)(2,1)} %broadcast_in_dim.2), calls=%async_computation.1 | async-start | bytes 655360 | tf_op jit(solution)/shard_map/all_to_all | solution.py:245
  77.0 3.2 %shard_map.64 = (bf16[6,160,128]{2,1,0:T(8,128)(2,1)S(1)}, bf16[6,160,128]{2,1,0:T(8,128)(2,1)S(1)}) custom-call(s32[2]{0:T(128)S(1)} %pad_add_fusion.par, bf16[3,3,256,128]{3,2,1,0:T(8,128)(2,1)S(1)} %copy-done, bf16[6,160,256]{2,1,0:T(8,128)(2,1)S(1)} %copy-done.2, bf16[6,160,256]{2,1,0:T(8,128)(2,1)} %collective-permute-done.f_par.refs_1_, ...), custom_call_target="tpu_custom_call" | custom-call | tf_op jit(solution)/shard_map/pallas_call | solution.py:129
  80.2 1.9 %collective-permute-start.11 = (bf16[6,160,128]{2,1,0:T(8,128)(2,1)S(1)}, bf16[6,160,128]{2,1,0:T(8,128)(2,1)S(1)}, u32[]{:S(2)}, u32[]{:S(2)}) collective-permute-start(bf16[6,160,128]{2,1,0:T(8,128)(2,1)S(1)} %get-tuple-element.47), channel_id=1, source_target_pairs={{0,4},{4,0},{8,12},{12,8},{16,20},{20,16},{24,28},{28,24},{1,5},{5... | collective-permute-start | bytes 737288 | tf_op jit(solution)/shard_map/ppermute | solution.py:256
  82.2 0.1 broadcast_select_fusion.1
  82.2 1.0 %pad_maximum_fusion.1 = bf16[12,160,256]{2,1,0:T(8,128)(2,1)} fusion(bf16[6,160,256]{2,1,0:T(8,128)(2,1)S(1)} %get-tuple-element.52, bf16[6,160,256]{2,1,0:T(8,128)(2,1)S(1)} %get-tuple-element.51), kind=kLoop, calls=%fused_computation.1 | loop fusion | flops 491520 | bytes 1966080 | tf_op jit(solution)/shard_map/concatenate | solution.py:162
  83.3 3.3 %all-to-all-done.1 = f16[16,80,128]{2,1,0:T(8,128)(2,1)} async-done(((f16[16,80,128]{2,1,0:T(8,128)(2,1)}), f16[16,80,128]{2,1,0:T(8,128)(2,1)}, u32[]{:S(2)}, u32[]{:S(2)}) %all-to-all-start.1) | async-done | bytes 327712 | tf_op jit(solution)/shard_map/all_to_all | solution.py:245
  86.6 1.8 %collective-permute-done.11 = bf16[6,160,128]{2,1,0:T(8,128)(2,1)S(1)} collective-permute-done((bf16[6,160,128]{2,1,0:T(8,128)(2,1)S(1)}, bf16[6,160,128]{2,1,0:T(8,128)(2,1)S(1)}, u32[]{:S(2)}, u32[]{:S(2)}) %collective-permute-start.11) | collective-permute-done | bytes 245792 | tf_op jit(solution)/shard_map/ppermute | solution.py:256
  88.4 0.1 broadcast_select_fusion.5
  88.4 0.8 pad_maximum_fusion.2
  89.3 1.1 %broadcast_select_fusion.3 = (f16[16,80,128]{2,1,0:T(8,128)(2,1)S(1)}, f16[16,80,128]{2,1,0:T(8,128)(2,1)S(1)}) fusion(f16[16,80,128]{2,1,0:T(8,128)(2,1)} %all-to-all-done.1, f16[16,80,128]{2,1,0:T(8,128)(2,1)S(1)} %collective-permute-done.13, pred[]{:T(512)S(6)} %eq.7), kind=kLoop, calls=%fused_computation.8 | loop fusion | flops 327680 | bytes 1310721 | tf_op jit(solution)/shard_map/jit(_where)/select_n | solution.py:261
  90.4 0.1 convert_multiply_fusion
  90.5 1.1 %pad_maximum_fusion = f32[2304,128]{1,0:T(8,128)} fusion(f32[1152,128]{1,0:T(8,128)S(1)} %bitcast.9, f32[1152,128]{1,0:T(8,128)S(1)} %bitcast.10), kind=kLoop, calls=%fused_computation | loop fusion | flops 294912 | bytes 2359296 | tf_op jit(solution)/shard_map/concatenate | solution.py:265
  (43 shorter events, 0.1 us)
Async XLA Ops:
  0.6 4.3 %copy-start.17 = (bf16[12,160,256]{2,1,0:T(8,128)(2,1)S(1)}, bf16[12,160,256]{2,1,0:T(8,128)(2,1)}, u32[]{:S(2)}) copy-start(bf16[12,160,256]{2,1,0:T(8,128)(2,1)} %param.3) | copy-start | bytes 2949124
  1.8 22.5 %copy-start.9 = (bf16[6,160,128]{2,1,0:T(8,128)(2,1)}, bf16[6,160,128]{2,1,0:T(8,128)(2,1)S(1)}, u32[]{:S(2)}) copy-start(bf16[6,160,128]{2,1,0:T(8,128)(2,1)S(1)} %get-tuple-element.59.refs_0_.d_own) | copy-start | bytes 737284
  1.9 9.8 %collective-permute-start.1 = (bf16[6,160,128]{2,1,0:T(8,128)(2,1)S(1)}, bf16[6,160,128]{2,1,0:T(8,128)(2,1)S(1)}, u32[]{:S(2)}, u32[]{:S(2)}) collective-permute-start(bf16[6,160,128]{2,1,0:T(8,128)(2,1)S(1)} %get-tuple-element.60), channel_id=1, source_target_pairs={{0,4},{4,0},{8,12},{12,8},{16,20},{20,16},{24,28},{28,24},{1,5},{5... | collective-permute-start | bytes 737288 | tf_op jit(solution)/shard_map/ppermute | solution.py:194
  5.0 38.2 %copy-start.1 = (bf16[6,160,256]{2,1,0:T(8,128)(2,1)}, bf16[6,160,256]{2,1,0:T(8,128)(2,1)S(1)}, u32[]{:S(2)}) copy-start(bf16[6,160,256]{2,1,0:T(8,128)(2,1)S(1)} %get-tuple-element.27.f_own.refs_0_) | copy-start | bytes 1474564
  5.0 23.4 %collective-permute-start = (bf16[6,160,256]{2,1,0:T(8,128)(2,1)S(1)}, bf16[6,160,256]{2,1,0:T(8,128)(2,1)}, u32[]{:S(2)}, u32[]{:S(2)}) collective-permute-start(bf16[6,160,256]{2,1,0:T(8,128)(2,1)S(1)} %get-tuple-element.53), channel_id=1, source_target_pairs={{0,4},{4,0},{8,12},{12,8},{16,20},{20,16},{24,28},{28,24},{1,5},{5... | collective-permute-start | bytes 1474568 | tf_op jit(solution)/shard_map/ppermute | solution.py:196
  11.7 12.7 %copy-start.11 = (bf16[6,160,128]{2,1,0:T(8,128)(2,1)}, bf16[6,160,128]{2,1,0:T(8,128)(2,1)S(1)}, u32[]{:S(2)}) copy-start(bf16[6,160,128]{2,1,0:T(8,128)(2,1)S(1)} %collective-permute-done.1.refs_1_.d_par) | copy-start | bytes 737284
  11.7 7.7 %collective-permute-start.2 = (bf16[6,160,128]{2,1,0:T(8,128)(2,1)S(1)}, bf16[6,160,128]{2,1,0:T(8,128)(2,1)S(1)}, u32[]{:S(2)}, u32[]{:S(2)}) collective-permute-start(bf16[6,160,128]{2,1,0:T(8,128)(2,1)S(1)} %collective-permute-done.1.refs_1_.d_par), channel_id=1, source_target_pairs={{12,4},{0,8},{20,12},{8,16},{28,20},{16,24},{13,5},{1,9},{21,13},{... | collective-permute-start | bytes 737288 | tf_op jit(solution)/shard_map/ppermute | solution.py:197
  15.7 8.1 %collective-permute-start.5 = (bf16[6,160,128]{2,1,0:T(8,128)(2,1)S(1)}, bf16[6,160,128]{2,1,0:T(8,128)(2,1)S(1)}, u32[]{:S(2)}, u32[]{:S(2)}) collective-permute-start(bf16[6,160,128]{2,1,0:T(8,128)(2,1)S(1)} %get-tuple-element.59.refs_0_.d_own), channel_id=1, source_target_pairs={{4,12},{8,0},{12,20},{16,8},{20,28},{24,16},{5,13},{9,1},{13,21},{... | collective-permute-start | bytes 737288 | tf_op jit(solution)/shard_map/ppermute | solution.py:195
  19.4 5.0 %copy-start.13 = (bf16[6,160,128]{2,1,0:T(8,128)(2,1)}, bf16[6,160,128]{2,1,0:T(8,128)(2,1)S(1)}, u32[]{:S(2)}) copy-start(bf16[6,160,128]{2,1,0:T(8,128)(2,1)S(1)} %collective-permute-done.2.refs_3_.d_far) | copy-start | bytes 737284
  23.8 0.7 copy-start.15
  24.5 8.5 %collective-permute-start.6 = (bf16[4,6,16,128]{3,2,1,0:T(8,128)(2,1)S(1)}, bf16[4,6,16,128]{3,2,1,0:T(8,128)(2,1)S(1)}, u32[]{:S(2)}, u32[]{:S(2)}) collective-permute-start(bf16[4,6,16,128]{3,2,1,0:T(8,128)(2,1)S(1)} %get-tuple-element.29), channel_id=1, source_target_pairs={{0,1},{1,2},{2,3},{4,5},{5,6},{6,7},{8,9},{9,10},{10,11},{12,13},{... | collective-permute-start | bytes 294920 | tf_op jit(solution)/shard_map/ppermute | solution.py:154
  25.8 7.2 %collective-permute-start.7 = (bf16[4,6,16,128]{3,2,1,0:T(8,128)(2,1)S(1)}, bf16[4,6,16,128]{3,2,1,0:T(8,128)(2,1)S(1)}, u32[]{:S(2)}, u32[]{:S(2)}) collective-permute-start(bf16[4,6,16,128]{3,2,1,0:T(8,128)(2,1)S(1)} %get-tuple-element.30), channel_id=1, source_target_pairs={{1,0},{2,1},{3,2},{5,4},{6,5},{7,6},{9,8},{10,9},{11,10},{13,12},{... | collective-permute-start | bytes 294920 | tf_op jit(solution)/shard_map/ppermute | solution.py:155
  27.1 15.3 %collective-permute-start.3 = (bf16[6,160,256]{2,1,0:T(8,128)(2,1)S(1)}, bf16[6,160,256]{2,1,0:T(8,128)(2,1)S(1)}, u32[]{:S(2)}, u32[]{:S(2)}) collective-permute-start(bf16[6,160,256]{2,1,0:T(8,128)(2,1)S(1)} %get-tuple-element.27.f_own.refs_0_), channel_id=1, source_target_pairs={{4,12},{8,0},{12,20},{16,8},{20,28},{24,16},{5,13},{9,1},{13,21},{... | collective-permute-start | bytes 1474568 | tf_op jit(solution)/shard_map/ppermute | solution.py:199
  28.4 14.8 %collective-permute-start.4 = (bf16[6,160,256]{2,1,0:T(8,128)(2,1)}, bf16[6,160,256]{2,1,0:T(8,128)(2,1)S(1)}, u32[]{:S(2)}, u32[]{:S(2)}) collective-permute-start(bf16[6,160,256]{2,1,0:T(8,128)(2,1)} %collective-permute-done.f_par.refs_1_), channel_id=1, source_target_pairs={{12,4},{0,8},{20,12},{8,16},{28,20},{16,24},{13,5},{1,9},{21,13},{... | collective-permute-start | bytes 1474568 | tf_op jit(solution)/shard_map/ppermute | solution.py:200
  33.0 0.9 %copy-start.10 = (bf16[6,160,128]{2,1,0:T(8,128)(2,1)S(1)}, bf16[6,160,128]{2,1,0:T(8,128)(2,1)}, u32[]{:S(2)}) copy-start(bf16[6,160,128]{2,1,0:T(8,128)(2,1)} %copy-done.9) | copy-start | bytes 737284
  34.0 0.9 %copy-start.12 = (bf16[6,160,128]{2,1,0:T(8,128)(2,1)S(1)}, bf16[6,160,128]{2,1,0:T(8,128)(2,1)}, u32[]{:S(2)}) copy-start(bf16[6,160,128]{2,1,0:T(8,128)(2,1)} %copy-done.11) | copy-start | bytes 737284
  34.9 0.9 %copy-start.14 = (bf16[6,160,128]{2,1,0:T(8,128)(2,1)S(1)}, bf16[6,160,128]{2,1,0:T(8,128)(2,1)}, u32[]{:S(2)}) copy-start(bf16[6,160,128]{2,1,0:T(8,128)(2,1)} %copy-done.13) | copy-start | bytes 737284
  35.8 0.9 %copy-start.16 = (bf16[6,160,128]{2,1,0:T(8,128)(2,1)S(1)}, bf16[6,160,128]{2,1,0:T(8,128)(2,1)}, u32[]{:S(2)}) copy-start(bf16[6,160,128]{2,1,0:T(8,128)(2,1)} %copy-done.15) | copy-start | bytes 737284
  40.1 5.1 %collective-permute-start.8 = (f32[1152,128]{1,0:T(8,128)S(1)}, f32[1152,128]{1,0:T(8,128)S(1)}, u32[]{:S(2)}, u32[]{:S(2)}) collective-permute-start(f32[1152,128]{1,0:T(8,128)S(1)} %get-tuple-element.32), channel_id=1, source_target_pairs={{0,1},{1,0},{2,3},{3,2},{4,5},{5,4},{6,7},{7,6},{8,9},{9,8},{10,11... | collective-permute-start | bytes 1769480 | tf_op jit(solution)/shard_map/ppermute | solution.py:213
  42.4 2.8 %copy-start.3 = (bf16[6,160,256]{2,1,0:T(8,128)(2,1)}, bf16[6,160,256]{2,1,0:T(8,128)(2,1)S(1)}, u32[]{:S(2)}) copy-start(bf16[6,160,256]{2,1,0:T(8,128)(2,1)S(1)} %collective-permute-done.3.refs_2_.f_near) | copy-start | bytes 1474564
  43.2 2.0 %copy-start.5 = (bf16[6,160,256]{2,1,0:T(8,128)(2,1)}, bf16[6,160,256]{2,1,0:T(8,128)(2,1)S(1)}, u32[]{:S(2)}) copy-start(bf16[6,160,256]{2,1,0:T(8,128)(2,1)S(1)} %collective-permute-done.4.refs_3_.f_far) | copy-start | bytes 1474564
  45.9 9.7 %copy-start = (bf16[3,3,256,128]{3,2,1,0:T(8,128)(2,1)S(1)}, bf16[3,3,256,128]{3,2,1,0:T(8,128)(2,1)}, u32[]{:S(2)}) copy-start(bf16[3,3,256,128]{3,2,1,0:T(8,128)(2,1)} %w.3) | copy-start | bytes 1769476
  46.7 19.0 %all-to-all-start = ((f16[16,80,128]{2,1,0:T(8,128)(2,1)}), f16[16,80,128]{2,1,0:T(8,128)(2,1)}, u32[]{:S(2)}, u32[]{:S(2)}) async-start(f16[16,80,128]{2,1,0:T(8,128)(2,1)} %convert_element_type.21), calls=%async_computation | async-start | bytes 655360 | tf_op jit(solution)/shard_map/all_to_all | solution.py:225
  58.8 0.8 copy-start.7
  59.6 17.4 %copy-start.2 = (bf16[6,160,256]{2,1,0:T(8,128)(2,1)S(1)}, bf16[6,160,256]{2,1,0:T(8,128)(2,1)}, u32[]{:S(2)}) copy-start(bf16[6,160,256]{2,1,0:T(8,128)(2,1)} %copy-done.1) | copy-start | bytes 1474564
  59.6 17.4 %copy-start.4 = (bf16[6,160,256]{2,1,0:T(8,128)(2,1)S(1)}, bf16[6,160,256]{2,1,0:T(8,128)(2,1)}, u32[]{:S(2)}) copy-start(bf16[6,160,256]{2,1,0:T(8,128)(2,1)} %copy-done.3) | copy-start | bytes 1474564
  59.6 17.4 %copy-start.6 = (bf16[6,160,256]{2,1,0:T(8,128)(2,1)S(1)}, bf16[6,160,256]{2,1,0:T(8,128)(2,1)}, u32[]{:S(2)}) copy-start(bf16[6,160,256]{2,1,0:T(8,128)(2,1)} %copy-done.5) | copy-start | bytes 1474564
  59.6 22.6 %collective-permute-start.12 = (bf16[6,160,256]{2,1,0:T(8,128)(2,1)}, bf16[6,160,256]{2,1,0:T(8,128)(2,1)S(1)}, u32[]{:S(2)}, u32[]{:S(2)}) collective-permute-start(bf16[6,160,256]{2,1,0:T(8,128)(2,1)} %get-tuple-element.43), channel_id=1, source_target_pairs={{0,4},{4,0},{8,12},{12,8},{16,20},{20,16},{24,28},{28,24},{1,5},{5... | collective-permute-start | bytes 1474568 | tf_op jit(solution)/shard_map/ppermute | solution.py:231
  61.4 6.0 %collective-permute-start.10 = (bf16[4,6,16,256]{3,2,1,0:T(8,128)(2,1)}, bf16[4,6,16,256]{3,2,1,0:T(8,128)(2,1)S(1)}, u32[]{:S(2)}, u32[]{:S(2)}) collective-permute-start(bf16[4,6,16,256]{3,2,1,0:T(8,128)(2,1)} %get-tuple-element.39), channel_id=1, source_target_pairs={{1,0},{2,1},{3,2},{5,4},{6,5},{7,6},{9,8},{10,9},{11,10},{13,12},{... | collective-permute-start | bytes 589832 | tf_op jit(solution)/shard_map/ppermute | solution.py:155
  62.7 4.7 %collective-permute-start.9 = (bf16[4,6,16,256]{3,2,1,0:T(8,128)(2,1)}, bf16[4,6,16,256]{3,2,1,0:T(8,128)(2,1)S(1)}, u32[]{:S(2)}, u32[]{:S(2)}) collective-permute-start(bf16[4,6,16,256]{3,2,1,0:T(8,128)(2,1)} %get-tuple-element.38), channel_id=1, source_target_pairs={{0,1},{1,2},{2,3},{4,5},{5,6},{6,7},{8,9},{9,10},{10,11},{12,13},{... | collective-permute-start | bytes 589832 | tf_op jit(solution)/shard_map/ppermute | solution.py:154
  68.2 18.4 %all-to-all-start.1 = ((f16[16,80,128]{2,1,0:T(8,128)(2,1)}), f16[16,80,128]{2,1,0:T(8,128)(2,1)}, u32[]{:S(2)}, u32[]{:S(2)}) async-start(f16[16,80,128]{2,1,0:T(8,128)(2,1)} %broadcast_in_dim.2), calls=%async_computation.1 | async-start | bytes 655360 | tf_op jit(solution)/shard_map/all_to_all | solution.py:245
  77.0 5.2 %copy-start.8 = (bf16[6,160,256]{2,1,0:T(8,128)(2,1)S(1)}, bf16[6,160,256]{2,1,0:T(8,128)(2,1)}, u32[]{:S(2)}) copy-start(bf16[6,160,256]{2,1,0:T(8,128)(2,1)} %copy-done.7) | copy-start | bytes 1474564
  80.2 8.1 %collective-permute-start.11 = (bf16[6,160,128]{2,1,0:T(8,128)(2,1)S(1)}, bf16[6,160,128]{2,1,0:T(8,128)(2,1)S(1)}, u32[]{:S(2)}, u32[]{:S(2)}) collective-permute-start(bf16[6,160,128]{2,1,0:T(8,128)(2,1)S(1)} %get-tuple-element.47), channel_id=1, source_target_pairs={{0,4},{4,0},{8,12},{12,8},{16,20},{20,16},{24,28},{28,24},{1,5},{5... | collective-permute-start | bytes 737288 | tf_op jit(solution)/shard_map/ppermute | solution.py:256
  86.6 2.7 %collective-permute-start.13 = (f16[16,80,128]{2,1,0:T(8,128)(2,1)}, f16[16,80,128]{2,1,0:T(8,128)(2,1)S(1)}, u32[]{:S(2)}, u32[]{:S(2)}) collective-permute-start(f16[16,80,128]{2,1,0:T(8,128)(2,1)} %all-to-all-done.1), channel_id=1, source_target_pairs={{0,1},{1,0},{2,3},{3,2},{4,5},{5,4},{6,7},{7,6},{8,9},{9,8},{10,11... | collective-permute-start | bytes 983048 | tf_op jit(solution)/shard_map/ppermute | solution.py:246

commit v10 on v8

--- a/solution.py
+++ b/solution.py
@@ -85,12 +85,20 @@
     out[pl.ds(chunk, deep - chunk), :] = jnp.broadcast_to(highest, (deep - chunk, cout))
 
 
-def kernel_back(par, w, d_own, d_par, d_near, d_far, left, right, out_own, out_par, ext, shifted):
+def kernel_back(par, d_own, d_par, d_near, d_far, w, left, right, out_own, out_par, ext, shifted, sems):
     odd = par[0]
     half, width, cout = d_own.shape
     cin = w.shape[2]
     pixels = half * width
-    gather_map(odd, (d_own, d_par, d_near, d_far), left, right, ext)
+    moves = []
+    for place, (block, slot) in enumerate(zip((d_own, d_par, d_near, d_far), slots(odd))):
+        move = pltpu.make_async_copy(block, ext.at[slot, :, pl.ds(STRIP, width), :], sems.at[place])
+        move.start()
+        moves.append(move)
+        ext[slot, :, pl.ds(0, STRIP), :] = left[place]
+        ext[slot, :, pl.ds(STRIP + width, STRIP), :] = right[place]
+    for move in moves:
+        move.wait()
     shift_columns(ext, shifted, width)
     own, partner = slots(odd)[:2]
     for out, slot in ((out_own, own), (out_par, partner)):
@@ -126,18 +134,32 @@
         out[...] = result.astype(jnp.bfloat16)
 
 
-def call(kernel, operands, outs, scratch, flops):
+def call(kernel, operands, outs, scratch, flops, outside=0):
     whole = pl.BlockSpec(memory_space=VMEM)
     size = sum(x.size * x.dtype.itemsize for x in operands) + sum(math.prod(o.shape) * o.dtype.itemsize for o in outs)
     return pl.pallas_call(
         kernel,
         out_shape=outs,
-        in_specs=[pl.BlockSpec(memory_space=pltpu.SMEM)] + [whole] * (len(operands) - 1),
+        in_specs=[pl.BlockSpec(memory_space=pltpu.SMEM)] + [pl.BlockSpec(memory_space=pl.ANY)] * outside
+        + [whole] * (len(operands) - 1 - outside),
         out_specs=[whole] * len(outs),
         scratch_shapes=scratch,
         compiler_params=pltpu.CompilerParams(vmem_limit_bytes=12 * 1024 * 1024),
         cost_estimate=pl.CostEstimate(flops=flops, bytes_accessed=size if flops else 0, transcendentals=0),
     )(*operands)
+
+
+def kernel_edges(par, *refs):
+    blocks, (tails, heads) = (refs[:-2], refs[-2:])
+    for place, block in enumerate(blocks):
+        tails[place] = block[:, pl.ds(block.shape[1] - STRIP, STRIP), :]
+        heads[place] = block[:, pl.ds(0, STRIP), :]
+
+
+def packed(par, blocks, flops):
+    half, _, depth = blocks[0].shape
+    strip = jax.ShapeDtypeStruct((len(blocks), half, STRIP, depth), jnp.bfloat16)
+    return call(kernel_edges, (par,) + blocks, [strip, strip], [], flops)
 
 
 def edges(blocks):
@@ -190,16 +212,16 @@
     f_own, f_give = (pick(features, odd), pick(features, 1 - odd))
     d_par = lax.ppermute(d_give, "rows", swap)
     d_near = lax.ppermute(d_own, "rows", near)
-    f_give, d_par = fence((f_give, d_par))
     f_par = lax.ppermute(f_give, "rows", swap)
+    f_first, d_par, d_near = fence((f_own, d_par, d_near))
     d_far = lax.ppermute(d_par, "rows", far)
-    f_first, d_far = fence((f_own, d_far))
     f_near = lax.ppermute(f_first, "rows", near)
     f_far = lax.ppermute(f_par, "rows", far)
     d_blocks = (d_own, d_par, d_near, d_far)
+    f_own, f_near = fence((f_own, f_near))
+    d_left, d_right = exchanged(*packed(par, d_blocks, flops), cols)
+
     f_blocks = (f_own, f_par, f_near, f_far)
-    d_left, d_right = exchanged(*edges(d_blocks), cols)
-
     part = jax.ShapeDtypeStruct((share, cout), jnp.float32)
     d_maps = [VMEM((4, half, wide, cout), jnp.bfloat16), VMEM((4, half, width, 3 * cout), jnp.bfloat16)]
     keep, give = call(
@@ -225,7 +247,12 @@
     d_left, _ = fence((d_left, scaled))
     half_grad = jax.ShapeDtypeStruct((half, width, cin), jnp.bfloat16)
     g_own, g_par = call(
-        kernel_back, (par, weight) + d_blocks + (d_left, d_right), [half_grad, half_grad], d_maps, 0
+        kernel_back,
+        (par,) + d_blocks + (weight, d_left, d_right),
+        [half_grad, half_grad],
+        d_maps + [pltpu.SemaphoreType.DMA((4,))],
+        0,
+        outside=4,
     )
     g_other = lax.ppermute(g_par, "rows", swap)
     got, g_par = fence((got, g_par))
@@ -240,7 +267,7 @@
         0,
     )
     mine = mine.astype(jnp.float16)
-    f_left, copies = fence((f_left, jnp.broadcast_to(mine[None], (chips, deep, cout))))
+    f_left, f_right, copies = fence((f_left, f_right, jnp.broadcast_to(mine[None], (chips, deep, cout))))
     spread = lax.all_to_all(copies, CHIPS, 0, 0)
     other = lax.ppermute(spread, "core", other_core)
 

time: 95.1 us -> 93.5 us (0.983); the launches traced: 93.2 us -> 92.7 us
  local copies, waits for them, and re-layouts: 8.98 us -> 6.69 us
    ppermute x1, starting transfers between devices: 4.35 us -> 0.01 us  [body(): other = lax.ppermute(spread, 'core', other_core)]
    ppermute x1, waiting for transfers between devices: 3.56 us -> 0.01 us  [body(): f_par = lax.ppermute(f_give, 'rows', swap)]
    all_to_all x1, waiting for transfers between devices: 0.01 us -> 3.45 us  [body(): spread = lax.all_to_all(copies, CHIPS, 0, 0)]
    ppermute x1, starting transfers between devices: 0.07 us -> 2.77 us  [body(): f_par = lax.ppermute(f_give, 'rows', swap)]
    all_to_all x1, starting transfers between devices: 5.98 us -> 8.58 us  [body(): got = lax.all_to_all(scaled, CHIPS, 0, 0)]
    ppermute x1, waiting for transfers between devices: 0.01 us -> 2.51 us  [body(): d_near = lax.ppermute(d_own, 'rows', near)]
    ppermute x1, waiting for transfers between devices: 0.01 us -> 2.33 us  [body(): o_other = lax.ppermute(o_par, 'rows', swap)]
    another operation x8 -> x3, local copies, waits for them, and re-layouts: 1.65 us -> 0.03 us  [edges(): heads = jnp.stack([x[:, :STRIP] for x in blocks])]
  transfers between devices with their start and end apart: 16 -> 16, of which waited for: 8 -> 8; matrix products, arithmetic and copies ran while one was open for 8% -> 7% of each run, Pallas kernels for 11% -> 12%
where the time goes in v10:
time: 93.5 us; the launch traced here: 92.7 us
  starting transfers between devices  42.8 us (46%)
  waiting for transfers between devices  21.7 us (23%)
  Pallas kernels  11.8 us (13%)
  other arithmetic  8.69 us (9%)
  local copies, waits for them, and re-layouts  6.69 us (7%)
  between operations  0.98 us (1%)
    pallas_call x6, Pallas kernels, call(): pl.pallas_call(kernel, out_shape=outs, in_specs=[pl.BlockSpec(memory_spac...  11.8 us
    all_to_all x1, starting transfers between devices, body(): got = lax.all_to_all(scaled, CHIPS, 0, 0)  8.58 us
    all_to_all x1, starting transfers between devices, body(): spread = lax.all_to_all(copies, CHIPS, 0, 0)  8.11 us
    unnamed x24, local copies, waits for them, and re-layouts  4.62 us
    ppermute x1, starting transfers between devices, body(): f_far = lax.ppermute(f_par, 'rows', far)  4.42 us
    ppermute x1, waiting for transfers between devices, body(): f_far = lax.ppermute(f_par, 'rows', far)  4.11 us
    ppermute x1, starting transfers between devices, body(): d_far = lax.ppermute(d_par, 'rows', far)  3.48 us
    all_to_all x1, waiting for transfers between devices, body(): spread = lax.all_to_all(copies, CHIPS, 0, 0)  3.45 us
  transfers between devices with their start and end apart: 16, of which 8 were waited for; matrix products, arithmetic and copies ran while one was open for 7% of the time, Pallas kernels for 12%

profile of v10, /device:TPU:0, one launch (start us, length us, event | category | flops | bytes accessed | tf_op | source)
XLA Modules:
  0.0 92.7 jit_solution(13544632039098787852)
XLA Ops:
  0.7 1.2 %constant_dynamic-slice_fusion.1 = (bf16[6,160,128]{2,1,0:T(8,128)(2,1)S(1)}, bf16[6,160,128]{2,1,0:T(8,128)(2,1)S(1)}) fusion(bf16[12,160,128]{2,1,0:T(8,128)(2,1)} %param.5, s32[]{:T(128)S(6)} %select_n.53, s32[]{:T(128)S(6)} %select_n.54), kind=kLoop, calls=%fused_computation.22 | loop fusion | bytes 983048 | tf_op jit(solution)/shard_map/dynamic_slice | solution.py:203
  1.8 3.0 %collective-permute-start = (bf16[6,160,128]{2,1,0:T(8,128)(2,1)S(1)}, bf16[6,160,128]{2,1,0:T(8,128)(2,1)S(1)}, u32[]{:S(2)}, u32[]{:S(2)}) collective-permute-start(bf16[6,160,128]{2,1,0:T(8,128)(2,1)S(1)} %get-tuple-element.68), channel_id=1, source_target_pairs={{0,4},{4,0},{8,12},{12,8},{16,20},{20,16},{24,28},{28,24},{1,5},{5... | collective-permute-start | bytes 737288 | tf_op jit(solution)/shard_map/ppermute | solution.py:213
  4.9 1.3 %collective-permute-start.1 = (bf16[6,160,128]{2,1,0:T(8,128)(2,1)S(1)}, bf16[6,160,128]{2,1,0:T(8,128)(2,1)S(1)}, u32[]{:S(2)}, u32[]{:S(2)}) collective-permute-start(bf16[6,160,128]{2,1,0:T(8,128)(2,1)S(1)} %get-tuple-element.67.refs_0_.d_own), channel_id=1, source_target_pairs={{4,12},{8,0},{12,20},{16,8},{20,28},{24,16},{5,13},{9,1},{13,21},{... | collective-permute-start | bytes 737288 | tf_op jit(solution)/shard_map/ppermute | solution.py:214
  6.2 0.1 constant_dynamic-slice_fusion
  6.3 2.8 %collective-permute-start.3 = (bf16[6,160,256]{2,1,0:T(8,128)(2,1)S(1)}, bf16[6,160,256]{2,1,0:T(8,128)(2,1)S(1)}, u32[]{:S(2)}, u32[]{:S(2)}) collective-permute-start(bf16[6,160,256]{2,1,0:T(8,128)(2,1)S(1)} %get-tuple-element.53), channel_id=1, source_target_pairs={{0,4},{4,0},{8,12},{12,8},{16,20},{20,16},{24,28},{28,24},{1,5},{5... | collective-permute-start | bytes 1474568 | tf_op jit(solution)/shard_map/ppermute | solution.py:215
  9.0 2.6 %collective-permute-done.refs_1_.d_par = bf16[6,160,128]{2,1,0:T(8,128)(2,1)S(1)} collective-permute-done((bf16[6,160,128]{2,1,0:T(8,128)(2,1)S(1)}, bf16[6,160,128]{2,1,0:T(8,128)(2,1)S(1)}, u32[]{:S(2)}, u32[]{:S(2)}) %collective-permute-start) | collective-permute-done | bytes 245792 | tf_op jit(solution)/shard_map/ppermute | solution.py:213
  11.7 2.5 %collective-permute-done.1.refs_2_.d_near = bf16[6,160,128]{2,1,0:T(8,128)(2,1)S(1)} collective-permute-done((bf16[6,160,128]{2,1,0:T(8,128)(2,1)S(1)}, bf16[6,160,128]{2,1,0:T(8,128)(2,1)S(1)}, u32[]{:S(2)}, u32[]{:S(2)}) %collective-permute-start.1) | collective-permute-done | bytes 245792 | tf_op jit(solution)/shard_map/ppermute | solution.py:214
  14.2 3.5 %collective-permute-start.5 = (bf16[6,160,128]{2,1,0:T(8,128)(2,1)S(1)}, bf16[6,160,128]{2,1,0:T(8,128)(2,1)S(1)}, u32[]{:S(2)}, u32[]{:S(2)}) collective-permute-start(bf16[6,160,128]{2,1,0:T(8,128)(2,1)S(1)} %collective-permute-done.refs_1_.d_par), channel_id=1, source_target_pairs={{12,4},{0,8},{20,12},{8,16},{28,20},{16,24},{13,5},{1,9},{21,13},{... | collective-permute-start | bytes 737288 | tf_op jit(solution)/shard_map/ppermute | solution.py:217
  17.7 1.3 %collective-permute-start.2 = (bf16[6,160,256]{2,1,0:T(8,128)(2,1)S(1)}, bf16[6,160,256]{2,1,0:T(8,128)(2,1)S(1)}, u32[]{:S(2)}, u32[]{:S(2)}) collective-permute-start(bf16[6,160,256]{2,1,0:T(8,128)(2,1)S(1)} %get-tuple-element.28.f_own), channel_id=1, source_target_pairs={{4,12},{8,0},{12,20},{16,8},{20,28},{24,16},{5,13},{9,1},{13,21},{... | collective-permute-start | bytes 1474568 | tf_op jit(solution)/shard_map/ppermute | solution.py:218
  19.0 0.1 pad_add_fusion.par
  19.0 2.6 %collective-permute-done.5.refs_3_.d_far = bf16[6,160,128]{2,1,0:T(8,128)(2,1)S(1)} collective-permute-done((bf16[6,160,128]{2,1,0:T(8,128)(2,1)S(1)}, bf16[6,160,128]{2,1,0:T(8,128)(2,1)S(1)}, u32[]{:S(2)}, u32[]{:S(2)}) %collective-permute-start.5) | collective-permute-done | bytes 245792 | tf_op jit(solution)/shard_map/ppermute | solution.py:217
  21.7 0.6 shard_map.58
  22.2 1.3 %collective-permute-start.6 = (bf16[4,6,16,128]{3,2,1,0:T(8,128)(2,1)S(1)}, bf16[4,6,16,128]{3,2,1,0:T(8,128)(2,1)S(1)}, u32[]{:S(2)}, u32[]{:S(2)}) collective-permute-start(bf16[4,6,16,128]{3,2,1,0:T(8,128)(2,1)S(1)} %get-tuple-element.32), channel_id=1, source_target_pairs={{0,1},{1,2},{2,3},{4,5},{5,6},{6,7},{8,9},{9,10},{10,11},{12,13},{... | collective-permute-start | bytes 294920 | tf_op jit(solution)/shard_map/ppermute | solution.py:173
  23.5 1.3 %collective-permute-start.7 = (bf16[4,6,16,128]{3,2,1,0:T(8,128)(2,1)S(1)}, bf16[4,6,16,128]{3,2,1,0:T(8,128)(2,1)S(1)}, u32[]{:S(2)}, u32[]{:S(2)}) collective-permute-start(bf16[4,6,16,128]{3,2,1,0:T(8,128)(2,1)S(1)} %get-tuple-element.33), channel_id=1, source_target_pairs={{1,0},{2,1},{3,2},{5,4},{6,5},{7,6},{9,8},{10,9},{11,10},{13,12},{... | collective-permute-start | bytes 294920 | tf_op jit(solution)/shard_map/ppermute | solution.py:174
  24.9 4.4 %collective-permute-start.4 = (bf16[6,160,256]{2,1,0:T(8,128)(2,1)S(1)}, bf16[6,160,256]{2,1,0:T(8,128)(2,1)S(1)}, u32[]{:S(2)}, u32[]{:S(2)}) collective-permute-start(bf16[6,160,256]{2,1,0:T(8,128)(2,1)S(1)} %collective-permute-done.3.f_par), channel_id=1, source_target_pairs={{12,4},{0,8},{20,12},{8,16},{28,20},{16,24},{13,5},{1,9},{21,13},{... | collective-permute-start | bytes 1474568 | tf_op jit(solution)/shard_map/ppermute | solution.py:219
  29.3 1.8 %collective-permute-done.2.f_near = bf16[6,160,256]{2,1,0:T(8,128)(2,1)S(1)} collective-permute-done((bf16[6,160,256]{2,1,0:T(8,128)(2,1)S(1)}, bf16[6,160,256]{2,1,0:T(8,128)(2,1)S(1)}, u32[]{:S(2)}, u32[]{:S(2)}) %collective-permute-start.2) | collective-permute-done | bytes 491552 | tf_op jit(solution)/shard_map/ppermute | solution.py:218
  31.1 2.8 %shard_map.59 = (f32[1152,128]{1,0:T(8,128)S(1)}, f32[1152,128]{1,0:T(8,128)S(1)}) custom-call(s32[2]{0:T(128)S(1)} %pad_add_fusion.par, bf16[6,160,256]{2,1,0:T(8,128)(2,1)S(1)} %get-tuple-element.28.f_own, bf16[6,160,256]{2,1,0:T(8,128)(2,1)S(1)} %collective-permute-done.3.f_par, bf16[6,160,128]{2,1,0:T(8,128)(2,1)S(1)} %get-tuple-element.67.refs_0_.d_own, ...), custom_call_target="tpu_custom_call" | custom-call | flops 33973862400 | bytes 3342344 | tf_op jit(solution)/shard_map/pallas_call | solution.py:140
  33.9 0.9 collective-permute-start.8
  34.8 4.1 %collective-permute-done.4.f_far = bf16[6,160,256]{2,1,0:T(8,128)(2,1)S(1)} collective-permute-done((bf16[6,160,256]{2,1,0:T(8,128)(2,1)S(1)}, bf16[6,160,256]{2,1,0:T(8,128)(2,1)S(1)}, u32[]{:S(2)}, u32[]{:S(2)}) %collective-permute-start.4) | collective-permute-done | bytes 491552 | tf_op jit(solution)/shard_map/ppermute | solution.py:219
  38.9 0.7 pad_maximum_fusion.4
  39.6 0.7 pad_maximum_fusion.3
  40.3 0.7 shard_map.60
  41.1 0.8 convert_element_type.21
  41.8 8.6 %all-to-all-start = ((f16[16,80,128]{2,1,0:T(8,128)(2,1)}), f16[16,80,128]{2,1,0:T(8,128)(2,1)}, u32[]{:S(2)}, u32[]{:S(2)}) async-start(f16[16,80,128]{2,1,0:T(8,128)(2,1)} %convert_element_type.21), calls=%async_computation | async-start | bytes 655360 | tf_op jit(solution)/shard_map/all_to_all | solution.py:246
  50.4 0.9 %copy-done.2 = bf16[6,160,128]{2,1,0:T(8,128)(2,1)S(1)} copy-done((bf16[6,160,128]{2,1,0:T(8,128)(2,1)S(1)}, bf16[6,160,128]{2,1,0:T(8,128)(2,1)}, u32[]{:S(2)}) %copy-start.2) | copy-done | bytes 245784
  51.4 0.9 %copy-done.4 = bf16[6,160,128]{2,1,0:T(8,128)(2,1)S(1)} copy-done((bf16[6,160,128]{2,1,0:T(8,128)(2,1)S(1)}, bf16[6,160,128]{2,1,0:T(8,128)(2,1)}, u32[]{:S(2)}) %copy-start.4) | copy-done | bytes 245784
  52.3 0.9 copy-done.8
  53.2 0.9 copy-done.10
  54.1 3.8 %shard_map.61 = (bf16[6,160,256]{2,1,0:T(8,128)(2,1)S(1)}, bf16[6,160,256]{2,1,0:T(8,128)(2,1)}) custom-call(s32[2]{0:T(128)S(1)} %pad_add_fusion.par, bf16[6,160,128]{2,1,0:T(8,128)(2,1)S(1)} %get-tuple-element.67.refs_0_.d_own, bf16[6,160,128]{2,1,0:T(8,128)(2,1)S(1)} %collective-permute-done.refs_1_.d_par, bf16[6,160,128]{2,1,0:T(8,128)(2,1)S(1)} %copy-done.2, ...), custom_call_target="tpu_custom_call" | custom-call | tf_op jit(solution)/shard_map/pallas_call | solution.py:140
  57.9 1.9 %collective-permute-start.12 = (bf16[6,160,256]{2,1,0:T(8,128)(2,1)}, bf16[6,160,256]{2,1,0:T(8,128)(2,1)}, u32[]{:S(2)}, u32[]{:S(2)}) collective-permute-start(bf16[6,160,256]{2,1,0:T(8,128)(2,1)} %get-tuple-element.43), channel_id=1, source_target_pairs={{0,4},{4,0},{8,12},{12,8},{16,20},{20,16},{24,28},{28,24},{1,5},{5... | collective-permute-start | bytes 1474568 | tf_op jit(solution)/shard_map/ppermute | solution.py:257
  59.8 1.3 %collective-permute-start.9 = (bf16[4,6,16,256]{3,2,1,0:T(8,128)(2,1)}, bf16[4,6,16,256]{3,2,1,0:T(8,128)(2,1)S(1)}, u32[]{:S(2)}, u32[]{:S(2)}) collective-permute-start(bf16[4,6,16,256]{3,2,1,0:T(8,128)(2,1)} %pad_maximum_fusion.3), channel_id=1, source_target_pairs={{0,1},{1,2},{2,3},{4,5},{5,6},{6,7},{8,9},{9,10},{10,11},{12,13},{... | collective-permute-start | bytes 589832 | tf_op jit(solution)/shard_map/ppermute | solution.py:173
  61.1 1.3 %collective-permute-start.10 = (bf16[4,6,16,256]{3,2,1,0:T(8,128)(2,1)}, bf16[4,6,16,256]{3,2,1,0:T(8,128)(2,1)S(1)}, u32[]{:S(2)}, u32[]{:S(2)}) collective-permute-start(bf16[4,6,16,256]{3,2,1,0:T(8,128)(2,1)} %pad_maximum_fusion.4), channel_id=1, source_target_pairs={{1,0},{2,1},{3,2},{5,4},{6,5},{7,6},{9,8},{10,9},{11,10},{13,12},{... | collective-permute-start | bytes 589832 | tf_op jit(solution)/shard_map/ppermute | solution.py:174
  62.5 1.0 %convert_element_type.22.got = f32[16,80,128]{2,1,0:T(8,128)S(1)} convert(f16[16,80,128]{2,1,0:T(8,128)(2,1)} %all-to-all-done) | non-fusion elementwise | flops 163840 | bytes 983040 | tf_op jit(solution)/shard_map/convert_element_type | solution.py:264
  63.5 0.6 shard_map.62
  64.1 2.3 %collective-permute-done.10.right = bf16[4,6,16,256]{3,2,1,0:T(8,128)(2,1)S(1)} collective-permute-done((bf16[4,6,16,256]{3,2,1,0:T(8,128)(2,1)}, bf16[4,6,16,256]{3,2,1,0:T(8,128)(2,1)S(1)}, u32[]{:S(2)}, u32[]{:S(2)}) %collective-permute-start.10) | collective-permute-done | bytes 196640 | tf_op jit(solution)/shard_map/ppermute | solution.py:174
  66.4 0.8 broadcast_in_dim.2
  67.2 8.1 %all-to-all-start.1 = ((f16[16,80,128]{2,1,0:T(8,128)(2,1)}), f16[16,80,128]{2,1,0:T(8,128)(2,1)}, u32[]{:S(2)}, u32[]{:S(2)}) async-start(f16[16,80,128]{2,1,0:T(8,128)(2,1)} %broadcast_in_dim.2), calls=%async_computation.1 | async-start | bytes 655360 | tf_op jit(solution)/shard_map/all_to_all | solution.py:271
  75.3 0.9 copy-done.6
  76.2 3.4 %shard_map.63 = (bf16[6,160,128]{2,1,0:T(8,128)(2,1)S(1)}, bf16[6,160,128]{2,1,0:T(8,128)(2,1)}) custom-call(s32[2]{0:T(128)S(1)} %pad_add_fusion.par, bf16[3,3,256,128]{3,2,1,0:T(8,128)(2,1)S(1)} %copy-done, bf16[6,160,256]{2,1,0:T(8,128)(2,1)S(1)} %get-tuple-element.28.f_own, bf16[6,160,256]{2,1,0:T(8,128)(2,1)S(1)} %collective-permute-done.3.f_par, ...), custom_call_target="tpu_custom_call" | custom-call | tf_op jit(solution)/shard_map/pallas_call | solution.py:140
  79.6 1.9 %collective-permute-start.11 = (bf16[6,160,128]{2,1,0:T(8,128)(2,1)}, bf16[6,160,128]{2,1,0:T(8,128)(2,1)S(1)}, u32[]{:S(2)}, u32[]{:S(2)}) collective-permute-start(bf16[6,160,128]{2,1,0:T(8,128)(2,1)} %get-tuple-element.47), channel_id=1, source_target_pairs={{0,4},{4,0},{8,12},{12,8},{16,20},{20,16},{24,28},{28,24},{1,5},{5... | collective-permute-start | bytes 737288 | tf_op jit(solution)/shard_map/ppermute | solution.py:282
  81.5 1.2 %broadcast_select_fusion.1 = (bf16[6,160,256]{2,1,0:T(8,128)(2,1)S(1)}, bf16[6,160,256]{2,1,0:T(8,128)(2,1)S(1)}) fusion(bf16[6,160,256]{2,1,0:T(8,128)(2,1)} %collective-permute-done.12, bf16[6,160,256]{2,1,0:T(8,128)(2,1)S(1)} %get-tuple-element.49, pred[]{:T(512)S(6)} %eq.6), kind=kLoop, calls=%fused_computation.6 | loop fusion | flops 491520 | bytes 1966081 | tf_op jit(solution)/shard_map/jit(_where)/select_n | solution.py:179
  82.6 1.0 %pad_maximum_fusion.1 = bf16[12,160,256]{2,1,0:T(8,128)(2,1)} fusion(bf16[6,160,256]{2,1,0:T(8,128)(2,1)S(1)} %get-tuple-element.52, bf16[6,160,256]{2,1,0:T(8,128)(2,1)S(1)} %get-tuple-element.51), kind=kLoop, calls=%fused_computation.1 | loop fusion | flops 491520 | bytes 1966080 | tf_op jit(solution)/shard_map/concatenate | solution.py:181
  83.7 3.5 %all-to-all-done.1 = f16[16,80,128]{2,1,0:T(8,128)(2,1)} async-done(((f16[16,80,128]{2,1,0:T(8,128)(2,1)}), f16[16,80,128]{2,1,0:T(8,128)(2,1)}, u32[]{:S(2)}, u32[]{:S(2)}) %all-to-all-start.1) | async-done | bytes 327712 | tf_op jit(solution)/shard_map/all_to_all | solution.py:271
  87.1 2.3 %collective-permute-done.11 = bf16[6,160,128]{2,1,0:T(8,128)(2,1)S(1)} collective-permute-done((bf16[6,160,128]{2,1,0:T(8,128)(2,1)}, bf16[6,160,128]{2,1,0:T(8,128)(2,1)S(1)}, u32[]{:S(2)}, u32[]{:S(2)}) %collective-permute-start.11) | collective-permute-done | bytes 245792 | tf_op jit(solution)/shard_map/ppermute | solution.py:282
  89.5 0.1 broadcast_select_fusion.5
  89.5 0.8 pad_maximum_fusion.2
  90.3 1.1 %broadcast_select_fusion.3 = (f16[16,80,128]{2,1,0:T(8,128)(2,1)S(1)}, f16[16,80,128]{2,1,0:T(8,128)(2,1)S(1)}) fusion(f16[16,80,128]{2,1,0:T(8,128)(2,1)} %all-to-all-done.1, f16[16,80,128]{2,1,0:T(8,128)(2,1)S(1)} %collective-permute-done.13, pred[]{:T(512)S(6)} %eq.7), kind=kLoop, calls=%fused_computation.8 | loop fusion | flops 327680 | bytes 1310721 | tf_op jit(solution)/shard_map/jit(_where)/select_n | solution.py:287
  91.6 1.1 %pad_maximum_fusion = f32[2304,128]{1,0:T(8,128)} fusion(f32[1152,128]{1,0:T(8,128)S(1)} %bitcast.25, f32[1152,128]{1,0:T(8,128)S(1)} %bitcast.26), kind=kLoop, calls=%fused_computation | loop fusion | flops 294912 | bytes 2359296 | tf_op jit(solution)/shard_map/concatenate | solution.py:291
  (36 shorter events, 0.2 us)
Async XLA Ops:
  0.6 5.5 %copy-start.11 = (bf16[12,160,256]{2,1,0:T(8,128)(2,1)S(1)}, bf16[12,160,256]{2,1,0:T(8,128)(2,1)}, u32[]{:S(2)}) copy-start(bf16[12,160,256]{2,1,0:T(8,128)(2,1)} %param.3) | copy-start | bytes 2949124
  1.8 9.8 %collective-permute-start = (bf16[6,160,128]{2,1,0:T(8,128)(2,1)S(1)}, bf16[6,160,128]{2,1,0:T(8,128)(2,1)S(1)}, u32[]{:S(2)}, u32[]{:S(2)}) collective-permute-start(bf16[6,160,128]{2,1,0:T(8,128)(2,1)S(1)} %get-tuple-element.68), channel_id=1, source_target_pairs={{0,4},{4,0},{8,12},{12,8},{16,20},{20,16},{24,28},{28,24},{1,5},{5... | collective-permute-start | bytes 737288 | tf_op jit(solution)/shard_map/ppermute | solution.py:213
  4.9 9.3 %collective-permute-start.1 = (bf16[6,160,128]{2,1,0:T(8,128)(2,1)S(1)}, bf16[6,160,128]{2,1,0:T(8,128)(2,1)S(1)}, u32[]{:S(2)}, u32[]{:S(2)}) collective-permute-start(bf16[6,160,128]{2,1,0:T(8,128)(2,1)S(1)} %get-tuple-element.67.refs_0_.d_own), channel_id=1, source_target_pairs={{4,12},{8,0},{12,20},{16,8},{20,28},{24,16},{5,13},{9,1},{13,21},{... | collective-permute-start | bytes 737288 | tf_op jit(solution)/shard_map/ppermute | solution.py:214
  6.3 18.6 %collective-permute-start.3 = (bf16[6,160,256]{2,1,0:T(8,128)(2,1)S(1)}, bf16[6,160,256]{2,1,0:T(8,128)(2,1)S(1)}, u32[]{:S(2)}, u32[]{:S(2)}) collective-permute-start(bf16[6,160,256]{2,1,0:T(8,128)(2,1)S(1)} %get-tuple-element.53), channel_id=1, source_target_pairs={{0,4},{4,0},{8,12},{12,8},{16,20},{20,16},{24,28},{28,24},{1,5},{5... | collective-permute-start | bytes 1474568 | tf_op jit(solution)/shard_map/ppermute | solution.py:215
  14.2 16.9 %copy-start.1 = (bf16[6,160,128]{2,1,0:T(8,128)(2,1)}, bf16[6,160,128]{2,1,0:T(8,128)(2,1)S(1)}, u32[]{:S(2)}) copy-start(bf16[6,160,128]{2,1,0:T(8,128)(2,1)S(1)} %collective-permute-done.1.refs_2_.d_near) | copy-start | bytes 737284
  14.2 7.5 %collective-permute-start.5 = (bf16[6,160,128]{2,1,0:T(8,128)(2,1)S(1)}, bf16[6,160,128]{2,1,0:T(8,128)(2,1)S(1)}, u32[]{:S(2)}, u32[]{:S(2)}) collective-permute-start(bf16[6,160,128]{2,1,0:T(8,128)(2,1)S(1)} %collective-permute-done.refs_1_.d_par), channel_id=1, source_target_pairs={{12,4},{0,8},{20,12},{8,16},{28,20},{16,24},{13,5},{1,9},{21,13},{... | collective-permute-start | bytes 737288 | tf_op jit(solution)/shard_map/ppermute | solution.py:217
  17.7 13.4 %collective-permute-start.2 = (bf16[6,160,256]{2,1,0:T(8,128)(2,1)S(1)}, bf16[6,160,256]{2,1,0:T(8,128)(2,1)S(1)}, u32[]{:S(2)}, u32[]{:S(2)}) collective-permute-start(bf16[6,160,256]{2,1,0:T(8,128)(2,1)S(1)} %get-tuple-element.28.f_own), channel_id=1, source_target_pairs={{4,12},{8,0},{12,20},{16,8},{20,28},{24,16},{5,13},{9,1},{13,21},{... | collective-permute-start | bytes 1474568 | tf_op jit(solution)/shard_map/ppermute | solution.py:218
  21.7 9.4 %copy-start.3 = (bf16[6,160,128]{2,1,0:T(8,128)(2,1)}, bf16[6,160,128]{2,1,0:T(8,128)(2,1)S(1)}, u32[]{:S(2)}) copy-start(bf16[6,160,128]{2,1,0:T(8,128)(2,1)S(1)} %collective-permute-done.5.refs_3_.d_far) | copy-start | bytes 737284
  22.2 8.8 %collective-permute-start.6 = (bf16[4,6,16,128]{3,2,1,0:T(8,128)(2,1)S(1)}, bf16[4,6,16,128]{3,2,1,0:T(8,128)(2,1)S(1)}, u32[]{:S(2)}, u32[]{:S(2)}) collective-permute-start(bf16[4,6,16,128]{3,2,1,0:T(8,128)(2,1)S(1)} %get-tuple-element.32), channel_id=1, source_target_pairs={{0,1},{1,2},{2,3},{4,5},{5,6},{6,7},{8,9},{9,10},{10,11},{12,13},{... | collective-permute-start | bytes 294920 | tf_op jit(solution)/shard_map/ppermute | solution.py:173
  23.5 7.5 %collective-permute-start.7 = (bf16[4,6,16,128]{3,2,1,0:T(8,128)(2,1)S(1)}, bf16[4,6,16,128]{3,2,1,0:T(8,128)(2,1)S(1)}, u32[]{:S(2)}, u32[]{:S(2)}) collective-permute-start(bf16[4,6,16,128]{3,2,1,0:T(8,128)(2,1)S(1)} %get-tuple-element.33), channel_id=1, source_target_pairs={{1,0},{2,1},{3,2},{5,4},{6,5},{7,6},{9,8},{10,9},{11,10},{13,12},{... | collective-permute-start | bytes 294920 | tf_op jit(solution)/shard_map/ppermute | solution.py:174
  24.9 14.0 %collective-permute-start.4 = (bf16[6,160,256]{2,1,0:T(8,128)(2,1)S(1)}, bf16[6,160,256]{2,1,0:T(8,128)(2,1)S(1)}, u32[]{:S(2)}, u32[]{:S(2)}) collective-permute-start(bf16[6,160,256]{2,1,0:T(8,128)(2,1)S(1)} %collective-permute-done.3.f_par), channel_id=1, source_target_pairs={{12,4},{0,8},{20,12},{8,16},{28,20},{16,24},{13,5},{1,9},{21,13},{... | collective-permute-start | bytes 1474568 | tf_op jit(solution)/shard_map/ppermute | solution.py:219
  31.1 2.8 %copy-start.7 = (bf16[4,6,16,128]{3,2,1,0:T(8,128)(2,1)}, bf16[4,6,16,128]{3,2,1,0:T(8,128)(2,1)S(1)}, u32[]{:S(2)}) copy-start(bf16[4,6,16,128]{3,2,1,0:T(8,128)(2,1)S(1)} %collective-permute-done.6.left) | copy-start | bytes 294916
  31.1 2.8 %copy-start.9 = (bf16[4,6,16,128]{3,2,1,0:T(8,128)(2,1)}, bf16[4,6,16,128]{3,2,1,0:T(8,128)(2,1)S(1)}, u32[]{:S(2)}) copy-start(bf16[4,6,16,128]{3,2,1,0:T(8,128)(2,1)S(1)} %collective-permute-done.7.right) | copy-start | bytes 294916
  33.9 6.4 %collective-permute-start.8 = (f32[1152,128]{1,0:T(8,128)S(1)}, f32[1152,128]{1,0:T(8,128)S(1)}, u32[]{:S(2)}, u32[]{:S(2)}) collective-permute-start(f32[1152,128]{1,0:T(8,128)S(1)} %get-tuple-element.35), channel_id=1, source_target_pairs={{0,1},{1,0},{2,3},{3,2},{4,5},{5,4},{6,7},{7,6},{8,9},{9,8},{10,11... | collective-permute-start | bytes 1769480 | tf_op jit(solution)/shard_map/ppermute | solution.py:234
  41.1 9.4 %copy-start = (bf16[3,3,256,128]{3,2,1,0:T(8,128)(2,1)S(1)}, bf16[3,3,256,128]{3,2,1,0:T(8,128)(2,1)}, u32[]{:S(2)}) copy-start(bf16[3,3,256,128]{3,2,1,0:T(8,128)(2,1)} %w.3) | copy-start | bytes 1769476
  41.8 20.6 %all-to-all-start = ((f16[16,80,128]{2,1,0:T(8,128)(2,1)}), f16[16,80,128]{2,1,0:T(8,128)(2,1)}, u32[]{:S(2)}, u32[]{:S(2)}) async-start(f16[16,80,128]{2,1,0:T(8,128)(2,1)} %convert_element_type.21), calls=%async_computation | async-start | bytes 655360 | tf_op jit(solution)/shard_map/all_to_all | solution.py:246
  50.4 0.9 %copy-start.2 = (bf16[6,160,128]{2,1,0:T(8,128)(2,1)S(1)}, bf16[6,160,128]{2,1,0:T(8,128)(2,1)}, u32[]{:S(2)}) copy-start(bf16[6,160,128]{2,1,0:T(8,128)(2,1)} %copy-done.1) | copy-start | bytes 737284
  51.4 0.9 %copy-start.4 = (bf16[6,160,128]{2,1,0:T(8,128)(2,1)S(1)}, bf16[6,160,128]{2,1,0:T(8,128)(2,1)}, u32[]{:S(2)}) copy-start(bf16[6,160,128]{2,1,0:T(8,128)(2,1)} %copy-done.3) | copy-start | bytes 737284
  52.3 0.9 copy-start.8
  53.2 0.9 copy-start.10
  57.9 23.6 %collective-permute-start.12 = (bf16[6,160,256]{2,1,0:T(8,128)(2,1)}, bf16[6,160,256]{2,1,0:T(8,128)(2,1)}, u32[]{:S(2)}, u32[]{:S(2)}) collective-permute-start(bf16[6,160,256]{2,1,0:T(8,128)(2,1)} %get-tuple-element.43), channel_id=1, source_target_pairs={{0,4},{4,0},{8,12},{12,8},{16,20},{20,16},{24,28},{28,24},{1,5},{5... | collective-permute-start | bytes 1474568 | tf_op jit(solution)/shard_map/ppermute | solution.py:257
  59.8 4.3 %collective-permute-start.9 = (bf16[4,6,16,256]{3,2,1,0:T(8,128)(2,1)}, bf16[4,6,16,256]{3,2,1,0:T(8,128)(2,1)S(1)}, u32[]{:S(2)}, u32[]{:S(2)}) collective-permute-start(bf16[4,6,16,256]{3,2,1,0:T(8,128)(2,1)} %pad_maximum_fusion.3), channel_id=1, source_target_pairs={{0,1},{1,2},{2,3},{4,5},{5,6},{6,7},{8,9},{9,10},{10,11},{12,13},{... | collective-permute-start | bytes 589832 | tf_op jit(solution)/shard_map/ppermute | solution.py:173
  61.1 5.2 %collective-permute-start.10 = (bf16[4,6,16,256]{3,2,1,0:T(8,128)(2,1)}, bf16[4,6,16,256]{3,2,1,0:T(8,128)(2,1)S(1)}, u32[]{:S(2)}, u32[]{:S(2)}) collective-permute-start(bf16[4,6,16,256]{3,2,1,0:T(8,128)(2,1)} %pad_maximum_fusion.4), channel_id=1, source_target_pairs={{1,0},{2,1},{3,2},{5,4},{6,5},{7,6},{9,8},{10,9},{11,10},{13,12},{... | collective-permute-start | bytes 589832 | tf_op jit(solution)/shard_map/ppermute | solution.py:174
  66.4 8.9 %copy-start.5 = (bf16[4,6,16,256]{3,2,1,0:T(8,128)(2,1)}, bf16[4,6,16,256]{3,2,1,0:T(8,128)(2,1)S(1)}, u32[]{:S(2)}) copy-start(bf16[4,6,16,256]{3,2,1,0:T(8,128)(2,1)S(1)} %collective-permute-done.10.right) | copy-start | bytes 589828
  67.2 20.0 %all-to-all-start.1 = ((f16[16,80,128]{2,1,0:T(8,128)(2,1)}), f16[16,80,128]{2,1,0:T(8,128)(2,1)}, u32[]{:S(2)}, u32[]{:S(2)}) async-start(f16[16,80,128]{2,1,0:T(8,128)(2,1)} %broadcast_in_dim.2), calls=%async_computation.1 | async-start | bytes 655360 | tf_op jit(solution)/shard_map/all_to_all | solution.py:271
  75.3 0.9 %copy-start.6 = (bf16[4,6,16,256]{3,2,1,0:T(8,128)(2,1)S(1)}, bf16[4,6,16,256]{3,2,1,0:T(8,128)(2,1)}, u32[]{:S(2)}) copy-start(bf16[4,6,16,256]{3,2,1,0:T(8,128)(2,1)} %copy-done.5) | copy-start | bytes 589828
  79.6 9.8 %collective-permute-start.11 = (bf16[6,160,128]{2,1,0:T(8,128)(2,1)}, bf16[6,160,128]{2,1,0:T(8,128)(2,1)S(1)}, u32[]{:S(2)}, u32[]{:S(2)}) collective-permute-start(bf16[6,160,128]{2,1,0:T(8,128)(2,1)} %get-tuple-element.47), channel_id=1, source_target_pairs={{0,4},{4,0},{8,12},{12,8},{16,20},{20,16},{24,28},{28,24},{1,5},{5... | collective-permute-start | bytes 737288 | tf_op jit(solution)/shard_map/ppermute | solution.py:282
  87.1 3.2 %collective-permute-start.13 = (f16[16,80,128]{2,1,0:T(8,128)(2,1)}, f16[16,80,128]{2,1,0:T(8,128)(2,1)S(1)}, u32[]{:S(2)}, u32[]{:S(2)}) collective-permute-start(f16[16,80,128]{2,1,0:T(8,128)(2,1)} %all-to-all-done.1), channel_id=1, source_target_pairs={{0,1},{1,0},{2,3},{3,2},{4,5},{5,4},{6,7},{7,6},{8,9},{9,8},{10,11... | collective-permute-start | bytes 983048 | tf_op jit(solution)/shard_map/ppermute | solution.py:272

commit v11 on v8

--- a/solution.py
+++ b/solution.py
@@ -140,6 +140,19 @@
     )(*operands)
 
 
+def kernel_edges(par, *refs):
+    blocks, (tails, heads) = (refs[:-2], refs[-2:])
+    for place, block in enumerate(blocks):
+        tails[place] = block[:, pl.ds(block.shape[1] - STRIP, STRIP), :]
+        heads[place] = block[:, pl.ds(0, STRIP), :]
+
+
+def packed(par, blocks, flops):
+    half, _, depth = blocks[0].shape
+    strip = jax.ShapeDtypeStruct((len(blocks), half, STRIP, depth), jnp.bfloat16)
+    return call(kernel_edges, (par,) + blocks, [strip, strip], [], flops)
+
+
 def edges(blocks):
     width = blocks[0].shape[1]
     tails = jnp.stack([x[:, width - STRIP :] for x in blocks])
@@ -190,24 +203,34 @@
     f_own, f_give = (pick(features, odd), pick(features, 1 - odd))
     d_par = lax.ppermute(d_give, "rows", swap)
     d_near = lax.ppermute(d_own, "rows", near)
-    f_give, d_par = fence((f_give, d_par))
     f_par = lax.ppermute(f_give, "rows", swap)
+    f_first, d_par, d_near = fence((f_own, d_par, d_near))
     d_far = lax.ppermute(d_par, "rows", far)
-    f_first, d_far = fence((f_own, d_far))
     f_near = lax.ppermute(f_first, "rows", near)
     f_far = lax.ppermute(f_par, "rows", far)
     d_blocks = (d_own, d_par, d_near, d_far)
+    f_own, f_near = fence((f_own, f_near))
+    d_left, d_right = exchanged(*packed(par, d_blocks, flops), cols)
+
     f_blocks = (f_own, f_par, f_near, f_far)
-    d_left, d_right = exchanged(*edges(d_blocks), cols)
-
     part = jax.ShapeDtypeStruct((share, cout), jnp.float32)
     d_maps = [VMEM((4, half, wide, cout), jnp.bfloat16), VMEM((4, half, width, 3 * cout), jnp.bfloat16)]
+    half_grad = jax.ShapeDtypeStruct((half, width, cin), jnp.bfloat16)
+    g_own, g_par = call(
+        kernel_back,
+        (par, weight) + d_blocks + (d_left, d_right),
+        [half_grad, half_grad],
+        d_maps,
+        30 * flops,
+    )
+    g_other = lax.ppermute(g_par, "rows", swap)
+    f_own, g_par = fence((f_own, g_par))
     keep, give = call(
         kernel_grad,
         (par, f_own, f_par) + d_blocks + (d_left, d_right),
         [part, part],
         d_maps + [VMEM((9 * cin, cout), jnp.float32)],
-        30 * flops,
+        0,
     )
     given = lax.ppermute(give, "core", other_core)
     f_tails, f_heads = edges(f_blocks)
@@ -222,14 +245,7 @@
     )
     scaled, f_tails, f_heads = fence((scaled.astype(jnp.float16), f_tails, f_heads))
     got = lax.all_to_all(scaled, CHIPS, 0, 0)
-    d_left, _ = fence((d_left, scaled))
-    half_grad = jax.ShapeDtypeStruct((half, width, cin), jnp.bfloat16)
-    g_own, g_par = call(
-        kernel_back, (par, weight) + d_blocks + (d_left, d_right), [half_grad, half_grad], d_maps, 0
-    )
-    g_other = lax.ppermute(g_par, "rows", swap)
-    got, g_par = fence((got, g_par))
-
+    g_own, _ = fence((g_own, scaled))
     f_left, f_right = exchanged(f_tails, f_heads, cols)
 
     (mine,) = call(
@@ -240,7 +256,7 @@
         0,
     )
     mine = mine.astype(jnp.float16)
-    f_left, copies = fence((f_left, jnp.broadcast_to(mine[None], (chips, deep, cout))))
+    f_left, f_right, copies = fence((f_left, f_right, jnp.broadcast_to(mine[None], (chips, deep, cout))))
     spread = lax.all_to_all(copies, CHIPS, 0, 0)
     other = lax.ppermute(spread, "core", other_core)
 

time: 95.1 us -> 86.4 us (0.909); the launches traced: 93.2 us -> 85.7 us
  local copies, waits for them, and re-layouts: 8.98 us -> 5.8 us
  starting transfers between devices: 42.3 us -> 39.6 us
  waiting for transfers between devices: 21.7 us -> 19.1 us
    ppermute x1, waiting for transfers between devices: 5.57 us -> 0.01 us  [body(): f_far = lax.ppermute(f_par, 'rows', far)]
    all_to_all x1, waiting for transfers between devices: 0.24 us -> 5.72 us  [body(): got = lax.all_to_all(scaled, CHIPS, 0, 0)]
    all_to_all x1, starting transfers between devices: 9.58 us -> 4.64 us  [body(): spread = lax.all_to_all(copies, CHIPS, 0, 0)]
    ppermute x1, starting transfers between devices: 4.35 us -> 0.01 us  [body(): other = lax.ppermute(spread, 'core', other_core)]
    all_to_all x1, waiting for transfers between devices: 0.01 us -> 3.62 us  [body(): spread = lax.all_to_all(copies, CHIPS, 0, 0)]
    ppermute x1, waiting for transfers between devices: 3.56 us -> 0.01 us  [body(): f_par = lax.ppermute(f_give, 'rows', swap)]
    ppermute x1, waiting for transfers between devices: 0.01 us -> 2.66 us  [body(): d_near = lax.ppermute(d_own, 'rows', near)]
    ppermute x1, starting transfers between devices: 0.07 us -> 2.71 us  [body(): f_par = lax.ppermute(f_give, 'rows', swap)]
  transfers between devices with their start and end apart: 16 -> 16, of which waited for: 8 -> 7; matrix products, arithmetic and copies ran while one was open for 8% -> 8% of each run, Pallas kernels for 11% -> 13%
where the time goes in v11:
time: 86.4 us; the launch traced here: 85.7 us
  starting transfers between devices  39.6 us (46%)
  waiting for transfers between devices  19.1 us (22%)
  Pallas kernels  11.6 us (13%)
  other arithmetic  8.68 us (10%)
  local copies, waits for them, and re-layouts  5.8 us (7%)
  between operations  0.97 us (1%)
    pallas_call x6, Pallas kernels, call(): pl.pallas_call(kernel, out_shape=outs, in_specs=[pl.BlockSpec(memory_spac...  11.6 us
    all_to_all x1, starting transfers between devices, body(): got = lax.all_to_all(scaled, CHIPS, 0, 0)  7.05 us
    all_to_all x1, waiting for transfers between devices, body(): got = lax.all_to_all(scaled, CHIPS, 0, 0)  5.72 us
    all_to_all x1, starting transfers between devices, body(): spread = lax.all_to_all(copies, CHIPS, 0, 0)  4.64 us
    ppermute x1, starting transfers between devices, body(): f_far = lax.ppermute(f_par, 'rows', far)  4.42 us
    all_to_all x1, waiting for transfers between devices, body(): spread = lax.all_to_all(copies, CHIPS, 0, 0)  3.62 us
    ppermute x1, starting transfers between devices, body(): d_far = lax.ppermute(d_par, 'rows', far)  3.48 us
    ppermute x1, starting transfers between devices, body(): d_par = lax.ppermute(d_give, 'rows', swap)  3.03 us
  transfers between devices with their start and end apart: 16, of which 7 were waited for; matrix products, arithmetic and copies ran while one was open for 8% of the time, Pallas kernels for 13%

profile of v11, /device:TPU:0, one launch (start us, length us, event | category | flops | bytes accessed | tf_op | source)
XLA Modules:
  0.0 85.7 jit_solution(12534956377197983843)
XLA Ops:
  0.7 1.2 %constant_dynamic-slice_fusion.1 = (bf16[6,160,128]{2,1,0:T(8,128)(2,1)S(1)}, bf16[6,160,128]{2,1,0:T(8,128)(2,1)S(1)}) fusion(bf16[12,160,128]{2,1,0:T(8,128)(2,1)} %param.5, s32[]{:T(128)S(6)} %select_n.53, s32[]{:T(128)S(6)} %select_n.54), kind=kLoop, calls=%fused_computation.22 | loop fusion | bytes 983048 | tf_op jit(solution)/shard_map/dynamic_slice | solution.py:194
  1.8 3.0 %collective-permute-start = (bf16[6,160,128]{2,1,0:T(8,128)(2,1)S(1)}, bf16[6,160,128]{2,1,0:T(8,128)(2,1)S(1)}, u32[]{:S(2)}, u32[]{:S(2)}) collective-permute-start(bf16[6,160,128]{2,1,0:T(8,128)(2,1)S(1)} %get-tuple-element.68), channel_id=1, source_target_pairs={{0,4},{4,0},{8,12},{12,8},{16,20},{20,16},{24,28},{28,24},{1,5},{5... | collective-permute-start | bytes 737288 | tf_op jit(solution)/shard_map/ppermute | solution.py:204
  4.9 1.3 %collective-permute-start.1 = (bf16[6,160,128]{2,1,0:T(8,128)(2,1)S(1)}, bf16[6,160,128]{2,1,0:T(8,128)(2,1)S(1)}, u32[]{:S(2)}, u32[]{:S(2)}) collective-permute-start(bf16[6,160,128]{2,1,0:T(8,128)(2,1)S(1)} %get-tuple-element.67.refs_0_.d_own), channel_id=1, source_target_pairs={{4,12},{8,0},{12,20},{16,8},{20,28},{24,16},{5,13},{9,1},{13,21},{... | collective-permute-start | bytes 737288 | tf_op jit(solution)/shard_map/ppermute | solution.py:205
  6.2 0.9 constant_dynamic-slice_fusion
  7.0 2.7 %collective-permute-start.3 = (bf16[6,160,256]{2,1,0:T(8,128)(2,1)}, bf16[6,160,256]{2,1,0:T(8,128)(2,1)S(1)}, u32[]{:S(2)}, u32[]{:S(2)}) collective-permute-start(bf16[6,160,256]{2,1,0:T(8,128)(2,1)} %get-tuple-element.53), channel_id=1, source_target_pairs={{0,4},{4,0},{8,12},{12,8},{16,20},{20,16},{24,28},{28,24},{1,5},{5... | collective-permute-start | bytes 1474568 | tf_op jit(solution)/shard_map/ppermute | solution.py:206
  9.7 1.8 %collective-permute-done.refs_1_.d_par = bf16[6,160,128]{2,1,0:T(8,128)(2,1)S(1)} collective-permute-done((bf16[6,160,128]{2,1,0:T(8,128)(2,1)S(1)}, bf16[6,160,128]{2,1,0:T(8,128)(2,1)S(1)}, u32[]{:S(2)}, u32[]{:S(2)}) %collective-permute-start) | collective-permute-done | bytes 245792 | tf_op jit(solution)/shard_map/ppermute | solution.py:204
  11.5 2.7 %collective-permute-done.1.refs_2_.d_near = bf16[6,160,128]{2,1,0:T(8,128)(2,1)S(1)} collective-permute-done((bf16[6,160,128]{2,1,0:T(8,128)(2,1)S(1)}, bf16[6,160,128]{2,1,0:T(8,128)(2,1)S(1)}, u32[]{:S(2)}, u32[]{:S(2)}) %collective-permute-start.1) | collective-permute-done | bytes 245792 | tf_op jit(solution)/shard_map/ppermute | solution.py:205
  14.2 3.5 %collective-permute-start.5 = (bf16[6,160,128]{2,1,0:T(8,128)(2,1)S(1)}, bf16[6,160,128]{2,1,0:T(8,128)(2,1)S(1)}, u32[]{:S(2)}, u32[]{:S(2)}) collective-permute-start(bf16[6,160,128]{2,1,0:T(8,128)(2,1)S(1)} %collective-permute-done.refs_1_.d_par), channel_id=1, source_target_pairs={{12,4},{0,8},{20,12},{8,16},{28,20},{16,24},{13,5},{1,9},{21,13},{... | collective-permute-start | bytes 737288 | tf_op jit(solution)/shard_map/ppermute | solution.py:208
  17.7 0.1 pad_add_fusion.par
  17.7 1.4 %collective-permute-start.2 = (bf16[6,160,256]{2,1,0:T(8,128)(2,1)S(1)}, bf16[6,160,256]{2,1,0:T(8,128)(2,1)S(1)}, u32[]{:S(2)}, u32[]{:S(2)}) collective-permute-start(bf16[6,160,256]{2,1,0:T(8,128)(2,1)S(1)} %get-tuple-element.35.f_own), channel_id=1, source_target_pairs={{4,12},{8,0},{12,20},{16,8},{20,28},{24,16},{5,13},{9,1},{13,21},{... | collective-permute-start | bytes 1474568 | tf_op jit(solution)/shard_map/ppermute | solution.py:209
  19.2 2.5 %collective-permute-done.5.refs_3_.d_far = bf16[6,160,128]{2,1,0:T(8,128)(2,1)S(1)} collective-permute-done((bf16[6,160,128]{2,1,0:T(8,128)(2,1)S(1)}, bf16[6,160,128]{2,1,0:T(8,128)(2,1)S(1)}, u32[]{:S(2)}, u32[]{:S(2)}) %collective-permute-start.5) | collective-permute-done | bytes 245792 | tf_op jit(solution)/shard_map/ppermute | solution.py:208
  21.7 0.6 shard_map.58
  22.2 0.1 copy-done.4
  22.4 1.3 %collective-permute-start.6 = (bf16[4,6,16,128]{3,2,1,0:T(8,128)(2,1)S(1)}, bf16[4,6,16,128]{3,2,1,0:T(8,128)(2,1)S(1)}, u32[]{:S(2)}, u32[]{:S(2)}) collective-permute-start(bf16[4,6,16,128]{3,2,1,0:T(8,128)(2,1)S(1)} %get-tuple-element.32), channel_id=1, source_target_pairs={{0,1},{1,2},{2,3},{4,5},{5,6},{6,7},{8,9},{9,10},{10,11},{12,13},{... | collective-permute-start | bytes 294920 | tf_op jit(solution)/shard_map/ppermute | solution.py:164
  23.6 1.3 %collective-permute-start.7 = (bf16[4,6,16,128]{3,2,1,0:T(8,128)(2,1)S(1)}, bf16[4,6,16,128]{3,2,1,0:T(8,128)(2,1)S(1)}, u32[]{:S(2)}, u32[]{:S(2)}) collective-permute-start(bf16[4,6,16,128]{3,2,1,0:T(8,128)(2,1)S(1)} %get-tuple-element.33), channel_id=1, source_target_pairs={{1,0},{2,1},{3,2},{5,4},{6,5},{7,6},{9,8},{10,9},{11,10},{13,12},{... | collective-permute-start | bytes 294920 | tf_op jit(solution)/shard_map/ppermute | solution.py:165
  25.0 4.4 %collective-permute-start.4 = (bf16[6,160,256]{2,1,0:T(8,128)(2,1)S(1)}, bf16[6,160,256]{2,1,0:T(8,128)(2,1)S(1)}, u32[]{:S(2)}, u32[]{:S(2)}) collective-permute-start(bf16[6,160,256]{2,1,0:T(8,128)(2,1)S(1)} %collective-permute-done.3.f_par), channel_id=1, source_target_pairs={{12,4},{0,8},{20,12},{8,16},{28,20},{16,24},{13,5},{1,9},{21,13},{... | collective-permute-start | bytes 1474568 | tf_op jit(solution)/shard_map/ppermute | solution.py:210
  29.4 0.0 copy-start.2
  29.4 0.9 %copy-done.2 = bf16[6,160,128]{2,1,0:T(8,128)(2,1)S(1)} copy-done((bf16[6,160,128]{2,1,0:T(8,128)(2,1)S(1)}, bf16[6,160,128]{2,1,0:T(8,128)(2,1)}, u32[]{:S(2)}) %copy-start.2) | copy-done | bytes 245784
  30.4 0.9 %copy-done.5 = bf16[6,160,128]{2,1,0:T(8,128)(2,1)S(1)} copy-done((bf16[6,160,128]{2,1,0:T(8,128)(2,1)S(1)}, bf16[6,160,128]{2,1,0:T(8,128)(2,1)}, u32[]{:S(2)}) %copy-start.5) | copy-done | bytes 245784
  31.3 3.6 %shard_map.59 = (bf16[6,160,256]{2,1,0:T(8,128)(2,1)S(1)}, bf16[6,160,256]{2,1,0:T(8,128)(2,1)}) custom-call(s32[2]{0:T(128)S(1)} %pad_add_fusion.par, bf16[3,3,256,128]{3,2,1,0:T(8,128)(2,1)S(1)} %copy-done, bf16[6,160,128]{2,1,0:T(8,128)(2,1)S(1)} %get-tuple-element.67.refs_0_.d_own, bf16[6,160,128]{2,1,0:T(8,128)(2,1)S(1)} %collective-permute-done.refs_1_.d_par, ...), custom_call_target="tpu_custom_call" | custom-call | flops 33973862400 | bytes 2752520 | tf_op jit(solution)/shard_map/pallas_call | solution.py:132
  34.9 2.8 %shard_map.60 = (f32[1152,128]{1,0:T(8,128)S(1)}, f32[1152,128]{1,0:T(8,128)S(1)}) custom-call(s32[2]{0:T(128)S(1)} %pad_add_fusion.par, bf16[6,160,256]{2,1,0:T(8,128)(2,1)S(1)} %get-tuple-element.35.f_own, bf16[6,160,256]{2,1,0:T(8,128)(2,1)S(1)} %collective-permute-done.3.f_par, bf16[6,160,128]{2,1,0:T(8,128)(2,1)S(1)} %get-tuple-element.67.refs_0_.d_own, ...), custom_call_target="tpu_custom_call" | custom-call | tf_op jit(solution)/shard_map/pallas_call | solution.py:132
  37.7 2.6 %collective-permute-start.8 = (f32[1152,128]{1,0:T(8,128)S(1)}, f32[1152,128]{1,0:T(8,128)S(1)}, u32[]{:S(2)}, u32[]{:S(2)}) collective-permute-start(f32[1152,128]{1,0:T(8,128)S(1)} %get-tuple-element.37), channel_id=1, source_target_pairs={{0,1},{1,0},{2,3},{3,2},{4,5},{5,4},{6,7},{7,6},{8,9},{9,8},{10,11... | collective-permute-start | bytes 1769480 | tf_op jit(solution)/shard_map/ppermute | solution.py:235
  40.4 0.7 pad_maximum_fusion.3
  41.1 0.7 pad_maximum_fusion.4
  41.8 0.2 collective-permute-done.8.given
  41.9 0.7 shard_map.61
  42.7 0.8 convert_element_type.21
  43.5 7.0 %all-to-all-start = ((f16[16,80,128]{2,1,0:T(8,128)(2,1)}), f16[16,80,128]{2,1,0:T(8,128)(2,1)}, u32[]{:S(2)}, u32[]{:S(2)}) async-start(f16[16,80,128]{2,1,0:T(8,128)(2,1)} %convert_element_type.21), calls=%async_computation | async-start | bytes 655360 | tf_op jit(solution)/shard_map/all_to_all | solution.py:247
  50.5 1.9 %collective-permute-start.12 = (bf16[6,160,256]{2,1,0:T(8,128)(2,1)}, bf16[6,160,256]{2,1,0:T(8,128)(2,1)}, u32[]{:S(2)}, u32[]{:S(2)}) collective-permute-start(bf16[6,160,256]{2,1,0:T(8,128)(2,1)} %get-tuple-element.34), channel_id=1, source_target_pairs={{0,4},{4,0},{8,12},{12,8},{16,20},{20,16},{24,28},{28,24},{1,5},{5... | collective-permute-start | bytes 1474568 | tf_op jit(solution)/shard_map/ppermute | solution.py:226
  52.4 1.3 %collective-permute-start.9 = (bf16[4,6,16,256]{3,2,1,0:T(8,128)(2,1)}, bf16[4,6,16,256]{3,2,1,0:T(8,128)(2,1)S(1)}, u32[]{:S(2)}, u32[]{:S(2)}) collective-permute-start(bf16[4,6,16,256]{3,2,1,0:T(8,128)(2,1)} %pad_maximum_fusion.3), channel_id=1, source_target_pairs={{0,1},{1,2},{2,3},{4,5},{5,6},{6,7},{8,9},{9,10},{10,11},{12,13},{... | collective-permute-start | bytes 589832 | tf_op jit(solution)/shard_map/ppermute | solution.py:164
  53.7 1.3 %collective-permute-start.10 = (bf16[4,6,16,256]{3,2,1,0:T(8,128)(2,1)}, bf16[4,6,16,256]{3,2,1,0:T(8,128)(2,1)S(1)}, u32[]{:S(2)}, u32[]{:S(2)}) collective-permute-start(bf16[4,6,16,256]{3,2,1,0:T(8,128)(2,1)} %pad_maximum_fusion.4), channel_id=1, source_target_pairs={{1,0},{2,1},{3,2},{5,4},{6,5},{7,6},{9,8},{10,9},{11,10},{13,12},{... | collective-permute-start | bytes 589832 | tf_op jit(solution)/shard_map/ppermute | solution.py:165
  55.0 5.7 %all-to-all-done = f16[16,80,128]{2,1,0:T(8,128)(2,1)} async-done(((f16[16,80,128]{2,1,0:T(8,128)(2,1)}), f16[16,80,128]{2,1,0:T(8,128)(2,1)}, u32[]{:S(2)}, u32[]{:S(2)}) %all-to-all-start) | async-done | bytes 327712 | tf_op jit(solution)/shard_map/all_to_all | solution.py:247
  60.7 1.0 %convert_element_type.22.got = f32[16,80,128]{2,1,0:T(8,128)S(1)} convert(f16[16,80,128]{2,1,0:T(8,128)(2,1)} %all-to-all-done) | non-fusion elementwise | flops 163840 | bytes 983040 | tf_op jit(solution)/shard_map/convert_element_type | solution.py:253
  61.7 0.6 shard_map.62
  62.4 0.0 copy-start.7
  62.4 0.8 broadcast_in_dim.2
  63.2 4.6 %all-to-all-start.1 = ((f16[16,80,128]{2,1,0:T(8,128)(2,1)}), f16[16,80,128]{2,1,0:T(8,128)(2,1)}, u32[]{:S(2)}, u32[]{:S(2)}) async-start(f16[16,80,128]{2,1,0:T(8,128)(2,1)} %broadcast_in_dim.2), calls=%async_computation.1 | async-start | bytes 655360 | tf_op jit(solution)/shard_map/all_to_all | solution.py:260
  67.9 0.9 %copy-done.8 = bf16[4,6,16,256]{3,2,1,0:T(8,128)(2,1)S(1)} copy-done((bf16[4,6,16,256]{3,2,1,0:T(8,128)(2,1)S(1)}, bf16[4,6,16,256]{3,2,1,0:T(8,128)(2,1)}, u32[]{:S(2)}) %copy-start.8) | copy-done | bytes 196632
  68.8 3.4 %shard_map.63 = (bf16[6,160,128]{2,1,0:T(8,128)(2,1)S(1)}, bf16[6,160,128]{2,1,0:T(8,128)(2,1)}) custom-call(s32[2]{0:T(128)S(1)} %pad_add_fusion.par, bf16[3,3,256,128]{3,2,1,0:T(8,128)(2,1)S(1)} %copy-done, bf16[6,160,256]{2,1,0:T(8,128)(2,1)S(1)} %get-tuple-element.35.f_own, bf16[6,160,256]{2,1,0:T(8,128)(2,1)S(1)} %collective-permute-done.3.f_par, ...), custom_call_target="tpu_custom_call" | custom-call | tf_op jit(solution)/shard_map/pallas_call | solution.py:132
  72.2 1.9 %collective-permute-start.11 = (bf16[6,160,128]{2,1,0:T(8,128)(2,1)}, bf16[6,160,128]{2,1,0:T(8,128)(2,1)S(1)}, u32[]{:S(2)}, u32[]{:S(2)}) collective-permute-start(bf16[6,160,128]{2,1,0:T(8,128)(2,1)} %get-tuple-element.46), channel_id=1, source_target_pairs={{0,4},{4,0},{8,12},{12,8},{16,20},{20,16},{24,28},{28,24},{1,5},{5... | collective-permute-start | bytes 737288 | tf_op jit(solution)/shard_map/ppermute | solution.py:271
  74.0 1.2 %broadcast_select_fusion.1 = (bf16[6,160,256]{2,1,0:T(8,128)(2,1)S(1)}, bf16[6,160,256]{2,1,0:T(8,128)(2,1)S(1)}) fusion(bf16[6,160,256]{2,1,0:T(8,128)(2,1)} %collective-permute-done.12, bf16[6,160,256]{2,1,0:T(8,128)(2,1)S(1)} %get-tuple-element.49, pred[]{:T(512)S(6)} %eq.6), kind=kLoop, calls=%fused_computation.6 | loop fusion | flops 491520 | bytes 1966081 | tf_op jit(solution)/shard_map/jit(_where)/select_n | solution.py:170
  75.2 1.0 %pad_maximum_fusion.1 = bf16[12,160,256]{2,1,0:T(8,128)(2,1)} fusion(bf16[6,160,256]{2,1,0:T(8,128)(2,1)S(1)} %get-tuple-element.52, bf16[6,160,256]{2,1,0:T(8,128)(2,1)S(1)} %get-tuple-element.51), kind=kLoop, calls=%fused_computation.1 | loop fusion | flops 491520 | bytes 1966080 | tf_op jit(solution)/shard_map/concatenate | solution.py:172
  76.2 3.6 %all-to-all-done.1 = f16[16,80,128]{2,1,0:T(8,128)(2,1)} async-done(((f16[16,80,128]{2,1,0:T(8,128)(2,1)}), f16[16,80,128]{2,1,0:T(8,128)(2,1)}, u32[]{:S(2)}, u32[]{:S(2)}) %all-to-all-start.1) | async-done | bytes 327712 | tf_op jit(solution)/shard_map/all_to_all | solution.py:260
  79.8 2.6 %collective-permute-done.11 = bf16[6,160,128]{2,1,0:T(8,128)(2,1)S(1)} collective-permute-done((bf16[6,160,128]{2,1,0:T(8,128)(2,1)}, bf16[6,160,128]{2,1,0:T(8,128)(2,1)S(1)}, u32[]{:S(2)}, u32[]{:S(2)}) %collective-permute-start.11) | collective-permute-done | bytes 245792 | tf_op jit(solution)/shard_map/ppermute | solution.py:271
  82.4 0.1 broadcast_select_fusion.5
  82.5 0.8 pad_maximum_fusion.2
  83.3 1.1 %broadcast_select_fusion.3 = (f16[16,80,128]{2,1,0:T(8,128)(2,1)S(1)}, f16[16,80,128]{2,1,0:T(8,128)(2,1)S(1)}) fusion(f16[16,80,128]{2,1,0:T(8,128)(2,1)} %all-to-all-done.1, f16[16,80,128]{2,1,0:T(8,128)(2,1)S(1)} %collective-permute-done.13, pred[]{:T(512)S(6)} %eq.7), kind=kLoop, calls=%fused_computation.8 | loop fusion | flops 327680 | bytes 1310721 | tf_op jit(solution)/shard_map/jit(_where)/select_n | solution.py:276
  84.6 1.1 %pad_maximum_fusion = f32[2304,128]{1,0:T(8,128)} fusion(f32[1152,128]{1,0:T(8,128)S(1)} %bitcast.25, f32[1152,128]{1,0:T(8,128)S(1)} %bitcast.26), kind=kLoop, calls=%fused_computation | loop fusion | flops 294912 | bytes 2359296 | tf_op jit(solution)/shard_map/concatenate | solution.py:280
  (32 shorter events, 0.2 us)
Async XLA Ops:
  0.6 5.5 %copy-start.9 = (bf16[12,160,256]{2,1,0:T(8,128)(2,1)S(1)}, bf16[12,160,256]{2,1,0:T(8,128)(2,1)}, u32[]{:S(2)}) copy-start(bf16[12,160,256]{2,1,0:T(8,128)(2,1)} %param.3) | copy-start | bytes 2949124
  1.8 9.7 %collective-permute-start = (bf16[6,160,128]{2,1,0:T(8,128)(2,1)S(1)}, bf16[6,160,128]{2,1,0:T(8,128)(2,1)S(1)}, u32[]{:S(2)}, u32[]{:S(2)}) collective-permute-start(bf16[6,160,128]{2,1,0:T(8,128)(2,1)S(1)} %get-tuple-element.68), channel_id=1, source_target_pairs={{0,4},{4,0},{8,12},{12,8},{16,20},{20,16},{24,28},{28,24},{1,5},{5... | collective-permute-start | bytes 737288 | tf_op jit(solution)/shard_map/ppermute | solution.py:204
  4.9 9.3 %collective-permute-start.1 = (bf16[6,160,128]{2,1,0:T(8,128)(2,1)S(1)}, bf16[6,160,128]{2,1,0:T(8,128)(2,1)S(1)}, u32[]{:S(2)}, u32[]{:S(2)}) collective-permute-start(bf16[6,160,128]{2,1,0:T(8,128)(2,1)S(1)} %get-tuple-element.67.refs_0_.d_own), channel_id=1, source_target_pairs={{4,12},{8,0},{12,20},{16,8},{20,28},{24,16},{5,13},{9,1},{13,21},{... | collective-permute-start | bytes 737288 | tf_op jit(solution)/shard_map/ppermute | solution.py:205
  7.0 17.9 %collective-permute-start.3 = (bf16[6,160,256]{2,1,0:T(8,128)(2,1)}, bf16[6,160,256]{2,1,0:T(8,128)(2,1)S(1)}, u32[]{:S(2)}, u32[]{:S(2)}) collective-permute-start(bf16[6,160,256]{2,1,0:T(8,128)(2,1)} %get-tuple-element.53), channel_id=1, source_target_pairs={{0,4},{4,0},{8,12},{12,8},{16,20},{20,16},{24,28},{28,24},{1,5},{5... | collective-permute-start | bytes 1474568 | tf_op jit(solution)/shard_map/ppermute | solution.py:206
  14.2 8.1 %copy-start.1 = (bf16[6,160,128]{2,1,0:T(8,128)(2,1)}, bf16[6,160,128]{2,1,0:T(8,128)(2,1)S(1)}, u32[]{:S(2)}) copy-start(bf16[6,160,128]{2,1,0:T(8,128)(2,1)S(1)} %collective-permute-done.1.refs_2_.d_near) | copy-start | bytes 737284
  14.2 7.5 %collective-permute-start.5 = (bf16[6,160,128]{2,1,0:T(8,128)(2,1)S(1)}, bf16[6,160,128]{2,1,0:T(8,128)(2,1)S(1)}, u32[]{:S(2)}, u32[]{:S(2)}) collective-permute-start(bf16[6,160,128]{2,1,0:T(8,128)(2,1)S(1)} %collective-permute-done.refs_1_.d_par), channel_id=1, source_target_pairs={{12,4},{0,8},{20,12},{8,16},{28,20},{16,24},{13,5},{1,9},{21,13},{... | collective-permute-start | bytes 737288 | tf_op jit(solution)/shard_map/ppermute | solution.py:208
  17.7 11.7 %copy-start = (bf16[3,3,256,128]{3,2,1,0:T(8,128)(2,1)S(1)}, bf16[3,3,256,128]{3,2,1,0:T(8,128)(2,1)}, u32[]{:S(2)}) copy-start(bf16[3,3,256,128]{3,2,1,0:T(8,128)(2,1)} %w.3) | copy-start | bytes 1769476
  17.7 17.2 %collective-permute-start.2 = (bf16[6,160,256]{2,1,0:T(8,128)(2,1)S(1)}, bf16[6,160,256]{2,1,0:T(8,128)(2,1)S(1)}, u32[]{:S(2)}, u32[]{:S(2)}) collective-permute-start(bf16[6,160,256]{2,1,0:T(8,128)(2,1)S(1)} %get-tuple-element.35.f_own), channel_id=1, source_target_pairs={{4,12},{8,0},{12,20},{16,8},{20,28},{24,16},{5,13},{9,1},{13,21},{... | collective-permute-start | bytes 1474568 | tf_op jit(solution)/shard_map/ppermute | solution.py:209
  21.7 0.7 copy-start.4
  22.4 7.0 %collective-permute-start.6 = (bf16[4,6,16,128]{3,2,1,0:T(8,128)(2,1)S(1)}, bf16[4,6,16,128]{3,2,1,0:T(8,128)(2,1)S(1)}, u32[]{:S(2)}, u32[]{:S(2)}) collective-permute-start(bf16[4,6,16,128]{3,2,1,0:T(8,128)(2,1)S(1)} %get-tuple-element.32), channel_id=1, source_target_pairs={{0,1},{1,2},{2,3},{4,5},{5,6},{6,7},{8,9},{9,10},{10,11},{12,13},{... | collective-permute-start | bytes 294920 | tf_op jit(solution)/shard_map/ppermute | solution.py:164
  23.6 5.8 %collective-permute-start.7 = (bf16[4,6,16,128]{3,2,1,0:T(8,128)(2,1)S(1)}, bf16[4,6,16,128]{3,2,1,0:T(8,128)(2,1)S(1)}, u32[]{:S(2)}, u32[]{:S(2)}) collective-permute-start(bf16[4,6,16,128]{3,2,1,0:T(8,128)(2,1)S(1)} %get-tuple-element.33), channel_id=1, source_target_pairs={{1,0},{2,1},{3,2},{5,4},{6,5},{7,6},{9,8},{10,9},{11,10},{13,12},{... | collective-permute-start | bytes 294920 | tf_op jit(solution)/shard_map/ppermute | solution.py:165
  25.0 15.4 %collective-permute-start.4 = (bf16[6,160,256]{2,1,0:T(8,128)(2,1)S(1)}, bf16[6,160,256]{2,1,0:T(8,128)(2,1)S(1)}, u32[]{:S(2)}, u32[]{:S(2)}) collective-permute-start(bf16[6,160,256]{2,1,0:T(8,128)(2,1)S(1)} %collective-permute-done.3.f_par), channel_id=1, source_target_pairs={{12,4},{0,8},{20,12},{8,16},{28,20},{16,24},{13,5},{1,9},{21,13},{... | collective-permute-start | bytes 1474568 | tf_op jit(solution)/shard_map/ppermute | solution.py:210
  29.4 0.9 %copy-start.2 = (bf16[6,160,128]{2,1,0:T(8,128)(2,1)S(1)}, bf16[6,160,128]{2,1,0:T(8,128)(2,1)}, u32[]{:S(2)}) copy-start(bf16[6,160,128]{2,1,0:T(8,128)(2,1)} %copy-done.1) | copy-start | bytes 737284
  30.4 0.9 %copy-start.5 = (bf16[6,160,128]{2,1,0:T(8,128)(2,1)S(1)}, bf16[6,160,128]{2,1,0:T(8,128)(2,1)}, u32[]{:S(2)}) copy-start(bf16[6,160,128]{2,1,0:T(8,128)(2,1)} %copy-done.4) | copy-start | bytes 737284
  31.3 3.6 %copy-start.3 = (bf16[6,160,128]{2,1,0:T(8,128)(2,1)S(1)}, bf16[6,160,128]{2,1,0:T(8,128)(2,1)}, u32[]{:S(2)}) copy-start(bf16[6,160,128]{2,1,0:T(8,128)(2,1)} %copy-done.1) | copy-start | bytes 737284
  31.3 3.6 %copy-start.6 = (bf16[6,160,128]{2,1,0:T(8,128)(2,1)S(1)}, bf16[6,160,128]{2,1,0:T(8,128)(2,1)}, u32[]{:S(2)}) copy-start(bf16[6,160,128]{2,1,0:T(8,128)(2,1)} %copy-done.4) | copy-start | bytes 737284
  37.7 4.3 %collective-permute-start.8 = (f32[1152,128]{1,0:T(8,128)S(1)}, f32[1152,128]{1,0:T(8,128)S(1)}, u32[]{:S(2)}, u32[]{:S(2)}) collective-permute-start(f32[1152,128]{1,0:T(8,128)S(1)} %get-tuple-element.37), channel_id=1, source_target_pairs={{0,1},{1,0},{2,3},{3,2},{4,5},{5,4},{6,7},{7,6},{8,9},{9,8},{10,11... | collective-permute-start | bytes 1769480 | tf_op jit(solution)/shard_map/ppermute | solution.py:235
  43.5 17.3 %all-to-all-start = ((f16[16,80,128]{2,1,0:T(8,128)(2,1)}), f16[16,80,128]{2,1,0:T(8,128)(2,1)}, u32[]{:S(2)}, u32[]{:S(2)}) async-start(f16[16,80,128]{2,1,0:T(8,128)(2,1)} %convert_element_type.21), calls=%async_computation | async-start | bytes 655360 | tf_op jit(solution)/shard_map/all_to_all | solution.py:247
  50.5 23.5 %collective-permute-start.12 = (bf16[6,160,256]{2,1,0:T(8,128)(2,1)}, bf16[6,160,256]{2,1,0:T(8,128)(2,1)}, u32[]{:S(2)}, u32[]{:S(2)}) collective-permute-start(bf16[6,160,256]{2,1,0:T(8,128)(2,1)} %get-tuple-element.34), channel_id=1, source_target_pairs={{0,4},{4,0},{8,12},{12,8},{16,20},{20,16},{24,28},{28,24},{1,5},{5... | collective-permute-start | bytes 1474568 | tf_op jit(solution)/shard_map/ppermute | solution.py:226
  52.4 10.0 %collective-permute-start.9 = (bf16[4,6,16,256]{3,2,1,0:T(8,128)(2,1)}, bf16[4,6,16,256]{3,2,1,0:T(8,128)(2,1)S(1)}, u32[]{:S(2)}, u32[]{:S(2)}) collective-permute-start(bf16[4,6,16,256]{3,2,1,0:T(8,128)(2,1)} %pad_maximum_fusion.3), channel_id=1, source_target_pairs={{0,1},{1,2},{2,3},{4,5},{5,6},{6,7},{8,9},{9,10},{10,11},{12,13},{... | collective-permute-start | bytes 589832 | tf_op jit(solution)/shard_map/ppermute | solution.py:164
  53.7 8.7 %collective-permute-start.10 = (bf16[4,6,16,256]{3,2,1,0:T(8,128)(2,1)}, bf16[4,6,16,256]{3,2,1,0:T(8,128)(2,1)S(1)}, u32[]{:S(2)}, u32[]{:S(2)}) collective-permute-start(bf16[4,6,16,256]{3,2,1,0:T(8,128)(2,1)} %pad_maximum_fusion.4), channel_id=1, source_target_pairs={{1,0},{2,1},{3,2},{5,4},{6,5},{7,6},{9,8},{10,9},{11,10},{13,12},{... | collective-permute-start | bytes 589832 | tf_op jit(solution)/shard_map/ppermute | solution.py:165
  62.4 5.5 %copy-start.7 = (bf16[4,6,16,256]{3,2,1,0:T(8,128)(2,1)}, bf16[4,6,16,256]{3,2,1,0:T(8,128)(2,1)S(1)}, u32[]{:S(2)}) copy-start(bf16[4,6,16,256]{3,2,1,0:T(8,128)(2,1)S(1)} %collective-permute-done.10.right) | copy-start | bytes 589828
  63.2 16.7 %all-to-all-start.1 = ((f16[16,80,128]{2,1,0:T(8,128)(2,1)}), f16[16,80,128]{2,1,0:T(8,128)(2,1)}, u32[]{:S(2)}, u32[]{:S(2)}) async-start(f16[16,80,128]{2,1,0:T(8,128)(2,1)} %broadcast_in_dim.2), calls=%async_computation.1 | async-start | bytes 655360 | tf_op jit(solution)/shard_map/all_to_all | solution.py:260
  67.8 0.9 %copy-start.8 = (bf16[4,6,16,256]{3,2,1,0:T(8,128)(2,1)S(1)}, bf16[4,6,16,256]{3,2,1,0:T(8,128)(2,1)}, u32[]{:S(2)}) copy-start(bf16[4,6,16,256]{3,2,1,0:T(8,128)(2,1)} %copy-done.7) | copy-start | bytes 589828
  72.2 10.3 %collective-permute-start.11 = (bf16[6,160,128]{2,1,0:T(8,128)(2,1)}, bf16[6,160,128]{2,1,0:T(8,128)(2,1)S(1)}, u32[]{:S(2)}, u32[]{:S(2)}) collective-permute-start(bf16[6,160,128]{2,1,0:T(8,128)(2,1)} %get-tuple-element.46), channel_id=1, source_target_pairs={{0,4},{4,0},{8,12},{12,8},{16,20},{20,16},{24,28},{28,24},{1,5},{5... | collective-permute-start | bytes 737288 | tf_op jit(solution)/shard_map/ppermute | solution.py:271
  79.8 3.5 %collective-permute-start.13 = (f16[16,80,128]{2,1,0:T(8,128)(2,1)}, f16[16,80,128]{2,1,0:T(8,128)(2,1)S(1)}, u32[]{:S(2)}, u32[]{:S(2)}) collective-permute-start(f16[16,80,128]{2,1,0:T(8,128)(2,1)} %all-to-all-done.1), channel_id=1, source_target_pairs={{0,1},{1,0},{2,3},{3,2},{4,5},{5,4},{6,7},{7,6},{8,9},{9,8},{10,11... | collective-permute-start | bytes 983048 | tf_op jit(solution)/shard_map/ppermute | solution.py:261

commit v12 on v11

--- a/solution.py
+++ b/solution.py
@@ -38,7 +38,7 @@
             shifted[slot, :, :, pl.ds(q * cout, cout)] = whole[:, start : start + width].astype(jnp.bfloat16)
 
 
-def kernel_grad(par, f_own, f_par, d_own, d_par, d_near, d_far, left, right, keep, give, ext, shifted, acc):
+def kernel_both(par, w, f_own, f_par, d_own, d_par, d_near, d_far, left, right, keep, give, g_own, g_par, ext, shifted, acc):
     odd, core = (par[0], par[1])
     half, width, cout = d_own.shape
     cin = f_own.shape[2]
@@ -59,6 +59,14 @@
     size = keep.shape[0]
     keep[...] = acc[pl.ds(core * size, size), :]
     give[...] = acc[pl.ds((1 - core) * size, size), :]
+    for out, slot in ((g_own, own), (g_par, partner)):
+        total = None
+        for a in range(3):
+            lhs = shifted[slot + 1 - a].reshape(pixels, 3 * cout)
+            rhs = jnp.concatenate([w[a, 2 - q] for q in range(3)], axis=1)
+            term = lax.dot_general(lhs, rhs, (((1,), (1,)), ((), ())), preferred_element_type=jnp.float32)
+            total = term if total is None else total + term
+        out[...] = total.astype(jnp.bfloat16).reshape(half, width, cin)
 
 
 def kernel_scale(chunk, par, keep, given, out):
@@ -83,24 +91,6 @@
         total = term if total is None else total + term
     out[pl.ds(0, chunk), :] = total * (1.0 / chips)
     out[pl.ds(chunk, deep - chunk), :] = jnp.broadcast_to(highest, (deep - chunk, cout))
-
-
-def kernel_back(par, w, d_own, d_par, d_near, d_far, left, right, out_own, out_par, ext, shifted):
-    odd = par[0]
-    half, width, cout = d_own.shape
-    cin = w.shape[2]
-    pixels = half * width
-    gather_map(odd, (d_own, d_par, d_near, d_far), left, right, ext)
-    shift_columns(ext, shifted, width)
-    own, partner = slots(odd)[:2]
-    for out, slot in ((out_own, own), (out_par, partner)):
-        total = None
-        for a in range(3):
-            lhs = shifted[slot + 1 - a].reshape(pixels, 3 * cout)
-            rhs = jnp.concatenate([w[a, 2 - q] for q in range(3)], axis=1)
-            term = lax.dot_general(lhs, rhs, (((1,), (1,)), ((), ())), preferred_element_type=jnp.float32)
-            total = term if total is None else total + term
-        out[...] = total.astype(jnp.bfloat16).reshape(half, width, cin)
 
 
 def kernel_out(par, w, f_own, f_par, f_near, f_far, left, right, out_own, out_par, ext):
@@ -135,7 +125,7 @@
         in_specs=[pl.BlockSpec(memory_space=pltpu.SMEM)] + [whole] * (len(operands) - 1),
         out_specs=[whole] * len(outs),
         scratch_shapes=scratch,
-        compiler_params=pltpu.CompilerParams(vmem_limit_bytes=12 * 1024 * 1024),
+        compiler_params=pltpu.CompilerParams(vmem_limit_bytes=16 * 1024 * 1024),
         cost_estimate=pl.CostEstimate(flops=flops, bytes_accessed=size if flops else 0, transcendentals=0),
     )(*operands)
 
@@ -210,28 +200,23 @@
     f_far = lax.ppermute(f_par, "rows", far)
     d_blocks = (d_own, d_par, d_near, d_far)
     f_own, f_near = fence((f_own, f_near))
-    d_left, d_right = exchanged(*packed(par, d_blocks, flops), cols)
+    d_left, d_right = exchanged(*edges(d_blocks), cols)
 
     f_blocks = (f_own, f_par, f_near, f_far)
     part = jax.ShapeDtypeStruct((share, cout), jnp.float32)
-    d_maps = [VMEM((4, half, wide, cout), jnp.bfloat16), VMEM((4, half, width, 3 * cout), jnp.bfloat16)]
     half_grad = jax.ShapeDtypeStruct((half, width, cin), jnp.bfloat16)
-    g_own, g_par = call(
-        kernel_back,
-        (par, weight) + d_blocks + (d_left, d_right),
-        [half_grad, half_grad],
-        d_maps,
+    keep, give, g_own, g_par = call(
+        kernel_both,
+        (par, weight, f_own, f_par) + d_blocks + (d_left, d_right),
+        [part, part, half_grad, half_grad],
+        [
+            VMEM((4, half, wide, cout), jnp.bfloat16),
+            VMEM((4, half, width, 3 * cout), jnp.bfloat16),
+            VMEM((9 * cin, cout), jnp.float32),
+        ],
         30 * flops,
     )
     g_other = lax.ppermute(g_par, "rows", swap)
-    f_own, g_par = fence((f_own, g_par))
-    keep, give = call(
-        kernel_grad,
-        (par, f_own, f_par) + d_blocks + (d_left, d_right),
-        [part, part],
-        d_maps + [VMEM((9 * cin, cout), jnp.float32)],
-        0,
-    )
     given = lax.ppermute(give, "core", other_core)
     f_tails, f_heads = edges(f_blocks)
     given, f_tails, f_heads = fence((given, f_tails, f_heads))

time: 86.4 us -> 86 us (level)
  waiting for transfers between devices: 19.1 us -> 22.3 us
  Pallas kernels: 11.6 us -> 8.94 us
  local copies, waits for them, and re-layouts: 5.8 us -> 4.73 us
    pallas_call x6 -> x4, Pallas kernels: 11.6 us -> 8.94 us  [call(): pl.pallas_call(kernel, out_shape=outs, in_specs=[pl.BlockSpec(memory_spac...]
    ppermute x1, waiting for transfers between devices: 0.01 us -> 2.35 us  [body(): f_near = lax.ppermute(f_first, 'rows', near)]
    ppermute x1, starting transfers between devices: 2.63 us -> 0.3 us  [body(): given = lax.ppermute(give, 'core', other_core)]
    ppermute x1, waiting for transfers between devices: 0.01 us -> 1.73 us  [body(): f_far = lax.ppermute(f_par, 'rows', far)]
    all_to_all x1, starting transfers between devices: 7.05 us -> 8.58 us  [body(): got = lax.all_to_all(scaled, CHIPS, 0, 0)]
    unnamed x20 -> x14, local copies, waits for them, and re-layouts: 2.95 us -> 1.89 us
  transfers between devices with their start and end apart: 16 -> 16, of which waited for: 7 -> 8; matrix products, arithmetic and copies ran while one was open for 8% -> 9% of each run, Pallas kernels for 13% -> 10%
where the time goes in v12:
time: 86 us; the launch traced here: 85.2 us
  starting transfers between devices  39.6 us (46%)
  waiting for transfers between devices  22.3 us (26%)
  Pallas kernels  8.94 us (10%)
  other arithmetic  8.73 us (10%)
  local copies, waits for them, and re-layouts  4.73 us (6%)
  between operations  0.96 us (1%)
    pallas_call x4, Pallas kernels, call(): pl.pallas_call(kernel, out_shape=outs, in_specs=[pl.BlockSpec(memory_spac...  8.94 us
    all_to_all x1, starting transfers between devices, body(): got = lax.all_to_all(scaled, CHIPS, 0, 0)  8.58 us
    all_to_all x1, starting transfers between devices, body(): spread = lax.all_to_all(copies, CHIPS, 0, 0)  5.4 us
    all_to_all x1, waiting for transfers between devices, body(): got = lax.all_to_all(scaled, CHIPS, 0, 0)  4.97 us
    ppermute x1, starting transfers between devices, body(): f_far = lax.ppermute(f_par, 'rows', far)  4.42 us
    all_to_all x1, waiting for transfers between devices, body(): spread = lax.all_to_all(copies, CHIPS, 0, 0)  3.62 us
    ppermute x1, starting transfers between devices, body(): d_far = lax.ppermute(d_par, 'rows', far)  3.48 us
    ppermute x1, starting transfers between devices, body(): d_par = lax.ppermute(d_give, 'rows', swap)  3.03 us
  transfers between devices with their start and end apart: 16, of which 8 were waited for; matrix products, arithmetic and copies ran while one was open for 9% of the time, Pallas kernels for 10%

profile of v12, /device:TPU:0, one launch (start us, length us, event | category | flops | bytes accessed | tf_op | source)
XLA Modules:
  0.0 85.2 jit_solution(7635686786942399098)
XLA Ops:
  0.7 1.2 %constant_dynamic-slice_fusion.1 = (bf16[6,160,128]{2,1,0:T(8,128)(2,1)S(1)}, bf16[6,160,128]{2,1,0:T(8,128)(2,1)S(1)}) fusion(bf16[12,160,128]{2,1,0:T(8,128)(2,1)} %param.5, s32[]{:T(128)S(6)} %select_n.53, s32[]{:T(128)S(6)} %select_n.54), kind=kLoop, calls=%fused_computation.32 | loop fusion | bytes 983048 | tf_op jit(solution)/shard_map/dynamic_slice | solution.py:184
  1.8 3.0 %collective-permute-start = (bf16[6,160,128]{2,1,0:T(8,128)(2,1)S(1)}, bf16[6,160,128]{2,1,0:T(8,128)(2,1)S(1)}, u32[]{:S(2)}, u32[]{:S(2)}) collective-permute-start(bf16[6,160,128]{2,1,0:T(8,128)(2,1)S(1)} %get-tuple-element.64), channel_id=1, source_target_pairs={{0,4},{4,0},{8,12},{12,8},{16,20},{20,16},{24,28},{28,24},{1,5},{5... | collective-permute-start | bytes 737288 | tf_op jit(solution)/shard_map/ppermute | solution.py:194
  4.9 1.4 %collective-permute-start.1 = (bf16[6,160,128]{2,1,0:T(8,128)(2,1)S(1)}, bf16[6,160,128]{2,1,0:T(8,128)(2,1)S(1)}, u32[]{:S(2)}, u32[]{:S(2)}) collective-permute-start(bf16[6,160,128]{2,1,0:T(8,128)(2,1)S(1)} %get-tuple-element.63.d_own), channel_id=1, source_target_pairs={{4,12},{8,0},{12,20},{16,8},{20,28},{24,16},{5,13},{9,1},{13,21},{... | collective-permute-start | bytes 737288 | tf_op jit(solution)/shard_map/ppermute | solution.py:195
  6.3 0.1 constant_dynamic-slice_fusion
  6.4 2.8 %collective-permute-start.3 = (bf16[6,160,256]{2,1,0:T(8,128)(2,1)S(1)}, bf16[6,160,256]{2,1,0:T(8,128)(2,1)S(1)}, u32[]{:S(2)}, u32[]{:S(2)}) collective-permute-start(bf16[6,160,256]{2,1,0:T(8,128)(2,1)S(1)} %get-tuple-element.47), channel_id=1, source_target_pairs={{0,4},{4,0},{8,12},{12,8},{16,20},{20,16},{24,28},{28,24},{1,5},{5... | collective-permute-start | bytes 1474568 | tf_op jit(solution)/shard_map/ppermute | solution.py:196
  9.2 0.8 dynamic-slice_bitcast_fusion
  9.9 1.7 %collective-permute-done.d_par = bf16[6,160,128]{2,1,0:T(8,128)(2,1)S(1)} collective-permute-done((bf16[6,160,128]{2,1,0:T(8,128)(2,1)S(1)}, bf16[6,160,128]{2,1,0:T(8,128)(2,1)S(1)}, u32[]{:S(2)}, u32[]{:S(2)}) %collective-permute-start) | collective-permute-done | bytes 245792 | tf_op jit(solution)/shard_map/ppermute | solution.py:194
  11.7 2.6 %collective-permute-done.1.d_near = bf16[6,160,128]{2,1,0:T(8,128)(2,1)S(1)} collective-permute-done((bf16[6,160,128]{2,1,0:T(8,128)(2,1)S(1)}, bf16[6,160,128]{2,1,0:T(8,128)(2,1)S(1)}, u32[]{:S(2)}, u32[]{:S(2)}) %collective-permute-start.1) | collective-permute-done | bytes 245792 | tf_op jit(solution)/shard_map/ppermute | solution.py:195
  14.3 3.5 %collective-permute-start.5 = (bf16[6,160,128]{2,1,0:T(8,128)(2,1)S(1)}, bf16[6,160,128]{2,1,0:T(8,128)(2,1)S(1)}, u32[]{:S(2)}, u32[]{:S(2)}) collective-permute-start(bf16[6,160,128]{2,1,0:T(8,128)(2,1)S(1)} %collective-permute-done.d_par), channel_id=1, source_target_pairs={{12,4},{0,8},{20,12},{8,16},{28,20},{16,24},{13,5},{1,9},{21,13},{... | collective-permute-start | bytes 737288 | tf_op jit(solution)/shard_map/ppermute | solution.py:198
  17.8 0.1 pad_add_fusion.par
  17.9 1.3 %collective-permute-start.2 = (bf16[6,160,256]{2,1,0:T(8,128)(2,1)S(1)}, bf16[6,160,256]{2,1,0:T(8,128)(2,1)S(1)}, u32[]{:S(2)}, u32[]{:S(2)}) collective-permute-start(bf16[6,160,256]{2,1,0:T(8,128)(2,1)S(1)} %get-tuple-element.25.f_own), channel_id=1, source_target_pairs={{4,12},{8,0},{12,20},{16,8},{20,28},{24,16},{5,13},{9,1},{13,21},{... | collective-permute-start | bytes 1474568 | tf_op jit(solution)/shard_map/ppermute | solution.py:199
  19.2 2.6 %collective-permute-done.5.d_far = bf16[6,160,128]{2,1,0:T(8,128)(2,1)S(1)} collective-permute-done((bf16[6,160,128]{2,1,0:T(8,128)(2,1)S(1)}, bf16[6,160,128]{2,1,0:T(8,128)(2,1)S(1)}, u32[]{:S(2)}, u32[]{:S(2)}) %collective-permute-start.5) | collective-permute-done | bytes 245792 | tf_op jit(solution)/shard_map/ppermute | solution.py:198
  21.8 1.3 %collective-permute-start.6 = (bf16[4,6,16,128]{3,2,1,0:T(8,128)(2,1)S(1)}, bf16[4,6,16,128]{3,2,1,0:T(8,128)(2,1)S(1)}, u32[]{:S(2)}, u32[]{:S(2)}) collective-permute-start(bf16[4,6,16,128]{3,2,1,0:T(8,128)(2,1)S(1)} %pad_maximum_fusion.5), channel_id=1, source_target_pairs={{0,1},{1,2},{2,3},{4,5},{5,6},{6,7},{8,9},{9,10},{10,11},{12,13},{... | collective-permute-start | bytes 294920 | tf_op jit(solution)/shard_map/ppermute | solution.py:154
  23.1 1.3 %collective-permute-start.7 = (bf16[4,6,16,128]{3,2,1,0:T(8,128)(2,1)S(1)}, bf16[4,6,16,128]{3,2,1,0:T(8,128)(2,1)S(1)}, u32[]{:S(2)}, u32[]{:S(2)}) collective-permute-start(bf16[4,6,16,128]{3,2,1,0:T(8,128)(2,1)S(1)} %pad_maximum_fusion.6), channel_id=1, source_target_pairs={{1,0},{2,1},{3,2},{5,4},{6,5},{7,6},{9,8},{10,9},{11,10},{13,12},{... | collective-permute-start | bytes 294920 | tf_op jit(solution)/shard_map/ppermute | solution.py:155
  24.5 4.4 %collective-permute-start.4 = (bf16[6,160,256]{2,1,0:T(8,128)(2,1)S(1)}, bf16[6,160,256]{2,1,0:T(8,128)(2,1)S(1)}, u32[]{:S(2)}, u32[]{:S(2)}) collective-permute-start(bf16[6,160,256]{2,1,0:T(8,128)(2,1)S(1)} %collective-permute-done.3.f_par), channel_id=1, source_target_pairs={{12,4},{0,8},{20,12},{8,16},{28,20},{16,24},{13,5},{1,9},{21,13},{... | collective-permute-start | bytes 1474568 | tf_op jit(solution)/shard_map/ppermute | solution.py:200
  28.9 2.4 %collective-permute-done.2.f_near = bf16[6,160,256]{2,1,0:T(8,128)(2,1)S(1)} collective-permute-done((bf16[6,160,256]{2,1,0:T(8,128)(2,1)S(1)}, bf16[6,160,256]{2,1,0:T(8,128)(2,1)S(1)}, u32[]{:S(2)}, u32[]{:S(2)}) %collective-permute-start.2) | collective-permute-done | bytes 491552 | tf_op jit(solution)/shard_map/ppermute | solution.py:199
  31.3 0.0 copy-start.4
  31.3 0.9 %copy-done.4 = bf16[6,160,128]{2,1,0:T(8,128)(2,1)S(1)} copy-done((bf16[6,160,128]{2,1,0:T(8,128)(2,1)S(1)}, bf16[6,160,128]{2,1,0:T(8,128)(2,1)}, u32[]{:S(2)}) %copy-start.4) | copy-done | bytes 245784
  32.2 4.2 %shard_map.58 = (f32[1152,128]{1,0:T(8,128)S(1)}, f32[1152,128]{1,0:T(8,128)S(1)}, bf16[6,160,256]{2,1,0:T(8,128)(2,1)S(1)}, bf16[6,160,256]{2,1,0:T(8,128)(2,1)S(1)}) custom-call(s32[2]{0:T(128)S(1)} %pad_add_fusion.par, bf16[3,3,256,128]{3,2,1,0:T(8,128)(2,1)S(1)} %copy-done, bf16[6,160,256]{2,1,0:T(8,128)(2,1)S(1)} %get-tuple-element.25.f_own, ...), custom_call_target="tpu_custom_call" | custom-call | flops 33973862400 | bytes 4915208 | tf_op jit(solution)/shard_map/pallas_call | solution.py:122
  36.5 0.0 copy-start.5
  36.5 0.3 collective-permute-start.8
  36.8 1.7 %collective-permute-done.4.f_far = bf16[6,160,256]{2,1,0:T(8,128)(2,1)S(1)} collective-permute-done((bf16[6,160,256]{2,1,0:T(8,128)(2,1)S(1)}, bf16[6,160,256]{2,1,0:T(8,128)(2,1)S(1)}, u32[]{:S(2)}, u32[]{:S(2)}) %collective-permute-start.4) | collective-permute-done | bytes 491552 | tf_op jit(solution)/shard_map/ppermute | solution.py:200
  38.5 0.7 pad_maximum_fusion.3
  39.2 0.7 pad_maximum_fusion.4
  39.9 0.7 shard_map.59
  40.7 0.8 convert_element_type.21
  41.5 8.6 %all-to-all-start = ((f16[16,80,128]{2,1,0:T(8,128)(2,1)}), f16[16,80,128]{2,1,0:T(8,128)(2,1)}, u32[]{:S(2)}, u32[]{:S(2)}) async-start(f16[16,80,128]{2,1,0:T(8,128)(2,1)} %convert_element_type.21), calls=%async_computation | async-start | bytes 655360 | tf_op jit(solution)/shard_map/all_to_all | solution.py:232
  50.1 1.9 %collective-permute-start.12 = (bf16[6,160,256]{2,1,0:T(8,128)(2,1)}, bf16[6,160,256]{2,1,0:T(8,128)(2,1)}, u32[]{:S(2)}, u32[]{:S(2)}) collective-permute-start(bf16[6,160,256]{2,1,0:T(8,128)(2,1)} %copy-done.5), channel_id=1, source_target_pairs={{0,4},{4,0},{8,12},{12,8},{16,20},{20,16},{24,28},{28,24},{1,5},{5... | collective-permute-start | bytes 1474568 | tf_op jit(solution)/shard_map/ppermute | solution.py:219
  51.9 1.3 %collective-permute-start.9 = (bf16[4,6,16,256]{3,2,1,0:T(8,128)(2,1)}, bf16[4,6,16,256]{3,2,1,0:T(8,128)(2,1)S(1)}, u32[]{:S(2)}, u32[]{:S(2)}) collective-permute-start(bf16[4,6,16,256]{3,2,1,0:T(8,128)(2,1)} %pad_maximum_fusion.3), channel_id=1, source_target_pairs={{0,1},{1,2},{2,3},{4,5},{5,6},{6,7},{8,9},{9,10},{10,11},{12,13},{... | collective-permute-start | bytes 589832 | tf_op jit(solution)/shard_map/ppermute | solution.py:154
  53.2 1.3 %collective-permute-start.10 = (bf16[4,6,16,256]{3,2,1,0:T(8,128)(2,1)}, bf16[4,6,16,256]{3,2,1,0:T(8,128)(2,1)S(1)}, u32[]{:S(2)}, u32[]{:S(2)}) collective-permute-start(bf16[4,6,16,256]{3,2,1,0:T(8,128)(2,1)} %pad_maximum_fusion.4), channel_id=1, source_target_pairs={{1,0},{2,1},{3,2},{5,4},{6,5},{7,6},{9,8},{10,9},{11,10},{13,12},{... | collective-permute-start | bytes 589832 | tf_op jit(solution)/shard_map/ppermute | solution.py:155
  54.5 5.0 %all-to-all-done = f16[16,80,128]{2,1,0:T(8,128)(2,1)} async-done(((f16[16,80,128]{2,1,0:T(8,128)(2,1)}), f16[16,80,128]{2,1,0:T(8,128)(2,1)}, u32[]{:S(2)}, u32[]{:S(2)}) %all-to-all-start) | async-done | bytes 327712 | tf_op jit(solution)/shard_map/all_to_all | solution.py:232
  59.5 1.0 %convert_element_type.22.got = f32[16,80,128]{2,1,0:T(8,128)S(1)} convert(f16[16,80,128]{2,1,0:T(8,128)(2,1)} %all-to-all-done) | non-fusion elementwise | flops 163840 | bytes 983040 | tf_op jit(solution)/shard_map/convert_element_type | solution.py:238
  60.5 0.6 shard_map.60
  61.2 0.0 copy-start.1
  61.2 0.8 broadcast_in_dim.2
  62.0 5.4 %all-to-all-start.1 = ((f16[16,80,128]{2,1,0:T(8,128)(2,1)}), f16[16,80,128]{2,1,0:T(8,128)(2,1)}, u32[]{:S(2)}, u32[]{:S(2)}) async-start(f16[16,80,128]{2,1,0:T(8,128)(2,1)} %broadcast_in_dim.2), calls=%async_computation.1 | async-start | bytes 655360 | tf_op jit(solution)/shard_map/all_to_all | solution.py:245
  67.4 0.0 copy-start.2
  67.4 0.9 %copy-done.2 = bf16[4,6,16,256]{3,2,1,0:T(8,128)(2,1)S(1)} copy-done((bf16[4,6,16,256]{3,2,1,0:T(8,128)(2,1)S(1)}, bf16[4,6,16,256]{3,2,1,0:T(8,128)(2,1)}, u32[]{:S(2)}) %copy-start.2) | copy-done | bytes 196632
  68.3 3.4 %shard_map.61 = (bf16[6,160,128]{2,1,0:T(8,128)(2,1)S(1)}, bf16[6,160,128]{2,1,0:T(8,128)(2,1)}) custom-call(s32[2]{0:T(128)S(1)} %pad_add_fusion.par, bf16[3,3,256,128]{3,2,1,0:T(8,128)(2,1)S(1)} %copy-done, bf16[6,160,256]{2,1,0:T(8,128)(2,1)S(1)} %get-tuple-element.25.f_own, bf16[6,160,256]{2,1,0:T(8,128)(2,1)S(1)} %collective-permute-done.3.f_par, ...), custom_call_target="tpu_custom_call" | custom-call | tf_op jit(solution)/shard_map/pallas_call | solution.py:122
  71.7 1.9 %collective-permute-start.11 = (bf16[6,160,128]{2,1,0:T(8,128)(2,1)}, bf16[6,160,128]{2,1,0:T(8,128)(2,1)S(1)}, u32[]{:S(2)}, u32[]{:S(2)}) collective-permute-start(bf16[6,160,128]{2,1,0:T(8,128)(2,1)} %get-tuple-element.39), channel_id=1, source_target_pairs={{0,4},{4,0},{8,12},{12,8},{16,20},{20,16},{24,28},{28,24},{1,5},{5... | collective-permute-start | bytes 737288 | tf_op jit(solution)/shard_map/ppermute | solution.py:256
  73.6 1.2 %broadcast_select_fusion.1 = (bf16[6,160,256]{2,1,0:T(8,128)(2,1)S(1)}, bf16[6,160,256]{2,1,0:T(8,128)(2,1)S(1)}) fusion(bf16[6,160,256]{2,1,0:T(8,128)(2,1)} %collective-permute-done.12, bf16[6,160,256]{2,1,0:T(8,128)(2,1)S(1)} %get-tuple-element.43, pred[]{:T(512)S(6)} %eq.6), kind=kLoop, calls=%fused_computation.6 | loop fusion | flops 491520 | bytes 1966081 | tf_op jit(solution)/shard_map/jit(_where)/select_n | solution.py:160
  74.7 1.0 %pad_maximum_fusion.1 = bf16[12,160,256]{2,1,0:T(8,128)(2,1)} fusion(bf16[6,160,256]{2,1,0:T(8,128)(2,1)S(1)} %get-tuple-element.46, bf16[6,160,256]{2,1,0:T(8,128)(2,1)S(1)} %get-tuple-element.45), kind=kLoop, calls=%fused_computation.1 | loop fusion | flops 491520 | bytes 1966080 | tf_op jit(solution)/shard_map/concatenate | solution.py:162
  75.7 3.6 %all-to-all-done.1 = f16[16,80,128]{2,1,0:T(8,128)(2,1)} async-done(((f16[16,80,128]{2,1,0:T(8,128)(2,1)}), f16[16,80,128]{2,1,0:T(8,128)(2,1)}, u32[]{:S(2)}, u32[]{:S(2)}) %all-to-all-start.1) | async-done | bytes 327712 | tf_op jit(solution)/shard_map/all_to_all | solution.py:245
  79.4 2.6 %collective-permute-done.11 = bf16[6,160,128]{2,1,0:T(8,128)(2,1)S(1)} collective-permute-done((bf16[6,160,128]{2,1,0:T(8,128)(2,1)}, bf16[6,160,128]{2,1,0:T(8,128)(2,1)S(1)}, u32[]{:S(2)}, u32[]{:S(2)}) %collective-permute-start.11) | collective-permute-done | bytes 245792 | tf_op jit(solution)/shard_map/ppermute | solution.py:256
  82.0 0.1 broadcast_select_fusion.5
  82.0 0.8 pad_maximum_fusion.2
  82.9 1.1 %broadcast_select_fusion.3 = (f16[16,80,128]{2,1,0:T(8,128)(2,1)S(1)}, f16[16,80,128]{2,1,0:T(8,128)(2,1)S(1)}) fusion(f16[16,80,128]{2,1,0:T(8,128)(2,1)} %all-to-all-done.1, f16[16,80,128]{2,1,0:T(8,128)(2,1)S(1)} %collective-permute-done.13, pred[]{:T(512)S(6)} %eq.7), kind=kLoop, calls=%fused_computation.8 | loop fusion | flops 327680 | bytes 1310721 | tf_op jit(solution)/shard_map/jit(_where)/select_n | solution.py:261
  84.1 1.1 %pad_maximum_fusion = f32[2304,128]{1,0:T(8,128)} fusion(f32[1152,128]{1,0:T(8,128)S(1)} %bitcast.41, f32[1152,128]{1,0:T(8,128)S(1)} %bitcast.42), kind=kLoop, calls=%fused_computation | loop fusion | flops 294912 | bytes 2359296 | tf_op jit(solution)/shard_map/concatenate | solution.py:265
  (29 shorter events, 0.2 us)
Async XLA Ops:
  0.7 5.7 %copy-start.6 = (bf16[12,160,256]{2,1,0:T(8,128)(2,1)S(1)}, bf16[12,160,256]{2,1,0:T(8,128)(2,1)}, u32[]{:S(2)}) copy-start(bf16[12,160,256]{2,1,0:T(8,128)(2,1)} %param.3) | copy-start | bytes 2949124
  1.8 9.8 %collective-permute-start = (bf16[6,160,128]{2,1,0:T(8,128)(2,1)S(1)}, bf16[6,160,128]{2,1,0:T(8,128)(2,1)S(1)}, u32[]{:S(2)}, u32[]{:S(2)}) collective-permute-start(bf16[6,160,128]{2,1,0:T(8,128)(2,1)S(1)} %get-tuple-element.64), channel_id=1, source_target_pairs={{0,4},{4,0},{8,12},{12,8},{16,20},{20,16},{24,28},{28,24},{1,5},{5... | collective-permute-start | bytes 737288 | tf_op jit(solution)/shard_map/ppermute | solution.py:194
  4.9 26.4 %copy-start = (bf16[3,3,256,128]{3,2,1,0:T(8,128)(2,1)S(1)}, bf16[3,3,256,128]{3,2,1,0:T(8,128)(2,1)}, u32[]{:S(2)}) copy-start(bf16[3,3,256,128]{3,2,1,0:T(8,128)(2,1)} %w.3) | copy-start | bytes 1769476
  4.9 9.4 %collective-permute-start.1 = (bf16[6,160,128]{2,1,0:T(8,128)(2,1)S(1)}, bf16[6,160,128]{2,1,0:T(8,128)(2,1)S(1)}, u32[]{:S(2)}, u32[]{:S(2)}) collective-permute-start(bf16[6,160,128]{2,1,0:T(8,128)(2,1)S(1)} %get-tuple-element.63.d_own), channel_id=1, source_target_pairs={{4,12},{8,0},{12,20},{16,8},{20,28},{24,16},{5,13},{9,1},{13,21},{... | collective-permute-start | bytes 737288 | tf_op jit(solution)/shard_map/ppermute | solution.py:195
  6.4 18.1 %collective-permute-start.3 = (bf16[6,160,256]{2,1,0:T(8,128)(2,1)S(1)}, bf16[6,160,256]{2,1,0:T(8,128)(2,1)S(1)}, u32[]{:S(2)}, u32[]{:S(2)}) collective-permute-start(bf16[6,160,256]{2,1,0:T(8,128)(2,1)S(1)} %get-tuple-element.47), channel_id=1, source_target_pairs={{0,4},{4,0},{8,12},{12,8},{16,20},{20,16},{24,28},{28,24},{1,5},{5... | collective-permute-start | bytes 1474568 | tf_op jit(solution)/shard_map/ppermute | solution.py:196
  14.3 10.1 %copy-start.3 = (bf16[6,160,128]{2,1,0:T(8,128)(2,1)}, bf16[6,160,128]{2,1,0:T(8,128)(2,1)S(1)}, u32[]{:S(2)}) copy-start(bf16[6,160,128]{2,1,0:T(8,128)(2,1)S(1)} %collective-permute-done.1.d_near) | copy-start | bytes 737284
  14.3 7.5 %collective-permute-start.5 = (bf16[6,160,128]{2,1,0:T(8,128)(2,1)S(1)}, bf16[6,160,128]{2,1,0:T(8,128)(2,1)S(1)}, u32[]{:S(2)}, u32[]{:S(2)}) collective-permute-start(bf16[6,160,128]{2,1,0:T(8,128)(2,1)S(1)} %collective-permute-done.d_par), channel_id=1, source_target_pairs={{12,4},{0,8},{20,12},{8,16},{28,20},{16,24},{13,5},{1,9},{21,13},{... | collective-permute-start | bytes 737288 | tf_op jit(solution)/shard_map/ppermute | solution.py:198
  17.9 13.4 %collective-permute-start.2 = (bf16[6,160,256]{2,1,0:T(8,128)(2,1)S(1)}, bf16[6,160,256]{2,1,0:T(8,128)(2,1)S(1)}, u32[]{:S(2)}, u32[]{:S(2)}) collective-permute-start(bf16[6,160,256]{2,1,0:T(8,128)(2,1)S(1)} %get-tuple-element.25.f_own), channel_id=1, source_target_pairs={{4,12},{8,0},{12,20},{16,8},{20,28},{24,16},{5,13},{9,1},{13,21},{... | collective-permute-start | bytes 1474568 | tf_op jit(solution)/shard_map/ppermute | solution.py:199
  21.8 9.4 %collective-permute-start.6 = (bf16[4,6,16,128]{3,2,1,0:T(8,128)(2,1)S(1)}, bf16[4,6,16,128]{3,2,1,0:T(8,128)(2,1)S(1)}, u32[]{:S(2)}, u32[]{:S(2)}) collective-permute-start(bf16[4,6,16,128]{3,2,1,0:T(8,128)(2,1)S(1)} %pad_maximum_fusion.5), channel_id=1, source_target_pairs={{0,1},{1,2},{2,3},{4,5},{5,6},{6,7},{8,9},{9,10},{10,11},{12,13},{... | collective-permute-start | bytes 294920 | tf_op jit(solution)/shard_map/ppermute | solution.py:154
  23.1 8.1 %collective-permute-start.7 = (bf16[4,6,16,128]{3,2,1,0:T(8,128)(2,1)S(1)}, bf16[4,6,16,128]{3,2,1,0:T(8,128)(2,1)S(1)}, u32[]{:S(2)}, u32[]{:S(2)}) collective-permute-start(bf16[4,6,16,128]{3,2,1,0:T(8,128)(2,1)S(1)} %pad_maximum_fusion.6), channel_id=1, source_target_pairs={{1,0},{2,1},{3,2},{5,4},{6,5},{7,6},{9,8},{10,9},{11,10},{13,12},{... | collective-permute-start | bytes 294920 | tf_op jit(solution)/shard_map/ppermute | solution.py:155
  24.5 14.0 %collective-permute-start.4 = (bf16[6,160,256]{2,1,0:T(8,128)(2,1)S(1)}, bf16[6,160,256]{2,1,0:T(8,128)(2,1)S(1)}, u32[]{:S(2)}, u32[]{:S(2)}) collective-permute-start(bf16[6,160,256]{2,1,0:T(8,128)(2,1)S(1)} %collective-permute-done.3.f_par), channel_id=1, source_target_pairs={{12,4},{0,8},{20,12},{8,16},{28,20},{16,24},{13,5},{1,9},{21,13},{... | collective-permute-start | bytes 1474568 | tf_op jit(solution)/shard_map/ppermute | solution.py:200
  31.3 0.9 %copy-start.4 = (bf16[6,160,128]{2,1,0:T(8,128)(2,1)S(1)}, bf16[6,160,128]{2,1,0:T(8,128)(2,1)}, u32[]{:S(2)}) copy-start(bf16[6,160,128]{2,1,0:T(8,128)(2,1)} %copy-done.3) | copy-start | bytes 737284
  36.5 4.2 %copy-start.5 = (bf16[6,160,256]{2,1,0:T(8,128)(2,1)}, bf16[6,160,256]{2,1,0:T(8,128)(2,1)S(1)}, u32[]{:S(2)}) copy-start(bf16[6,160,256]{2,1,0:T(8,128)(2,1)S(1)} %get-tuple-element.41) | copy-start | bytes 1474564
  36.5 3.5 %collective-permute-start.8 = (f32[1152,128]{1,0:T(8,128)S(1)}, f32[1152,128]{1,0:T(8,128)S(1)}, u32[]{:S(2)}, u32[]{:S(2)}) collective-permute-start(f32[1152,128]{1,0:T(8,128)S(1)} %get-tuple-element.30), channel_id=1, source_target_pairs={{0,1},{1,0},{2,3},{3,2},{4,5},{5,4},{6,7},{7,6},{8,9},{9,8},{10,11... | collective-permute-start | bytes 1769480 | tf_op jit(solution)/shard_map/ppermute | solution.py:220
  41.5 18.0 %all-to-all-start = ((f16[16,80,128]{2,1,0:T(8,128)(2,1)}), f16[16,80,128]{2,1,0:T(8,128)(2,1)}, u32[]{:S(2)}, u32[]{:S(2)}) async-start(f16[16,80,128]{2,1,0:T(8,128)(2,1)} %convert_element_type.21), calls=%async_computation | async-start | bytes 655360 | tf_op jit(solution)/shard_map/all_to_all | solution.py:232
  50.1 23.5 %collective-permute-start.12 = (bf16[6,160,256]{2,1,0:T(8,128)(2,1)}, bf16[6,160,256]{2,1,0:T(8,128)(2,1)}, u32[]{:S(2)}, u32[]{:S(2)}) collective-permute-start(bf16[6,160,256]{2,1,0:T(8,128)(2,1)} %copy-done.5), channel_id=1, source_target_pairs={{0,4},{4,0},{8,12},{12,8},{16,20},{20,16},{24,28},{28,24},{1,5},{5... | collective-permute-start | bytes 1474568 | tf_op jit(solution)/shard_map/ppermute | solution.py:219
  51.9 9.2 %collective-permute-start.9 = (bf16[4,6,16,256]{3,2,1,0:T(8,128)(2,1)}, bf16[4,6,16,256]{3,2,1,0:T(8,128)(2,1)S(1)}, u32[]{:S(2)}, u32[]{:S(2)}) collective-permute-start(bf16[4,6,16,256]{3,2,1,0:T(8,128)(2,1)} %pad_maximum_fusion.3), channel_id=1, source_target_pairs={{0,1},{1,2},{2,3},{4,5},{5,6},{6,7},{8,9},{9,10},{10,11},{12,13},{... | collective-permute-start | bytes 589832 | tf_op jit(solution)/shard_map/ppermute | solution.py:154
  53.2 7.9 %collective-permute-start.10 = (bf16[4,6,16,256]{3,2,1,0:T(8,128)(2,1)}, bf16[4,6,16,256]{3,2,1,0:T(8,128)(2,1)S(1)}, u32[]{:S(2)}, u32[]{:S(2)}) collective-permute-start(bf16[4,6,16,256]{3,2,1,0:T(8,128)(2,1)} %pad_maximum_fusion.4), channel_id=1, source_target_pairs={{1,0},{2,1},{3,2},{5,4},{6,5},{7,6},{9,8},{10,9},{11,10},{13,12},{... | collective-permute-start | bytes 589832 | tf_op jit(solution)/shard_map/ppermute | solution.py:155
  61.2 6.2 %copy-start.1 = (bf16[4,6,16,256]{3,2,1,0:T(8,128)(2,1)}, bf16[4,6,16,256]{3,2,1,0:T(8,128)(2,1)S(1)}, u32[]{:S(2)}) copy-start(bf16[4,6,16,256]{3,2,1,0:T(8,128)(2,1)S(1)} %collective-permute-done.10.right) | copy-start | bytes 589828
  62.0 17.4 %all-to-all-start.1 = ((f16[16,80,128]{2,1,0:T(8,128)(2,1)}), f16[16,80,128]{2,1,0:T(8,128)(2,1)}, u32[]{:S(2)}, u32[]{:S(2)}) async-start(f16[16,80,128]{2,1,0:T(8,128)(2,1)} %broadcast_in_dim.2), calls=%async_computation.1 | async-start | bytes 655360 | tf_op jit(solution)/shard_map/all_to_all | solution.py:245
  67.4 0.9 %copy-start.2 = (bf16[4,6,16,256]{3,2,1,0:T(8,128)(2,1)S(1)}, bf16[4,6,16,256]{3,2,1,0:T(8,128)(2,1)}, u32[]{:S(2)}) copy-start(bf16[4,6,16,256]{3,2,1,0:T(8,128)(2,1)} %copy-done.1) | copy-start | bytes 589828
  71.7 10.3 %collective-permute-start.11 = (bf16[6,160,128]{2,1,0:T(8,128)(2,1)}, bf16[6,160,128]{2,1,0:T(8,128)(2,1)S(1)}, u32[]{:S(2)}, u32[]{:S(2)}) collective-permute-start(bf16[6,160,128]{2,1,0:T(8,128)(2,1)} %get-tuple-element.39), channel_id=1, source_target_pairs={{0,4},{4,0},{8,12},{12,8},{16,20},{20,16},{24,28},{28,24},{1,5},{5... | collective-permute-start | bytes 737288 | tf_op jit(solution)/shard_map/ppermute | solution.py:256
  79.4 3.5 %collective-permute-start.13 = (f16[16,80,128]{2,1,0:T(8,128)(2,1)}, f16[16,80,128]{2,1,0:T(8,128)(2,1)S(1)}, u32[]{:S(2)}, u32[]{:S(2)}) collective-permute-start(f16[16,80,128]{2,1,0:T(8,128)(2,1)} %all-to-all-done.1), channel_id=1, source_target_pairs={{0,1},{1,0},{2,3},{3,2},{4,5},{5,4},{6,7},{7,6},{8,9},{9,8},{10,11... | collective-permute-start | bytes 983048 | tf_op jit(solution)/shard_map/ppermute | solution.py:246

commit v13 on v12

--- a/solution.py
+++ b/solution.py
@@ -130,19 +130,6 @@
     )(*operands)
 
 
-def kernel_edges(par, *refs):
-    blocks, (tails, heads) = (refs[:-2], refs[-2:])
-    for place, block in enumerate(blocks):
-        tails[place] = block[:, pl.ds(block.shape[1] - STRIP, STRIP), :]
-        heads[place] = block[:, pl.ds(0, STRIP), :]
-
-
-def packed(par, blocks, flops):
-    half, _, depth = blocks[0].shape
-    strip = jax.ShapeDtypeStruct((len(blocks), half, STRIP, depth), jnp.bfloat16)
-    return call(kernel_edges, (par,) + blocks, [strip, strip], [], flops)
-
-
 def edges(blocks):
     width = blocks[0].shape[1]
     tails = jnp.stack([x[:, width - STRIP :] for x in blocks])
@@ -156,10 +143,9 @@
     return left, right
 
 
-def joined(odd, own, other):
-    low = jnp.where(odd == 1, other, own)
-    high = jnp.where(odd == 1, own, other)
-    return jnp.concatenate([low, high], axis=0)
+def paired(place, own, other):
+    lead = lax.broadcasted_iota(jnp.int32, (2,) + (1,) * own.ndim, 0)
+    return jnp.where(lead == place, own[None], other[None])
 
 
 def body(features, weight, cotangent):
@@ -257,15 +243,12 @@
 
     norm = chips / jnp.sqrt(jnp.float32(height * width * chips * 2))
 
-    def restored(low, high):
-        picked = jnp.where(core == 0, low, high)
-        factor = jnp.exp2(picked[:1, chunk : chunk + 1].astype(jnp.float32) - TOP) * norm
-        return (picked[:, :chunk].astype(jnp.float32) * factor).reshape(share, cout)
-
-    weight_grad = jnp.concatenate([restored(spread, other), restored(other, spread)], axis=0)
+    levels = paired(core, spread[:1, chunk : chunk + 1], other[:1, chunk : chunk + 1])
+    factor = jnp.exp2(levels.astype(jnp.float32) - TOP) * norm
+    weight_grad = paired(core, spread[:, :chunk], other[:, :chunk]).astype(jnp.float32) * factor
     return (
-        joined(odd, o_own, o_other),
-        joined(odd, g_own, g_other),
+        paired(odd, o_own, o_other).reshape(height, width, cout),
+        paired(odd, g_own, g_other).reshape(height, width, cin),
         weight_grad.reshape(weight.shape),
     )
 

time: 86 us -> 94.3 us (1.097)
  waiting for transfers between devices: 22.3 us -> 30.7 us
  local copies, waits for them, and re-layouts: 4.73 us -> 7.83 us
  starting transfers between devices: 39.6 us -> 37.3 us
  other arithmetic: 8.73 us -> 7.73 us
    ppermute x1, waiting for transfers between devices: 0.01 us -> 5.74 us  [body(): g_other = lax.ppermute(g_par, 'rows', swap)]
    concatenate x3 -> x0, other arithmetic: 2.94 us -> none  [the longest x2 1.85 us: joined(): return jnp.concatenate([low, high], axis=0)]
    all_to_all x1, waiting for transfers between devices: 4.97 us -> 6.83 us  [body(): got = lax.all_to_all(scaled, CHIPS, 0, 0)]
    ppermute x1, starting transfers between devices: 1.87 us -> 0.15 us  [body(): o_other = lax.ppermute(o_par, 'rows', swap)]
    all_to_all x1, waiting for transfers between devices: 3.62 us -> 5.27 us  [body(): spread = lax.all_to_all(copies, CHIPS, 0, 0)]
    mul x4 -> x2, other arithmetic: 0.1 us -> 1.37 us  [the longest x1 1.29 us: body(): paired(core, spread[:, :chunk], other[:, :chunk]).astype(jnp.float32)]
    broadcast_in_dim x0 -> x8, local copies, waits for them, and re-layouts: none -> 1.18 us  [paired(): return jnp.where(lead == place, own[None], other[None])]
    slice x0 -> x2, local copies, waits for them, and re-layouts: none -> 1.08 us  [the longest x1 1.02 us: body(): spread[:, :chunk]]
  transfers between devices with their start and end apart: 16 -> 16, of which waited for: 8 -> 9; matrix products, arithmetic and copies ran while one was open for 9% -> 9% of each run, Pallas kernels for 10% -> 9%
where the time goes in v13:
time: 94.3 us; the launch traced here: 93.5 us
  starting transfers between devices  37.3 us (40%)
  waiting for transfers between devices  30.7 us (33%)
  Pallas kernels  8.94 us (9%)
  local copies, waits for them, and re-layouts  7.83 us (8%)
  other arithmetic  7.73 us (8%)
    pallas_call x4, Pallas kernels, call(): pl.pallas_call(kernel, out_shape=outs, in_specs=[pl.BlockSpec(memory_spac...  8.94 us
    all_to_all x1, starting transfers between devices, body(): got = lax.all_to_all(scaled, CHIPS, 0, 0)  8.58 us
    all_to_all x1, waiting for transfers between devices, body(): got = lax.all_to_all(scaled, CHIPS, 0, 0)  6.83 us
    ppermute x1, waiting for transfers between devices, body(): g_other = lax.ppermute(g_par, 'rows', swap)  5.74 us
    all_to_all x1, waiting for transfers between devices, body(): spread = lax.all_to_all(copies, CHIPS, 0, 0)  5.27 us
    all_to_all x1, starting transfers between devices, body(): spread = lax.all_to_all(copies, CHIPS, 0, 0)  4.85 us
    ppermute x1, starting transfers between devices, body(): f_far = lax.ppermute(f_par, 'rows', far)  4.42 us
    ppermute x1, starting transfers between devices, body(): d_far = lax.ppermute(d_par, 'rows', far)  3.48 us
  transfers between devices with their start and end apart: 16, of which 9 were waited for; matrix products, arithmetic and copies ran while one was open for 9% of the time, Pallas kernels for 9%

profile of v13, /device:TPU:0, one launch (start us, length us, event | category | flops | bytes accessed | tf_op | source)
XLA Modules:
  0.0 93.5 jit_solution(5317246396588423782)
XLA Ops:
  0.7 1.2 %constant_dynamic-slice_fusion.1 = (bf16[6,160,128]{2,1,0:T(8,128)(2,1)S(1)}, bf16[6,160,128]{2,1,0:T(8,128)(2,1)S(1)}) fusion(bf16[12,160,128]{2,1,0:T(8,128)(2,1)} %param.5, s32[]{:T(128)S(6)} %select_n.40, s32[]{:T(128)S(6)} %select_n.41), kind=kLoop, calls=%fused_computation.24 | loop fusion | bytes 983048 | tf_op jit(solution)/shard_map/dynamic_slice | solution.py:170
  1.8 3.0 %collective-permute-start = (bf16[6,160,128]{2,1,0:T(8,128)(2,1)S(1)}, bf16[6,160,128]{2,1,0:T(8,128)(2,1)S(1)}, u32[]{:S(2)}, u32[]{:S(2)}) collective-permute-start(bf16[6,160,128]{2,1,0:T(8,128)(2,1)S(1)} %get-tuple-element.58), channel_id=1, source_target_pairs={{0,4},{4,0},{8,12},{12,8},{16,20},{20,16},{24,28},{28,24},{1,5},{5... | collective-permute-start | bytes 737288 | tf_op jit(solution)/shard_map/ppermute | solution.py:180
  4.9 1.4 %collective-permute-start.1 = (bf16[6,160,128]{2,1,0:T(8,128)(2,1)S(1)}, bf16[6,160,128]{2,1,0:T(8,128)(2,1)S(1)}, u32[]{:S(2)}, u32[]{:S(2)}) collective-permute-start(bf16[6,160,128]{2,1,0:T(8,128)(2,1)S(1)} %get-tuple-element.57.d_own), channel_id=1, source_target_pairs={{4,12},{8,0},{12,20},{16,8},{20,28},{24,16},{5,13},{9,1},{13,21},{... | collective-permute-start | bytes 737288 | tf_op jit(solution)/shard_map/ppermute | solution.py:181
  6.4 2.8 %collective-permute-start.3 = (bf16[6,160,256]{2,1,0:T(8,128)(2,1)S(1)}, bf16[6,160,256]{2,1,0:T(8,128)(2,1)S(1)}, u32[]{:S(2)}, u32[]{:S(2)}) collective-permute-start(bf16[6,160,256]{2,1,0:T(8,128)(2,1)S(1)} %get-tuple-element.45), channel_id=1, source_target_pairs={{0,4},{4,0},{8,12},{12,8},{16,20},{20,16},{24,28},{28,24},{1,5},{5... | collective-permute-start | bytes 1474568 | tf_op jit(solution)/shard_map/ppermute | solution.py:182
  9.2 0.8 dynamic-slice_bitcast_fusion
  9.9 1.7 %collective-permute-done.d_par = bf16[6,160,128]{2,1,0:T(8,128)(2,1)S(1)} collective-permute-done((bf16[6,160,128]{2,1,0:T(8,128)(2,1)S(1)}, bf16[6,160,128]{2,1,0:T(8,128)(2,1)S(1)}, u32[]{:S(2)}, u32[]{:S(2)}) %collective-permute-start) | collective-permute-done | bytes 245792 | tf_op jit(solution)/shard_map/ppermute | solution.py:180
  11.7 2.6 %collective-permute-done.1.d_near = bf16[6,160,128]{2,1,0:T(8,128)(2,1)S(1)} collective-permute-done((bf16[6,160,128]{2,1,0:T(8,128)(2,1)S(1)}, bf16[6,160,128]{2,1,0:T(8,128)(2,1)S(1)}, u32[]{:S(2)}, u32[]{:S(2)}) %collective-permute-start.1) | collective-permute-done | bytes 245792 | tf_op jit(solution)/shard_map/ppermute | solution.py:181
  14.3 3.5 %collective-permute-start.5 = (bf16[6,160,128]{2,1,0:T(8,128)(2,1)S(1)}, bf16[6,160,128]{2,1,0:T(8,128)(2,1)S(1)}, u32[]{:S(2)}, u32[]{:S(2)}) collective-permute-start(bf16[6,160,128]{2,1,0:T(8,128)(2,1)S(1)} %collective-permute-done.d_par), channel_id=1, source_target_pairs={{12,4},{0,8},{20,12},{8,16},{28,20},{16,24},{13,5},{1,9},{21,13},{... | collective-permute-start | bytes 737288 | tf_op jit(solution)/shard_map/ppermute | solution.py:184
  17.9 1.3 %collective-permute-start.2 = (bf16[6,160,256]{2,1,0:T(8,128)(2,1)S(1)}, bf16[6,160,256]{2,1,0:T(8,128)(2,1)S(1)}, u32[]{:S(2)}, u32[]{:S(2)}) collective-permute-start(bf16[6,160,256]{2,1,0:T(8,128)(2,1)S(1)} %get-tuple-element.25.f_own), channel_id=1, source_target_pairs={{4,12},{8,0},{12,20},{16,8},{20,28},{24,16},{5,13},{9,1},{13,21},{... | collective-permute-start | bytes 1474568 | tf_op jit(solution)/shard_map/ppermute | solution.py:185
  19.2 2.6 %collective-permute-done.5.d_far = bf16[6,160,128]{2,1,0:T(8,128)(2,1)S(1)} collective-permute-done((bf16[6,160,128]{2,1,0:T(8,128)(2,1)S(1)}, bf16[6,160,128]{2,1,0:T(8,128)(2,1)S(1)}, u32[]{:S(2)}, u32[]{:S(2)}) %collective-permute-start.5) | collective-permute-done | bytes 245792 | tf_op jit(solution)/shard_map/ppermute | solution.py:184
  21.8 1.3 %collective-permute-start.6 = (bf16[4,6,16,128]{3,2,1,0:T(8,128)(2,1)S(1)}, bf16[4,6,16,128]{3,2,1,0:T(8,128)(2,1)S(1)}, u32[]{:S(2)}, u32[]{:S(2)}) collective-permute-start(bf16[4,6,16,128]{3,2,1,0:T(8,128)(2,1)S(1)} %pad_maximum_fusion.2), channel_id=1, source_target_pairs={{0,1},{1,2},{2,3},{4,5},{5,6},{6,7},{8,9},{9,10},{10,11},{12,13},{... | collective-permute-start | bytes 294920 | tf_op jit(solution)/shard_map/ppermute | solution.py:141
  23.1 1.3 %collective-permute-start.7 = (bf16[4,6,16,128]{3,2,1,0:T(8,128)(2,1)S(1)}, bf16[4,6,16,128]{3,2,1,0:T(8,128)(2,1)S(1)}, u32[]{:S(2)}, u32[]{:S(2)}) collective-permute-start(bf16[4,6,16,128]{3,2,1,0:T(8,128)(2,1)S(1)} %pad_maximum_fusion.3), channel_id=1, source_target_pairs={{1,0},{2,1},{3,2},{5,4},{6,5},{7,6},{9,8},{10,9},{11,10},{13,12},{... | collective-permute-start | bytes 294920 | tf_op jit(solution)/shard_map/ppermute | solution.py:142
  24.5 4.4 %collective-permute-start.4 = (bf16[6,160,256]{2,1,0:T(8,128)(2,1)S(1)}, bf16[6,160,256]{2,1,0:T(8,128)(2,1)S(1)}, u32[]{:S(2)}, u32[]{:S(2)}) collective-permute-start(bf16[6,160,256]{2,1,0:T(8,128)(2,1)S(1)} %collective-permute-done.3.f_par), channel_id=1, source_target_pairs={{12,4},{0,8},{20,12},{8,16},{28,20},{16,24},{13,5},{1,9},{21,13},{... | collective-permute-start | bytes 1474568 | tf_op jit(solution)/shard_map/ppermute | solution.py:186
  28.9 2.4 %collective-permute-done.2.f_near = bf16[6,160,256]{2,1,0:T(8,128)(2,1)S(1)} collective-permute-done((bf16[6,160,256]{2,1,0:T(8,128)(2,1)S(1)}, bf16[6,160,256]{2,1,0:T(8,128)(2,1)S(1)}, u32[]{:S(2)}, u32[]{:S(2)}) %collective-permute-start.2) | collective-permute-done | bytes 491552 | tf_op jit(solution)/shard_map/ppermute | solution.py:185
  31.3 0.9 %copy-done.4 = bf16[6,160,128]{2,1,0:T(8,128)(2,1)S(1)} copy-done((bf16[6,160,128]{2,1,0:T(8,128)(2,1)S(1)}, bf16[6,160,128]{2,1,0:T(8,128)(2,1)}, u32[]{:S(2)}) %copy-start.4) | copy-done | bytes 245784
  32.2 4.2 %shard_map.58 = (f32[1152,128]{1,0:T(8,128)S(1)}, f32[1152,128]{1,0:T(8,128)S(1)}, bf16[6,160,256]{2,1,0:T(8,128)(2,1)S(1)}, bf16[6,160,256]{2,1,0:T(8,128)(2,1)S(1)}) custom-call(s32[2]{0:T(128)S(1)} %pad_add_fusion.par, bf16[3,3,256,128]{3,2,1,0:T(8,128)(2,1)S(1)} %copy-done, bf16[6,160,256]{2,1,0:T(8,128)(2,1)S(1)} %get-tuple-element.25.f_own, ...), custom_call_target="tpu_custom_call" | custom-call | flops 33973862400 | bytes 4915208 | tf_op jit(solution)/shard_map/pallas_call | solution.py:122
  36.5 0.8 copy-done.5
  37.2 0.2 collective-permute-start.8
  37.5 1.0 %collective-permute-done.4.f_far = bf16[6,160,256]{2,1,0:T(8,128)(2,1)S(1)} collective-permute-done((bf16[6,160,256]{2,1,0:T(8,128)(2,1)S(1)}, bf16[6,160,256]{2,1,0:T(8,128)(2,1)S(1)}, u32[]{:S(2)}, u32[]{:S(2)}) %collective-permute-start.4) | collective-permute-done | bytes 491552 | tf_op jit(solution)/shard_map/ppermute | solution.py:186
  38.5 0.7 pad_maximum_fusion
  39.2 0.7 pad_maximum_fusion.1
  39.9 0.7 shard_map.59
  40.7 0.8 convert_element_type.21
  41.4 8.6 %all-to-all-start = ((f16[16,80,128]{2,1,0:T(8,128)(2,1)}), f16[16,80,128]{2,1,0:T(8,128)(2,1)}, u32[]{:S(2)}, u32[]{:S(2)}) async-start(f16[16,80,128]{2,1,0:T(8,128)(2,1)} %convert_element_type.21), calls=%async_computation | async-start | bytes 655360 | tf_op jit(solution)/shard_map/all_to_all | solution.py:218
  50.0 1.3 %collective-permute-start.9 = (bf16[4,6,16,256]{3,2,1,0:T(8,128)(2,1)}, bf16[4,6,16,256]{3,2,1,0:T(8,128)(2,1)S(1)}, u32[]{:S(2)}, u32[]{:S(2)}) collective-permute-start(bf16[4,6,16,256]{3,2,1,0:T(8,128)(2,1)} %pad_maximum_fusion), channel_id=1, source_target_pairs={{0,1},{1,2},{2,3},{4,5},{5,6},{6,7},{8,9},{9,10},{10,11},{12,13},{... | collective-permute-start | bytes 589832 | tf_op jit(solution)/shard_map/ppermute | solution.py:141
  51.3 1.3 %collective-permute-start.10 = (bf16[4,6,16,256]{3,2,1,0:T(8,128)(2,1)}, bf16[4,6,16,256]{3,2,1,0:T(8,128)(2,1)S(1)}, u32[]{:S(2)}, u32[]{:S(2)}) collective-permute-start(bf16[4,6,16,256]{3,2,1,0:T(8,128)(2,1)} %pad_maximum_fusion.1), channel_id=1, source_target_pairs={{1,0},{2,1},{3,2},{5,4},{6,5},{7,6},{9,8},{10,9},{11,10},{13,12},{... | collective-permute-start | bytes 589832 | tf_op jit(solution)/shard_map/ppermute | solution.py:142
  52.6 6.8 %all-to-all-done = f16[16,80,128]{2,1,0:T(8,128)(2,1)} async-done(((f16[16,80,128]{2,1,0:T(8,128)(2,1)}), f16[16,80,128]{2,1,0:T(8,128)(2,1)}, u32[]{:S(2)}, u32[]{:S(2)}) %all-to-all-start) | async-done | bytes 327712 | tf_op jit(solution)/shard_map/all_to_all | solution.py:218
  59.5 1.0 %convert_element_type.22.got = f32[16,80,128]{2,1,0:T(8,128)S(1)} convert(f16[16,80,128]{2,1,0:T(8,128)(2,1)} %all-to-all-done) | non-fusion elementwise | flops 163840 | bytes 983040 | tf_op jit(solution)/shard_map/convert_element_type | solution.py:224
  60.5 0.6 shard_map.60
  61.1 0.8 broadcast_in_dim.137
  61.9 4.8 %all-to-all-start.1 = ((f16[16,80,128]{2,1,0:T(8,128)(2,1)}), f16[16,80,128]{2,1,0:T(8,128)(2,1)}, u32[]{:S(2)}, u32[]{:S(2)}) async-start(f16[16,80,128]{2,1,0:T(8,128)(2,1)} %broadcast_in_dim.137), calls=%async_computation.1 | async-start | bytes 655360 | tf_op jit(solution)/shard_map/all_to_all | solution.py:231
  66.8 1.9 %collective-permute-start.12 = (bf16[6,160,256]{2,1,0:T(8,128)(2,1)}, bf16[6,160,256]{2,1,0:T(8,128)(2,1)}, u32[]{:S(2)}, u32[]{:S(2)}) collective-permute-start(bf16[6,160,256]{2,1,0:T(8,128)(2,1)} %copy-done.5), channel_id=1, source_target_pairs={{0,4},{4,0},{8,12},{12,8},{16,20},{20,16},{24,28},{28,24},{1,5},{5... | collective-permute-start | bytes 1474568 | tf_op jit(solution)/shard_map/ppermute | solution.py:205
  68.7 0.9 copy-done.2
  69.7 3.4 %shard_map.61 = (bf16[6,160,128]{2,1,0:T(8,128)(2,1)S(1)}, bf16[6,160,128]{2,1,0:T(8,128)(2,1)}) custom-call(s32[2]{0:T(128)S(1)} %pad_add_fusion.par, bf16[3,3,256,128]{3,2,1,0:T(8,128)(2,1)S(1)} %copy-done, bf16[6,160,256]{2,1,0:T(8,128)(2,1)S(1)} %get-tuple-element.25.f_own, bf16[6,160,256]{2,1,0:T(8,128)(2,1)S(1)} %collective-permute-done.3.f_par, ...), custom_call_target="tpu_custom_call" | custom-call | tf_op jit(solution)/shard_map/pallas_call | solution.py:122
  73.0 0.1 collective-permute-start.11
  73.3 0.1 broadcast_in_dim.135
  73.4 5.3 %all-to-all-done.1 = f16[16,80,128]{2,1,0:T(8,128)(2,1)} async-done(((f16[16,80,128]{2,1,0:T(8,128)(2,1)}), f16[16,80,128]{2,1,0:T(8,128)(2,1)}, u32[]{:S(2)}, u32[]{:S(2)}) %all-to-all-start.1) | async-done | bytes 327712 | tf_op jit(solution)/shard_map/all_to_all | solution.py:231
  78.7 0.1 broadcast_in_dim.148
  78.8 5.7 %collective-permute-done.12 = bf16[6,160,256]{2,1,0:T(8,128)(2,1)} collective-permute-done((bf16[6,160,256]{2,1,0:T(8,128)(2,1)}, bf16[6,160,256]{2,1,0:T(8,128)(2,1)}, u32[]{:S(2)}, u32[]{:S(2)}) %collective-permute-start.12) | collective-permute-done | bytes 491552 | tf_op jit(solution)/shard_map/ppermute | solution.py:205
  84.6 2.1 %bitcast_select_fusion = bf16[12,160,256]{2,1,0:T(8,128)(2,1)} fusion(pred[12]{0:T(512)(128)(4,1)S(1)} %broadcast_in_dim.135, bf16[6,160,256]{2,1,0:T(8,128)(2,1)} %collective-permute-done.12, bf16[6,160,256]{2,1,0:T(8,128)(2,1)S(1)} %get-tuple-element.42), kind=kLoop, calls=%fused_computation.1 | loop fusion | flops 491520 | bytes 1966092 | tf_op jit(solution)/shard_map/jit(_where)/select_n | solution.py:148
  86.7 2.5 %collective-permute-done.11 = bf16[6,160,128]{2,1,0:T(8,128)(2,1)S(1)} collective-permute-done((bf16[6,160,128]{2,1,0:T(8,128)(2,1)}, bf16[6,160,128]{2,1,0:T(8,128)(2,1)S(1)}, u32[]{:S(2)}, u32[]{:S(2)}) %collective-permute-start.11) | collective-permute-done | bytes 245792 | tf_op jit(solution)/shard_map/ppermute | solution.py:242
  89.2 0.9 bitcast_select_fusion.1
  90.1 1.0 %slice.86 = f16[16,72,128]{2,1,0:T(8,128)(2,1)S(1)} slice(f16[16,80,128]{2,1,0:T(8,128)(2,1)} %all-to-all-done.1), slice={[0:16], [0:72], [0:128]} | slice | bytes 589824 | tf_op jit(solution)/shard_map/slice | solution.py:248
  91.1 0.7 slice_bitcast_fusion.15
  91.8 0.1 exponential_multiply_fusion
  92.0 0.1 broadcast_in_dim.150
  92.1 0.1 broadcast_in_dim.152
  92.2 1.3 %convert_multiply_fusion = f32[3,3,256,128]{3,2,1,0:T(8,128)} fusion(f32[3,3,256,128]{3,2,1,0:T(8,128)S(1)} %bitcast.49, f16[3,3,256,128]{3,2,1,0:T(8,128)(2,1)S(1)} %bitcast.50, f16[3,3,256,128]{3,2,1,0:T(8,128)(2,1)S(1)} %bitcast.51, pred[3,3,256]{2,1,0:T(4,128)(4,1)S(1)} %broadcast_in_dim.148), kind=kLoop, calls=%fused_computation | loop fusion | flops 884736 | bytes 3541248 | tf_op jit(solution)/shard_map/mul | solution.py:248
  (36 shorter events, 0.6 us)
Async XLA Ops:
  0.6 5.7 %copy-start.6 = (bf16[12,160,256]{2,1,0:T(8,128)(2,1)S(1)}, bf16[12,160,256]{2,1,0:T(8,128)(2,1)}, u32[]{:S(2)}) copy-start(bf16[12,160,256]{2,1,0:T(8,128)(2,1)} %param.3) | copy-start | bytes 2949124
  1.8 9.8 %collective-permute-start = (bf16[6,160,128]{2,1,0:T(8,128)(2,1)S(1)}, bf16[6,160,128]{2,1,0:T(8,128)(2,1)S(1)}, u32[]{:S(2)}, u32[]{:S(2)}) collective-permute-start(bf16[6,160,128]{2,1,0:T(8,128)(2,1)S(1)} %get-tuple-element.58), channel_id=1, source_target_pairs={{0,4},{4,0},{8,12},{12,8},{16,20},{20,16},{24,28},{28,24},{1,5},{5... | collective-permute-start | bytes 737288 | tf_op jit(solution)/shard_map/ppermute | solution.py:180
  4.9 26.4 %copy-start = (bf16[3,3,256,128]{3,2,1,0:T(8,128)(2,1)S(1)}, bf16[3,3,256,128]{3,2,1,0:T(8,128)(2,1)}, u32[]{:S(2)}) copy-start(bf16[3,3,256,128]{3,2,1,0:T(8,128)(2,1)} %w.3) | copy-start | bytes 1769476
  4.9 9.4 %collective-permute-start.1 = (bf16[6,160,128]{2,1,0:T(8,128)(2,1)S(1)}, bf16[6,160,128]{2,1,0:T(8,128)(2,1)S(1)}, u32[]{:S(2)}, u32[]{:S(2)}) collective-permute-start(bf16[6,160,128]{2,1,0:T(8,128)(2,1)S(1)} %get-tuple-element.57.d_own), channel_id=1, source_target_pairs={{4,12},{8,0},{12,20},{16,8},{20,28},{24,16},{5,13},{9,1},{13,21},{... | collective-permute-start | bytes 737288 | tf_op jit(solution)/shard_map/ppermute | solution.py:181
  6.4 18.1 %collective-permute-start.3 = (bf16[6,160,256]{2,1,0:T(8,128)(2,1)S(1)}, bf16[6,160,256]{2,1,0:T(8,128)(2,1)S(1)}, u32[]{:S(2)}, u32[]{:S(2)}) collective-permute-start(bf16[6,160,256]{2,1,0:T(8,128)(2,1)S(1)} %get-tuple-element.45), channel_id=1, source_target_pairs={{0,4},{4,0},{8,12},{12,8},{16,20},{20,16},{24,28},{28,24},{1,5},{5... | collective-permute-start | bytes 1474568 | tf_op jit(solution)/shard_map/ppermute | solution.py:182
  14.3 10.1 %copy-start.3 = (bf16[6,160,128]{2,1,0:T(8,128)(2,1)}, bf16[6,160,128]{2,1,0:T(8,128)(2,1)S(1)}, u32[]{:S(2)}) copy-start(bf16[6,160,128]{2,1,0:T(8,128)(2,1)S(1)} %collective-permute-done.1.d_near) | copy-start | bytes 737284
  14.3 7.5 %collective-permute-start.5 = (bf16[6,160,128]{2,1,0:T(8,128)(2,1)S(1)}, bf16[6,160,128]{2,1,0:T(8,128)(2,1)S(1)}, u32[]{:S(2)}, u32[]{:S(2)}) collective-permute-start(bf16[6,160,128]{2,1,0:T(8,128)(2,1)S(1)} %collective-permute-done.d_par), channel_id=1, source_target_pairs={{12,4},{0,8},{20,12},{8,16},{28,20},{16,24},{13,5},{1,9},{21,13},{... | collective-permute-start | bytes 737288 | tf_op jit(solution)/shard_map/ppermute | solution.py:184
  17.9 13.4 %collective-permute-start.2 = (bf16[6,160,256]{2,1,0:T(8,128)(2,1)S(1)}, bf16[6,160,256]{2,1,0:T(8,128)(2,1)S(1)}, u32[]{:S(2)}, u32[]{:S(2)}) collective-permute-start(bf16[6,160,256]{2,1,0:T(8,128)(2,1)S(1)} %get-tuple-element.25.f_own), channel_id=1, source_target_pairs={{4,12},{8,0},{12,20},{16,8},{20,28},{24,16},{5,13},{9,1},{13,21},{... | collective-permute-start | bytes 1474568 | tf_op jit(solution)/shard_map/ppermute | solution.py:185
  21.8 9.4 %collective-permute-start.6 = (bf16[4,6,16,128]{3,2,1,0:T(8,128)(2,1)S(1)}, bf16[4,6,16,128]{3,2,1,0:T(8,128)(2,1)S(1)}, u32[]{:S(2)}, u32[]{:S(2)}) collective-permute-start(bf16[4,6,16,128]{3,2,1,0:T(8,128)(2,1)S(1)} %pad_maximum_fusion.2), channel_id=1, source_target_pairs={{0,1},{1,2},{2,3},{4,5},{5,6},{6,7},{8,9},{9,10},{10,11},{12,13},{... | collective-permute-start | bytes 294920 | tf_op jit(solution)/shard_map/ppermute | solution.py:141
  23.1 8.1 %collective-permute-start.7 = (bf16[4,6,16,128]{3,2,1,0:T(8,128)(2,1)S(1)}, bf16[4,6,16,128]{3,2,1,0:T(8,128)(2,1)S(1)}, u32[]{:S(2)}, u32[]{:S(2)}) collective-permute-start(bf16[4,6,16,128]{3,2,1,0:T(8,128)(2,1)S(1)} %pad_maximum_fusion.3), channel_id=1, source_target_pairs={{1,0},{2,1},{3,2},{5,4},{6,5},{7,6},{9,8},{10,9},{11,10},{13,12},{... | collective-permute-start | bytes 294920 | tf_op jit(solution)/shard_map/ppermute | solution.py:142
  24.5 14.0 %collective-permute-start.4 = (bf16[6,160,256]{2,1,0:T(8,128)(2,1)S(1)}, bf16[6,160,256]{2,1,0:T(8,128)(2,1)S(1)}, u32[]{:S(2)}, u32[]{:S(2)}) collective-permute-start(bf16[6,160,256]{2,1,0:T(8,128)(2,1)S(1)} %collective-permute-done.3.f_par), channel_id=1, source_target_pairs={{12,4},{0,8},{20,12},{8,16},{28,20},{16,24},{13,5},{1,9},{21,13},{... | collective-permute-start | bytes 1474568 | tf_op jit(solution)/shard_map/ppermute | solution.py:186
  31.3 0.9 %copy-start.4 = (bf16[6,160,128]{2,1,0:T(8,128)(2,1)S(1)}, bf16[6,160,128]{2,1,0:T(8,128)(2,1)}, u32[]{:S(2)}) copy-start(bf16[6,160,128]{2,1,0:T(8,128)(2,1)} %copy-done.3) | copy-start | bytes 737284
  36.4 0.8 copy-start.5
  37.2 2.7 %collective-permute-start.8 = (f32[1152,128]{1,0:T(8,128)S(1)}, f32[1152,128]{1,0:T(8,128)S(1)}, u32[]{:S(2)}, u32[]{:S(2)}) collective-permute-start(f32[1152,128]{1,0:T(8,128)S(1)} %get-tuple-element.30), channel_id=1, source_target_pairs={{0,1},{1,0},{2,3},{3,2},{4,5},{5,4},{6,7},{7,6},{8,9},{9,8},{10,11... | collective-permute-start | bytes 1769480 | tf_op jit(solution)/shard_map/ppermute | solution.py:206
  41.4 18.0 %all-to-all-start = ((f16[16,80,128]{2,1,0:T(8,128)(2,1)}), f16[16,80,128]{2,1,0:T(8,128)(2,1)}, u32[]{:S(2)}, u32[]{:S(2)}) async-start(f16[16,80,128]{2,1,0:T(8,128)(2,1)} %convert_element_type.21), calls=%async_computation | async-start | bytes 655360 | tf_op jit(solution)/shard_map/all_to_all | solution.py:218
  50.0 11.1 %collective-permute-start.9 = (bf16[4,6,16,256]{3,2,1,0:T(8,128)(2,1)}, bf16[4,6,16,256]{3,2,1,0:T(8,128)(2,1)S(1)}, u32[]{:S(2)}, u32[]{:S(2)}) collective-permute-start(bf16[4,6,16,256]{3,2,1,0:T(8,128)(2,1)} %pad_maximum_fusion), channel_id=1, source_target_pairs={{0,1},{1,2},{2,3},{4,5},{5,6},{6,7},{8,9},{9,10},{10,11},{12,13},{... | collective-permute-start | bytes 589832 | tf_op jit(solution)/shard_map/ppermute | solution.py:141
  51.3 9.8 %collective-permute-start.10 = (bf16[4,6,16,256]{3,2,1,0:T(8,128)(2,1)}, bf16[4,6,16,256]{3,2,1,0:T(8,128)(2,1)S(1)}, u32[]{:S(2)}, u32[]{:S(2)}) collective-permute-start(bf16[4,6,16,256]{3,2,1,0:T(8,128)(2,1)} %pad_maximum_fusion.1), channel_id=1, source_target_pairs={{1,0},{2,1},{3,2},{5,4},{6,5},{7,6},{9,8},{10,9},{11,10},{13,12},{... | collective-permute-start | bytes 589832 | tf_op jit(solution)/shard_map/ppermute | solution.py:142
  61.1 5.7 %copy-start.1 = (bf16[4,6,16,256]{3,2,1,0:T(8,128)(2,1)}, bf16[4,6,16,256]{3,2,1,0:T(8,128)(2,1)S(1)}, u32[]{:S(2)}) copy-start(bf16[4,6,16,256]{3,2,1,0:T(8,128)(2,1)S(1)} %collective-permute-done.10.right) | copy-start | bytes 589828
  61.9 16.7 %all-to-all-start.1 = ((f16[16,80,128]{2,1,0:T(8,128)(2,1)}), f16[16,80,128]{2,1,0:T(8,128)(2,1)}, u32[]{:S(2)}, u32[]{:S(2)}) async-start(f16[16,80,128]{2,1,0:T(8,128)(2,1)} %broadcast_in_dim.137), calls=%async_computation.1 | async-start | bytes 655360 | tf_op jit(solution)/shard_map/all_to_all | solution.py:231
  66.8 17.8 %collective-permute-start.12 = (bf16[6,160,256]{2,1,0:T(8,128)(2,1)}, bf16[6,160,256]{2,1,0:T(8,128)(2,1)}, u32[]{:S(2)}, u32[]{:S(2)}) collective-permute-start(bf16[6,160,256]{2,1,0:T(8,128)(2,1)} %copy-done.5), channel_id=1, source_target_pairs={{0,4},{4,0},{8,12},{12,8},{16,20},{20,16},{24,28},{28,24},{1,5},{5... | collective-permute-start | bytes 1474568 | tf_op jit(solution)/shard_map/ppermute | solution.py:205
  68.7 0.9 copy-start.2
  73.0 16.2 %collective-permute-start.11 = (bf16[6,160,128]{2,1,0:T(8,128)(2,1)}, bf16[6,160,128]{2,1,0:T(8,128)(2,1)S(1)}, u32[]{:S(2)}, u32[]{:S(2)}) collective-permute-start(bf16[6,160,128]{2,1,0:T(8,128)(2,1)} %get-tuple-element.40), channel_id=1, source_target_pairs={{0,4},{4,0},{8,12},{12,8},{16,20},{20,16},{24,28},{28,24},{1,5},{5... | collective-permute-start | bytes 737288 | tf_op jit(solution)/shard_map/ppermute | solution.py:242
  78.6 13.2 %collective-permute-start.13 = (f16[16,80,128]{2,1,0:T(8,128)(2,1)}, f16[16,80,128]{2,1,0:T(8,128)(2,1)S(1)}, u32[]{:S(2)}, u32[]{:S(2)}) collective-permute-start(f16[16,80,128]{2,1,0:T(8,128)(2,1)} %all-to-all-done.1), channel_id=1, source_target_pairs={{0,1},{1,0},{2,3},{3,2},{4,5},{5,4},{6,7},{7,6},{8,9},{9,8},{10,11... | collective-permute-start | bytes 983048 | tf_op jit(solution)/shard_map/ppermute | solution.py:232
